TPU v7x, 512 devices: a whole 4x8x8 slice. The times are simulated.
512 devices in a mesh: dp: 64 (over x, y, z_hi), tensor: 8 (over z_lo, core).
Axes of the slice: x: 4, y: 8, z: 8 (z_hi: 2, z_lo: 4; z = z_hi * 4 + z_lo), core: 2. Of those that a mesh axis runs over, the one named last changes fastest.
Arguments:
- layer_input: bfloat16 [8192, 8192], P('dp', 'tensor'), may hold values from -60 to 60
- residual_grad: bfloat16 [8192, 8192], P('dp', 'tensor'), may hold values from -4 to 4
- key_value_grad: bfloat16 [8192, 1024], P('dp', 'tensor'), may hold values from -12 to 12
- kv_weight: bfloat16 [1024, 8192], P('tensor', 'dp'), may hold values from -0.0625 to 0.0625
- norm_gain: float32 [8192], P('tensor'), may hold values from 0.1 to 1.9
Outputs:
- input_grad: bfloat16 [8192, 8192], P('dp', 'tensor')
- weight_grad: float32 [1024, 8192], P('tensor', 'dp')
- gain_grad: float32 [8192], P('tensor')
All inputs are finite; a program needn't handle non-finite values.
Results may differ from a plain program's by a relative error of at most 0.0039.
Values may be sent and summed in bfloat16 or wider, within the bound.
No kernel may reach another device: no remote copies, remote signals or barrier semaphores. Data moves between devices by JAX's collectives and lax.ppermute only.
A program may use at most 64 MiB of HBM per device.

v0:
```python
import jax
import jax.numpy as jnp
from jax import lax
from jax.sharding import PartitionSpec as P

D = 8192
HD = 128


rope_theta = 500000.0
norm_eps = 1e-05


def rope_tables(positions_count, head_size):
    half_head = head_size // 2
    frequency = rope_theta ** (-(jnp.arange(half_head, dtype=jnp.float32) * 2.0 / head_size))
    angles = jnp.arange(positions_count, dtype=jnp.float32)[:, None] * frequency[None, :]
    return (jnp.cos(angles), jnp.sin(angles))


def unrotate(grads, cosine, sine):
    half_head = grads.shape[-1] // 2
    lower_part = grads[..., :half_head]
    upper_part = grads[..., half_head:]
    return jnp.concatenate(
        [lower_part * cosine + upper_part * sine, upper_part * cosine - lower_part * sine], axis=-1
    )


def shards(layer_input, residual_grad, key_value_grad, kv_weight, norm_gain):
    token_count = key_value_grad.shape[0]
    local_cols = key_value_grad.shape[1]
    feature_count = layer_input.shape[1]
    block_count = local_cols // HD
    members = lax.axis_size("tensor")
    member_idx = lax.axis_index("tensor")
    cosine, sine = rope_tables(token_count, HD)
    blocks = key_value_grad.astype(jnp.float32).reshape(token_count, block_count, HD)
    turned = unrotate(blocks, cosine[:, None, :], sine[:, None, :])
    first_block = member_idx * block_count
    is_key = ((first_block + jnp.arange(block_count)) % 2 == 0)[None, :, None]
    kv_pre = jnp.where(is_key, turned, blocks).reshape(token_count, local_cols).astype(jnp.bfloat16)
    widened = layer_input.astype(jnp.float32)
    square_part = jnp.sum(widened * widened, axis=1)
    square_total = lax.psum(square_part, "tensor")
    inv_scale = lax.rsqrt(square_total[:, None] / D + norm_eps)
    normal = widened * inv_scale
    normed = (normal * norm_gain[None, :]).astype(jnp.bfloat16)
    gathered = lax.all_gather(normed, "tensor", axis=1, tiled=True)
    partial_value = jnp.dot(
        kv_pre,
        lax.all_gather(kv_weight, "dp", axis=1, tiled=True),
        preferred_element_type=jnp.float32,
    ).astype(jnp.bfloat16)
    pieces = partial_value.reshape(token_count, members, feature_count)
    arrived = lax.all_to_all(pieces, "tensor", split_axis=1, concat_axis=1, tiled=True)
    norm_grad = jnp.sum(arrived.astype(jnp.float32), axis=1)
    scaled = norm_gain[None, :] * norm_grad
    inner_part = jnp.sum(scaled * normal, axis=1)
    inner = lax.psum(inner_part, "tensor")[:, None] / D
    input_grad = (residual_grad.astype(jnp.float32) + inv_scale * (scaled - normal * inner)).astype(
        jnp.bfloat16
    )
    scattered = lax.psum_scatter(
        lax.dot_general(
            gathered, kv_pre, (((0,), (0,)), ((), ())), preferred_element_type=jnp.float32
        ),
        "dp",
        scatter_dimension=0,
        tiled=True,
    )
    weight_grad = scattered.T
    gain_part = jnp.sum(norm_grad * normal, axis=0)
    gain_grad = lax.psum(gain_part, "dp")
    return (input_grad, weight_grad, gain_grad)


def solution(mesh):
    return jax.shard_map(
        shards,
        mesh=mesh,
        in_specs=(
            P("dp", "tensor"),
            P("dp", "tensor"),
            P("dp", "tensor"),
            P("tensor", "dp"),
            P("tensor"),
        ),
        out_specs=(P("dp", "tensor"), P("tensor", "dp"), P("tensor")),
        check_vma=False,
    )
```

profile of v0, /device:TPU:64, one launch (start us, length us, event | category | flops | bytes accessed | tf_op | source)
XLA Modules:
  0.0 714.9 jit_solution(9119424642721960501)
XLA Ops:
  7.2 0.0 all-gather.3.cloned.1.call-start
  7.2 0.7 all-gather.3.cloned.1.call-update
  7.9 0.8 convert_bitcast_fusion
  8.7 0.3 add_bitcast_fusion
  9.0 0.8 fusion.12
  9.8 140.2 %all-gather.3.cloned.1.call-done = bf16[128,8192]{1,0:T(8,128)(2,1)} async-done(((bf16[128,128]{1,0:T(8,128)(2,1)}), bf16[128,8192]{1,0:T(8,128)(2,1)}) %all-gather.3.cloned.1.call-update) | async-done | bytes 2097168 | tf_op jit(solution)/shard_map/all_gather | solution.py:52
  150.0 2.3 convolution_convert_fusion
  152.3 1.5 copy.13
  153.8 0.0 copy-start
  153.8 5.5 all-to-all-start
  159.3 0.0 copy-start.2
  159.3 0.0 all-gather.5.cloned.1.call-start
  159.3 0.0 copy-done
  159.4 0.1 fusion.11
  159.5 52.5 %psum.21 = f32[128]{0:T(128)S(1)} all-reduce(f32[128]{0:T(128)S(1)} %fusion.11), channel_id=1, replica_groups=mesh['dp'=64,'tensor'=8] {'tensor'}, use_global_device_ids=true, to_apply=%region_1.2 | all-reduce | flops 128 | bytes 1024 | tf_op jit(solution)/shard_map/psum | solution.py:45
  212.0 0.0 all-to-all-done
  212.1 0.3 convert_reduce_fusion
  212.4 0.0 copy-done.2
  212.4 0.9 fusion.10
  213.3 0.0 all-gather.5.cloned.1.call-update
  213.4 0.0 reduce-scatter.2.cloned.1.call-start
  213.4 35.2 %all-gather.5.cloned.1.call-done = bf16[128,8192]{1,0:T(8,128)(2,1)} async-done(((bf16[128,1024]{1,0:T(8,128)(2,1)}), bf16[128,8192]{1,0:T(8,128)(2,1)}) %all-gather.5.cloned.1.call-update) | async-done | bytes 2097168 | tf_op jit(solution)/shard_map/all_gather | solution.py:49
  248.6 4.3 fusion.15
  252.9 0.0 copy-start.1
  252.9 0.0 reduce-scatter.2.cloned.1.call-update
  252.9 15.2 %psum.22 = f32[128]{0:T(128)S(1)} all-reduce(f32[128]{0:T(128)S(1)} %get-tuple-element.10), channel_id=1, replica_groups=mesh['dp'=64,'tensor'=8] {'tensor'}, use_global_device_ids=true, to_apply=%region_4.5 | all-reduce | flops 128 | bytes 1024 | tf_op jit(solution)/shard_map/psum | solution.py:60
  268.1 224.9 %psum.23 = f32[1024]{0:T(1024)} all-reduce(f32[1024]{0:T(1024)S(1)} %get-tuple-element.9), channel_id=1, replica_groups=mesh['dp'=64,'tensor'=8] {'dp'}, use_global_device_ids=true, to_apply=%region_7.8 | all-reduce | flops 1024 | bytes 8192 | tf_op jit(solution)/shard_map/psum | solution.py:74
  492.9 0.0 copy-done.1
  492.9 1.0 fusion.8
  493.9 212.9 %reduce-scatter.2.cloned.1.call-done = f32[128,128]{1,0:T(8,128)} async-done(((f32[8192,128]{1,0:T(8,128)}), f32[128,128]{1,0:T(8,128)}) %reduce-scatter.2.cloned.1.call-update) | async-done | bytes 65552 | tf_op jit(solution)/shard_map/reduce_scatter | solution.py:64
  706.8 1.6 copy.10
  (3 shorter events, 0.0 us)
Async XLA Ops:
  7.2 142.8 %all-gather.3.cloned.1.call-start = ((), (), s32[]{:S(2)}) async-start(), calls=%async_computation.2 | async-start | bytes 2129920 | tf_op jit(solution)/shard_map/all_gather | solution.py:52
  153.8 5.6 copy-start
  153.8 58.3 %all-to-all-start = ((bf16[128,8,1024]{2,0,1:T(8,128)(2,1)}), bf16[128,8,1024]{2,0,1:T(8,128)(2,1)S(1)}, u32[]{:S(2)}, u32[]{:S(2)}) async-start(bf16[128,8,1024]{2,0,1:T(8,128)(2,1)} %bitcast.17), calls=%async_computation | async-start | bytes 4194304 | tf_op jit(solution)/shard_map/all_to_all | solution.py:56
  159.3 53.1 %copy-start.2 = (f32[1024]{0:T(1024)S(1)}, f32[1024]{0:T(1024)}, u32[]{:S(2)}) copy-start(f32[1024]{0:T(1024)} %param.9) | copy-start | bytes 12292
  159.3 89.2 %all-gather.5.cloned.1.call-start = ((), (), s32[]{:S(2)}) async-start(), calls=%async_computation.3 | async-start | bytes 2359296 | tf_op jit(solution)/shard_map/all_gather | solution.py:49
  213.4 493.4 %reduce-scatter.2.cloned.1.call-start = ((), (), s32[]{:S(2)}) async-start(), calls=%async_computation.4 | async-start | bytes 4259840 | tf_op jit(solution)/shard_map/reduce_scatter | solution.py:64
  252.9 240.1 %copy-start.1 = (bf16[128,1024]{1,0:T(8,128)(2,1)S(1)}, bf16[128,1024]{1,0:T(8,128)(2,1)}, u32[]{:S(2)}) copy-start(bf16[128,1024]{1,0:T(8,128)(2,1)} %param.6) | copy-start | bytes 786436
Sparse Core Ops, SparseCore 0:
  12.4 137.5 all-gather.2
  213.5 35.0 all-gather.4
  253.0 453.7 reduce-scatter.1
where the time goes:
time: 715 us
  waiting for transfers between devices  389 us (54%)
  blocking collectives  293 us (41%)
  between operations  13.8 us (2%)
    psum x1, blocking collectives, shards(): gain_grad = lax.psum(gain_part, 'dp')  225 us
    reduce_scatter x1, waiting for transfers between devices, shards(): lax.psum_scatter(lax.dot_general(gathered, kv_pre, (((0,), (0,)), ((), ()...  213 us
    all_gather x1, waiting for transfers between devices, shards(): lax.all_gather(kv_weight, 'dp', axis=1, tiled=True)  140 us
    psum x1, blocking collectives, shards(): square_total = lax.psum(square_part, 'tensor')  52.5 us
    all_gather x1, waiting for transfers between devices, shards(): gathered = lax.all_gather(normed, 'tensor', axis=1, tiled=True)  35.2 us
    psum x1, blocking collectives, shards(): inner = lax.psum(inner_part, 'tensor')[:, None] / D  15.2 us
  transfers between devices with their start and end apart: 4, of which 3 were waited for; matrix products, arithmetic and copies ran while one was open for 0% of the time, Pallas kernels for 0%

commit v1 on v0

v1 whole, which is shorter than its diff:
```python
import jax
import jax.numpy as jnp
from jax import lax
from jax.sharding import Mesh
from jax.sharding import PartitionSpec as P

D = 8192
HD = 128
TOK = 128

rope_theta = 500000.0
norm_eps = 1e-05

SIZES = (4, 8, 2, 4, 2)
AXES = ("x", "y", "zh", "zl", "core")
DP = ("x", "y", "zh")
TENSOR = ("zl", "core")
ROW = ("y", "zh")


def flat_index(x, y, zh, zl, core):
    return (((x * 8 + y) * 2 + zh) * 4 + zl) * 2 + core


def weight_moves():
    moves = []
    for x in range(4):
        for y in range(8):
            for zh in range(2):
                for zl in range(4):
                    for core in range(2):
                        there = flat_index(y % 4, zl * 2 + core, zh, x, y // 4)
                        moves.append((flat_index(x, y, zh, zl, core), there))
    return moves


def exchange(value, axes):
    return lax.all_to_all(value, axes, split_axis=0, concat_axis=0, tiled=True)


def spread(value, axes, count):
    return exchange(jnp.broadcast_to(value[None], (count,) + value.shape), axes)


def rope_tables(positions_count, head_size):
    half_head = head_size // 2
    frequency = rope_theta ** (-(jnp.arange(half_head, dtype=jnp.float32) * 2.0 / head_size))
    angles = jnp.arange(positions_count, dtype=jnp.float32)[:, None] * frequency[None, :]
    return (jnp.cos(angles), jnp.sin(angles))


def shards(layer_input, residual_grad, key_value_grad, kv_weight, norm_gain):
    moves = weight_moves()
    quarter = layer_input.shape[1] // 4

    cut = layer_input.reshape(TOK, 4, quarter).transpose(1, 0, 2)
    rows = exchange(cut, "x").reshape(4 * TOK, quarter)

    moved = lax.ppermute(kv_weight, AXES, moves)
    weights = spread(moved, ROW, 16).reshape(8, 2, HD, HD)

    cosine, sine = rope_tables(TOK, HD)
    grads = key_value_grad.astype(jnp.float32)
    low, high = grads[:, : HD // 2], grads[:, HD // 2 :]
    turned = jnp.concatenate([low * cosine + high * sine, high * cosine - low * sine], axis=1)
    is_key = lax.axis_index("core") == 0
    kv_pre = jnp.where(is_key, turned, grads).astype(jnp.bfloat16)

    widened = layer_input.astype(jnp.float32)
    squares = jnp.sum(widened * widened, axis=1)
    first = lax.reduce_precision(squares, 8, 7)
    second = lax.reduce_precision(squares - first, 8, 7)
    third = squares - first - second
    terms = jnp.stack([first, second, third]).astype(jnp.bfloat16)
    terms = jnp.pad(terms, ((0, 13), (0, 0)))
    packet = jnp.concatenate([kv_pre, terms], axis=0)

    packets = spread(packet, "zl", 4)
    packets = spread(packets, "x", 4)
    packets = spread(packets, "core", 2)
    packets = packets.reshape(2, 4, 4, TOK + 16, HD)
    kv = packets[:, :, :, :TOK].transpose(2, 0, 1, 3, 4).reshape(8, 4 * TOK, HD)
    total = jnp.sum(packets[:, :, :, TOK : TOK + 3].astype(jnp.float32), axis=(0, 2, 3))
    inv_all = lax.rsqrt(total / D + norm_eps)
    inv_rows = inv_all.reshape(4 * TOK, 1)
    mine = lax.axis_index("x")
    inv_scale = lax.dynamic_index_in_dim(inv_all, mine, 0, keepdims=False)[:, None]
    gain_quarter = lax.dynamic_slice_in_dim(norm_gain, mine * quarter, quarter)

    normal = rows.astype(jnp.float32) * inv_rows
    normed = (normal * gain_quarter[None, :]).astype(jnp.bfloat16)

    pieces = jnp.einsum(
        "ktc,tbf->kbcf",
        kv,
        normed.reshape(4 * TOK, 2, HD),
        preferred_element_type=jnp.float32,
    ).astype(jnp.bfloat16)
    arrived = exchange(pieces.reshape(16, HD, HD), ROW)
    block = jnp.sum(arrived.astype(jnp.float32), axis=0)
    weight_grad = lax.ppermute(block, AXES, [(b, a) for a, b in moves])

    products = jnp.einsum(
        "ktc,kbcf->ktbf", kv, weights, preferred_element_type=jnp.float32
    ).astype(jnp.bfloat16)
    norm_grad = jnp.sum(products.astype(jnp.float32), axis=0).reshape(4 * TOK, quarter)
    back = exchange(norm_grad.reshape(4, TOK, quarter), "x")
    scaled_rows = norm_grad * gain_quarter[None, :]
    inner_part = jnp.sum(scaled_rows * normal, axis=1).reshape(4, 1, TOK)
    inner_parts = exchange(
        jnp.broadcast_to(inner_part, (4, 8, TOK)).reshape(32, TOK), ("x",) + TENSOR
    )
    inner = jnp.sum(inner_parts, axis=0)[:, None] / D

    gain_part = jnp.sum(norm_grad * normal, axis=0)
    gain_parts = spread(gain_part, DP, 64)
    gain_grad = jnp.sum(gain_parts.reshape(4, 16, quarter), axis=1).reshape(4 * quarter)

    scaled = back.transpose(1, 0, 2).reshape(TOK, 4 * quarter) * norm_gain[None, :]
    input_grad = (
        residual_grad.astype(jnp.float32)
        + inv_scale * (scaled - widened * inv_scale * inner)
    ).astype(jnp.bfloat16)
    return (input_grad, weight_grad, gain_grad)


def solution(mesh):
    fine = Mesh(mesh.devices.reshape(SIZES), AXES)
    return jax.shard_map(
        shards,
        mesh=fine,
        in_specs=(
            P(DP, TENSOR),
            P(DP, TENSOR),
            P(DP, TENSOR),
            P(TENSOR, DP),
            P(TENSOR),
        ),
        out_specs=(P(DP, TENSOR), P(TENSOR, DP), P(TENSOR)),
        check_vma=False,
    )
```

time: 715 us -> 165 us (0.23)
  the two profiles are of different devices: /device:TPU:64 before, /device:TPU:6 now
where the time goes in v1:
time: 165 us; the launch traced here: 163 us
  waiting for transfers between devices  56.5 us (34%)
  blocking collectives  46.7 us (28%)
  starting transfers between devices  43 us (26%)
  local copies, waits for them, and re-layouts  10.5 us (6%)
  other arithmetic  3.85 us (2%)
    all_to_all x6, waiting for transfers between devices, exchange(): return lax.all_to_all(value, axes, split_axis=0, concat_axis=0, tiled=True)  51.9 us
    all_to_all x3, blocking collectives, exchange(): return lax.all_to_all(value, axes, split_axis=0, concat_axis=0, tiled=True)  46.7 us
    all_to_all x6, starting transfers between devices, exchange(): return lax.all_to_all(value, axes, split_axis=0, concat_axis=0, tiled=True)  35.6 us
    ppermute x1, starting transfers between devices, shards(): weight_grad = lax.ppermute(block, AXES, [(b, a) for a, b in moves])  4.94 us
    ppermute x1, waiting for transfers between devices, shards(): weight_grad = lax.ppermute(block, AXES, [(b, a) for a, b in moves])  4.58 us
    unnamed x12, local copies, waits for them, and re-layouts  3.39 us
  transfers between devices with their start and end apart: 8, of which 7 were waited for; matrix products, arithmetic and copies ran while one was open for 5% of the time, Pallas kernels for 0%

profile of v1, /device:TPU:6, one launch (start us, length us, event | category | flops | bytes accessed | tf_op | source)
XLA Modules:
  0.0 162.6 jit_solution(4061737728559322014)
XLA Ops:
  0.6 1.1 copy.43
  1.8 0.2 fusion.1
  1.9 0.8 convert_element_type.61
  2.7 0.3 multiply_add_fusion
  3.0 0.9 fusion.8
  3.9 0.0 copy-start.2
  3.9 13.7 %all_to_all.50 = bf16[4,144,128]{2,1,0:T(8,128)(2,1)S(1)} all-to-all(bf16[4,144,128]{2,1,0:T(8,128)(2,1)S(1)} %broadcast_in_dim.12), channel_id=1, replica_groups=mesh['x'=4,'y'=8,'zh'=2,'zl'=4,'core'=2] {'zl'}, dimensions={0} | all-to-all | bytes 294912 | tf_op jit(solution)/shard_map/all_to_all | solution.py:38
  17.6 0.9 broadcast_in_dim.13
  18.5 4.8 %all-to-all-start.1 = ((bf16[4,4,144,128]{3,2,1,0:T(8,128)(2,1)}), bf16[4,4,144,128]{3,2,1,0:T(8,128)(2,1)S(1)}, u32[]{:S(2)}, u32[]{:S(2)}) async-start(bf16[4,4,144,128]{3,2,1,0:T(8,128)(2,1)} %broadcast_in_dim.13), calls=%async_computation.1 | async-start | bytes 1179648 | tf_op jit(solution)/shard_map/all_to_all | solution.py:38
  23.3 0.0 copy-done.2
  23.3 2.5 %collective-permute-start = (bf16[128,128]{1,0:T(8,128)(2,1)S(1)}, bf16[128,128]{1,0:T(8,128)(2,1)S(1)}, u32[]{:S(2)}, u32[]{:S(2)}) collective-permute-start(bf16[128,128]{1,0:T(8,128)(2,1)S(1)} %copy-done.2), channel_id=1, source_target_pairs={{0,0},{1,16},{2,32},{3,48},{4,64},{5,80},{6,96},{7,112},{8,8},{9,2... | collective-permute-start | bytes 98312 | tf_op jit(solution)/shard_map/ppermute | solution.py:59
  25.9 4.6 %all-to-all-done.1 = bf16[4,4,144,128]{3,2,1,0:T(8,128)(2,1)S(1)} async-done(((bf16[4,4,144,128]{3,2,1,0:T(8,128)(2,1)}), bf16[4,4,144,128]{3,2,1,0:T(8,128)(2,1)S(1)}, u32[]{:S(2)}, u32[]{:S(2)}) %all-to-all-start.1) | async-done | bytes 589856 | tf_op jit(solution)/shard_map/all_to_all | solution.py:38
  30.5 1.2 broadcast_in_dim.14
  31.7 3.6 %all-to-all-start.2 = ((bf16[2,4,4,144,128]{4,3,1,2,0:T(8,128)(2,1)}), bf16[2,4,4,144,128]{4,3,1,2,0:T(8,128)(2,1)S(1)}, u32[]{:S(2)}, u32[]{:S(2)}) async-start(bf16[2,4,4,144,128]{4,3,1,2,0:T(8,128)(2,1)} %broadcast_in_dim.14), calls=%async_computation.2 | async-start | bytes 2359296 | tf_op jit(solution)/shard_map/all_to_all | solution.py:38
  35.3 0.0 copy-start.1
  35.3 0.0 collective-permute-done
  35.3 2.2 %all-to-all-done.2 = bf16[2,4,4,144,128]{4,3,1,2,0:T(8,128)(2,1)S(1)} async-done(((bf16[2,4,4,144,128]{4,3,1,2,0:T(8,128)(2,1)}), bf16[2,4,4,144,128]{4,3,1,2,0:T(8,128)(2,1)S(1)}, u32[]{:S(2)}, u32[]{:S(2)}) %all-to-all-start.2) | async-done | bytes 1179680 | tf_op jit(solution)/shard_map/all_to_all | solution.py:38
  37.5 0.9 broadcast_in_dim.15
  38.4 12.6 %all-to-all-start.3 = ((bf16[16,128,128]{2,1,0:T(8,128)(2,1)}), bf16[16,128,128]{2,1,0:T(8,128)(2,1)S(1)}, u32[]{:S(2)}, u32[]{:S(2)}) async-start(bf16[16,128,128]{2,1,0:T(8,128)(2,1)} %broadcast_in_dim.15), calls=%async_computation.3 | async-start | bytes 1048576 | tf_op jit(solution)/shard_map/all_to_all | solution.py:38
  51.0 0.9 copy.49
  51.8 0.0 copy-done.1
  51.8 0.1 dynamic_slice.8
  51.9 0.1 slice_bitcast_fusion
  52.0 0.1 copy.45
  52.2 20.6 %all-to-all-done.3 = bf16[16,128,128]{2,1,0:T(8,128)(2,1)S(1)} async-done(((bf16[16,128,128]{2,1,0:T(8,128)(2,1)}), bf16[16,128,128]{2,1,0:T(8,128)(2,1)S(1)}, u32[]{:S(2)}, u32[]{:S(2)}) %all-to-all-start.3) | async-done | bytes 524320 | tf_op jit(solution)/shard_map/all_to_all | solution.py:38
  72.8 5.4 %all-to-all-start.5 = ((bf16[4,128,256]{2,1,0:T(8,128)(2,1)}), bf16[4,128,256]{2,1,0:T(8,128)(2,1)S(1)}, u32[]{:S(2)}, u32[]{:S(2)}) async-start(bf16[4,128,256]{2,1,0:T(8,128)(2,1)} %bitcast.10), calls=%async_computation.5 | async-start | bytes 524288 | tf_op jit(solution)/shard_map/all_to_all | solution.py:38
  78.2 0.7 convert_reduce_fusion
  78.9 0.4 copy.46
  79.3 1.2 reshape_reshape.3
  80.5 2.3 %all-to-all-done.5 = bf16[4,128,256]{2,1,0:T(8,128)(2,1)S(1)} async-done(((bf16[4,128,256]{2,1,0:T(8,128)(2,1)}), bf16[4,128,256]{2,1,0:T(8,128)(2,1)S(1)}, u32[]{:S(2)}, u32[]{:S(2)}) %all-to-all-start.5) | async-done | bytes 262176 | tf_op jit(solution)/shard_map/all_to_all | solution.py:38
  82.8 1.3 multiply_reduce_fusion
  84.2 12.1 %all_to_all.51 = f32[32,1,128]{2,1,0:T(1,128)S(1)} all-to-all(f32[32,1,128]{2,1,0:T(1,128)S(1)} %bitcast.42), channel_id=1, replica_groups=mesh['x'=4,'y'=8,'zh'=2,'zl'=4,'core'=2] {'x','zl','core'}, dimensions={0} | all-to-all | bytes 32768 | tf_op jit(solution)/shard_map/all_to_all | solution.py:38
  96.3 20.8 %all_to_all.52 = f32[64,1,256]{2,1,0:T(1,128)S(1)} all-to-all(f32[64,1,256]{2,1,0:T(1,128)S(1)} %broadcast_in_dim.17), channel_id=1, replica_groups=mesh['x'=4,'y'=8,'zh'=2,'zl'=4,'core'=2] {'x','y','zh'}, dimensions={0} | all-to-all | bytes 131072 | tf_op jit(solution)/shard_map/all_to_all | solution.py:38
  117.2 5.6 %all-to-all-start.4 = ((f32[4,128,256]{2,1,0:T(8,128)}), f32[4,128,256]{2,1,0:T(8,128)S(1)}, u32[]{:S(2)}, u32[]{:S(2)}) async-start(f32[4,128,256]{2,1,0:T(8,128)} %reshape_reshape.3), calls=%async_computation.4 | async-start | bytes 1048576 | tf_op jit(solution)/shard_map/all_to_all | solution.py:38
  122.8 0.1 convert_element_type.70
  122.9 0.5 fusion
  123.3 0.0 copy-start
  123.4 1.0 copy.51
  124.4 4.6 %all-to-all-done.4 = f32[4,128,256]{2,1,0:T(8,128)S(1)} async-done(((f32[4,128,256]{2,1,0:T(8,128)}), f32[4,128,256]{2,1,0:T(8,128)S(1)}, u32[]{:S(2)}, u32[]{:S(2)}) %all-to-all-start.4) | async-done | bytes 524320 | tf_op jit(solution)/shard_map/all_to_all | solution.py:38
  129.0 3.6 %all-to-all-start.7 = ((bf16[16,128,128]{2,1,0:T(8,128)(2,1)}), bf16[16,128,128]{2,1,0:T(8,128)(2,1)S(1)}, u32[]{:S(2)}, u32[]{:S(2)}) async-start(bf16[16,128,128]{2,1,0:T(8,128)(2,1)} %bitcast.15), calls=%async_computation.7 | async-start | bytes 1048576 | tf_op jit(solution)/shard_map/all_to_all | solution.py:38
  132.6 0.0 copy-done
  132.6 0.2 copy.42
  132.8 0.1 reduce_sum.79
  132.9 0.6 copy.58
  133.5 0.2 copy.47
  133.7 17.6 %all-to-all-done.7 = bf16[16,128,128]{2,1,0:T(8,128)(2,1)S(1)} async-done(((bf16[16,128,128]{2,1,0:T(8,128)(2,1)}), bf16[16,128,128]{2,1,0:T(8,128)(2,1)S(1)}, u32[]{:S(2)}, u32[]{:S(2)}) %all-to-all-start.7) | async-done | bytes 524320 | tf_op jit(solution)/shard_map/all_to_all | solution.py:38
  151.3 0.1 convert_reduce_fusion.1
  151.3 4.9 %collective-permute-start.1 = (f32[128,128]{1,0:T(8,128)S(1)}, f32[128,128]{1,0:T(8,128)S(1)}, u32[]{:S(2)}, u32[]{:S(2)}) collective-permute-start(f32[128,128]{1,0:T(8,128)S(1)} %convert_reduce_fusion.1), channel_id=1, source_target_pairs={{0,0},{16,1},{32,2},{48,3},{64,4},{80,5},{96,6},{112,7},{8,8},{24,... | collective-permute-start | bytes 196616 | tf_op jit(solution)/shard_map/ppermute | solution.py:101
  156.3 0.2 fusion.6
  156.5 0.9 copy.52
  157.4 4.6 %collective-permute-done.1 = f32[128,128]{1,0:T(8,128)S(1)} collective-permute-done((f32[128,128]{1,0:T(8,128)S(1)}, f32[128,128]{1,0:T(8,128)S(1)}, u32[]{:S(2)}, u32[]{:S(2)}) %collective-permute-start.1) | collective-permute-done | bytes 65568 | tf_op jit(solution)/shard_map/ppermute | solution.py:101
  161.9 0.6 copy.62
  (14 shorter events, 0.2 us)
Async XLA Ops:
  3.9 19.4 %copy-start.2 = (bf16[128,128]{1,0:T(8,128)(2,1)S(1)}, bf16[128,128]{1,0:T(8,128)(2,1)}, u32[]{:S(2)}) copy-start(bf16[128,128]{1,0:T(8,128)(2,1)} %param.8) | copy-start | bytes 98308
  18.5 11.9 %all-to-all-start.1 = ((bf16[4,4,144,128]{3,2,1,0:T(8,128)(2,1)}), bf16[4,4,144,128]{3,2,1,0:T(8,128)(2,1)S(1)}, u32[]{:S(2)}, u32[]{:S(2)}) async-start(bf16[4,4,144,128]{3,2,1,0:T(8,128)(2,1)} %broadcast_in_dim.13), calls=%async_computation.1 | async-start | bytes 1179648 | tf_op jit(solution)/shard_map/all_to_all | solution.py:38
  23.3 12.0 %collective-permute-start = (bf16[128,128]{1,0:T(8,128)(2,1)S(1)}, bf16[128,128]{1,0:T(8,128)(2,1)S(1)}, u32[]{:S(2)}, u32[]{:S(2)}) collective-permute-start(bf16[128,128]{1,0:T(8,128)(2,1)S(1)} %copy-done.2), channel_id=1, source_target_pairs={{0,0},{1,16},{2,32},{3,48},{4,64},{5,80},{6,96},{7,112},{8,8},{9,2... | collective-permute-start | bytes 98312 | tf_op jit(solution)/shard_map/ppermute | solution.py:59
  31.7 5.8 %all-to-all-start.2 = ((bf16[2,4,4,144,128]{4,3,1,2,0:T(8,128)(2,1)}), bf16[2,4,4,144,128]{4,3,1,2,0:T(8,128)(2,1)S(1)}, u32[]{:S(2)}, u32[]{:S(2)}) async-start(bf16[2,4,4,144,128]{4,3,1,2,0:T(8,128)(2,1)} %broadcast_in_dim.14), calls=%async_computation.2 | async-start | bytes 2359296 | tf_op jit(solution)/shard_map/all_to_all | solution.py:38
  35.3 16.6 %copy-start.1 = (f32[1024]{0:T(1024)S(1)}, f32[1024]{0:T(1024)}, u32[]{:S(2)}) copy-start(f32[1024]{0:T(1024)} %param.9) | copy-start | bytes 12292
  38.4 34.4 %all-to-all-start.3 = ((bf16[16,128,128]{2,1,0:T(8,128)(2,1)}), bf16[16,128,128]{2,1,0:T(8,128)(2,1)S(1)}, u32[]{:S(2)}, u32[]{:S(2)}) async-start(bf16[16,128,128]{2,1,0:T(8,128)(2,1)} %broadcast_in_dim.15), calls=%async_computation.3 | async-start | bytes 1048576 | tf_op jit(solution)/shard_map/all_to_all | solution.py:38
  72.8 10.0 %all-to-all-start.5 = ((bf16[4,128,256]{2,1,0:T(8,128)(2,1)}), bf16[4,128,256]{2,1,0:T(8,128)(2,1)S(1)}, u32[]{:S(2)}, u32[]{:S(2)}) async-start(bf16[4,128,256]{2,1,0:T(8,128)(2,1)} %bitcast.10), calls=%async_computation.5 | async-start | bytes 524288 | tf_op jit(solution)/shard_map/all_to_all | solution.py:38
  117.2 11.8 %all-to-all-start.4 = ((f32[4,128,256]{2,1,0:T(8,128)}), f32[4,128,256]{2,1,0:T(8,128)S(1)}, u32[]{:S(2)}, u32[]{:S(2)}) async-start(f32[4,128,256]{2,1,0:T(8,128)} %reshape_reshape.3), calls=%async_computation.4 | async-start | bytes 1048576 | tf_op jit(solution)/shard_map/all_to_all | solution.py:38
  123.3 9.3 %copy-start = (bf16[128,1024]{1,0:T(8,128)(2,1)S(1)}, bf16[128,1024]{1,0:T(8,128)(2,1)}, u32[]{:S(2)}) copy-start(bf16[128,1024]{1,0:T(8,128)(2,1)} %param.6) | copy-start | bytes 786436
  129.0 22.2 %all-to-all-start.7 = ((bf16[16,128,128]{2,1,0:T(8,128)(2,1)}), bf16[16,128,128]{2,1,0:T(8,128)(2,1)S(1)}, u32[]{:S(2)}, u32[]{:S(2)}) async-start(bf16[16,128,128]{2,1,0:T(8,128)(2,1)} %bitcast.15), calls=%async_computation.7 | async-start | bytes 1048576 | tf_op jit(solution)/shard_map/all_to_all | solution.py:38
  151.3 10.6 %collective-permute-start.1 = (f32[128,128]{1,0:T(8,128)S(1)}, f32[128,128]{1,0:T(8,128)S(1)}, u32[]{:S(2)}, u32[]{:S(2)}) collective-permute-start(f32[128,128]{1,0:T(8,128)S(1)} %convert_reduce_fusion.1), channel_id=1, source_target_pairs={{0,0},{16,1},{32,2},{48,3},{64,4},{80,5},{96,6},{112,7},{8,8},{24,... | collective-permute-start | bytes 196616 | tf_op jit(solution)/shard_map/ppermute | solution.py:101

commit v2 on v1

v2 whole, which is shorter than its diff:
```python
import jax
import jax.numpy as jnp
from jax import lax
from jax.sharding import Mesh
from jax.sharding import PartitionSpec as P

D = 8192
HD = 128
TOK = 128
QUARTER = 256

rope_theta = 500000.0
norm_eps = 1e-05

SIZES = (4, 8, 2, 4, 2)
AXES = ("x", "y", "zh", "zl", "core")
DP = ("x", "y", "zh")
TENSOR = ("zl", "core")
ROW = ("y", "zh")


def flat_index(x, y, zh, zl, core):
    return (((x * 8 + y) * 2 + zh) * 4 + zl) * 2 + core


def weight_moves():
    moves = []
    for x in range(4):
        for y in range(8):
            for zh in range(2):
                for zl in range(4):
                    for core in range(2):
                        far_zl, far_core = x, y // 4
                        place = ((far_zl - zl) % 4) * 2 + (far_core ^ core)
                        there = flat_index(y % 4, place, zh, far_zl, far_core)
                        moves.append((flat_index(x, y, zh, zl, core), there))
    return moves


def exchange(value, axes):
    return lax.all_to_all(value, axes, split_axis=0, concat_axis=0, tiled=True)


def shift(value, axis, count, step):
    return lax.ppermute(value, axis, [(i, (i + step) % count) for i in range(count)])


def gather(value, axis, count):
    return jnp.stack([value] + [shift(value, axis, count, r) for r in range(1, count)])


def terms_of(value):
    first = lax.reduce_precision(value, 8, 7)
    second = lax.reduce_precision(value - first, 8, 7)
    third = value - first - second
    return jnp.stack([first, second, third]).astype(jnp.bfloat16)


def rope_tables(positions_count, head_size):
    half_head = head_size // 2
    frequency = rope_theta ** (-(jnp.arange(half_head, dtype=jnp.float32) * 2.0 / head_size))
    angles = jnp.arange(positions_count, dtype=jnp.float32)[:, None] * frequency[None, :]
    return (jnp.cos(angles), jnp.sin(angles))


def shards(layer_input, residual_grad, key_value_grad, kv_weight, norm_gain):
    moves = weight_moves()
    mine = lax.axis_index("x")

    moved = lax.ppermute(kv_weight, AXES, moves)

    cosine, sine = rope_tables(TOK, HD)
    grads = key_value_grad.astype(jnp.float32)
    low, high = grads[:, : HD // 2], grads[:, HD // 2 :]
    turned = jnp.concatenate([low * cosine + high * sine, high * cosine - low * sine], axis=1)
    kv_pre = jnp.where(lax.axis_index("core") == 0, turned, grads).astype(jnp.bfloat16)
    widened = layer_input.astype(jnp.float32)
    squares = terms_of(jnp.sum(widened * widened, axis=1))
    packet = jnp.concatenate([kv_pre, jnp.pad(squares, ((0, 13), (0, 0)))], axis=0)

    packets = gather(packet, "zl", 4)
    pieces_x = [
        lax.dynamic_slice_in_dim(layer_input, ((mine + r) % 4) * QUARTER, QUARTER, axis=1)
        for r in range(4)
    ]
    rows = jnp.concatenate([pieces_x[0]] + [shift(pieces_x[r], "x", 4, r) for r in range(1, 4)])
    packets, moved = lax.optimization_barrier((packets, moved))
    weights = exchange(jnp.broadcast_to(moved[None], (16, HD, HD)), ROW).reshape(4, 2, 2, HD, HD)
    packets = gather(packets, "x", 4)
    packets = gather(packets, "core", 2)
    kv = packets[:, :, :, :TOK].transpose(2, 0, 1, 3, 4).reshape(4, 2, 4 * TOK, HD)
    total = jnp.sum(packets[:, :, :, TOK : TOK + 3].astype(jnp.float32), axis=(0, 2, 3))
    inv_all = lax.rsqrt(total / D + norm_eps)
    inv_scale = inv_all[0][:, None]
    gain_quarter = lax.dynamic_slice_in_dim(norm_gain, mine * QUARTER, QUARTER)
    normal = rows.astype(jnp.float32) * inv_all.reshape(4 * TOK, 1)
    normed = (normal * gain_quarter[None, :]).astype(jnp.bfloat16)

    products = jnp.einsum(
        "zktc,zkbcf->zktbf", kv, weights, preferred_element_type=jnp.float32
    ).astype(jnp.bfloat16)
    norm_grad = jnp.sum(products.astype(jnp.float32), axis=(0, 1)).reshape(4 * TOK, QUARTER)
    gain_part = jnp.sum(norm_grad * normal, axis=0)

    pieces = jnp.einsum(
        "zktc,tbf->zkbcf",
        kv,
        normed.reshape(4 * TOK, 2, HD),
        preferred_element_type=jnp.float32,
    ).astype(jnp.bfloat16).reshape(16, HD, HD)
    gain_terms = jnp.pad(terms_of(gain_part).reshape(6, HD), ((0, 10), (0, 0)))
    gain_terms = jnp.broadcast_to(gain_terms[None], (16, 16, HD))
    arrived = exchange(jnp.concatenate([pieces, gain_terms], axis=1), ROW)
    block = jnp.sum(arrived[:, :HD].astype(jnp.float32), axis=0)
    weight_grad = lax.ppermute(block, AXES, [(b, a) for a, b in moves])
    gain_sum = jnp.sum(arrived[:, HD : HD + 6].astype(jnp.float32), axis=0)
    gain_sum = jnp.sum(gain_sum.reshape(3, 1, QUARTER), axis=0)
    gain_sums = gather(gain_sum, "x", 4).reshape(4, 1, QUARTER)
    place = (mine - jnp.arange(4)) % 4
    chosen = place[None, :, None] == jnp.arange(4)[:, None, None]
    gain_grad = jnp.sum(jnp.where(chosen, gain_sums, 0.0), axis=0).reshape(4 * QUARTER)

    full = jnp.zeros((TOK, 4 * QUARTER), jnp.float32)
    for r in range(4):
        part = norm_grad[r * TOK : (r + 1) * TOK]
        if r:
            part = shift(part, "x", 4, -r)
        full = lax.dynamic_update_slice_in_dim(full, part, ((mine + r) % 4) * QUARTER, axis=1)
    scaled = full * norm_gain[None, :]
    normal = widened * inv_scale
    inner = jnp.sum(scaled * normal, axis=1)
    inner = inner + shift(inner, "core", 2, 1)
    inner_all = gather(inner, "zl", 4)
    inner = jnp.sum(inner_all, axis=0)[:, None] / D
    input_grad = (
        residual_grad.astype(jnp.float32) + inv_scale * (scaled - normal * inner)
    ).astype(jnp.bfloat16)
    return (input_grad, weight_grad, gain_grad)


def solution(mesh):
    fine = Mesh(mesh.devices.reshape(SIZES), AXES)
    return jax.shard_map(
        shards,
        mesh=fine,
        in_specs=(
            P(DP, TENSOR),
            P(DP, TENSOR),
            P(DP, TENSOR),
            P(TENSOR, DP),
            P(TENSOR),
        ),
        out_specs=(P(DP, TENSOR), P(TENSOR, DP), P(TENSOR)),
        check_vma=False,
    )
```

time: 165 us -> 149 us (0.903)
  the two profiles are of different devices: /device:TPU:6 before, /device:TPU:4 now
where the time goes in v2:
time: 149 us; the launch traced here: 148 us
  starting transfers between devices  102 us (68%)
  waiting for transfers between devices  33.3 us (22%)
  other arithmetic  5.73 us (4%)
  local copies, waits for them, and re-layouts  4.29 us (3%)
    ppermute x20, starting transfers between devices, shift(): lax.ppermute(value, axis, [(i, (i + step) % count) for i in range(count)])  65.5 us
    all_to_all x2, starting transfers between devices, exchange(): return lax.all_to_all(value, axes, split_axis=0, concat_axis=0, tiled=True)  22.5 us
    ppermute x20, waiting for transfers between devices, shift(): lax.ppermute(value, axis, [(i, (i + step) % count) for i in range(count)])  14.5 us
    ppermute x1, waiting for transfers between devices, shards(): weight_grad = lax.ppermute(block, AXES, [(b, a) for a, b in moves])  8.51 us
    ppermute x1, starting transfers between devices, shards(): moved = lax.ppermute(kv_weight, AXES, moves)  8.04 us
    all_to_all x2, waiting for transfers between devices, exchange(): return lax.all_to_all(value, axes, split_axis=0, concat_axis=0, tiled=True)  7.67 us
    ppermute x1, starting transfers between devices, shards(): weight_grad = lax.ppermute(block, AXES, [(b, a) for a, b in moves])  5.88 us
  transfers between devices with their start and end apart: 24, of which 12 were waited for; matrix products, arithmetic and copies ran while one was open for 4% of the time, Pallas kernels for 0%

profile of v2, /device:TPU:4, one launch (start us, length us, event | category | flops | bytes accessed | tf_op | source)
XLA Modules:
  0.0 147.9 jit_solution(15627674772888331744)
XLA Ops:
  0.6 1.1 fusion.9
  1.7 0.8 convert_element_type.64
  2.5 0.3 multiply_add_fusion
  2.8 0.9 fusion.14
  3.7 4.3 %collective-permute-start = (bf16[144,128]{1,0:T(8,128)(2,1)S(1)}, bf16[144,128]{1,0:T(8,128)(2,1)S(1)}, u32[]{:S(2)}, u32[]{:S(2)}) collective-permute-start(bf16[144,128]{1,0:T(8,128)(2,1)S(1)} %get-tuple-element.20), channel_id=1, source_target_pairs={{0,2},{2,4},{4,6},{6,0},{1,3},{3,5},{5,7},{7,1},{8,10},{10,12},{12... | collective-permute-start | bytes 110600 | tf_op jit(solution)/shard_map/ppermute | solution.py:45
  8.0 6.1 %collective-permute-start.1 = (bf16[144,128]{1,0:T(8,128)(2,1)S(1)}, bf16[144,128]{1,0:T(8,128)(2,1)S(1)}, u32[]{:S(2)}, u32[]{:S(2)}) collective-permute-start(bf16[144,128]{1,0:T(8,128)(2,1)S(1)} %get-tuple-element.20), channel_id=1, source_target_pairs={{0,4},{2,6},{4,0},{6,2},{1,5},{3,7},{5,1},{7,3},{8,12},{10,14},{12... | collective-permute-start | bytes 110600 | tf_op jit(solution)/shard_map/ppermute | solution.py:45
  14.1 2.5 %collective-permute-start.2 = (bf16[144,128]{1,0:T(8,128)(2,1)S(1)}, bf16[144,128]{1,0:T(8,128)(2,1)S(1)}, u32[]{:S(2)}, u32[]{:S(2)}) collective-permute-start(bf16[144,128]{1,0:T(8,128)(2,1)S(1)} %get-tuple-element.20), channel_id=1, source_target_pairs={{0,6},{2,0},{4,2},{6,4},{1,7},{3,1},{5,3},{7,5},{8,14},{10,8},{12,... | collective-permute-start | bytes 110600 | tf_op jit(solution)/shard_map/ppermute | solution.py:45
  16.5 8.0 %collective-permute-start.3 = (bf16[128,128]{1,0:T(8,128)(2,1)}, bf16[128,128]{1,0:T(8,128)(2,1)S(1)}, u32[]{:S(2)}, u32[]{:S(2)}) collective-permute-start(bf16[128,128]{1,0:T(8,128)(2,1)} %param.8), channel_id=1, source_target_pairs={{0,0},{1,16},{2,96},{3,112},{4,64},{5,80},{6,32},{7,48},{8,8},{9,2... | collective-permute-start | bytes 98312 | tf_op jit(solution)/shard_map/ppermute | solution.py:70
  24.6 2.6 %collective-permute-done.3 = bf16[128,128]{1,0:T(8,128)(2,1)S(1)} collective-permute-done((bf16[128,128]{1,0:T(8,128)(2,1)}, bf16[128,128]{1,0:T(8,128)(2,1)S(1)}, u32[]{:S(2)}, u32[]{:S(2)}) %collective-permute-start.3) | collective-permute-done | bytes 32800 | tf_op jit(solution)/shard_map/ppermute | solution.py:70
  27.3 3.0 %collective-permute-start.4 = (bf16[4,144,128]{2,1,0:T(8,128)(2,1)S(1)}, bf16[4,144,128]{2,1,0:T(8,128)(2,1)S(1)}, u32[]{:S(2)}, u32[]{:S(2)}) collective-permute-start(bf16[4,144,128]{2,1,0:T(8,128)(2,1)S(1)} %pad_maximum_fusion.4), channel_id=1, source_target_pairs={{0,128},{128,256},{256,384},{384,0},{1,129},{129,257},{257,385},{3... | collective-permute-start | bytes 442376 | tf_op jit(solution)/shard_map/ppermute | solution.py:45
  30.3 1.9 %collective-permute-start.5 = (bf16[4,144,128]{2,1,0:T(8,128)(2,1)S(1)}, bf16[4,144,128]{2,1,0:T(8,128)(2,1)S(1)}, u32[]{:S(2)}, u32[]{:S(2)}) collective-permute-start(bf16[4,144,128]{2,1,0:T(8,128)(2,1)S(1)} %pad_maximum_fusion.4), channel_id=1, source_target_pairs={{0,256},{128,384},{256,0},{384,128},{1,257},{129,385},{257,1},{385... | collective-permute-start | bytes 442376 | tf_op jit(solution)/shard_map/ppermute | solution.py:45
  32.2 3.4 %collective-permute-start.6 = (bf16[4,144,128]{2,1,0:T(8,128)(2,1)S(1)}, bf16[4,144,128]{2,1,0:T(8,128)(2,1)S(1)}, u32[]{:S(2)}, u32[]{:S(2)}) collective-permute-start(bf16[4,144,128]{2,1,0:T(8,128)(2,1)S(1)} %pad_maximum_fusion.4), channel_id=1, source_target_pairs={{0,384},{128,0},{256,128},{384,256},{1,385},{129,1},{257,129},{385... | collective-permute-start | bytes 442376 | tf_op jit(solution)/shard_map/ppermute | solution.py:45
  35.6 0.3 collective-permute-done.4
  35.9 2.9 %collective-permute-done.5 = bf16[4,144,128]{2,1,0:T(8,128)(2,1)S(1)} collective-permute-done((bf16[4,144,128]{2,1,0:T(8,128)(2,1)S(1)}, bf16[4,144,128]{2,1,0:T(8,128)(2,1)S(1)}, u32[]{:S(2)}, u32[]{:S(2)}) %collective-permute-start.5) | collective-permute-done | bytes 147488 | tf_op jit(solution)/shard_map/ppermute | solution.py:45
  38.8 1.4 collective-permute-done.6
  40.2 0.1 fusion.28
  40.3 2.1 %collective-permute-start.7 = (bf16[4,4,144,128]{3,2,1,0:T(8,128)(2,1)S(1)}, bf16[4,4,144,128]{3,2,1,0:T(8,128)(2,1)S(1)}, u32[]{:S(2)}, u32[]{:S(2)}) collective-permute-start(bf16[4,4,144,128]{3,2,1,0:T(8,128)(2,1)S(1)} %get-tuple-element.8), channel_id=1, source_target_pairs={{0,1},{1,0},{2,3},{3,2},{4,5},{5,4},{6,7},{7,6},{8,9},{9,8},{10,11... | collective-permute-start | bytes 1769480 | tf_op jit(solution)/shard_map/ppermute | solution.py:45
  42.4 0.9 broadcast_in_dim.29
  43.3 16.0 %all-to-all-start = ((bf16[16,128,128]{2,1,0:T(8,128)(2,1)}), bf16[16,128,128]{2,1,0:T(8,128)(2,1)S(1)}, u32[]{:S(2)}, u32[]{:S(2)}) async-start(bf16[16,128,128]{2,1,0:T(8,128)(2,1)} %broadcast_in_dim.29), calls=%async_computation | async-start | bytes 1048576 | tf_op jit(solution)/shard_map/all_to_all | solution.py:41
  59.4 0.1 copy.77
  59.5 5.1 %collective-permute-start.15 = (bf16[128,256]{0,1:T(8,128)(2,1)S(1)}, bf16[128,256]{0,1:T(8,128)(2,1)S(1)}, u32[]{:S(2)}, u32[]{:S(2)}) collective-permute-start(bf16[128,256]{0,1:T(8,128)(2,1)S(1)} %copy.77), channel_id=1, source_target_pairs={{0,128},{128,256},{256,384},{384,0},{1,129},{129,257},{257,385},{3... | collective-permute-start | bytes 196616 | tf_op jit(solution)/shard_map/ppermute | solution.py:45
  64.6 0.1 copy.78
  64.8 1.9 %collective-permute-start.16 = (bf16[128,256]{0,1:T(8,128)(2,1)S(1)}, bf16[128,256]{0,1:T(8,128)(2,1)S(1)}, u32[]{:S(2)}, u32[]{:S(2)}) collective-permute-start(bf16[128,256]{0,1:T(8,128)(2,1)S(1)} %copy.78), channel_id=1, source_target_pairs={{0,256},{128,384},{256,0},{384,128},{1,257},{129,385},{257,1},{385... | collective-permute-start | bytes 196616 | tf_op jit(solution)/shard_map/ppermute | solution.py:45
  66.7 0.1 copy.79
  66.8 3.4 %collective-permute-start.17 = (bf16[128,256]{0,1:T(8,128)(2,1)S(1)}, bf16[128,256]{0,1:T(8,128)(2,1)S(1)}, u32[]{:S(2)}, u32[]{:S(2)}) collective-permute-start(bf16[128,256]{0,1:T(8,128)(2,1)S(1)} %copy.79), channel_id=1, source_target_pairs={{0,384},{128,0},{256,128},{384,256},{1,385},{129,1},{257,129},{385... | collective-permute-start | bytes 196616 | tf_op jit(solution)/shard_map/ppermute | solution.py:45
  70.2 0.1 copy.76
  70.3 0.1 copy.66
  70.5 0.1 copy.67
  70.7 1.8 %collective-permute-done.16 = bf16[128,256]{0,1:T(8,128)(2,1)S(1)} collective-permute-done((bf16[128,256]{0,1:T(8,128)(2,1)S(1)}, bf16[128,256]{0,1:T(8,128)(2,1)S(1)}, u32[]{:S(2)}, u32[]{:S(2)}) %collective-permute-start.16) | collective-permute-done | bytes 65568 | tf_op jit(solution)/shard_map/ppermute | solution.py:45
  72.4 0.1 copy.68
  72.6 0.4 collective-permute-done.17
  73.0 0.1 copy.69
  73.1 0.1 fusion.1
  73.2 0.1 copy.53
  73.4 0.7 fusion
  74.1 7.7 %all-to-all-done = bf16[16,128,128]{2,1,0:T(8,128)(2,1)S(1)} async-done(((bf16[16,128,128]{2,1,0:T(8,128)(2,1)}), bf16[16,128,128]{2,1,0:T(8,128)(2,1)S(1)}, u32[]{:S(2)}, u32[]{:S(2)}) %all-to-all-start) | async-done | bytes 524320 | tf_op jit(solution)/shard_map/all_to_all | solution.py:41
  81.8 0.7 convert_reduce_fusion
  82.5 0.2 multiply_reduce_fusion
  82.8 3.0 %collective-permute-start.8 = (f32[128,256]{0,1:T(8,128)S(1)}, f32[128,256]{0,1:T(8,128)S(1)}, u32[]{:S(2)}, u32[]{:S(2)}) collective-permute-start(f32[128,256]{0,1:T(8,128)S(1)} %bitcast.75), channel_id=1, source_target_pairs={{0,384},{128,0},{256,128},{384,256},{1,385},{129,1},{257,129},{385... | collective-permute-start | bytes 393224 | tf_op jit(solution)/shard_map/ppermute | solution.py:45
  85.9 0.9 pad_maximum_fusion.2
  86.7 6.5 %all-to-all-start.1 = ((bf16[16,144,128]{2,1,0:T(8,128)(2,1)}), bf16[16,144,128]{2,1,0:T(8,128)(2,1)S(1)}, u32[]{:S(2)}, u32[]{:S(2)}) async-start(bf16[16,144,128]{2,1,0:T(8,128)(2,1)} %pad_maximum_fusion.2), calls=%async_computation.1 | async-start | bytes 1179648 | tf_op jit(solution)/shard_map/all_to_all | solution.py:41
  93.3 0.1 copy.54
  93.4 0.1 copy.55
  93.5 0.1 copy.58
  93.6 5.3 %collective-permute-start.9 = (f32[128,256]{0,1:T(8,128)S(1)}, f32[128,256]{0,1:T(8,128)S(1)}, u32[]{:S(2)}, u32[]{:S(2)}) collective-permute-start(f32[128,256]{0,1:T(8,128)S(1)} %bitcast.77), channel_id=1, source_target_pairs={{0,256},{128,384},{256,0},{384,128},{1,257},{129,385},{257,1},{385... | collective-permute-start | bytes 393224 | tf_op jit(solution)/shard_map/ppermute | solution.py:45
  98.9 0.1 copy.60
  99.0 1.9 %collective-permute-start.10 = (f32[128,256]{0,1:T(8,128)S(1)}, f32[128,256]{0,1:T(8,128)S(1)}, u32[]{:S(2)}, u32[]{:S(2)}) collective-permute-start(f32[128,256]{0,1:T(8,128)S(1)} %bitcast.76), channel_id=1, source_target_pairs={{0,128},{128,256},{256,384},{384,0},{1,129},{129,257},{257,385},{3... | collective-permute-start | bytes 393224 | tf_op jit(solution)/shard_map/ppermute | solution.py:45
  101.1 1.9 %collective-permute-done.9 = f32[128,256]{0,1:T(8,128)S(1)} collective-permute-done((f32[128,256]{0,1:T(8,128)S(1)}, f32[128,256]{0,1:T(8,128)S(1)}, u32[]{:S(2)}, u32[]{:S(2)}) %collective-permute-start.9) | collective-permute-done | bytes 131104 | tf_op jit(solution)/shard_map/ppermute | solution.py:45
  103.2 2.7 %collective-permute-done.10 = f32[128,256]{0,1:T(8,128)S(1)} collective-permute-done((f32[128,256]{0,1:T(8,128)S(1)}, f32[128,256]{0,1:T(8,128)S(1)}, u32[]{:S(2)}, u32[]{:S(2)}) %collective-permute-start.10) | collective-permute-done | bytes 131104 | tf_op jit(solution)/shard_map/ppermute | solution.py:45
  106.0 0.2 fusion.4
  106.2 1.9 %collective-permute-start.11 = (f32[128]{0:T(128)S(1)}, f32[128]{0:T(128)S(1)}, u32[]{:S(2)}, u32[]{:S(2)}) collective-permute-start(f32[128]{0:T(128)S(1)} %fusion.4), channel_id=1, source_target_pairs={{0,1},{1,0},{2,3},{3,2},{4,5},{5,4},{6,7},{7,6},{8,9},{9,8},{10,11... | collective-permute-start | bytes 1544 | tf_op jit(solution)/shard_map/ppermute | solution.py:45
  108.1 1.1 collective-permute-done.11
  109.2 1.9 %collective-permute-start.12 = (f32[128]{0:T(128)S(1)}, f32[128]{0:T(128)S(1)}, u32[]{:S(2)}, u32[]{:S(2)}) collective-permute-start(f32[128]{0:T(128)S(1)} %add.96), channel_id=1, source_target_pairs={{0,2},{2,4},{4,6},{6,0},{1,3},{3,5},{5,7},{7,1},{8,10},{10,12},{12... | collective-permute-start | bytes 1544 | tf_op jit(solution)/shard_map/ppermute | solution.py:45
  111.1 2.1 %collective-permute-start.13 = (f32[128]{0:T(128)S(1)}, f32[128]{0:T(128)S(1)}, u32[]{:S(2)}, u32[]{:S(2)}) collective-permute-start(f32[128]{0:T(128)S(1)} %add.96), channel_id=1, source_target_pairs={{0,4},{2,6},{4,0},{6,2},{1,5},{3,7},{5,1},{7,3},{8,12},{10,14},{12... | collective-permute-start | bytes 1544 | tf_op jit(solution)/shard_map/ppermute | solution.py:45
  113.2 5.6 %collective-permute-start.14 = (f32[128]{0:T(128)S(1)}, f32[128]{0:T(128)S(1)}, u32[]{:S(2)}, u32[]{:S(2)}) collective-permute-start(f32[128]{0:T(128)S(1)} %add.96), channel_id=1, source_target_pairs={{0,6},{2,0},{4,2},{6,4},{1,7},{3,1},{5,3},{7,5},{8,14},{10,8},{12,... | collective-permute-start | bytes 1544 | tf_op jit(solution)/shard_map/ppermute | solution.py:45
  118.8 2.0 %collective-permute-done.14 = f32[128]{0:T(128)S(1)} collective-permute-done((f32[128]{0:T(128)S(1)}, f32[128]{0:T(128)S(1)}, u32[]{:S(2)}, u32[]{:S(2)}) %collective-permute-start.14) | collective-permute-done | bytes 544 | tf_op jit(solution)/shard_map/ppermute | solution.py:45
  120.8 1.0 fusion.8
  121.9 2.4 %collective-permute-start.19 = (f32[1,256]{1,0:T(1,128)S(1)}, f32[1,256]{1,0:T(1,128)S(1)}, u32[]{:S(2)}, u32[]{:S(2)}) collective-permute-start(f32[1,256]{1,0:T(1,128)S(1)} %bitcast.87), channel_id=1, source_target_pairs={{0,128},{128,256},{256,384},{384,0},{1,129},{129,257},{257,385},{3... | collective-permute-start | bytes 3080 | tf_op jit(solution)/shard_map/ppermute | solution.py:45
  124.2 3.3 %collective-permute-start.20 = (f32[1,256]{1,0:T(1,128)S(1)}, f32[1,256]{1,0:T(1,128)S(1)}, u32[]{:S(2)}, u32[]{:S(2)}) collective-permute-start(f32[1,256]{1,0:T(1,128)S(1)} %bitcast.88), channel_id=1, source_target_pairs={{0,256},{128,384},{256,0},{384,128},{1,257},{129,385},{257,1},{385... | collective-permute-start | bytes 3080 | tf_op jit(solution)/shard_map/ppermute | solution.py:45
  127.5 4.5 %collective-permute-start.21 = (f32[1,256]{1,0:T(1,128)S(1)}, f32[1,256]{1,0:T(1,128)S(1)}, u32[]{:S(2)}, u32[]{:S(2)}) collective-permute-start(f32[1,256]{1,0:T(1,128)S(1)} %bitcast.89), channel_id=1, source_target_pairs={{0,384},{128,0},{256,128},{384,256},{1,385},{129,1},{257,129},{385... | collective-permute-start | bytes 3080 | tf_op jit(solution)/shard_map/ppermute | solution.py:45
  132.1 5.9 %collective-permute-start.18 = (f32[128,128]{1,0:T(8,128)S(1)}, f32[128,128]{1,0:T(8,128)S(1)}, u32[]{:S(2)}, u32[]{:S(2)}) collective-permute-start(f32[128,128]{1,0:T(8,128)S(1)} %convert_reduce_fusion.1), channel_id=1, source_target_pairs={{0,0},{16,1},{96,2},{112,3},{64,4},{80,5},{32,6},{48,7},{8,8},{24,... | collective-permute-start | bytes 196616 | tf_op jit(solution)/shard_map/ppermute | solution.py:115
  138.2 0.6 copy.80
  138.8 8.5 %collective-permute-done.18 = f32[128,128]{1,0:T(8,128)S(1)} collective-permute-done((f32[128,128]{1,0:T(8,128)S(1)}, f32[128,128]{1,0:T(8,128)S(1)}, u32[]{:S(2)}, u32[]{:S(2)}) %collective-permute-start.18) | collective-permute-done | bytes 65568 | tf_op jit(solution)/shard_map/ppermute | solution.py:115
  147.3 0.6 copy.86
  (54 shorter events, 1.1 us)
Async XLA Ops:
  3.7 20.9 %collective-permute-start = (bf16[144,128]{1,0:T(8,128)(2,1)S(1)}, bf16[144,128]{1,0:T(8,128)(2,1)S(1)}, u32[]{:S(2)}, u32[]{:S(2)}) collective-permute-start(bf16[144,128]{1,0:T(8,128)(2,1)S(1)} %get-tuple-element.20), channel_id=1, source_target_pairs={{0,2},{2,4},{4,6},{6,0},{1,3},{3,5},{5,7},{7,1},{8,10},{10,12},{12... | collective-permute-start | bytes 110600 | tf_op jit(solution)/shard_map/ppermute | solution.py:45
  8.0 16.6 %collective-permute-start.1 = (bf16[144,128]{1,0:T(8,128)(2,1)S(1)}, bf16[144,128]{1,0:T(8,128)(2,1)S(1)}, u32[]{:S(2)}, u32[]{:S(2)}) collective-permute-start(bf16[144,128]{1,0:T(8,128)(2,1)S(1)} %get-tuple-element.20), channel_id=1, source_target_pairs={{0,4},{2,6},{4,0},{6,2},{1,5},{3,7},{5,1},{7,3},{8,12},{10,14},{12... | collective-permute-start | bytes 110600 | tf_op jit(solution)/shard_map/ppermute | solution.py:45
  14.1 10.5 %collective-permute-start.2 = (bf16[144,128]{1,0:T(8,128)(2,1)S(1)}, bf16[144,128]{1,0:T(8,128)(2,1)S(1)}, u32[]{:S(2)}, u32[]{:S(2)}) collective-permute-start(bf16[144,128]{1,0:T(8,128)(2,1)S(1)} %get-tuple-element.20), channel_id=1, source_target_pairs={{0,6},{2,0},{4,2},{6,4},{1,7},{3,1},{5,3},{7,5},{8,14},{10,8},{12,... | collective-permute-start | bytes 110600 | tf_op jit(solution)/shard_map/ppermute | solution.py:45
  16.5 10.7 %collective-permute-start.3 = (bf16[128,128]{1,0:T(8,128)(2,1)}, bf16[128,128]{1,0:T(8,128)(2,1)S(1)}, u32[]{:S(2)}, u32[]{:S(2)}) collective-permute-start(bf16[128,128]{1,0:T(8,128)(2,1)} %param.8), channel_id=1, source_target_pairs={{0,0},{1,16},{2,96},{3,112},{4,64},{5,80},{6,32},{7,48},{8,8},{9,2... | collective-permute-start | bytes 98312 | tf_op jit(solution)/shard_map/ppermute | solution.py:70
  27.3 8.6 %collective-permute-start.4 = (bf16[4,144,128]{2,1,0:T(8,128)(2,1)S(1)}, bf16[4,144,128]{2,1,0:T(8,128)(2,1)S(1)}, u32[]{:S(2)}, u32[]{:S(2)}) collective-permute-start(bf16[4,144,128]{2,1,0:T(8,128)(2,1)S(1)} %pad_maximum_fusion.4), channel_id=1, source_target_pairs={{0,128},{128,256},{256,384},{384,0},{1,129},{129,257},{257,385},{3... | collective-permute-start | bytes 442376 | tf_op jit(solution)/shard_map/ppermute | solution.py:45
  30.3 8.5 %collective-permute-start.5 = (bf16[4,144,128]{2,1,0:T(8,128)(2,1)S(1)}, bf16[4,144,128]{2,1,0:T(8,128)(2,1)S(1)}, u32[]{:S(2)}, u32[]{:S(2)}) collective-permute-start(bf16[4,144,128]{2,1,0:T(8,128)(2,1)S(1)} %pad_maximum_fusion.4), channel_id=1, source_target_pairs={{0,256},{128,384},{256,0},{384,128},{1,257},{129,385},{257,1},{385... | collective-permute-start | bytes 442376 | tf_op jit(solution)/shard_map/ppermute | solution.py:45
  32.2 8.0 %collective-permute-start.6 = (bf16[4,144,128]{2,1,0:T(8,128)(2,1)S(1)}, bf16[4,144,128]{2,1,0:T(8,128)(2,1)S(1)}, u32[]{:S(2)}, u32[]{:S(2)}) collective-permute-start(bf16[4,144,128]{2,1,0:T(8,128)(2,1)S(1)} %pad_maximum_fusion.4), channel_id=1, source_target_pairs={{0,384},{128,0},{256,128},{384,256},{1,385},{129,1},{257,129},{385... | collective-permute-start | bytes 442376 | tf_op jit(solution)/shard_map/ppermute | solution.py:45
  40.3 19.0 %copy-start = (bf16[128,1024]{1,0:T(8,128)(2,1)S(1)}, bf16[128,1024]{1,0:T(8,128)(2,1)}, u32[]{:S(2)}) copy-start(bf16[128,1024]{1,0:T(8,128)(2,1)} %param.5) | copy-start | bytes 786436
  40.3 32.8 %collective-permute-start.7 = (bf16[4,4,144,128]{3,2,1,0:T(8,128)(2,1)S(1)}, bf16[4,4,144,128]{3,2,1,0:T(8,128)(2,1)S(1)}, u32[]{:S(2)}, u32[]{:S(2)}) collective-permute-start(bf16[4,4,144,128]{3,2,1,0:T(8,128)(2,1)S(1)} %get-tuple-element.8), channel_id=1, source_target_pairs={{0,1},{1,0},{2,3},{3,2},{4,5},{5,4},{6,7},{7,6},{8,9},{9,8},{10,11... | collective-permute-start | bytes 1769480 | tf_op jit(solution)/shard_map/ppermute | solution.py:45
  43.3 27.1 %copy-start.2 = (f32[1024]{0:T(1024)S(1)}, f32[1024]{0:T(1024)}, u32[]{:S(2)}) copy-start(f32[1024]{0:T(1024)} %param.9) | copy-start | bytes 12292
  43.3 38.4 %all-to-all-start = ((bf16[16,128,128]{2,1,0:T(8,128)(2,1)}), bf16[16,128,128]{2,1,0:T(8,128)(2,1)S(1)}, u32[]{:S(2)}, u32[]{:S(2)}) async-start(bf16[16,128,128]{2,1,0:T(8,128)(2,1)} %broadcast_in_dim.29), calls=%async_computation | async-start | bytes 1048576 | tf_op jit(solution)/shard_map/all_to_all | solution.py:41
  59.5 11.0 %collective-permute-start.15 = (bf16[128,256]{0,1:T(8,128)(2,1)S(1)}, bf16[128,256]{0,1:T(8,128)(2,1)S(1)}, u32[]{:S(2)}, u32[]{:S(2)}) collective-permute-start(bf16[128,256]{0,1:T(8,128)(2,1)S(1)} %copy.77), channel_id=1, source_target_pairs={{0,128},{128,256},{256,384},{384,0},{1,129},{129,257},{257,385},{3... | collective-permute-start | bytes 196616 | tf_op jit(solution)/shard_map/ppermute | solution.py:45
  64.8 7.7 %collective-permute-start.16 = (bf16[128,256]{0,1:T(8,128)(2,1)S(1)}, bf16[128,256]{0,1:T(8,128)(2,1)S(1)}, u32[]{:S(2)}, u32[]{:S(2)}) collective-permute-start(bf16[128,256]{0,1:T(8,128)(2,1)S(1)} %copy.78), channel_id=1, source_target_pairs={{0,256},{128,384},{256,0},{384,128},{1,257},{129,385},{257,1},{385... | collective-permute-start | bytes 196616 | tf_op jit(solution)/shard_map/ppermute | solution.py:45
  66.8 6.2 %collective-permute-start.17 = (bf16[128,256]{0,1:T(8,128)(2,1)S(1)}, bf16[128,256]{0,1:T(8,128)(2,1)S(1)}, u32[]{:S(2)}, u32[]{:S(2)}) collective-permute-start(bf16[128,256]{0,1:T(8,128)(2,1)S(1)} %copy.79), channel_id=1, source_target_pairs={{0,384},{128,0},{256,128},{384,256},{1,385},{129,1},{257,129},{385... | collective-permute-start | bytes 196616 | tf_op jit(solution)/shard_map/ppermute | solution.py:45
  82.8 18.2 %collective-permute-start.8 = (f32[128,256]{0,1:T(8,128)S(1)}, f32[128,256]{0,1:T(8,128)S(1)}, u32[]{:S(2)}, u32[]{:S(2)}) collective-permute-start(f32[128,256]{0,1:T(8,128)S(1)} %bitcast.75), channel_id=1, source_target_pairs={{0,384},{128,0},{256,128},{384,256},{1,385},{129,1},{257,129},{385... | collective-permute-start | bytes 393224 | tf_op jit(solution)/shard_map/ppermute | solution.py:45
  86.7 35.1 %all-to-all-start.1 = ((bf16[16,144,128]{2,1,0:T(8,128)(2,1)}), bf16[16,144,128]{2,1,0:T(8,128)(2,1)S(1)}, u32[]{:S(2)}, u32[]{:S(2)}) async-start(bf16[16,144,128]{2,1,0:T(8,128)(2,1)} %pad_maximum_fusion.2), calls=%async_computation.1 | async-start | bytes 1179648 | tf_op jit(solution)/shard_map/all_to_all | solution.py:41
  93.6 9.5 %collective-permute-start.9 = (f32[128,256]{0,1:T(8,128)S(1)}, f32[128,256]{0,1:T(8,128)S(1)}, u32[]{:S(2)}, u32[]{:S(2)}) collective-permute-start(f32[128,256]{0,1:T(8,128)S(1)} %bitcast.77), channel_id=1, source_target_pairs={{0,256},{128,384},{256,0},{384,128},{1,257},{129,385},{257,1},{385... | collective-permute-start | bytes 393224 | tf_op jit(solution)/shard_map/ppermute | solution.py:45
  99.0 6.9 %collective-permute-start.10 = (f32[128,256]{0,1:T(8,128)S(1)}, f32[128,256]{0,1:T(8,128)S(1)}, u32[]{:S(2)}, u32[]{:S(2)}) collective-permute-start(f32[128,256]{0,1:T(8,128)S(1)} %bitcast.76), channel_id=1, source_target_pairs={{0,128},{128,256},{256,384},{384,0},{1,129},{129,257},{257,385},{3... | collective-permute-start | bytes 393224 | tf_op jit(solution)/shard_map/ppermute | solution.py:45
  101.1 19.7 %copy-start.1 = (bf16[128,1024]{1,0:T(8,128)(2,1)S(1)}, bf16[128,1024]{1,0:T(8,128)(2,1)}, u32[]{:S(2)}) copy-start(bf16[128,1024]{1,0:T(8,128)(2,1)} %param.6) | copy-start | bytes 786436
  106.2 3.0 %collective-permute-start.11 = (f32[128]{0:T(128)S(1)}, f32[128]{0:T(128)S(1)}, u32[]{:S(2)}, u32[]{:S(2)}) collective-permute-start(f32[128]{0:T(128)S(1)} %fusion.4), channel_id=1, source_target_pairs={{0,1},{1,0},{2,3},{3,2},{4,5},{5,4},{6,7},{7,6},{8,9},{9,8},{10,11... | collective-permute-start | bytes 1544 | tf_op jit(solution)/shard_map/ppermute | solution.py:45
  109.2 9.6 %collective-permute-start.12 = (f32[128]{0:T(128)S(1)}, f32[128]{0:T(128)S(1)}, u32[]{:S(2)}, u32[]{:S(2)}) collective-permute-start(f32[128]{0:T(128)S(1)} %add.96), channel_id=1, source_target_pairs={{0,2},{2,4},{4,6},{6,0},{1,3},{3,5},{5,7},{7,1},{8,10},{10,12},{12... | collective-permute-start | bytes 1544 | tf_op jit(solution)/shard_map/ppermute | solution.py:45
  111.1 7.7 %collective-permute-start.13 = (f32[128]{0:T(128)S(1)}, f32[128]{0:T(128)S(1)}, u32[]{:S(2)}, u32[]{:S(2)}) collective-permute-start(f32[128]{0:T(128)S(1)} %add.96), channel_id=1, source_target_pairs={{0,4},{2,6},{4,0},{6,2},{1,5},{3,7},{5,1},{7,3},{8,12},{10,14},{12... | collective-permute-start | bytes 1544 | tf_op jit(solution)/shard_map/ppermute | solution.py:45
  113.2 7.6 %collective-permute-start.14 = (f32[128]{0:T(128)S(1)}, f32[128]{0:T(128)S(1)}, u32[]{:S(2)}, u32[]{:S(2)}) collective-permute-start(f32[128]{0:T(128)S(1)} %add.96), channel_id=1, source_target_pairs={{0,6},{2,0},{4,2},{6,4},{1,7},{3,1},{5,3},{7,5},{8,14},{10,8},{12,... | collective-permute-start | bytes 1544 | tf_op jit(solution)/shard_map/ppermute | solution.py:45
  121.9 16.2 %collective-permute-start.19 = (f32[1,256]{1,0:T(1,128)S(1)}, f32[1,256]{1,0:T(1,128)S(1)}, u32[]{:S(2)}, u32[]{:S(2)}) collective-permute-start(f32[1,256]{1,0:T(1,128)S(1)} %bitcast.87), channel_id=1, source_target_pairs={{0,128},{128,256},{256,384},{384,0},{1,129},{129,257},{257,385},{3... | collective-permute-start | bytes 3080 | tf_op jit(solution)/shard_map/ppermute | solution.py:45
  124.2 13.8 %collective-permute-start.20 = (f32[1,256]{1,0:T(1,128)S(1)}, f32[1,256]{1,0:T(1,128)S(1)}, u32[]{:S(2)}, u32[]{:S(2)}) collective-permute-start(f32[1,256]{1,0:T(1,128)S(1)} %bitcast.88), channel_id=1, source_target_pairs={{0,256},{128,384},{256,0},{384,128},{1,257},{129,385},{257,1},{385... | collective-permute-start | bytes 3080 | tf_op jit(solution)/shard_map/ppermute | solution.py:45
  127.5 10.5 %collective-permute-start.21 = (f32[1,256]{1,0:T(1,128)S(1)}, f32[1,256]{1,0:T(1,128)S(1)}, u32[]{:S(2)}, u32[]{:S(2)}) collective-permute-start(f32[1,256]{1,0:T(1,128)S(1)} %bitcast.89), channel_id=1, source_target_pairs={{0,384},{128,0},{256,128},{384,256},{1,385},{129,1},{257,129},{385... | collective-permute-start | bytes 3080 | tf_op jit(solution)/shard_map/ppermute | solution.py:45
  132.1 15.1 %collective-permute-start.18 = (f32[128,128]{1,0:T(8,128)S(1)}, f32[128,128]{1,0:T(8,128)S(1)}, u32[]{:S(2)}, u32[]{:S(2)}) collective-permute-start(f32[128,128]{1,0:T(8,128)S(1)} %convert_reduce_fusion.1), channel_id=1, source_target_pairs={{0,0},{16,1},{96,2},{112,3},{64,4},{80,5},{32,6},{48,7},{8,8},{24,... | collective-permute-start | bytes 196616 | tf_op jit(solution)/shard_map/ppermute | solution.py:115

commit v3 on v2

--- a/solution.py
+++ b/solution.py
@@ -31,7 +31,7 @@
                 for zl in range(4):
                     for core in range(2):
                         far_zl, far_core = x, y // 4
-                        place = ((far_zl - zl) % 4) * 2 + (far_core ^ core)
+                        place = (far_zl ^ zl) * 2 + (far_core ^ core)
                         there = flat_index(y % 4, place, zh, far_zl, far_core)
                         moves.append((flat_index(x, y, zh, zl, core), there))
     return moves
@@ -41,12 +41,9 @@
     return lax.all_to_all(value, axes, split_axis=0, concat_axis=0, tiled=True)
 
 
-def shift(value, axis, count, step):
-    return lax.ppermute(value, axis, [(i, (i + step) % count) for i in range(count)])
-
-
-def gather(value, axis, count):
-    return jnp.stack([value] + [shift(value, axis, count, r) for r in range(1, count)])
+def swap(value, axis, mask):
+    count = lax.axis_size(axis)
+    return lax.ppermute(value, axis, [(i, i ^ mask) for i in range(count)])
 
 
 def terms_of(value):
@@ -67,7 +64,15 @@
     moves = weight_moves()
     mine = lax.axis_index("x")
 
+    def quarter(value, r):
+        return lax.dynamic_slice_in_dim(value, (mine ^ r) * QUARTER, QUARTER, axis=value.ndim - 1)
+
     moved = lax.ppermute(kv_weight, AXES, moves)
+
+    near = swap(jnp.concatenate([quarter(layer_input, 3), quarter(layer_input, 2)]), "x", 3)
+    own = quarter(layer_input, 0)
+    far = swap(jnp.concatenate([quarter(layer_input, 1), near[TOK:]]), "x", 1)
+    rows = jnp.concatenate([own, far[:TOK], near[:TOK], far[TOK:]])
 
     cosine, sine = rope_tables(TOK, HD)
     grads = key_value_grad.astype(jnp.float32)
@@ -76,23 +81,24 @@
     kv_pre = jnp.where(lax.axis_index("core") == 0, turned, grads).astype(jnp.bfloat16)
     widened = layer_input.astype(jnp.float32)
     squares = terms_of(jnp.sum(widened * widened, axis=1))
-    packet = jnp.concatenate([kv_pre, jnp.pad(squares, ((0, 13), (0, 0)))], axis=0)
+    packet = jnp.concatenate([kv_pre, jnp.pad(squares, ((0, 13), (0, 0)))], axis=0)[None]
 
-    packets = gather(packet, "zl", 4)
-    pieces_x = [
-        lax.dynamic_slice_in_dim(layer_input, ((mine + r) % 4) * QUARTER, QUARTER, axis=1)
-        for r in range(4)
-    ]
-    rows = jnp.concatenate([pieces_x[0]] + [shift(pieces_x[r], "x", 4, r) for r in range(1, 4)])
-    packets, moved = lax.optimization_barrier((packets, moved))
-    weights = exchange(jnp.broadcast_to(moved[None], (16, HD, HD)), ROW).reshape(4, 2, 2, HD, HD)
-    packets = gather(packets, "x", 4)
-    packets = gather(packets, "core", 2)
-    kv = packets[:, :, :, :TOK].transpose(2, 0, 1, 3, 4).reshape(4, 2, 4 * TOK, HD)
-    total = jnp.sum(packets[:, :, :, TOK : TOK + 3].astype(jnp.float32), axis=(0, 2, 3))
+    for mask in (1, 2):
+        packet = jnp.concatenate([packet, swap(packet, "zl", mask)])
+    packet, moved = lax.optimization_barrier((packet, moved))
+    weights = exchange(jnp.broadcast_to(moved[None], (16, HD, HD)), ROW)
+    packet = packet[None]
+    for mask in (1, 3):
+        packet = jnp.concatenate([packet, swap(packet, "x", mask)])
+    packet, weights = lax.optimization_barrier((packet, weights))
+    weights = weights.reshape(4, 2, 2, HD, HD)
+    packet = jnp.stack([packet, swap(packet, "core", 1)])
+
+    kv = packet[:, :, :, :TOK].transpose(2, 0, 1, 3, 4).reshape(4, 2, 4 * TOK, HD)
+    total = jnp.sum(packet[:, :, :, TOK : TOK + 3].astype(jnp.float32), axis=(0, 2, 3))
     inv_all = lax.rsqrt(total / D + norm_eps)
     inv_scale = inv_all[0][:, None]
-    gain_quarter = lax.dynamic_slice_in_dim(norm_gain, mine * QUARTER, QUARTER)
+    gain_quarter = quarter(norm_gain, 0)
     normal = rows.astype(jnp.float32) * inv_all.reshape(4 * TOK, 1)
     normed = (normal * gain_quarter[None, :]).astype(jnp.bfloat16)
 
@@ -101,6 +107,10 @@
     ).astype(jnp.bfloat16)
     norm_grad = jnp.sum(products.astype(jnp.float32), axis=(0, 1)).reshape(4 * TOK, QUARTER)
     gain_part = jnp.sum(norm_grad * normal, axis=0)
+
+    sent = norm_grad.astype(jnp.bfloat16)
+    near = swap(sent[2 * TOK :], "x", 3)
+    far = swap(jnp.concatenate([sent[TOK : 2 * TOK], near[TOK:]]), "x", 1)
 
     pieces = jnp.einsum(
         "zktc,tbf->zkbcf",
@@ -115,23 +125,22 @@
     weight_grad = lax.ppermute(block, AXES, [(b, a) for a, b in moves])
     gain_sum = jnp.sum(arrived[:, HD : HD + 6].astype(jnp.float32), axis=0)
     gain_sum = jnp.sum(gain_sum.reshape(3, 1, QUARTER), axis=0)
-    gain_sums = gather(gain_sum, "x", 4).reshape(4, 1, QUARTER)
-    place = (mine - jnp.arange(4)) % 4
+    gain_sum, block = lax.optimization_barrier((gain_sum, block))
+    for mask in (1, 3):
+        gain_sum = jnp.concatenate([gain_sum, swap(gain_sum, "x", mask)])
+    place = mine ^ jnp.array([0, 1, 3, 2])
     chosen = place[None, :, None] == jnp.arange(4)[:, None, None]
-    gain_grad = jnp.sum(jnp.where(chosen, gain_sums, 0.0), axis=0).reshape(4 * QUARTER)
+    gain_grad = jnp.sum(jnp.where(chosen, gain_sum[None], 0.0), axis=1).reshape(4 * QUARTER)
 
-    full = jnp.zeros((TOK, 4 * QUARTER), jnp.float32)
-    for r in range(4):
-        part = norm_grad[r * TOK : (r + 1) * TOK]
-        if r:
-            part = shift(part, "x", 4, -r)
-        full = lax.dynamic_update_slice_in_dim(full, part, ((mine + r) % 4) * QUARTER, axis=1)
-    scaled = full * norm_gain[None, :]
+    full = jnp.zeros((TOK, 4 * QUARTER), jnp.bfloat16)
+    for part, r in ((sent[:TOK], 0), (far[:TOK], 1), (near[:TOK], 3), (far[TOK:], 2)):
+        full = lax.dynamic_update_slice_in_dim(full, part, (mine ^ r) * QUARTER, axis=1)
+    scaled = full.astype(jnp.float32) * norm_gain[None, :]
     normal = widened * inv_scale
     inner = jnp.sum(scaled * normal, axis=1)
-    inner = inner + shift(inner, "core", 2, 1)
-    inner_all = gather(inner, "zl", 4)
-    inner = jnp.sum(inner_all, axis=0)[:, None] / D
+    for axis, mask in (("core", 1), ("zl", 1), ("zl", 2)):
+        inner = inner + swap(inner, axis, mask)
+    inner = inner[:, None] / D
     input_grad = (
         residual_grad.astype(jnp.float32) + inv_scale * (scaled - normal * inner)
     ).astype(jnp.bfloat16)

time: 149 us -> 138 us (0.926)
  the two profiles are of different devices: /device:TPU:4 before, /device:TPU:6 now
where the time goes in v3:
time: 138 us; the launch traced here: 137 us
  starting transfers between devices  84.2 us (61%)
  waiting for transfers between devices  39.9 us (29%)
  other arithmetic  5.81 us (4%)
  local copies, waits for them, and re-layouts  4.33 us (3%)
    ppermute x14, starting transfers between devices, swap(): return lax.ppermute(value, axis, [(i, i ^ mask) for i in range(count)])  45.4 us
    ppermute x14, waiting for transfers between devices, swap(): return lax.ppermute(value, axis, [(i, i ^ mask) for i in range(count)])  27.3 us
    all_to_all x2, starting transfers between devices, exchange(): return lax.all_to_all(value, axes, split_axis=0, concat_axis=0, tiled=True)  25.9 us
    ppermute x1, waiting for transfers between devices, shards(): weight_grad = lax.ppermute(block, AXES, [(b, a) for a, b in moves])  7.68 us
    ppermute x1, starting transfers between devices, shards(): moved = lax.ppermute(kv_weight, AXES, moves)  6.98 us
    ppermute x1, starting transfers between devices, shards(): weight_grad = lax.ppermute(block, AXES, [(b, a) for a, b in moves])  5.86 us
    ppermute x1, waiting for transfers between devices, shards(): moved = lax.ppermute(kv_weight, AXES, moves)  3.59 us
  transfers between devices with their start and end apart: 18, of which 13 were waited for; matrix products, arithmetic and copies ran while one was open for 3% of the time, Pallas kernels for 0%

profile of v3, /device:TPU:6, one launch (start us, length us, event | category | flops | bytes accessed | tf_op | source)
XLA Modules:
  0.0 136.8 jit_solution(2109557834508020260)
XLA Ops:
  0.6 1.1 fusion.9
  1.7 0.8 convert_element_type.71
  2.5 0.3 multiply_add_fusion
  2.8 0.9 fusion.14
  3.7 4.3 %collective-permute-start = (bf16[1,144,128]{2,1,0:T(8,128)(2,1)S(1)}, bf16[1,144,128]{2,1,0:T(8,128)(2,1)S(1)}, u32[]{:S(2)}, u32[]{:S(2)}) collective-permute-start(bf16[1,144,128]{2,1,0:T(8,128)(2,1)S(1)} %maximum_bitcast_fusion), channel_id=1, source_target_pairs={{0,2},{2,0},{4,6},{6,4},{1,3},{3,1},{5,7},{7,5},{8,10},{10,8},{12,... | collective-permute-start | bytes 110600 | tf_op jit(solution)/shard_map/ppermute | solution.py:46
  8.0 1.9 %collective-permute-done = bf16[1,144,128]{2,1,0:T(8,128)(2,1)S(1)} collective-permute-done((bf16[1,144,128]{2,1,0:T(8,128)(2,1)S(1)}, bf16[1,144,128]{2,1,0:T(8,128)(2,1)S(1)}, u32[]{:S(2)}, u32[]{:S(2)}) %collective-permute-start) | collective-permute-done | bytes 36896 | tf_op jit(solution)/shard_map/ppermute | solution.py:46
  9.9 6.1 %collective-permute-start.1 = (bf16[2,144,128]{2,1,0:T(8,128)(2,1)S(1)}, bf16[2,144,128]{2,1,0:T(8,128)(2,1)S(1)}, u32[]{:S(2)}, u32[]{:S(2)}) collective-permute-start(bf16[2,144,128]{2,1,0:T(8,128)(2,1)S(1)} %pad_maximum_fusion.9), channel_id=1, source_target_pairs={{0,4},{2,6},{4,0},{6,2},{1,5},{3,7},{5,1},{7,3},{8,12},{10,14},{12... | collective-permute-start | bytes 221192 | tf_op jit(solution)/shard_map/ppermute | solution.py:46
  16.0 7.0 %collective-permute-start.2 = (bf16[128,128]{1,0:T(8,128)(2,1)}, bf16[128,128]{1,0:T(8,128)(2,1)S(1)}, u32[]{:S(2)}, u32[]{:S(2)}) collective-permute-start(bf16[128,128]{1,0:T(8,128)(2,1)} %param.9), channel_id=1, source_target_pairs={{0,0},{1,16},{2,32},{3,48},{4,64},{5,80},{6,96},{7,112},{8,8},{9,2... | collective-permute-start | bytes 98312 | tf_op jit(solution)/shard_map/ppermute | solution.py:70
  23.0 3.6 %collective-permute-done.2 = bf16[128,128]{1,0:T(8,128)(2,1)S(1)} collective-permute-done((bf16[128,128]{1,0:T(8,128)(2,1)}, bf16[128,128]{1,0:T(8,128)(2,1)S(1)}, u32[]{:S(2)}, u32[]{:S(2)}) %collective-permute-start.2) | collective-permute-done | bytes 32800 | tf_op jit(solution)/shard_map/ppermute | solution.py:70
  26.6 0.9 broadcast_in_dim.32
  27.5 15.1 %all-to-all-start = ((bf16[16,128,128]{2,1,0:T(8,128)(2,1)}), bf16[16,128,128]{2,1,0:T(8,128)(2,1)S(1)}, u32[]{:S(2)}, u32[]{:S(2)}) async-start(bf16[16,128,128]{2,1,0:T(8,128)(2,1)} %broadcast_in_dim.32), calls=%async_computation | async-start | bytes 1048576 | tf_op jit(solution)/shard_map/all_to_all | solution.py:41
  42.7 3.9 %collective-permute-start.3 = (bf16[1,4,144,128]{3,2,1,0:T(8,128)(2,1)S(1)}, bf16[1,4,144,128]{3,2,1,0:T(8,128)(2,1)S(1)}, u32[]{:S(2)}, u32[]{:S(2)}) collective-permute-start(bf16[1,4,144,128]{3,2,1,0:T(8,128)(2,1)S(1)} %bitcast.54), channel_id=1, source_target_pairs={{0,128},{128,0},{256,384},{384,256},{1,129},{129,1},{257,385},{385... | collective-permute-start | bytes 442376 | tf_op jit(solution)/shard_map/ppermute | solution.py:46
  46.6 3.1 %collective-permute-done.3 = bf16[1,4,144,128]{3,2,1,0:T(8,128)(2,1)S(1)} collective-permute-done((bf16[1,4,144,128]{3,2,1,0:T(8,128)(2,1)S(1)}, bf16[1,4,144,128]{3,2,1,0:T(8,128)(2,1)S(1)}, u32[]{:S(2)}, u32[]{:S(2)}) %collective-permute-start.3) | collective-permute-done | bytes 147488 | tf_op jit(solution)/shard_map/ppermute | solution.py:46
  49.8 1.9 %collective-permute-start.4 = (bf16[2,4,144,128]{3,2,1,0:T(8,128)(2,1)S(1)}, bf16[2,4,144,128]{3,2,1,0:T(8,128)(2,1)S(1)}, u32[]{:S(2)}, u32[]{:S(2)}) collective-permute-start(bf16[2,4,144,128]{3,2,1,0:T(8,128)(2,1)S(1)} %pad_maximum_fusion.3), channel_id=1, source_target_pairs={{0,384},{128,256},{256,128},{384,0},{1,385},{129,257},{257,129},{3... | collective-permute-start | bytes 884744 | tf_op jit(solution)/shard_map/ppermute | solution.py:46
  51.8 0.1 copy.75
  51.9 0.1 copy.76
  52.0 5.1 %collective-permute-start.11 = (bf16[256,256]{0,1:T(8,128)(2,1)S(1)}, bf16[256,256]{0,1:T(8,128)(2,1)S(1)}, u32[]{:S(2)}, u32[]{:S(2)}) collective-permute-start(bf16[256,256]{0,1:T(8,128)(2,1)S(1)} %pad_maximum_fusion.7), channel_id=1, source_target_pairs={{0,384},{128,256},{256,128},{384,0},{1,385},{129,257},{257,129},{3... | collective-permute-start | bytes 393224 | tf_op jit(solution)/shard_map/ppermute | solution.py:46
  57.2 0.1 copy.74
  57.3 2.3 %collective-permute-done.4 = bf16[2,4,144,128]{3,2,1,0:T(8,128)(2,1)S(1)} collective-permute-done((bf16[2,4,144,128]{3,2,1,0:T(8,128)(2,1)S(1)}, bf16[2,4,144,128]{3,2,1,0:T(8,128)(2,1)S(1)}, u32[]{:S(2)}, u32[]{:S(2)}) %collective-permute-start.4) | collective-permute-done | bytes 294944 | tf_op jit(solution)/shard_map/ppermute | solution.py:46
  59.6 1.3 all-to-all-done
  60.9 1.9 %collective-permute-start.5 = (bf16[4,4,144,128]{3,2,1,0:T(8,128)(2,1)S(1)}, bf16[4,4,144,128]{3,2,1,0:T(8,128)(2,1)S(1)}, u32[]{:S(2)}, u32[]{:S(2)}) collective-permute-start(bf16[4,4,144,128]{3,2,1,0:T(8,128)(2,1)S(1)} %pad_maximum_fusion.1), channel_id=1, source_target_pairs={{0,1},{1,0},{2,3},{3,2},{4,5},{5,4},{6,7},{7,6},{8,9},{9,8},{10,11... | collective-permute-start | bytes 1769480 | tf_op jit(solution)/shard_map/ppermute | solution.py:46
  62.9 2.8 %collective-permute-start.12 = (bf16[256,256]{0,1:T(8,128)(2,1)S(1)}, bf16[256,256]{0,1:T(8,128)(2,1)S(1)}, u32[]{:S(2)}, u32[]{:S(2)}) collective-permute-start(bf16[256,256]{0,1:T(8,128)(2,1)S(1)} %pad_maximum_fusion.8), channel_id=1, source_target_pairs={{0,128},{128,0},{256,384},{384,256},{1,129},{129,1},{257,385},{385... | collective-permute-start | bytes 393224 | tf_op jit(solution)/shard_map/ppermute | solution.py:46
  65.7 0.1 copy.73
  65.9 0.1 copy.63
  66.0 0.1 dynamic-slice_bitcast_fusion
  66.1 0.1 copy.65
  66.2 4.5 %collective-permute-done.12 = bf16[256,256]{0,1:T(8,128)(2,1)S(1)} collective-permute-done((bf16[256,256]{0,1:T(8,128)(2,1)S(1)}, bf16[256,256]{0,1:T(8,128)(2,1)S(1)}, u32[]{:S(2)}, u32[]{:S(2)}) %collective-permute-start.12) | collective-permute-done | bytes 131104 | tf_op jit(solution)/shard_map/ppermute | solution.py:46
  70.7 0.1 copy.64
  70.8 0.1 copy.66
  71.0 0.1 fusion.1
  71.1 0.1 copy.51
  71.2 0.7 fusion
  72.0 0.7 convert_reduce_fusion
  72.7 0.2 multiply_reduce_fusion
  72.9 0.9 pad_maximum_fusion.2
  73.8 10.8 %all-to-all-start.1 = ((bf16[16,144,128]{2,1,0:T(8,128)(2,1)}), bf16[16,144,128]{2,1,0:T(8,128)(2,1)S(1)}, u32[]{:S(2)}, u32[]{:S(2)}) async-start(bf16[16,144,128]{2,1,0:T(8,128)(2,1)} %pad_maximum_fusion.2), calls=%async_computation.1 | async-start | bytes 1179648 | tf_op jit(solution)/shard_map/all_to_all | solution.py:41
  84.6 0.1 copy.55
  84.7 3.1 %collective-permute-start.6 = (bf16[256,256]{0,1:T(8,128)(2,1)S(1)}, bf16[256,256]{0,1:T(8,128)(2,1)S(1)}, u32[]{:S(2)}, u32[]{:S(2)}) collective-permute-start(bf16[256,256]{0,1:T(8,128)(2,1)S(1)} %bitcast.66), channel_id=1, source_target_pairs={{0,384},{128,256},{256,128},{384,0},{1,385},{129,257},{257,129},{3... | collective-permute-start | bytes 393224 | tf_op jit(solution)/shard_map/ppermute | solution.py:46
  87.8 0.1 copy.54
  87.9 4.8 %collective-permute-done.6 = bf16[256,256]{0,1:T(8,128)(2,1)S(1)} collective-permute-done((bf16[256,256]{0,1:T(8,128)(2,1)S(1)}, bf16[256,256]{0,1:T(8,128)(2,1)S(1)}, u32[]{:S(2)}, u32[]{:S(2)}) %collective-permute-start.6) | collective-permute-done | bytes 131104 | tf_op jit(solution)/shard_map/ppermute | solution.py:46
  92.8 1.9 %collective-permute-start.7 = (bf16[256,256]{0,1:T(8,128)(2,1)S(1)}, bf16[256,256]{0,1:T(8,128)(2,1)S(1)}, u32[]{:S(2)}, u32[]{:S(2)}) collective-permute-start(bf16[256,256]{0,1:T(8,128)(2,1)S(1)} %pad_maximum_fusion.6), channel_id=1, source_target_pairs={{0,128},{128,0},{256,384},{384,256},{1,129},{129,1},{257,385},{385... | collective-permute-start | bytes 393224 | tf_op jit(solution)/shard_map/ppermute | solution.py:46
  94.7 0.1 copy.52
  94.9 0.1 copy.53
  95.0 0.1 copy.57
  95.2 4.5 %collective-permute-done.7 = bf16[256,256]{0,1:T(8,128)(2,1)S(1)} collective-permute-done((bf16[256,256]{0,1:T(8,128)(2,1)S(1)}, bf16[256,256]{0,1:T(8,128)(2,1)S(1)}, u32[]{:S(2)}, u32[]{:S(2)}) %collective-permute-start.7) | collective-permute-done | bytes 131104 | tf_op jit(solution)/shard_map/ppermute | solution.py:46
  99.7 0.1 copy.56
  99.8 0.1 copy.58
  99.9 0.2 fusion.4
  100.2 1.9 %collective-permute-start.8 = (f32[128]{0:T(128)S(1)}, f32[128]{0:T(128)S(1)}, u32[]{:S(2)}, u32[]{:S(2)}) collective-permute-start(f32[128]{0:T(128)S(1)} %fusion.4), channel_id=1, source_target_pairs={{0,1},{1,0},{2,3},{3,2},{4,5},{5,4},{6,7},{7,6},{8,9},{9,8},{10,11... | collective-permute-start | bytes 1544 | tf_op jit(solution)/shard_map/ppermute | solution.py:46
  102.1 1.1 collective-permute-done.8
  103.2 3.8 %collective-permute-start.9 = (f32[128]{0:T(128)S(1)}, f32[128]{0:T(128)S(1)}, u32[]{:S(2)}, u32[]{:S(2)}) collective-permute-start(f32[128]{0:T(128)S(1)} %add.54), channel_id=1, source_target_pairs={{0,2},{2,0},{4,6},{6,4},{1,3},{3,1},{5,7},{7,5},{8,10},{10,8},{12,... | collective-permute-start | bytes 1544 | tf_op jit(solution)/shard_map/ppermute | solution.py:46
  107.0 1.6 %collective-permute-done.9 = f32[128]{0:T(128)S(1)} collective-permute-done((f32[128]{0:T(128)S(1)}, f32[128]{0:T(128)S(1)}, u32[]{:S(2)}, u32[]{:S(2)}) %collective-permute-start.9) | collective-permute-done | bytes 544 | tf_op jit(solution)/shard_map/ppermute | solution.py:46
  108.6 2.3 %collective-permute-start.10 = (f32[128]{0:T(128)S(1)}, f32[128]{0:T(128)S(1)}, u32[]{:S(2)}, u32[]{:S(2)}) collective-permute-start(f32[128]{0:T(128)S(1)} %add.55), channel_id=1, source_target_pairs={{0,4},{2,6},{4,0},{6,2},{1,5},{3,7},{5,1},{7,3},{8,12},{10,14},{12... | collective-permute-start | bytes 1544 | tf_op jit(solution)/shard_map/ppermute | solution.py:46
  111.0 0.1 convert_reduce_fusion.1
  111.1 1.9 %collective-permute-start.14 = (f32[1,256]{1,0:T(1,128)S(1)}, f32[1,256]{1,0:T(1,128)S(1)}, u32[]{:S(2)}, u32[]{:S(2)}) collective-permute-start(f32[1,256]{1,0:T(1,128)S(1)} %bitcast.68), channel_id=1, source_target_pairs={{0,128},{128,0},{256,384},{384,256},{1,129},{129,1},{257,385},{385... | collective-permute-start | bytes 3080 | tf_op jit(solution)/shard_map/ppermute | solution.py:46
  113.0 1.9 %collective-permute-done.10 = f32[128]{0:T(128)S(1)} collective-permute-done((f32[128]{0:T(128)S(1)}, f32[128]{0:T(128)S(1)}, u32[]{:S(2)}, u32[]{:S(2)}) %collective-permute-start.10) | collective-permute-done | bytes 544 | tf_op jit(solution)/shard_map/ppermute | solution.py:46
  114.9 1.6 %collective-permute-done.14 = f32[1,256]{1,0:T(1,128)S(1)} collective-permute-done((f32[1,256]{1,0:T(1,128)S(1)}, f32[1,256]{1,0:T(1,128)S(1)}, u32[]{:S(2)}, u32[]{:S(2)}) %collective-permute-start.14) | collective-permute-done | bytes 1056 | tf_op jit(solution)/shard_map/ppermute | solution.py:46
  116.6 4.3 %collective-permute-start.15 = (f32[2,256]{1,0:T(2,128)S(1)}, f32[2,256]{1,0:T(2,128)S(1)}, u32[]{:S(2)}, u32[]{:S(2)}) collective-permute-start(f32[2,256]{1,0:T(2,128)S(1)} %pad_maximum_fusion.13), channel_id=1, source_target_pairs={{0,384},{128,256},{256,128},{384,0},{1,385},{129,257},{257,129},{3... | collective-permute-start | bytes 6152 | tf_op jit(solution)/shard_map/ppermute | solution.py:46
  120.9 1.0 fusion.8
  121.9 5.9 %collective-permute-start.13 = (f32[128,128]{1,0:T(8,128)S(1)}, f32[128,128]{1,0:T(8,128)S(1)}, u32[]{:S(2)}, u32[]{:S(2)}) collective-permute-start(f32[128,128]{1,0:T(8,128)S(1)} %convert_reduce_fusion.1), channel_id=1, source_target_pairs={{0,0},{16,1},{32,2},{48,3},{64,4},{80,5},{96,6},{112,7},{8,8},{24,... | collective-permute-start | bytes 196616 | tf_op jit(solution)/shard_map/ppermute | solution.py:125
  127.8 0.1 select_reduce_fusion
  127.9 0.6 copy.77
  128.5 7.7 %collective-permute-done.13 = f32[128,128]{1,0:T(8,128)S(1)} collective-permute-done((f32[128,128]{1,0:T(8,128)S(1)}, f32[128,128]{1,0:T(8,128)S(1)}, u32[]{:S(2)}, u32[]{:S(2)}) %collective-permute-start.13) | collective-permute-done | bytes 65568 | tf_op jit(solution)/shard_map/ppermute | solution.py:125
  136.1 0.6 copy.83
  (55 shorter events, 0.7 us)
Async XLA Ops:
  3.7 6.2 %collective-permute-start = (bf16[1,144,128]{2,1,0:T(8,128)(2,1)S(1)}, bf16[1,144,128]{2,1,0:T(8,128)(2,1)S(1)}, u32[]{:S(2)}, u32[]{:S(2)}) collective-permute-start(bf16[1,144,128]{2,1,0:T(8,128)(2,1)S(1)} %maximum_bitcast_fusion), channel_id=1, source_target_pairs={{0,2},{2,0},{4,6},{6,4},{1,3},{3,1},{5,7},{7,5},{8,10},{10,8},{12,... | collective-permute-start | bytes 110600 | tf_op jit(solution)/shard_map/ppermute | solution.py:46
  9.9 13.1 %collective-permute-start.1 = (bf16[2,144,128]{2,1,0:T(8,128)(2,1)S(1)}, bf16[2,144,128]{2,1,0:T(8,128)(2,1)S(1)}, u32[]{:S(2)}, u32[]{:S(2)}) collective-permute-start(bf16[2,144,128]{2,1,0:T(8,128)(2,1)S(1)} %pad_maximum_fusion.9), channel_id=1, source_target_pairs={{0,4},{2,6},{4,0},{6,2},{1,5},{3,7},{5,1},{7,3},{8,12},{10,14},{12... | collective-permute-start | bytes 221192 | tf_op jit(solution)/shard_map/ppermute | solution.py:46
  16.0 10.6 %collective-permute-start.2 = (bf16[128,128]{1,0:T(8,128)(2,1)}, bf16[128,128]{1,0:T(8,128)(2,1)S(1)}, u32[]{:S(2)}, u32[]{:S(2)}) collective-permute-start(bf16[128,128]{1,0:T(8,128)(2,1)} %param.9), channel_id=1, source_target_pairs={{0,0},{1,16},{2,32},{3,48},{4,64},{5,80},{6,96},{7,112},{8,8},{9,2... | collective-permute-start | bytes 98312 | tf_op jit(solution)/shard_map/ppermute | solution.py:70
  23.0 28.7 %copy-start = (bf16[128,1024]{1,0:T(8,128)(2,1)S(1)}, bf16[128,1024]{1,0:T(8,128)(2,1)}, u32[]{:S(2)}) copy-start(bf16[128,1024]{1,0:T(8,128)(2,1)} %param.6) | copy-start | bytes 786436
  27.5 33.4 %all-to-all-start = ((bf16[16,128,128]{2,1,0:T(8,128)(2,1)}), bf16[16,128,128]{2,1,0:T(8,128)(2,1)S(1)}, u32[]{:S(2)}, u32[]{:S(2)}) async-start(bf16[16,128,128]{2,1,0:T(8,128)(2,1)} %broadcast_in_dim.32), calls=%async_computation | async-start | bytes 1048576 | tf_op jit(solution)/shard_map/all_to_all | solution.py:41
  42.7 7.0 %collective-permute-start.3 = (bf16[1,4,144,128]{3,2,1,0:T(8,128)(2,1)S(1)}, bf16[1,4,144,128]{3,2,1,0:T(8,128)(2,1)S(1)}, u32[]{:S(2)}, u32[]{:S(2)}) collective-permute-start(bf16[1,4,144,128]{3,2,1,0:T(8,128)(2,1)S(1)} %bitcast.54), channel_id=1, source_target_pairs={{0,128},{128,0},{256,384},{384,256},{1,129},{129,1},{257,385},{385... | collective-permute-start | bytes 442376 | tf_op jit(solution)/shard_map/ppermute | solution.py:46
  49.8 9.8 %collective-permute-start.4 = (bf16[2,4,144,128]{3,2,1,0:T(8,128)(2,1)S(1)}, bf16[2,4,144,128]{3,2,1,0:T(8,128)(2,1)S(1)}, u32[]{:S(2)}, u32[]{:S(2)}) collective-permute-start(bf16[2,4,144,128]{3,2,1,0:T(8,128)(2,1)S(1)} %pad_maximum_fusion.3), channel_id=1, source_target_pairs={{0,384},{128,256},{256,128},{384,0},{1,385},{129,257},{257,129},{3... | collective-permute-start | bytes 884744 | tf_op jit(solution)/shard_map/ppermute | solution.py:46
  52.0 10.8 %collective-permute-start.11 = (bf16[256,256]{0,1:T(8,128)(2,1)S(1)}, bf16[256,256]{0,1:T(8,128)(2,1)S(1)}, u32[]{:S(2)}, u32[]{:S(2)}) collective-permute-start(bf16[256,256]{0,1:T(8,128)(2,1)S(1)} %pad_maximum_fusion.7), channel_id=1, source_target_pairs={{0,384},{128,256},{256,128},{384,0},{1,385},{129,257},{257,129},{3... | collective-permute-start | bytes 393224 | tf_op jit(solution)/shard_map/ppermute | solution.py:46
  57.2 8.8 %copy-start.2 = (f32[1024]{0:T(1024)S(1)}, f32[1024]{0:T(1024)}, u32[]{:S(2)}) copy-start(f32[1024]{0:T(1024)} %param.10) | copy-start | bytes 12292
  60.9 10.0 %collective-permute-start.5 = (bf16[4,4,144,128]{3,2,1,0:T(8,128)(2,1)S(1)}, bf16[4,4,144,128]{3,2,1,0:T(8,128)(2,1)S(1)}, u32[]{:S(2)}, u32[]{:S(2)}) collective-permute-start(bf16[4,4,144,128]{3,2,1,0:T(8,128)(2,1)S(1)} %pad_maximum_fusion.1), channel_id=1, source_target_pairs={{0,1},{1,0},{2,3},{3,2},{4,5},{5,4},{6,7},{7,6},{8,9},{9,8},{10,11... | collective-permute-start | bytes 1769480 | tf_op jit(solution)/shard_map/ppermute | solution.py:46
  62.9 7.8 %collective-permute-start.12 = (bf16[256,256]{0,1:T(8,128)(2,1)S(1)}, bf16[256,256]{0,1:T(8,128)(2,1)S(1)}, u32[]{:S(2)}, u32[]{:S(2)}) collective-permute-start(bf16[256,256]{0,1:T(8,128)(2,1)S(1)} %pad_maximum_fusion.8), channel_id=1, source_target_pairs={{0,128},{128,0},{256,384},{384,256},{1,129},{129,1},{257,385},{385... | collective-permute-start | bytes 393224 | tf_op jit(solution)/shard_map/ppermute | solution.py:46
  73.8 37.2 %all-to-all-start.1 = ((bf16[16,144,128]{2,1,0:T(8,128)(2,1)}), bf16[16,144,128]{2,1,0:T(8,128)(2,1)S(1)}, u32[]{:S(2)}, u32[]{:S(2)}) async-start(bf16[16,144,128]{2,1,0:T(8,128)(2,1)} %pad_maximum_fusion.2), calls=%async_computation.1 | async-start | bytes 1179648 | tf_op jit(solution)/shard_map/all_to_all | solution.py:41
  84.7 8.1 %collective-permute-start.6 = (bf16[256,256]{0,1:T(8,128)(2,1)S(1)}, bf16[256,256]{0,1:T(8,128)(2,1)S(1)}, u32[]{:S(2)}, u32[]{:S(2)}) collective-permute-start(bf16[256,256]{0,1:T(8,128)(2,1)S(1)} %bitcast.66), channel_id=1, source_target_pairs={{0,384},{128,256},{256,128},{384,0},{1,385},{129,257},{257,129},{3... | collective-permute-start | bytes 393224 | tf_op jit(solution)/shard_map/ppermute | solution.py:46
  92.8 6.9 %collective-permute-start.7 = (bf16[256,256]{0,1:T(8,128)(2,1)S(1)}, bf16[256,256]{0,1:T(8,128)(2,1)S(1)}, u32[]{:S(2)}, u32[]{:S(2)}) collective-permute-start(bf16[256,256]{0,1:T(8,128)(2,1)S(1)} %pad_maximum_fusion.6), channel_id=1, source_target_pairs={{0,128},{128,0},{256,384},{384,256},{1,129},{129,1},{257,385},{385... | collective-permute-start | bytes 393224 | tf_op jit(solution)/shard_map/ppermute | solution.py:46
  94.8 7.2 %copy-start.3 = (s32[4]{0:T(128)S(1)}, s32[4]{0:T(128)}, u32[]{:S(2)}) copy-start(s32[4]{0:T(128)} %constant.43.clone) | copy-start | bytes 52
  95.1 25.8 %copy-start.1 = (bf16[128,1024]{1,0:T(8,128)(2,1)S(1)}, bf16[128,1024]{1,0:T(8,128)(2,1)}, u32[]{:S(2)}) copy-start(bf16[128,1024]{1,0:T(8,128)(2,1)} %param.7) | copy-start | bytes 786436
  100.2 3.0 %collective-permute-start.8 = (f32[128]{0:T(128)S(1)}, f32[128]{0:T(128)S(1)}, u32[]{:S(2)}, u32[]{:S(2)}) collective-permute-start(f32[128]{0:T(128)S(1)} %fusion.4), channel_id=1, source_target_pairs={{0,1},{1,0},{2,3},{3,2},{4,5},{5,4},{6,7},{7,6},{8,9},{9,8},{10,11... | collective-permute-start | bytes 1544 | tf_op jit(solution)/shard_map/ppermute | solution.py:46
  103.2 5.4 %collective-permute-start.9 = (f32[128]{0:T(128)S(1)}, f32[128]{0:T(128)S(1)}, u32[]{:S(2)}, u32[]{:S(2)}) collective-permute-start(f32[128]{0:T(128)S(1)} %add.54), channel_id=1, source_target_pairs={{0,2},{2,0},{4,6},{6,4},{1,3},{3,1},{5,7},{7,5},{8,10},{10,8},{12,... | collective-permute-start | bytes 1544 | tf_op jit(solution)/shard_map/ppermute | solution.py:46
  108.6 6.3 %collective-permute-start.10 = (f32[128]{0:T(128)S(1)}, f32[128]{0:T(128)S(1)}, u32[]{:S(2)}, u32[]{:S(2)}) collective-permute-start(f32[128]{0:T(128)S(1)} %add.55), channel_id=1, source_target_pairs={{0,4},{2,6},{4,0},{6,2},{1,5},{3,7},{5,1},{7,3},{8,12},{10,14},{12... | collective-permute-start | bytes 1544 | tf_op jit(solution)/shard_map/ppermute | solution.py:46
  111.1 5.5 %collective-permute-start.14 = (f32[1,256]{1,0:T(1,128)S(1)}, f32[1,256]{1,0:T(1,128)S(1)}, u32[]{:S(2)}, u32[]{:S(2)}) collective-permute-start(f32[1,256]{1,0:T(1,128)S(1)} %bitcast.68), channel_id=1, source_target_pairs={{0,128},{128,0},{256,384},{384,256},{1,129},{129,1},{257,385},{385... | collective-permute-start | bytes 3080 | tf_op jit(solution)/shard_map/ppermute | solution.py:46
  116.6 11.2 %collective-permute-start.15 = (f32[2,256]{1,0:T(2,128)S(1)}, f32[2,256]{1,0:T(2,128)S(1)}, u32[]{:S(2)}, u32[]{:S(2)}) collective-permute-start(f32[2,256]{1,0:T(2,128)S(1)} %pad_maximum_fusion.13), channel_id=1, source_target_pairs={{0,384},{128,256},{256,128},{384,0},{1,385},{129,257},{257,129},{3... | collective-permute-start | bytes 6152 | tf_op jit(solution)/shard_map/ppermute | solution.py:46
  121.9 14.3 %collective-permute-start.13 = (f32[128,128]{1,0:T(8,128)S(1)}, f32[128,128]{1,0:T(8,128)S(1)}, u32[]{:S(2)}, u32[]{:S(2)}) collective-permute-start(f32[128,128]{1,0:T(8,128)S(1)} %convert_reduce_fusion.1), channel_id=1, source_target_pairs={{0,0},{16,1},{32,2},{48,3},{64,4},{80,5},{96,6},{112,7},{8,8},{24,... | collective-permute-start | bytes 196616 | tf_op jit(solution)/shard_map/ppermute | solution.py:125

commit v4 on v3

--- a/solution.py
+++ b/solution.py
@@ -70,9 +70,6 @@
     moved = lax.ppermute(kv_weight, AXES, moves)
 
     near = swap(jnp.concatenate([quarter(layer_input, 3), quarter(layer_input, 2)]), "x", 3)
-    own = quarter(layer_input, 0)
-    far = swap(jnp.concatenate([quarter(layer_input, 1), near[TOK:]]), "x", 1)
-    rows = jnp.concatenate([own, far[:TOK], near[:TOK], far[TOK:]])
 
     cosine, sine = rope_tables(TOK, HD)
     grads = key_value_grad.astype(jnp.float32)
@@ -83,14 +80,17 @@
     squares = terms_of(jnp.sum(widened * widened, axis=1))
     packet = jnp.concatenate([kv_pre, jnp.pad(squares, ((0, 13), (0, 0)))], axis=0)[None]
 
-    for mask in (1, 2):
-        packet = jnp.concatenate([packet, swap(packet, "zl", mask)])
-    packet, moved = lax.optimization_barrier((packet, moved))
+    packet = jnp.concatenate([packet, swap(packet, "zl", 1)])
+    packet, moved, near = lax.optimization_barrier((packet, moved, near))
     weights = exchange(jnp.broadcast_to(moved[None], (16, HD, HD)), ROW)
+    far = swap(jnp.concatenate([quarter(layer_input, 1), near[TOK:]]), "x", 1)
+    packet = jnp.concatenate([packet, swap(packet, "zl", 2)])
+    packet, far = lax.optimization_barrier((packet, far))
+    rows = jnp.concatenate([quarter(layer_input, 0), far[:TOK], near[:TOK], far[TOK:]])
     packet = packet[None]
-    for mask in (1, 3):
-        packet = jnp.concatenate([packet, swap(packet, "x", mask)])
+    packet = jnp.concatenate([packet, swap(packet, "x", 1)])
     packet, weights = lax.optimization_barrier((packet, weights))
+    packet = jnp.concatenate([packet, swap(packet, "x", 3)])
     weights = weights.reshape(4, 2, 2, HD, HD)
     packet = jnp.stack([packet, swap(packet, "core", 1)])
 
@@ -110,7 +110,6 @@
 
     sent = norm_grad.astype(jnp.bfloat16)
     near = swap(sent[2 * TOK :], "x", 3)
-    far = swap(jnp.concatenate([sent[TOK : 2 * TOK], near[TOK:]]), "x", 1)
 
     pieces = jnp.einsum(
         "zktc,tbf->zkbcf",
@@ -120,14 +119,16 @@
     ).astype(jnp.bfloat16).reshape(16, HD, HD)
     gain_terms = jnp.pad(terms_of(gain_part).reshape(6, HD), ((0, 10), (0, 0)))
     gain_terms = jnp.broadcast_to(gain_terms[None], (16, 16, HD))
+    gain_terms, near = lax.optimization_barrier((gain_terms, near))
+    far = swap(jnp.concatenate([sent[TOK : 2 * TOK], near[TOK:]]), "x", 1)
     arrived = exchange(jnp.concatenate([pieces, gain_terms], axis=1), ROW)
     block = jnp.sum(arrived[:, :HD].astype(jnp.float32), axis=0)
     weight_grad = lax.ppermute(block, AXES, [(b, a) for a, b in moves])
     gain_sum = jnp.sum(arrived[:, HD : HD + 6].astype(jnp.float32), axis=0)
     gain_sum = jnp.sum(gain_sum.reshape(3, 1, QUARTER), axis=0)
-    gain_sum, block = lax.optimization_barrier((gain_sum, block))
-    for mask in (1, 3):
-        gain_sum = jnp.concatenate([gain_sum, swap(gain_sum, "x", mask)])
+    gain_sum = jnp.concatenate([gain_sum, swap(gain_sum, "x", 1)])
+    gain_sum, weight_grad = lax.optimization_barrier((gain_sum, weight_grad))
+    gain_sum = jnp.concatenate([gain_sum, swap(gain_sum, "x", 3)])
     place = mine ^ jnp.array([0, 1, 3, 2])
     chosen = place[None, :, None] == jnp.arange(4)[:, None, None]
     gain_grad = jnp.sum(jnp.where(chosen, gain_sum[None], 0.0), axis=1).reshape(4 * QUARTER)

time: 138 us -> 149 us (1.080)
  waiting for transfers between devices: 39.9 us -> 50.3 us
    ppermute x14, waiting for transfers between devices: 27.3 us -> 32.6 us  [swap(): return lax.ppermute(value, axis, [(i, i ^ mask) for i in range(count)])]
    all_to_all x2, waiting for transfers between devices: 1.28 us -> 6.37 us  [exchange(): return lax.all_to_all(value, axes, split_axis=0, concat_axis=0, tiled=True)]
    ppermute x1, starting transfers between devices: 5.86 us -> 3.33 us  [shards(): weight_grad = lax.ppermute(block, AXES, [(b, a) for a, b in moves])]
    ppermute x1, waiting for transfers between devices: 7.68 us -> 9.79 us  [shards(): weight_grad = lax.ppermute(block, AXES, [(b, a) for a, b in moves])]
    ppermute x1, waiting for transfers between devices: 3.59 us -> 1.55 us  [shards(): moved = lax.ppermute(kv_weight, AXES, moves)]
  transfers between devices with their start and end apart: 18 -> 18, of which waited for: 13 -> 12; matrix products, arithmetic and copies ran while one was open for 3% -> 4% of each run, Pallas kernels for 0% -> 0%
where the time goes in v4:
time: 149 us; the launch traced here: 148 us
  starting transfers between devices  84.5 us (57%)
  waiting for transfers between devices  50.3 us (34%)
  other arithmetic  5.75 us (4%)
  local copies, waits for them, and re-layouts  5.31 us (4%)
    ppermute x14, starting transfers between devices, swap(): return lax.ppermute(value, axis, [(i, i ^ mask) for i in range(count)])  46.5 us
    ppermute x14, waiting for transfers between devices, swap(): return lax.ppermute(value, axis, [(i, i ^ mask) for i in range(count)])  32.6 us
    all_to_all x2, starting transfers between devices, exchange(): return lax.all_to_all(value, axes, split_axis=0, concat_axis=0, tiled=True)  26.3 us
    ppermute x1, waiting for transfers between devices, shards(): weight_grad = lax.ppermute(block, AXES, [(b, a) for a, b in moves])  9.79 us
    ppermute x1, starting transfers between devices, shards(): moved = lax.ppermute(kv_weight, AXES, moves)  8.41 us
    all_to_all x2, waiting for transfers between devices, exchange(): return lax.all_to_all(value, axes, split_axis=0, concat_axis=0, tiled=True)  6.37 us
    ppermute x1, starting transfers between devices, shards(): weight_grad = lax.ppermute(block, AXES, [(b, a) for a, b in moves])  3.33 us
  transfers between devices with their start and end apart: 18, of which 12 were waited for; matrix products, arithmetic and copies ran while one was open for 4% of the time, Pallas kernels for 0%

profile of v4, /device:TPU:6, one launch (start us, length us, event | category | flops | bytes accessed | tf_op | source)
XLA Modules:
  0.0 148.5 jit_solution(3072051472461247991)
XLA Ops:
  0.7 1.1 fusion.9
  1.8 0.8 convert_element_type.71
  2.5 0.3 multiply_add_fusion
  2.8 0.9 fusion.14
  3.7 4.3 %collective-permute-start = (bf16[1,144,128]{2,1,0:T(8,128)(2,1)S(1)}, bf16[1,144,128]{2,1,0:T(8,128)(2,1)S(1)}, u32[]{:S(2)}, u32[]{:S(2)}) collective-permute-start(bf16[1,144,128]{2,1,0:T(8,128)(2,1)S(1)} %maximum_bitcast_fusion), channel_id=1, source_target_pairs={{0,2},{2,0},{4,6},{6,4},{1,3},{3,1},{5,7},{7,5},{8,10},{10,8},{12,... | collective-permute-start | bytes 110600 | tf_op jit(solution)/shard_map/ppermute | solution.py:46
  8.0 1.0 constant_dynamic-slice_fusion
  9.0 0.1 copy.73
  9.1 0.1 copy.74
  9.2 5.4 %collective-permute-start.2 = (bf16[256,256]{0,1:T(8,128)(2,1)S(1)}, bf16[256,256]{0,1:T(8,128)(2,1)S(1)}, u32[]{:S(2)}, u32[]{:S(2)}) collective-permute-start(bf16[256,256]{0,1:T(8,128)(2,1)S(1)} %pad_maximum_fusion.5), channel_id=1, source_target_pairs={{0,384},{128,256},{256,128},{384,0},{1,385},{129,257},{257,129},{3... | collective-permute-start | bytes 393224 | tf_op jit(solution)/shard_map/ppermute | solution.py:46
  14.7 8.4 %collective-permute-start.1 = (bf16[128,128]{1,0:T(8,128)(2,1)S(1)}, bf16[128,128]{1,0:T(8,128)(2,1)S(1)}, u32[]{:S(2)}, u32[]{:S(2)}) collective-permute-start(bf16[128,128]{1,0:T(8,128)(2,1)S(1)} %copy-done.3), channel_id=1, source_target_pairs={{0,0},{1,16},{2,32},{3,48},{4,64},{5,80},{6,96},{7,112},{8,8},{9,2... | collective-permute-start | bytes 98312 | tf_op jit(solution)/shard_map/ppermute | solution.py:70
  23.1 1.5 %collective-permute-done.1 = bf16[128,128]{1,0:T(8,128)(2,1)S(1)} collective-permute-done((bf16[128,128]{1,0:T(8,128)(2,1)S(1)}, bf16[128,128]{1,0:T(8,128)(2,1)S(1)}, u32[]{:S(2)}, u32[]{:S(2)}) %collective-permute-start.1) | collective-permute-done | bytes 32800 | tf_op jit(solution)/shard_map/ppermute | solution.py:70
  24.7 0.9 broadcast_in_dim.32
  25.6 13.8 %all-to-all-start = ((bf16[16,128,128]{2,1,0:T(8,128)(2,1)}), bf16[16,128,128]{2,1,0:T(8,128)(2,1)S(1)}, u32[]{:S(2)}, u32[]{:S(2)}) async-start(bf16[16,128,128]{2,1,0:T(8,128)(2,1)} %broadcast_in_dim.32), calls=%async_computation | async-start | bytes 1048576 | tf_op jit(solution)/shard_map/all_to_all | solution.py:41
  39.4 0.1 copy.75
  39.5 2.5 %collective-permute-start.3 = (bf16[2,144,128]{2,1,0:T(8,128)(2,1)S(1)}, bf16[2,144,128]{2,1,0:T(8,128)(2,1)S(1)}, u32[]{:S(2)}, u32[]{:S(2)}) collective-permute-start(bf16[2,144,128]{2,1,0:T(8,128)(2,1)S(1)} %pad_maximum_fusion.8), channel_id=1, source_target_pairs={{0,4},{2,6},{4,0},{6,2},{1,5},{3,7},{5,1},{7,3},{8,12},{10,14},{12... | collective-permute-start | bytes 221192 | tf_op jit(solution)/shard_map/ppermute | solution.py:46
  42.1 3.4 %collective-permute-start.4 = (bf16[256,256]{0,1:T(8,128)(2,1)S(1)}, bf16[256,256]{0,1:T(8,128)(2,1)S(1)}, u32[]{:S(2)}, u32[]{:S(2)}) collective-permute-start(bf16[256,256]{0,1:T(8,128)(2,1)S(1)} %pad_maximum_fusion.6), channel_id=1, source_target_pairs={{0,128},{128,0},{256,384},{384,256},{1,129},{129,1},{257,385},{385... | collective-permute-start | bytes 393224 | tf_op jit(solution)/shard_map/ppermute | solution.py:46
  45.4 8.0 %collective-permute-done.3 = bf16[2,144,128]{2,1,0:T(8,128)(2,1)S(1)} collective-permute-done((bf16[2,144,128]{2,1,0:T(8,128)(2,1)S(1)}, bf16[2,144,128]{2,1,0:T(8,128)(2,1)S(1)}, u32[]{:S(2)}, u32[]{:S(2)}) %collective-permute-start.3) | collective-permute-done | bytes 73760 | tf_op jit(solution)/shard_map/ppermute | solution.py:46
  53.5 4.4 %collective-permute-start.5 = (bf16[1,4,144,128]{3,2,1,0:T(8,128)(2,1)S(1)}, bf16[1,4,144,128]{3,2,1,0:T(8,128)(2,1)S(1)}, u32[]{:S(2)}, u32[]{:S(2)}) collective-permute-start(bf16[1,4,144,128]{3,2,1,0:T(8,128)(2,1)S(1)} %bitcast.56), channel_id=1, source_target_pairs={{0,128},{128,0},{256,384},{384,256},{1,129},{129,1},{257,385},{385... | collective-permute-start | bytes 442376 | tf_op jit(solution)/shard_map/ppermute | solution.py:46
  57.9 3.1 %collective-permute-done.5 = bf16[1,4,144,128]{3,2,1,0:T(8,128)(2,1)S(1)} collective-permute-done((bf16[1,4,144,128]{3,2,1,0:T(8,128)(2,1)S(1)}, bf16[1,4,144,128]{3,2,1,0:T(8,128)(2,1)S(1)}, u32[]{:S(2)}, u32[]{:S(2)}) %collective-permute-start.5) | collective-permute-done | bytes 147488 | tf_op jit(solution)/shard_map/ppermute | solution.py:46
  61.0 6.2 %collective-permute-start.6 = (bf16[2,4,144,128]{3,2,1,0:T(8,128)(2,1)S(1)}, bf16[2,4,144,128]{3,2,1,0:T(8,128)(2,1)S(1)}, u32[]{:S(2)}, u32[]{:S(2)}) collective-permute-start(bf16[2,4,144,128]{3,2,1,0:T(8,128)(2,1)S(1)} %pad_maximum_fusion.2), channel_id=1, source_target_pairs={{0,384},{128,256},{256,128},{384,0},{1,385},{129,257},{257,129},{3... | collective-permute-start | bytes 884744 | tf_op jit(solution)/shard_map/ppermute | solution.py:46
  67.3 4.7 %collective-permute-done.6 = bf16[2,4,144,128]{3,2,1,0:T(8,128)(2,1)S(1)} collective-permute-done((bf16[2,4,144,128]{3,2,1,0:T(8,128)(2,1)S(1)}, bf16[2,4,144,128]{3,2,1,0:T(8,128)(2,1)S(1)}, u32[]{:S(2)}, u32[]{:S(2)}) %collective-permute-start.6) | collective-permute-done | bytes 294944 | tf_op jit(solution)/shard_map/ppermute | solution.py:46
  72.0 1.9 %collective-permute-start.7 = (bf16[4,4,144,128]{3,2,1,0:T(8,128)(2,1)S(1)}, bf16[4,4,144,128]{3,2,1,0:T(8,128)(2,1)S(1)}, u32[]{:S(2)}, u32[]{:S(2)}) collective-permute-start(bf16[4,4,144,128]{3,2,1,0:T(8,128)(2,1)S(1)} %constant_dynamic-update-slice_fusion), channel_id=1, source_target_pairs={{0,1},{1,0},{2,3},{3,2},{4,5},{5,4},{6,7},{7,6},{8,9},{9,8},{10,11... | collective-permute-start | bytes 1769480 | tf_op jit(solution)/shard_map/ppermute | solution.py:46
  73.9 0.1 copy.76
  74.1 0.1 copy.59
  74.2 0.1 dynamic-slice_bitcast_fusion
  74.3 0.1 copy.61
  74.4 0.1 copy.60
  74.6 0.1 copy.62
  74.7 1.2 collective-permute-done.7
  75.9 0.1 fusion.1
  76.1 0.1 copy.54
  76.2 0.7 convert_reduce_fusion
  76.9 0.2 multiply_reduce_fusion
  77.1 0.1 copy.63
  77.3 5.1 %collective-permute-start.8 = (bf16[256,256]{0,1:T(8,128)(2,1)S(1)}, bf16[256,256]{0,1:T(8,128)(2,1)S(1)}, u32[]{:S(2)}, u32[]{:S(2)}) collective-permute-start(bf16[256,256]{0,1:T(8,128)(2,1)S(1)} %bitcast.65), channel_id=1, source_target_pairs={{0,384},{128,256},{256,128},{384,0},{1,385},{129,257},{257,129},{3... | collective-permute-start | bytes 393224 | tf_op jit(solution)/shard_map/ppermute | solution.py:46
  82.4 0.1 copy.57
  82.5 0.1 copy.55
  82.7 0.1 copy.56
  82.8 0.7 fusion
  83.5 2.7 %collective-permute-done.8 = bf16[256,256]{0,1:T(8,128)(2,1)S(1)} collective-permute-done((bf16[256,256]{0,1:T(8,128)(2,1)S(1)}, bf16[256,256]{0,1:T(8,128)(2,1)S(1)}, u32[]{:S(2)}, u32[]{:S(2)}) %collective-permute-start.8) | collective-permute-done | bytes 131104 | tf_op jit(solution)/shard_map/ppermute | solution.py:46
  86.2 1.9 %collective-permute-start.9 = (bf16[256,256]{0,1:T(8,128)(2,1)S(1)}, bf16[256,256]{0,1:T(8,128)(2,1)S(1)}, u32[]{:S(2)}, u32[]{:S(2)}) collective-permute-start(bf16[256,256]{0,1:T(8,128)(2,1)S(1)} %pad_maximum_fusion.7), channel_id=1, source_target_pairs={{0,128},{128,0},{256,384},{384,256},{1,129},{129,1},{257,385},{385... | collective-permute-start | bytes 393224 | tf_op jit(solution)/shard_map/ppermute | solution.py:46
  88.3 0.9 pad_maximum_fusion.1
  89.1 12.4 %all-to-all-start.1 = ((bf16[16,144,128]{2,1,0:T(8,128)(2,1)}), bf16[16,144,128]{2,1,0:T(8,128)(2,1)S(1)}, u32[]{:S(2)}, u32[]{:S(2)}) async-start(bf16[16,144,128]{2,1,0:T(8,128)(2,1)} %pad_maximum_fusion.1), calls=%async_computation.1 | async-start | bytes 1179648 | tf_op jit(solution)/shard_map/all_to_all | solution.py:41
  101.6 0.1 copy.65
  101.8 0.1 copy.64
  101.9 0.1 copy.66
  102.1 0.2 fusion.4
  102.3 1.9 %collective-permute-start.10 = (f32[128]{0:T(128)S(1)}, f32[128]{0:T(128)S(1)}, u32[]{:S(2)}, u32[]{:S(2)}) collective-permute-start(f32[128]{0:T(128)S(1)} %fusion.4), channel_id=1, source_target_pairs={{0,1},{1,0},{2,3},{3,2},{4,5},{5,4},{6,7},{7,6},{8,9},{9,8},{10,11... | collective-permute-start | bytes 1544 | tf_op jit(solution)/shard_map/ppermute | solution.py:46
  104.2 1.1 collective-permute-done.10
  105.3 1.9 %collective-permute-start.11 = (f32[128]{0:T(128)S(1)}, f32[128]{0:T(128)S(1)}, u32[]{:S(2)}, u32[]{:S(2)}) collective-permute-start(f32[128]{0:T(128)S(1)} %add.54), channel_id=1, source_target_pairs={{0,2},{2,0},{4,6},{6,4},{1,3},{3,1},{5,7},{7,5},{8,10},{10,8},{12,... | collective-permute-start | bytes 1544 | tf_op jit(solution)/shard_map/ppermute | solution.py:46
  107.2 3.5 %collective-permute-done.11 = f32[128]{0:T(128)S(1)} collective-permute-done((f32[128]{0:T(128)S(1)}, f32[128]{0:T(128)S(1)}, u32[]{:S(2)}, u32[]{:S(2)}) %collective-permute-start.11) | collective-permute-done | bytes 544 | tf_op jit(solution)/shard_map/ppermute | solution.py:46
  110.8 1.9 %collective-permute-start.12 = (f32[128]{0:T(128)S(1)}, f32[128]{0:T(128)S(1)}, u32[]{:S(2)}, u32[]{:S(2)}) collective-permute-start(f32[128]{0:T(128)S(1)} %add.55), channel_id=1, source_target_pairs={{0,4},{2,6},{4,0},{6,2},{1,5},{3,7},{5,1},{7,3},{8,12},{10,14},{12... | collective-permute-start | bytes 1544 | tf_op jit(solution)/shard_map/ppermute | solution.py:46
  112.7 4.5 %collective-permute-done.12 = f32[128]{0:T(128)S(1)} collective-permute-done((f32[128]{0:T(128)S(1)}, f32[128]{0:T(128)S(1)}, u32[]{:S(2)}, u32[]{:S(2)}) %collective-permute-start.12) | collective-permute-done | bytes 544 | tf_op jit(solution)/shard_map/ppermute | solution.py:46
  117.2 6.4 %all-to-all-done.1 = bf16[16,144,128]{2,1,0:T(8,128)(2,1)S(1)} async-done(((bf16[16,144,128]{2,1,0:T(8,128)(2,1)}), bf16[16,144,128]{2,1,0:T(8,128)(2,1)S(1)}, u32[]{:S(2)}, u32[]{:S(2)}) %all-to-all-start.1) | async-done | bytes 589856 | tf_op jit(solution)/shard_map/all_to_all | solution.py:41
  123.6 3.6 %collective-permute-start.13 = (f32[1,256]{1,0:T(1,128)S(1)}, f32[1,256]{1,0:T(1,128)S(1)}, u32[]{:S(2)}, u32[]{:S(2)}) collective-permute-start(f32[1,256]{1,0:T(1,128)S(1)} %bitcast.69), channel_id=1, source_target_pairs={{0,128},{128,0},{256,384},{384,256},{1,129},{129,1},{257,385},{385... | collective-permute-start | bytes 3080 | tf_op jit(solution)/shard_map/ppermute | solution.py:46
  127.2 0.1 convert_reduce_fusion.1
  127.3 3.3 %collective-permute-start.14 = (f32[128,128]{1,0:T(8,128)S(1)}, f32[128,128]{1,0:T(8,128)S(1)}, u32[]{:S(2)}, u32[]{:S(2)}) collective-permute-start(f32[128,128]{1,0:T(8,128)S(1)} %convert_reduce_fusion.1), channel_id=1, source_target_pairs={{0,0},{16,1},{32,2},{48,3},{64,4},{80,5},{96,6},{112,7},{8,8},{24,... | collective-permute-start | bytes 196616 | tf_op jit(solution)/shard_map/ppermute | solution.py:126
  130.7 9.8 %collective-permute-done.14 = f32[128,128]{1,0:T(8,128)S(1)} collective-permute-done((f32[128,128]{1,0:T(8,128)S(1)}, f32[128,128]{1,0:T(8,128)S(1)}, u32[]{:S(2)}, u32[]{:S(2)}) %collective-permute-start.14) | collective-permute-done | bytes 65568 | tf_op jit(solution)/shard_map/ppermute | solution.py:126
  140.5 1.9 %collective-permute-start.15 = (f32[2,256]{1,0:T(2,128)S(1)}, f32[2,256]{1,0:T(2,128)S(1)}, u32[]{:S(2)}, u32[]{:S(2)}) collective-permute-start(f32[2,256]{1,0:T(2,128)S(1)} %pad_maximum_fusion.12), channel_id=1, source_target_pairs={{0,384},{128,256},{256,128},{384,0},{1,385},{129,257},{257,129},{3... | collective-permute-start | bytes 6152 | tf_op jit(solution)/shard_map/ppermute | solution.py:46
  142.4 1.0 fusion.8
  143.4 3.8 %collective-permute-done.15 = f32[2,256]{1,0:T(2,128)S(1)} collective-permute-done((f32[2,256]{1,0:T(2,128)S(1)}, f32[2,256]{1,0:T(2,128)S(1)}, u32[]{:S(2)}, u32[]{:S(2)}) %collective-permute-start.15) | collective-permute-done | bytes 2080 | tf_op jit(solution)/shard_map/ppermute | solution.py:46
  147.2 0.1 select_reduce_fusion
  147.3 0.6 copy.77
  147.9 0.6 copy.84
  (58 shorter events, 0.6 us)
Async XLA Ops:
  0.6 14.0 %copy-start.3 = (bf16[128,128]{1,0:T(8,128)(2,1)S(1)}, bf16[128,128]{1,0:T(8,128)(2,1)}, u32[]{:S(2)}) copy-start(bf16[128,128]{1,0:T(8,128)(2,1)} %param.9) | copy-start | bytes 98308
  3.7 19.4 %collective-permute-start = (bf16[1,144,128]{2,1,0:T(8,128)(2,1)S(1)}, bf16[1,144,128]{2,1,0:T(8,128)(2,1)S(1)}, u32[]{:S(2)}, u32[]{:S(2)}) collective-permute-start(bf16[1,144,128]{2,1,0:T(8,128)(2,1)S(1)} %maximum_bitcast_fusion), channel_id=1, source_target_pairs={{0,2},{2,0},{4,6},{6,4},{1,3},{3,1},{5,7},{7,5},{8,10},{10,8},{12,... | collective-permute-start | bytes 110600 | tf_op jit(solution)/shard_map/ppermute | solution.py:46
  9.2 15.4 %collective-permute-start.2 = (bf16[256,256]{0,1:T(8,128)(2,1)S(1)}, bf16[256,256]{0,1:T(8,128)(2,1)S(1)}, u32[]{:S(2)}, u32[]{:S(2)}) collective-permute-start(bf16[256,256]{0,1:T(8,128)(2,1)S(1)} %pad_maximum_fusion.5), channel_id=1, source_target_pairs={{0,384},{128,256},{256,128},{384,0},{1,385},{129,257},{257,129},{3... | collective-permute-start | bytes 393224 | tf_op jit(solution)/shard_map/ppermute | solution.py:46
  14.7 10.0 %collective-permute-start.1 = (bf16[128,128]{1,0:T(8,128)(2,1)S(1)}, bf16[128,128]{1,0:T(8,128)(2,1)S(1)}, u32[]{:S(2)}, u32[]{:S(2)}) collective-permute-start(bf16[128,128]{1,0:T(8,128)(2,1)S(1)} %copy-done.3), channel_id=1, source_target_pairs={{0,0},{1,16},{2,32},{3,48},{4,64},{5,80},{6,96},{7,112},{8,8},{9,2... | collective-permute-start | bytes 98312 | tf_op jit(solution)/shard_map/ppermute | solution.py:70
  25.6 35.5 %all-to-all-start = ((bf16[16,128,128]{2,1,0:T(8,128)(2,1)}), bf16[16,128,128]{2,1,0:T(8,128)(2,1)S(1)}, u32[]{:S(2)}, u32[]{:S(2)}) async-start(bf16[16,128,128]{2,1,0:T(8,128)(2,1)} %broadcast_in_dim.32), calls=%async_computation | async-start | bytes 1048576 | tf_op jit(solution)/shard_map/all_to_all | solution.py:41
  39.5 13.9 %collective-permute-start.3 = (bf16[2,144,128]{2,1,0:T(8,128)(2,1)S(1)}, bf16[2,144,128]{2,1,0:T(8,128)(2,1)S(1)}, u32[]{:S(2)}, u32[]{:S(2)}) collective-permute-start(bf16[2,144,128]{2,1,0:T(8,128)(2,1)S(1)} %pad_maximum_fusion.8), channel_id=1, source_target_pairs={{0,4},{2,6},{4,0},{6,2},{1,5},{3,7},{5,1},{7,3},{8,12},{10,14},{12... | collective-permute-start | bytes 221192 | tf_op jit(solution)/shard_map/ppermute | solution.py:46
  42.1 11.4 %collective-permute-start.4 = (bf16[256,256]{0,1:T(8,128)(2,1)S(1)}, bf16[256,256]{0,1:T(8,128)(2,1)S(1)}, u32[]{:S(2)}, u32[]{:S(2)}) collective-permute-start(bf16[256,256]{0,1:T(8,128)(2,1)S(1)} %pad_maximum_fusion.6), channel_id=1, source_target_pairs={{0,128},{128,0},{256,384},{384,256},{1,129},{129,1},{257,385},{385... | collective-permute-start | bytes 393224 | tf_op jit(solution)/shard_map/ppermute | solution.py:46
  53.4 20.8 %copy-start.2 = (f32[1024]{0:T(1024)S(1)}, f32[1024]{0:T(1024)}, u32[]{:S(2)}) copy-start(f32[1024]{0:T(1024)} %param.10) | copy-start | bytes 12292
  53.5 7.5 %collective-permute-start.5 = (bf16[1,4,144,128]{3,2,1,0:T(8,128)(2,1)S(1)}, bf16[1,4,144,128]{3,2,1,0:T(8,128)(2,1)S(1)}, u32[]{:S(2)}, u32[]{:S(2)}) collective-permute-start(bf16[1,4,144,128]{3,2,1,0:T(8,128)(2,1)S(1)} %bitcast.56), channel_id=1, source_target_pairs={{0,128},{128,0},{256,384},{384,256},{1,129},{129,1},{257,385},{385... | collective-permute-start | bytes 442376 | tf_op jit(solution)/shard_map/ppermute | solution.py:46
  61.0 10.9 %collective-permute-start.6 = (bf16[2,4,144,128]{3,2,1,0:T(8,128)(2,1)S(1)}, bf16[2,4,144,128]{3,2,1,0:T(8,128)(2,1)S(1)}, u32[]{:S(2)}, u32[]{:S(2)}) collective-permute-start(bf16[2,4,144,128]{3,2,1,0:T(8,128)(2,1)S(1)} %pad_maximum_fusion.2), channel_id=1, source_target_pairs={{0,384},{128,256},{256,128},{384,0},{1,385},{129,257},{257,129},{3... | collective-permute-start | bytes 884744 | tf_op jit(solution)/shard_map/ppermute | solution.py:46
  72.0 3.9 %collective-permute-start.7 = (bf16[4,4,144,128]{3,2,1,0:T(8,128)(2,1)S(1)}, bf16[4,4,144,128]{3,2,1,0:T(8,128)(2,1)S(1)}, u32[]{:S(2)}, u32[]{:S(2)}) collective-permute-start(bf16[4,4,144,128]{3,2,1,0:T(8,128)(2,1)S(1)} %constant_dynamic-update-slice_fusion), channel_id=1, source_target_pairs={{0,1},{1,0},{2,3},{3,2},{4,5},{5,4},{6,7},{7,6},{8,9},{9,8},{10,11... | collective-permute-start | bytes 1769480 | tf_op jit(solution)/shard_map/ppermute | solution.py:46
  77.3 8.9 %collective-permute-start.8 = (bf16[256,256]{0,1:T(8,128)(2,1)S(1)}, bf16[256,256]{0,1:T(8,128)(2,1)S(1)}, u32[]{:S(2)}, u32[]{:S(2)}) collective-permute-start(bf16[256,256]{0,1:T(8,128)(2,1)S(1)} %bitcast.65), channel_id=1, source_target_pairs={{0,384},{128,256},{256,128},{384,0},{1,385},{129,257},{257,129},{3... | collective-permute-start | bytes 393224 | tf_op jit(solution)/shard_map/ppermute | solution.py:46
  86.2 15.5 %collective-permute-start.9 = (bf16[256,256]{0,1:T(8,128)(2,1)S(1)}, bf16[256,256]{0,1:T(8,128)(2,1)S(1)}, u32[]{:S(2)}, u32[]{:S(2)}) collective-permute-start(bf16[256,256]{0,1:T(8,128)(2,1)S(1)} %pad_maximum_fusion.7), channel_id=1, source_target_pairs={{0,128},{128,0},{256,384},{384,256},{1,129},{129,1},{257,385},{385... | collective-permute-start | bytes 393224 | tf_op jit(solution)/shard_map/ppermute | solution.py:46
  89.1 12.9 %copy-start = (bf16[128,1024]{1,0:T(8,128)(2,1)S(1)}, bf16[128,1024]{1,0:T(8,128)(2,1)}, u32[]{:S(2)}) copy-start(bf16[128,1024]{1,0:T(8,128)(2,1)} %param.6) | copy-start | bytes 786436
  89.1 34.4 %all-to-all-start.1 = ((bf16[16,144,128]{2,1,0:T(8,128)(2,1)}), bf16[16,144,128]{2,1,0:T(8,128)(2,1)S(1)}, u32[]{:S(2)}, u32[]{:S(2)}) async-start(bf16[16,144,128]{2,1,0:T(8,128)(2,1)} %pad_maximum_fusion.1), calls=%async_computation.1 | async-start | bytes 1179648 | tf_op jit(solution)/shard_map/all_to_all | solution.py:41
  101.6 5.6 %copy-start.4 = (s32[4]{0:T(128)S(1)}, s32[4]{0:T(128)}, u32[]{:S(2)}) copy-start(s32[4]{0:T(128)} %constant.43.clone) | copy-start | bytes 52
  101.7 40.7 %copy-start.1 = (bf16[128,1024]{1,0:T(8,128)(2,1)S(1)}, bf16[128,1024]{1,0:T(8,128)(2,1)}, u32[]{:S(2)}) copy-start(bf16[128,1024]{1,0:T(8,128)(2,1)} %param.7) | copy-start | bytes 786436
  102.3 3.0 %collective-permute-start.10 = (f32[128]{0:T(128)S(1)}, f32[128]{0:T(128)S(1)}, u32[]{:S(2)}, u32[]{:S(2)}) collective-permute-start(f32[128]{0:T(128)S(1)} %fusion.4), channel_id=1, source_target_pairs={{0,1},{1,0},{2,3},{3,2},{4,5},{5,4},{6,7},{7,6},{8,9},{9,8},{10,11... | collective-permute-start | bytes 1544 | tf_op jit(solution)/shard_map/ppermute | solution.py:46
  105.3 5.5 %collective-permute-start.11 = (f32[128]{0:T(128)S(1)}, f32[128]{0:T(128)S(1)}, u32[]{:S(2)}, u32[]{:S(2)}) collective-permute-start(f32[128]{0:T(128)S(1)} %add.54), channel_id=1, source_target_pairs={{0,2},{2,0},{4,6},{6,4},{1,3},{3,1},{5,7},{7,5},{8,10},{10,8},{12,... | collective-permute-start | bytes 1544 | tf_op jit(solution)/shard_map/ppermute | solution.py:46
  110.8 6.4 %collective-permute-start.12 = (f32[128]{0:T(128)S(1)}, f32[128]{0:T(128)S(1)}, u32[]{:S(2)}, u32[]{:S(2)}) collective-permute-start(f32[128]{0:T(128)S(1)} %add.55), channel_id=1, source_target_pairs={{0,4},{2,6},{4,0},{6,2},{1,5},{3,7},{5,1},{7,3},{8,12},{10,14},{12... | collective-permute-start | bytes 1544 | tf_op jit(solution)/shard_map/ppermute | solution.py:46
  123.6 7.1 %collective-permute-start.13 = (f32[1,256]{1,0:T(1,128)S(1)}, f32[1,256]{1,0:T(1,128)S(1)}, u32[]{:S(2)}, u32[]{:S(2)}) collective-permute-start(f32[1,256]{1,0:T(1,128)S(1)} %bitcast.69), channel_id=1, source_target_pairs={{0,128},{128,0},{256,384},{384,256},{1,129},{129,1},{257,385},{385... | collective-permute-start | bytes 3080 | tf_op jit(solution)/shard_map/ppermute | solution.py:46
  127.3 13.2 %collective-permute-start.14 = (f32[128,128]{1,0:T(8,128)S(1)}, f32[128,128]{1,0:T(8,128)S(1)}, u32[]{:S(2)}, u32[]{:S(2)}) collective-permute-start(f32[128,128]{1,0:T(8,128)S(1)} %convert_reduce_fusion.1), channel_id=1, source_target_pairs={{0,0},{16,1},{32,2},{48,3},{64,4},{80,5},{96,6},{112,7},{8,8},{24,... | collective-permute-start | bytes 196616 | tf_op jit(solution)/shard_map/ppermute | solution.py:126
  140.5 6.7 %collective-permute-start.15 = (f32[2,256]{1,0:T(2,128)S(1)}, f32[2,256]{1,0:T(2,128)S(1)}, u32[]{:S(2)}, u32[]{:S(2)}) collective-permute-start(f32[2,256]{1,0:T(2,128)S(1)} %pad_maximum_fusion.12), channel_id=1, source_target_pairs={{0,384},{128,256},{256,128},{384,0},{1,385},{129,257},{257,129},{3... | collective-permute-start | bytes 6152 | tf_op jit(solution)/shard_map/ppermute | solution.py:46

commit v5 on v3

v5 whole, which is shorter than its diff:
```python
import jax
import jax.numpy as jnp
from jax import lax
from jax.sharding import Mesh
from jax.sharding import PartitionSpec as P

D = 8192
HD = 128
TOK = 128
HALF = 512

rope_theta = 500000.0
norm_eps = 1e-05

SIZES = (2, 2, 8, 2, 4, 2)
AXES = ("xh", "xl", "y", "zh", "zl", "core")
DP = ("xh", "xl", "y", "zh")
TENSOR = ("zl", "core")
ROW = ("xh", "y", "zh")


def flat_index(x, y, zh, zl, core):
    return (((x * 8 + y) * 2 + zh) * 4 + zl) * 2 + core


def weight_moves():
    moves = []
    for x in range(4):
        for y in range(8):
            for zh in range(2):
                for zl in range(4):
                    for core in range(2):
                        far_zl, far_core = x, y // 4
                        place = (far_zl ^ zl) * 2 + (far_core ^ core)
                        far_x = (y % 2) * 2 + y // 2 % 2
                        there = flat_index(far_x, place, zh, far_zl, far_core)
                        moves.append((flat_index(x, y, zh, zl, core), there))
    return moves


def exchange(value, axes):
    return lax.all_to_all(value, axes, split_axis=0, concat_axis=0, tiled=True)


def swap(value, axis, mask):
    count = lax.axis_size(axis)
    return lax.ppermute(value, axis, [(i, i ^ mask) for i in range(count)])


def terms_of(value):
    first = lax.reduce_precision(value, 8, 7)
    second = lax.reduce_precision(value - first, 8, 7)
    third = value - first - second
    return jnp.stack([first, second, third]).astype(jnp.bfloat16)


def rope_tables(positions_count, head_size):
    half_head = head_size // 2
    frequency = rope_theta ** (-(jnp.arange(half_head, dtype=jnp.float32) * 2.0 / head_size))
    angles = jnp.arange(positions_count, dtype=jnp.float32)[:, None] * frequency[None, :]
    return (jnp.cos(angles), jnp.sin(angles))


def shards(layer_input, residual_grad, key_value_grad, kv_weight, norm_gain):
    moves = weight_moves()
    low_half = lax.axis_index("xl") == 0

    moved = lax.ppermute(kv_weight, AXES, moves)
    weights = exchange(jnp.broadcast_to(moved[None], (32, HD, HD)), ROW)

    cosine, sine = rope_tables(TOK, HD)
    grads = key_value_grad.astype(jnp.float32)
    low, high = grads[:, : HD // 2], grads[:, HD // 2 :]
    turned = jnp.concatenate([low * cosine + high * sine, high * cosine - low * sine], axis=1)
    kv_pre = jnp.where(lax.axis_index("core") == 0, turned, grads).astype(jnp.bfloat16)
    widened = layer_input.astype(jnp.float32)
    squares = terms_of(jnp.sum(widened * widened, axis=1))
    packet = jnp.concatenate([kv_pre, jnp.pad(squares, ((0, 13), (0, 0)))], axis=0)[None]
    for mask in (1, 2):
        packet = jnp.concatenate([packet, swap(packet, "zl", mask)])

    split = jnp.stack([layer_input[:, i * HD : (i + 1) * HD] for i in range(8)]).reshape(2, 4, TOK, HD)
    kept = jnp.where(low_half, split[0], split[1])
    given = jnp.where(low_half, split[1], split[0])
    sent = jnp.concatenate([packet.reshape(4 * (TOK + 16), HD), given.reshape(4 * TOK, HD)])
    came = swap(sent, "xl", 1)
    rows = jnp.concatenate([kept, came[4 * (TOK + 16) :].reshape(4, TOK, HD)], axis=1)
    packet = jnp.stack([packet, came[: 4 * (TOK + 16)].reshape(4, TOK + 16, HD)])
    packet, weights = lax.optimization_barrier((packet, weights))
    packet = jnp.stack([packet, swap(packet, "core", 1)])

    kv = packet[:, :, :, :TOK].transpose(2, 0, 1, 3, 4).reshape(8, 2 * TOK, HD)
    total = jnp.sum(packet[:, :, :, TOK : TOK + 3].astype(jnp.float32), axis=(0, 2, 3))
    inv_all = lax.rsqrt(total / D + norm_eps)
    inv_scale = inv_all[0][:, None]
    gain_half = jnp.where(low_half, norm_gain[:HALF], norm_gain[HALF:]).reshape(4, 1, HD)
    normal = rows.astype(jnp.float32) * inv_all.reshape(1, 2 * TOK, 1)
    normed = (normal * gain_half).astype(jnp.bfloat16)

    pieces = jnp.einsum(
        "ktc,xbtf->xkbcf",
        kv,
        normed.reshape(2, 2, 2 * TOK, HD),
        preferred_element_type=jnp.float32,
    ).astype(jnp.bfloat16)
    arrived = exchange(pieces.reshape(32, HD, HD), ROW)
    block = jnp.sum(arrived.astype(jnp.float32), axis=0)
    weight_grad = lax.ppermute(block, AXES, [(b, a) for a, b in moves])

    products = jnp.einsum(
        "ktc,xkbcf->kxbtf",
        kv,
        weights.reshape(2, 8, 2, HD, HD),
        preferred_element_type=jnp.float32,
    ).astype(jnp.bfloat16)
    norm_grad = jnp.sum(products.astype(jnp.float32), axis=0).reshape(4, 2 * TOK, HD)
    gain_sum = jnp.sum(norm_grad * normal, axis=1).reshape(HALF)
    for axis, mask in (("y", 1), ("y", 2), ("zh", 1), ("y", 4), ("xh", 1)):
        gain_sum = gain_sum + swap(gain_sum, axis, mask)
    gain_far = swap(gain_sum, "xl", 1)
    gain_grad = jnp.where(
        low_half, jnp.concatenate([gain_sum, gain_far]), jnp.concatenate([gain_far, gain_sum])
    )

    back = norm_grad.astype(jnp.bfloat16)
    here, far = back[:, :TOK], swap(back[:, TOK:], "xl", 1)
    full = jnp.where(low_half, jnp.concatenate([here, far]), jnp.concatenate([far, here]))
    full = full.transpose(1, 0, 2).reshape(TOK, 2 * HALF)
    scaled = full.astype(jnp.float32) * norm_gain[None, :]
    normal = widened * inv_scale
    inner = jnp.sum(scaled * normal, axis=1)
    for axis, mask in (("core", 1), ("zl", 1), ("zl", 2)):
        inner = inner + swap(inner, axis, mask)
    inner = inner[:, None] / D
    input_grad = (
        residual_grad.astype(jnp.float32) + inv_scale * (scaled - normal * inner)
    ).astype(jnp.bfloat16)
    return (input_grad, weight_grad, gain_grad)


def solution(mesh):
    fine = Mesh(mesh.devices.reshape(SIZES), AXES)
    return jax.shard_map(
        shards,
        mesh=fine,
        in_specs=(
            P(DP, TENSOR),
            P(DP, TENSOR),
            P(DP, TENSOR),
            P(TENSOR, DP),
            P(TENSOR),
        ),
        out_specs=(P(DP, TENSOR), P(TENSOR, DP), P(TENSOR)),
        check_vma=False,
    )
```

time: 138 us -> 186 us (1.35)
  waiting for transfers between devices: 39.9 us -> 80.3 us
  starting transfers between devices: 84.2 us -> 94.4 us
  other arithmetic: 5.81 us -> 3.9 us
    ppermute x14, waiting for transfers between devices: 27.3 us -> 70.1 us  [swap(): return lax.ppermute(value, axis, [(i, i ^ mask) for i in range(count)])]
    all_to_all x2, starting transfers between devices: 25.9 us -> 34.8 us  [exchange(): return lax.all_to_all(value, axes, split_axis=0, concat_axis=0, tiled=True)]
    ppermute x1, starting transfers between devices: 6.98 us -> 11.5 us  [shards(): moved = lax.ppermute(kv_weight, AXES, moves)]
    ppermute x1, waiting for transfers between devices: 3.59 us -> 0.91 us  [shards(): moved = lax.ppermute(kv_weight, AXES, moves)]
    ppermute x1, starting transfers between devices: 5.86 us -> 3.67 us  [shards(): weight_grad = lax.ppermute(block, AXES, [(b, a) for a, b in moves])]
  transfers between devices with their start and end apart: 18 -> 18, of which waited for: 13 -> 14; matrix products, arithmetic and copies ran while one was open for 3% -> 3% of each run, Pallas kernels for 0% -> 0%
where the time goes in v5:
time: 186 us; the launch traced here: 185 us
  starting transfers between devices  94.4 us (51%)
  waiting for transfers between devices  80.3 us (43%)
  other arithmetic  3.9 us (2%)
  local copies, waits for them, and re-layouts  3.78 us (2%)
    ppermute x14, waiting for transfers between devices, swap(): return lax.ppermute(value, axis, [(i, i ^ mask) for i in range(count)])  70.1 us
    ppermute x14, starting transfers between devices, swap(): return lax.ppermute(value, axis, [(i, i ^ mask) for i in range(count)])  44.5 us
    all_to_all x2, starting transfers between devices, exchange(): return lax.all_to_all(value, axes, split_axis=0, concat_axis=0, tiled=True)  34.8 us
    ppermute x1, starting transfers between devices, shards(): moved = lax.ppermute(kv_weight, AXES, moves)  11.5 us
    ppermute x1, waiting for transfers between devices, shards(): weight_grad = lax.ppermute(block, AXES, [(b, a) for a, b in moves])  9.25 us
  transfers between devices with their start and end apart: 18, of which 14 were waited for; matrix products, arithmetic and copies ran while one was open for 3% of the time, Pallas kernels for 0%

profile of v5, /device:TPU:6, one launch (start us, length us, event | category | flops | bytes accessed | tf_op | source)
XLA Modules:
  0.0 184.7 jit_solution(16554600081106829983)
XLA Ops:
  0.6 11.5 %collective-permute-start.3 = (bf16[128,128]{1,0:T(8,128)(2,1)}, bf16[128,128]{1,0:T(8,128)(2,1)S(1)}, u32[]{:S(2)}, u32[]{:S(2)}) collective-permute-start(bf16[128,128]{1,0:T(8,128)(2,1)} %param.8), channel_id=1, source_target_pairs={{0,0},{1,16},{2,32},{3,48},{4,64},{5,80},{6,96},{7,112},{8,8},{9,2... | collective-permute-start | bytes 98312 | tf_op jit(solution)/shard_map/ppermute | solution.py:68
  12.1 1.1 fusion.9
  13.2 0.9 collective-permute-done.3
  14.1 1.2 broadcast_in_dim.5
  15.3 0.0 copy-start.2
  15.3 0.0 copy-start
  15.4 17.6 %all-to-all-start = ((bf16[32,128,128]{2,1,0:T(8,128)(2,1)}), bf16[32,128,128]{2,1,0:T(8,128)(2,1)S(1)}, u32[]{:S(2)}, u32[]{:S(2)}) async-start(bf16[32,128,128]{2,1,0:T(8,128)(2,1)} %broadcast_in_dim.5), calls=%async_computation | async-start | bytes 2097152 | tf_op jit(solution)/shard_map/all_to_all | solution.py:42
  33.0 0.0 copy-done.2
  33.1 0.3 multiply_add_fusion
  33.4 0.1 fusion.17
  33.5 2.6 %collective-permute-start = (bf16[1,144,128]{2,1,0:T(8,128)(2,1)S(1)}, bf16[1,144,128]{2,1,0:T(8,128)(2,1)S(1)}, u32[]{:S(2)}, u32[]{:S(2)}) collective-permute-start(bf16[1,144,128]{2,1,0:T(8,128)(2,1)S(1)} %maximum_bitcast_fusion), channel_id=1, source_target_pairs={{0,2},{2,0},{4,6},{6,4},{1,3},{3,1},{5,7},{7,5},{8,10},{10,8},{12,... | collective-permute-start | bytes 110600 | tf_op jit(solution)/shard_map/ppermute | solution.py:47
  36.1 0.0 copy-done
  36.2 7.0 %collective-permute-done = bf16[1,144,128]{2,1,0:T(8,128)(2,1)S(1)} collective-permute-done((bf16[1,144,128]{2,1,0:T(8,128)(2,1)S(1)}, bf16[1,144,128]{2,1,0:T(8,128)(2,1)S(1)}, u32[]{:S(2)}, u32[]{:S(2)}) %collective-permute-start) | collective-permute-done | bytes 36896 | tf_op jit(solution)/shard_map/ppermute | solution.py:47
  43.1 5.2 %collective-permute-start.1 = (bf16[2,144,128]{2,1,0:T(8,128)(2,1)S(1)}, bf16[2,144,128]{2,1,0:T(8,128)(2,1)S(1)}, u32[]{:S(2)}, u32[]{:S(2)}) collective-permute-start(bf16[2,144,128]{2,1,0:T(8,128)(2,1)S(1)} %pad_maximum_fusion.8), channel_id=1, source_target_pairs={{0,4},{2,6},{4,0},{6,2},{1,5},{3,7},{5,1},{7,3},{8,12},{10,14},{12... | collective-permute-start | bytes 221192 | tf_op jit(solution)/shard_map/ppermute | solution.py:47
  48.4 0.0 copy-start.3
  48.4 13.6 %collective-permute-done.1 = bf16[2,144,128]{2,1,0:T(8,128)(2,1)S(1)} collective-permute-done((bf16[2,144,128]{2,1,0:T(8,128)(2,1)S(1)}, bf16[2,144,128]{2,1,0:T(8,128)(2,1)S(1)}, u32[]{:S(2)}, u32[]{:S(2)}) %collective-permute-start.1) | collective-permute-done | bytes 73760 | tf_op jit(solution)/shard_map/ppermute | solution.py:47
  62.1 1.9 %collective-permute-start.2 = (bf16[1088,128]{1,0:T(8,128)(2,1)S(1)}, bf16[1088,128]{1,0:T(8,128)(2,1)S(1)}, u32[]{:S(2)}, u32[]{:S(2)}) collective-permute-start(bf16[1088,128]{1,0:T(8,128)(2,1)S(1)} %pad_maximum_fusion.2), channel_id=1, source_target_pairs={{0,128},{128,0},{1,129},{129,1},{2,130},{130,2},{3,131},{131,3},{4... | collective-permute-start | bytes 835592 | tf_op jit(solution)/shard_map/ppermute | solution.py:47
  64.0 8.5 %collective-permute-done.2 = bf16[1088,128]{1,0:T(8,128)(2,1)S(1)} collective-permute-done((bf16[1088,128]{1,0:T(8,128)(2,1)S(1)}, bf16[1088,128]{1,0:T(8,128)(2,1)S(1)}, u32[]{:S(2)}, u32[]{:S(2)}) %collective-permute-start.2) | collective-permute-done | bytes 278560 | tf_op jit(solution)/shard_map/ppermute | solution.py:47
  72.6 0.0 all-to-all-done
  72.6 1.9 %collective-permute-start.4 = (bf16[2,4,144,128]{3,2,1,0:T(8,128)(2,1)S(1)}, bf16[2,4,144,128]{3,2,1,0:T(8,128)(2,1)S(1)}, u32[]{:S(2)}, u32[]{:S(2)}) collective-permute-start(bf16[2,4,144,128]{3,2,1,0:T(8,128)(2,1)S(1)} %pad_maximum_fusion.1), channel_id=1, source_target_pairs={{0,1},{1,0},{2,3},{3,2},{4,5},{5,4},{6,7},{7,6},{8,9},{9,8},{10,11... | collective-permute-start | bytes 884744 | tf_op jit(solution)/shard_map/ppermute | solution.py:47
  74.5 0.1 copy.20
  74.7 0.0 copy-done.3
  74.7 0.1 copy.21
  74.8 1.2 collective-permute-done.4
  76.2 0.5 fusion
  76.7 1.3 copy.22
  78.0 17.1 %all-to-all-start.1 = ((bf16[32,128,128]{2,1,0:T(8,128)(2,1)}), bf16[32,128,128]{2,1,0:T(8,128)(2,1)S(1)}, u32[]{:S(2)}, u32[]{:S(2)}) async-start(bf16[32,128,128]{2,1,0:T(8,128)(2,1)} %bitcast.35), calls=%async_computation.1 | async-start | bytes 2097152 | tf_op jit(solution)/shard_map/all_to_all | solution.py:42
  95.1 0.8 convert_reduce_fusion
  95.9 0.2 fusion.11
  96.1 3.4 %collective-permute-start.10 = (f32[512]{0:T(512)S(1)}, f32[512]{0:T(512)S(1)}, u32[]{:S(2)}, u32[]{:S(2)}) collective-permute-start(f32[512]{0:T(512)S(1)} %bitcast.84), channel_id=1, source_target_pairs={{0,16},{16,0},{32,48},{48,32},{64,80},{80,64},{96,112},{112,96},{1... | collective-permute-start | bytes 6152 | tf_op jit(solution)/shard_map/ppermute | solution.py:47
  99.5 20.2 %collective-permute-done.10 = f32[512]{0:T(512)S(1)} collective-permute-done((f32[512]{0:T(512)S(1)}, f32[512]{0:T(512)S(1)}, u32[]{:S(2)}, u32[]{:S(2)}) %collective-permute-start.10) | collective-permute-done | bytes 2080 | tf_op jit(solution)/shard_map/ppermute | solution.py:47
  119.6 2.4 %collective-permute-start.11 = (f32[512]{0:T(512)S(1)}, f32[512]{0:T(512)S(1)}, u32[]{:S(2)}, u32[]{:S(2)}) collective-permute-start(f32[512]{0:T(512)S(1)} %add.50), channel_id=1, source_target_pairs={{0,32},{16,48},{32,0},{48,16},{64,96},{80,112},{96,64},{112,80},{1... | collective-permute-start | bytes 6152 | tf_op jit(solution)/shard_map/ppermute | solution.py:47
  122.1 3.9 %collective-permute-done.11 = f32[512]{0:T(512)S(1)} collective-permute-done((f32[512]{0:T(512)S(1)}, f32[512]{0:T(512)S(1)}, u32[]{:S(2)}, u32[]{:S(2)}) %collective-permute-start.11) | collective-permute-done | bytes 2080 | tf_op jit(solution)/shard_map/ppermute | solution.py:47
  126.0 7.3 %collective-permute-start.12 = (f32[512]{0:T(512)S(1)}, f32[512]{0:T(512)S(1)}, u32[]{:S(2)}, u32[]{:S(2)}) collective-permute-start(f32[512]{0:T(512)S(1)} %add.51), channel_id=1, source_target_pairs={{0,8},{8,0},{1,9},{9,1},{2,10},{10,2},{3,11},{11,3},{4,12},{12,4},... | collective-permute-start | bytes 6152 | tf_op jit(solution)/shard_map/ppermute | solution.py:47
  133.3 2.1 %collective-permute-done.12 = f32[512]{0:T(512)S(1)} collective-permute-done((f32[512]{0:T(512)S(1)}, f32[512]{0:T(512)S(1)}, u32[]{:S(2)}, u32[]{:S(2)}) %collective-permute-start.12) | collective-permute-done | bytes 2080 | tf_op jit(solution)/shard_map/ppermute | solution.py:47
  135.4 6.4 %collective-permute-start.13 = (f32[512]{0:T(512)S(1)}, f32[512]{0:T(512)S(1)}, u32[]{:S(2)}, u32[]{:S(2)}) collective-permute-start(f32[512]{0:T(512)S(1)} %add.52), channel_id=1, source_target_pairs={{0,64},{16,80},{32,96},{48,112},{64,0},{80,16},{96,32},{112,48},{1... | collective-permute-start | bytes 6152 | tf_op jit(solution)/shard_map/ppermute | solution.py:47
  141.9 2.2 %collective-permute-start.5 = (bf16[4,128,128]{1,2,0:T(8,128)(2,1)S(1)}, bf16[4,128,128]{1,2,0:T(8,128)(2,1)S(1)}, u32[]{:S(2)}, u32[]{:S(2)}) collective-permute-start(bf16[4,128,128]{1,2,0:T(8,128)(2,1)S(1)} %get-tuple-element.10), channel_id=1, source_target_pairs={{0,128},{128,0},{1,129},{129,1},{2,130},{130,2},{3,131},{131,3},{4... | collective-permute-start | bytes 393224 | tf_op jit(solution)/shard_map/ppermute | solution.py:47
  144.1 0.7 collective-permute-done.13
  144.8 2.5 %collective-permute-start.14 = (f32[512]{0:T(512)S(1)}, f32[512]{0:T(512)S(1)}, u32[]{:S(2)}, u32[]{:S(2)}) collective-permute-start(f32[512]{0:T(512)S(1)} %add.53), channel_id=1, source_target_pairs={{0,256},{256,0},{1,257},{257,1},{2,258},{258,2},{3,259},{259,3},{4... | collective-permute-start | bytes 6152 | tf_op jit(solution)/shard_map/ppermute | solution.py:47
  147.2 4.5 %collective-permute-done.14 = f32[512]{0:T(512)S(1)} collective-permute-done((f32[512]{0:T(512)S(1)}, f32[512]{0:T(512)S(1)}, u32[]{:S(2)}, u32[]{:S(2)}) %collective-permute-start.14) | collective-permute-done | bytes 2080 | tf_op jit(solution)/shard_map/ppermute | solution.py:47
  151.7 3.0 %collective-permute-start.15 = (f32[512]{0:T(512)S(1)}, f32[512]{0:T(512)S(1)}, u32[]{:S(2)}, u32[]{:S(2)}) collective-permute-start(f32[512]{0:T(512)S(1)} %add.54), channel_id=1, source_target_pairs={{0,128},{128,0},{1,129},{129,1},{2,130},{130,2},{3,131},{131,3},{4... | collective-permute-start | bytes 6152 | tf_op jit(solution)/shard_map/ppermute | solution.py:47
  154.7 0.0 collective-permute-done.5
  154.8 0.2 copy.28
  155.0 0.0 copy-start.1
  155.0 0.2 fusion.4
  155.2 1.9 %collective-permute-start.6 = (f32[128]{0:T(128)S(1)}, f32[128]{0:T(128)S(1)}, u32[]{:S(2)}, u32[]{:S(2)}) collective-permute-start(f32[128]{0:T(128)S(1)} %fusion.4), channel_id=1, source_target_pairs={{0,1},{1,0},{2,3},{3,2},{4,5},{5,4},{6,7},{7,6},{8,9},{9,8},{10,11... | collective-permute-start | bytes 1544 | tf_op jit(solution)/shard_map/ppermute | solution.py:47
  157.1 1.1 collective-permute-done.6
  158.2 1.9 %collective-permute-start.7 = (f32[128]{0:T(128)S(1)}, f32[128]{0:T(128)S(1)}, u32[]{:S(2)}, u32[]{:S(2)}) collective-permute-start(f32[128]{0:T(128)S(1)} %add.46), channel_id=1, source_target_pairs={{0,2},{2,0},{4,6},{6,4},{1,3},{3,1},{5,7},{7,5},{8,10},{10,8},{12,... | collective-permute-start | bytes 1544 | tf_op jit(solution)/shard_map/ppermute | solution.py:47
  160.2 3.5 %collective-permute-done.7 = f32[128]{0:T(128)S(1)} collective-permute-done((f32[128]{0:T(128)S(1)}, f32[128]{0:T(128)S(1)}, u32[]{:S(2)}, u32[]{:S(2)}) %collective-permute-start.7) | collective-permute-done | bytes 544 | tf_op jit(solution)/shard_map/ppermute | solution.py:47
  163.7 1.9 %collective-permute-start.8 = (f32[128]{0:T(128)S(1)}, f32[128]{0:T(128)S(1)}, u32[]{:S(2)}, u32[]{:S(2)}) collective-permute-start(f32[128]{0:T(128)S(1)} %add.47), channel_id=1, source_target_pairs={{0,4},{2,6},{4,0},{6,2},{1,5},{3,7},{5,1},{7,3},{8,12},{10,14},{12... | collective-permute-start | bytes 1544 | tf_op jit(solution)/shard_map/ppermute | solution.py:47
  165.6 0.0 collective-permute-done.15
  165.6 0.6 maximum_select_fusion.2
  166.2 3.8 %collective-permute-done.8 = f32[128]{0:T(128)S(1)} collective-permute-done((f32[128]{0:T(128)S(1)}, f32[128]{0:T(128)S(1)}, u32[]{:S(2)}, u32[]{:S(2)}) %collective-permute-start.8) | collective-permute-done | bytes 544 | tf_op jit(solution)/shard_map/ppermute | solution.py:47
  170.0 0.0 all-to-all-done.1
  170.0 0.2 convert_reduce_fusion.1
  170.1 3.7 %collective-permute-start.9 = (f32[128,128]{1,0:T(8,128)S(1)}, f32[128,128]{1,0:T(8,128)S(1)}, u32[]{:S(2)}, u32[]{:S(2)}) collective-permute-start(f32[128,128]{1,0:T(8,128)S(1)} %convert_reduce_fusion.1), channel_id=1, source_target_pairs={{0,0},{16,1},{32,2},{48,3},{64,4},{80,5},{96,6},{112,7},{8,8},{24,... | collective-permute-start | bytes 196616 | tf_op jit(solution)/shard_map/ppermute | solution.py:108
  173.8 0.0 copy-done.1
  173.8 1.0 fusion.8
  174.8 9.2 %collective-permute-done.9 = f32[128,128]{1,0:T(8,128)S(1)} collective-permute-done((f32[128,128]{1,0:T(8,128)S(1)}, f32[128,128]{1,0:T(8,128)S(1)}, u32[]{:S(2)}, u32[]{:S(2)}) %collective-permute-start.9) | collective-permute-done | bytes 65568 | tf_op jit(solution)/shard_map/ppermute | solution.py:108
  184.0 0.6 copy.32
  (30 shorter events, 0.5 us)
Async XLA Ops:
  0.6 13.5 %collective-permute-start.3 = (bf16[128,128]{1,0:T(8,128)(2,1)}, bf16[128,128]{1,0:T(8,128)(2,1)S(1)}, u32[]{:S(2)}, u32[]{:S(2)}) collective-permute-start(bf16[128,128]{1,0:T(8,128)(2,1)} %param.8), channel_id=1, source_target_pairs={{0,0},{1,16},{2,32},{3,48},{4,64},{5,80},{6,96},{7,112},{8,8},{9,2... | collective-permute-start | bytes 98312 | tf_op jit(solution)/shard_map/ppermute | solution.py:68
  15.3 17.7 %copy-start.2 = (bf16[128,128]{1,0:T(8,128)(2,1)S(1)}, bf16[128,128]{1,0:T(8,128)(2,1)}, u32[]{:S(2)}) copy-start(bf16[128,128]{1,0:T(8,128)(2,1)} %param.7) | copy-start | bytes 98308
  15.3 20.7 %copy-start = (bf16[128,1024]{1,0:T(8,128)(2,1)S(1)}, bf16[128,1024]{1,0:T(8,128)(2,1)}, u32[]{:S(2)}) copy-start(bf16[128,1024]{1,0:T(8,128)(2,1)} %param.5) | copy-start | bytes 786436
  15.4 57.2 %all-to-all-start = ((bf16[32,128,128]{2,1,0:T(8,128)(2,1)}), bf16[32,128,128]{2,1,0:T(8,128)(2,1)S(1)}, u32[]{:S(2)}, u32[]{:S(2)}) async-start(bf16[32,128,128]{2,1,0:T(8,128)(2,1)} %broadcast_in_dim.5), calls=%async_computation | async-start | bytes 2097152 | tf_op jit(solution)/shard_map/all_to_all | solution.py:42
  33.5 9.6 %collective-permute-start = (bf16[1,144,128]{2,1,0:T(8,128)(2,1)S(1)}, bf16[1,144,128]{2,1,0:T(8,128)(2,1)S(1)}, u32[]{:S(2)}, u32[]{:S(2)}) collective-permute-start(bf16[1,144,128]{2,1,0:T(8,128)(2,1)S(1)} %maximum_bitcast_fusion), channel_id=1, source_target_pairs={{0,2},{2,0},{4,6},{6,4},{1,3},{3,1},{5,7},{7,5},{8,10},{10,8},{12,... | collective-permute-start | bytes 110600 | tf_op jit(solution)/shard_map/ppermute | solution.py:47
  43.1 18.9 %collective-permute-start.1 = (bf16[2,144,128]{2,1,0:T(8,128)(2,1)S(1)}, bf16[2,144,128]{2,1,0:T(8,128)(2,1)S(1)}, u32[]{:S(2)}, u32[]{:S(2)}) collective-permute-start(bf16[2,144,128]{2,1,0:T(8,128)(2,1)S(1)} %pad_maximum_fusion.8), channel_id=1, source_target_pairs={{0,4},{2,6},{4,0},{6,2},{1,5},{3,7},{5,1},{7,3},{8,12},{10,14},{12... | collective-permute-start | bytes 221192 | tf_op jit(solution)/shard_map/ppermute | solution.py:47
  48.4 26.3 %copy-start.3 = (f32[1024]{0:T(1024)S(1)}, f32[1024]{0:T(1024)}, u32[]{:S(2)}) copy-start(f32[1024]{0:T(1024)} %param.9) | copy-start | bytes 12292
  62.1 10.4 %collective-permute-start.2 = (bf16[1088,128]{1,0:T(8,128)(2,1)S(1)}, bf16[1088,128]{1,0:T(8,128)(2,1)S(1)}, u32[]{:S(2)}, u32[]{:S(2)}) collective-permute-start(bf16[1088,128]{1,0:T(8,128)(2,1)S(1)} %pad_maximum_fusion.2), channel_id=1, source_target_pairs={{0,128},{128,0},{1,129},{129,1},{2,130},{130,2},{3,131},{131,3},{4... | collective-permute-start | bytes 835592 | tf_op jit(solution)/shard_map/ppermute | solution.py:47
  72.6 3.5 %collective-permute-start.4 = (bf16[2,4,144,128]{3,2,1,0:T(8,128)(2,1)S(1)}, bf16[2,4,144,128]{3,2,1,0:T(8,128)(2,1)S(1)}, u32[]{:S(2)}, u32[]{:S(2)}) collective-permute-start(bf16[2,4,144,128]{3,2,1,0:T(8,128)(2,1)S(1)} %pad_maximum_fusion.1), channel_id=1, source_target_pairs={{0,1},{1,0},{2,3},{3,2},{4,5},{5,4},{6,7},{7,6},{8,9},{9,8},{10,11... | collective-permute-start | bytes 884744 | tf_op jit(solution)/shard_map/ppermute | solution.py:47
  78.0 92.0 %all-to-all-start.1 = ((bf16[32,128,128]{2,1,0:T(8,128)(2,1)}), bf16[32,128,128]{2,1,0:T(8,128)(2,1)S(1)}, u32[]{:S(2)}, u32[]{:S(2)}) async-start(bf16[32,128,128]{2,1,0:T(8,128)(2,1)} %bitcast.35), calls=%async_computation.1 | async-start | bytes 2097152 | tf_op jit(solution)/shard_map/all_to_all | solution.py:42
  96.1 23.6 %collective-permute-start.10 = (f32[512]{0:T(512)S(1)}, f32[512]{0:T(512)S(1)}, u32[]{:S(2)}, u32[]{:S(2)}) collective-permute-start(f32[512]{0:T(512)S(1)} %bitcast.84), channel_id=1, source_target_pairs={{0,16},{16,0},{32,48},{48,32},{64,80},{80,64},{96,112},{112,96},{1... | collective-permute-start | bytes 6152 | tf_op jit(solution)/shard_map/ppermute | solution.py:47
  119.6 6.4 %collective-permute-start.11 = (f32[512]{0:T(512)S(1)}, f32[512]{0:T(512)S(1)}, u32[]{:S(2)}, u32[]{:S(2)}) collective-permute-start(f32[512]{0:T(512)S(1)} %add.50), channel_id=1, source_target_pairs={{0,32},{16,48},{32,0},{48,16},{64,96},{80,112},{96,64},{112,80},{1... | collective-permute-start | bytes 6152 | tf_op jit(solution)/shard_map/ppermute | solution.py:47
  126.0 9.4 %collective-permute-start.12 = (f32[512]{0:T(512)S(1)}, f32[512]{0:T(512)S(1)}, u32[]{:S(2)}, u32[]{:S(2)}) collective-permute-start(f32[512]{0:T(512)S(1)} %add.51), channel_id=1, source_target_pairs={{0,8},{8,0},{1,9},{9,1},{2,10},{10,2},{3,11},{11,3},{4,12},{12,4},... | collective-permute-start | bytes 6152 | tf_op jit(solution)/shard_map/ppermute | solution.py:47
  135.4 9.4 %collective-permute-start.13 = (f32[512]{0:T(512)S(1)}, f32[512]{0:T(512)S(1)}, u32[]{:S(2)}, u32[]{:S(2)}) collective-permute-start(f32[512]{0:T(512)S(1)} %add.52), channel_id=1, source_target_pairs={{0,64},{16,80},{32,96},{48,112},{64,0},{80,16},{96,32},{112,48},{1... | collective-permute-start | bytes 6152 | tf_op jit(solution)/shard_map/ppermute | solution.py:47
  141.9 12.9 %collective-permute-start.5 = (bf16[4,128,128]{1,2,0:T(8,128)(2,1)S(1)}, bf16[4,128,128]{1,2,0:T(8,128)(2,1)S(1)}, u32[]{:S(2)}, u32[]{:S(2)}) collective-permute-start(bf16[4,128,128]{1,2,0:T(8,128)(2,1)S(1)} %get-tuple-element.10), channel_id=1, source_target_pairs={{0,128},{128,0},{1,129},{129,1},{2,130},{130,2},{3,131},{131,3},{4... | collective-permute-start | bytes 393224 | tf_op jit(solution)/shard_map/ppermute | solution.py:47
  144.8 7.0 %collective-permute-start.14 = (f32[512]{0:T(512)S(1)}, f32[512]{0:T(512)S(1)}, u32[]{:S(2)}, u32[]{:S(2)}) collective-permute-start(f32[512]{0:T(512)S(1)} %add.53), channel_id=1, source_target_pairs={{0,256},{256,0},{1,257},{257,1},{2,258},{258,2},{3,259},{259,3},{4... | collective-permute-start | bytes 6152 | tf_op jit(solution)/shard_map/ppermute | solution.py:47
  151.7 13.8 %collective-permute-start.15 = (f32[512]{0:T(512)S(1)}, f32[512]{0:T(512)S(1)}, u32[]{:S(2)}, u32[]{:S(2)}) collective-permute-start(f32[512]{0:T(512)S(1)} %add.54), channel_id=1, source_target_pairs={{0,128},{128,0},{1,129},{129,1},{2,130},{130,2},{3,131},{131,3},{4... | collective-permute-start | bytes 6152 | tf_op jit(solution)/shard_map/ppermute | solution.py:47
  155.0 18.8 %copy-start.1 = (bf16[128,1024]{1,0:T(8,128)(2,1)S(1)}, bf16[128,1024]{1,0:T(8,128)(2,1)}, u32[]{:S(2)}) copy-start(bf16[128,1024]{1,0:T(8,128)(2,1)} %param.6) | copy-start | bytes 786436
  155.2 3.0 %collective-permute-start.6 = (f32[128]{0:T(128)S(1)}, f32[128]{0:T(128)S(1)}, u32[]{:S(2)}, u32[]{:S(2)}) collective-permute-start(f32[128]{0:T(128)S(1)} %fusion.4), channel_id=1, source_target_pairs={{0,1},{1,0},{2,3},{3,2},{4,5},{5,4},{6,7},{7,6},{8,9},{9,8},{10,11... | collective-permute-start | bytes 1544 | tf_op jit(solution)/shard_map/ppermute | solution.py:47
  158.2 5.4 %collective-permute-start.7 = (f32[128]{0:T(128)S(1)}, f32[128]{0:T(128)S(1)}, u32[]{:S(2)}, u32[]{:S(2)}) collective-permute-start(f32[128]{0:T(128)S(1)} %add.46), channel_id=1, source_target_pairs={{0,2},{2,0},{4,6},{6,4},{1,3},{3,1},{5,7},{7,5},{8,10},{10,8},{12,... | collective-permute-start | bytes 1544 | tf_op jit(solution)/shard_map/ppermute | solution.py:47
  163.7 6.3 %collective-permute-start.8 = (f32[128]{0:T(128)S(1)}, f32[128]{0:T(128)S(1)}, u32[]{:S(2)}, u32[]{:S(2)}) collective-permute-start(f32[128]{0:T(128)S(1)} %add.47), channel_id=1, source_target_pairs={{0,4},{2,6},{4,0},{6,2},{1,5},{3,7},{5,1},{7,3},{8,12},{10,14},{12... | collective-permute-start | bytes 1544 | tf_op jit(solution)/shard_map/ppermute | solution.py:47
  170.1 13.9 %collective-permute-start.9 = (f32[128,128]{1,0:T(8,128)S(1)}, f32[128,128]{1,0:T(8,128)S(1)}, u32[]{:S(2)}, u32[]{:S(2)}) collective-permute-start(f32[128,128]{1,0:T(8,128)S(1)} %convert_reduce_fusion.1), channel_id=1, source_target_pairs={{0,0},{16,1},{32,2},{48,3},{64,4},{80,5},{96,6},{112,7},{8,8},{24,... | collective-permute-start | bytes 196616 | tf_op jit(solution)/shard_map/ppermute | solution.py:108

commit v6 on v5

v6 whole, which is shorter than its diff:
```python
import jax
import jax.numpy as jnp
from jax import lax
from jax.sharding import Mesh
from jax.sharding import PartitionSpec as P

D = 8192
HD = 128
TOK = 128
QUARTER = 256

rope_theta = 500000.0
norm_eps = 1e-05

SIZES = (4, 8, 2, 4, 2)
AXES = ("x", "y", "zh", "zl", "core")
DP = ("x", "y", "zh")
TENSOR = ("zl", "core")
ROW = ("y", "zh")


def flat_index(x, y, zh, zl, core):
    return (((x * 8 + y) * 2 + zh) * 4 + zl) * 2 + core


def weight_moves():
    moves = []
    for x in range(4):
        for y in range(8):
            for zh in range(2):
                for zl in range(4):
                    for core in range(2):
                        far_zl, far_core = x, y // 4
                        place = (far_zl ^ zl) * 2 + (far_core ^ core)
                        there = flat_index(y % 4, place, zh, far_zl, far_core)
                        moves.append((flat_index(x, y, zh, zl, core), there))
    return moves


def exchange(value, axes):
    return lax.all_to_all(value, axes, split_axis=0, concat_axis=0, tiled=True)


def swap(value, axis, mask):
    count = lax.axis_size(axis)
    return lax.ppermute(value, axis, [(i, i ^ mask) for i in range(count)])


def terms_of(value):
    first = lax.reduce_precision(value, 8, 7)
    second = lax.reduce_precision(value - first, 8, 7)
    third = value - first - second
    return jnp.stack([first, second, third]).astype(jnp.bfloat16)


def rope_tables(positions_count, head_size):
    half_head = head_size // 2
    frequency = rope_theta ** (-(jnp.arange(half_head, dtype=jnp.float32) * 2.0 / head_size))
    angles = jnp.arange(positions_count, dtype=jnp.float32)[:, None] * frequency[None, :]
    return (jnp.cos(angles), jnp.sin(angles))


def shards(layer_input, residual_grad, key_value_grad, kv_weight, norm_gain):
    moves = weight_moves()
    mine = lax.axis_index("x")

    moved = lax.ppermute(kv_weight, AXES, moves)

    cosine, sine = rope_tables(TOK, HD)
    grads = key_value_grad.astype(jnp.float32)
    low, high = grads[:, : HD // 2], grads[:, HD // 2 :]
    turned = jnp.concatenate([low * cosine + high * sine, high * cosine - low * sine], axis=1)
    kv_pre = jnp.where(lax.axis_index("core") == 0, turned, grads).astype(jnp.bfloat16)
    widened = layer_input.astype(jnp.float32)
    squares = terms_of(jnp.sum(widened * widened, axis=1))
    packet = jnp.concatenate([kv_pre, jnp.pad(squares, ((0, 13), (0, 0)))], axis=0)[None]

    blocks = jnp.stack([layer_input[:, i * HD : (i + 1) * HD] for i in range(8)])

    def quarter(r):
        return lax.dynamic_slice_in_dim(blocks, (mine ^ r) * 2, 2, axis=0)

    packet, moved = lax.optimization_barrier((packet, moved))
    packet = jnp.concatenate([packet, swap(packet, "zl", 1)])
    given = jnp.concatenate([quarter(3), quarter(2)]).reshape(4 * TOK, HD)
    near = swap(given, "x", 3)
    packet = jnp.concatenate([packet, swap(packet, "zl", 2)])
    packet, moved, near = lax.optimization_barrier((packet, moved, near))
    weights = exchange(jnp.broadcast_to(moved[None], (16, HD, HD)), ROW)

    near = near.reshape(2, 2, TOK, HD)
    given = jnp.concatenate([quarter(1), near[1]]).reshape(4 * TOK, HD)
    came = swap(jnp.concatenate([packet.reshape(4 * (TOK + 16), HD), given]), "x", 1)
    far = came[4 * (TOK + 16) :].reshape(2, 2, TOK, HD)
    rows = jnp.concatenate([quarter(0), far[0], near[0], far[1]], axis=1)
    packet = jnp.stack([packet, came[: 4 * (TOK + 16)].reshape(4, TOK + 16, HD)])
    packet = jnp.concatenate([packet, swap(packet, "x", 3)])
    packet, weights = lax.optimization_barrier((packet, weights))
    packet = jnp.stack([packet, swap(packet, "core", 1)])

    kv = packet[:, :, :, :TOK].transpose(2, 0, 1, 3, 4).reshape(8, 4 * TOK, HD)
    total = jnp.sum(packet[:, :, :, TOK : TOK + 3].astype(jnp.float32), axis=(0, 2, 3))
    inv_all = lax.rsqrt(total / D + norm_eps)
    inv_scale = inv_all[0][:, None]
    gain_quarter = lax.dynamic_slice_in_dim(norm_gain, mine * QUARTER, QUARTER).reshape(2, 1, HD)
    normal = rows.astype(jnp.float32) * inv_all.reshape(1, 4 * TOK, 1)
    normed = (normal * gain_quarter).astype(jnp.bfloat16)

    pieces = jnp.einsum(
        "ktc,btf->kbcf", kv, normed, preferred_element_type=jnp.float32
    ).astype(jnp.bfloat16)
    arrived = exchange(pieces.reshape(16, HD, HD), ROW)
    block = jnp.sum(arrived.astype(jnp.float32), axis=0)
    weight_grad = lax.ppermute(block, AXES, [(b, a) for a, b in moves])

    products = jnp.einsum(
        "ktc,kbcf->kbtf",
        kv,
        weights.reshape(8, 2, HD, HD),
        preferred_element_type=jnp.float32,
    ).astype(jnp.bfloat16)
    norm_grad = jnp.sum(products.astype(jnp.float32), axis=0)
    gain_part = terms_of(jnp.sum(norm_grad * normal, axis=1)).reshape(6, HD)

    back = norm_grad.astype(jnp.bfloat16)
    given = jnp.concatenate(
        [back[:, 2 * TOK :].reshape(4 * TOK, HD), jnp.pad(gain_part, ((0, 10), (0, 0)))]
    )
    came = swap(given, "x", 3)
    near, gain_near = came[: 4 * TOK].reshape(2, 2 * TOK, HD), came[4 * TOK : 4 * TOK + 6]
    given = jnp.concatenate(
        [
            back[:, TOK : 2 * TOK].reshape(2 * TOK, HD),
            near[:, TOK:].reshape(2 * TOK, HD),
            gain_part,
            gain_near,
            jnp.zeros((4, HD), jnp.bfloat16),
        ]
    )
    came = swap(given, "x", 1)
    far, gain_far = came[: 4 * TOK].reshape(2, 2, TOK, HD), came[4 * TOK : 4 * TOK + 12]
    gains = jnp.concatenate([gain_part, gain_near, gain_far]).astype(jnp.float32)
    gains = jnp.sum(gains.reshape(4, 3, 2, HD), axis=1)
    place = mine ^ jnp.array([0, 3, 1, 2])
    chosen = place[None, :, None, None] == jnp.arange(4)[:, None, None, None]
    gains = jnp.sum(jnp.where(chosen, gains[None], 0.0), axis=1).reshape(8, HD)
    gains, block = lax.optimization_barrier((gains, block))
    gain_parts = exchange(jnp.broadcast_to(gains[None], (16, 8, HD)), ROW)
    gain_grad = jnp.sum(gain_parts, axis=0).reshape(4 * QUARTER)

    full = jnp.zeros((8, TOK, HD), jnp.bfloat16)
    for part, r in ((back[:, :TOK], 0), (far[0], 1), (near[:, :TOK], 3), (far[1], 2)):
        full = lax.dynamic_update_slice_in_dim(full, part, (mine ^ r) * 2, axis=0)
    full = jnp.concatenate([full[i] for i in range(8)], axis=1)
    scaled = full.astype(jnp.float32) * norm_gain[None, :]
    normal = widened * inv_scale
    inner = jnp.sum(scaled * normal, axis=1)
    for axis, mask in (("core", 1), ("zl", 1), ("zl", 2)):
        inner = inner + swap(inner, axis, mask)
    inner = inner[:, None] / D
    input_grad = (
        residual_grad.astype(jnp.float32) + inv_scale * (scaled - normal * inner)
    ).astype(jnp.bfloat16)
    return (input_grad, weight_grad, gain_grad)


def solution(mesh):
    fine = Mesh(mesh.devices.reshape(SIZES), AXES)
    return jax.shard_map(
        shards,
        mesh=fine,
        in_specs=(
            P(DP, TENSOR),
            P(DP, TENSOR),
            P(DP, TENSOR),
            P(TENSOR, DP),
            P(TENSOR),
        ),
        out_specs=(P(DP, TENSOR), P(TENSOR, DP), P(TENSOR)),
        check_vma=False,
    )
```

time: 186 us -> 145 us (0.78)
  waiting for transfers between devices: 80.3 us -> 44.8 us
  starting transfers between devices: 94.4 us -> 85 us
  local copies, waits for them, and re-layouts: 3.78 us -> 7.07 us
    ppermute x14 -> x11, waiting for transfers between devices: 70.1 us -> 32.8 us  [swap(): return lax.ppermute(value, axis, [(i, i ^ mask) for i in range(count)])]
    ppermute x14 -> x11, starting transfers between devices: 44.5 us -> 31.1 us  [swap(): return lax.ppermute(value, axis, [(i, i ^ mask) for i in range(count)])]
    all_to_all x2 -> x3, waiting for transfers between devices: 0.01 us -> 12 us  [exchange(): return lax.all_to_all(value, axes, split_axis=0, concat_axis=0, tiled=True)]
    ppermute x1, waiting for transfers between devices: 9.25 us -> 0.01 us  [shards(): weight_grad = lax.ppermute(block, AXES, [(b, a) for a, b in moves])]
    all_to_all x2 -> x3, starting transfers between devices: 34.8 us -> 37.2 us  [exchange(): return lax.all_to_all(value, axes, split_axis=0, concat_axis=0, tiled=True)]
  transfers between devices with their start and end apart: 18 -> 16, of which waited for: 14 -> 11; matrix products, arithmetic and copies ran while one was open for 3% -> 6% of each run, Pallas kernels for 0% -> 0%
where the time goes in v6:
time: 145 us; the launch traced here: 143 us
  starting transfers between devices  85 us (59%)
  waiting for transfers between devices  44.8 us (31%)
  local copies, waits for them, and re-layouts  7.07 us (5%)
  other arithmetic  4.04 us (3%)
    all_to_all x3, starting transfers between devices, exchange(): return lax.all_to_all(value, axes, split_axis=0, concat_axis=0, tiled=True)  37.2 us
    ppermute x11, waiting for transfers between devices, swap(): return lax.ppermute(value, axis, [(i, i ^ mask) for i in range(count)])  32.8 us
    ppermute x11, starting transfers between devices, swap(): return lax.ppermute(value, axis, [(i, i ^ mask) for i in range(count)])  31.1 us
    all_to_all x3, waiting for transfers between devices, exchange(): return lax.all_to_all(value, axes, split_axis=0, concat_axis=0, tiled=True)  12 us
    ppermute x1, starting transfers between devices, shards(): moved = lax.ppermute(kv_weight, AXES, moves)  11.5 us
    ppermute x1, starting transfers between devices, shards(): weight_grad = lax.ppermute(block, AXES, [(b, a) for a, b in moves])  5.09 us
  transfers between devices with their start and end apart: 16, of which 11 were waited for; matrix products, arithmetic and copies ran while one was open for 6% of the time, Pallas kernels for 0%

profile of v6, /device:TPU:6, one launch (start us, length us, event | category | flops | bytes accessed | tf_op | source)
XLA Modules:
  0.0 143.4 jit_solution(4193657976683156485)
XLA Ops:
  0.6 11.5 %collective-permute-start = (bf16[128,128]{1,0:T(8,128)(2,1)}, bf16[128,128]{1,0:T(8,128)(2,1)S(1)}, u32[]{:S(2)}, u32[]{:S(2)}) collective-permute-start(bf16[128,128]{1,0:T(8,128)(2,1)} %param.9), channel_id=1, source_target_pairs={{0,0},{1,16},{2,32},{3,48},{4,64},{5,80},{6,96},{7,112},{8,8},{9,2... | collective-permute-start | bytes 98312 | tf_op jit(solution)/shard_map/ppermute | solution.py:67
  12.2 0.9 fusion.31
  13.1 1.1 fusion.9
  14.2 0.1 copy.91
  14.3 0.1 copy.92
  14.4 0.1 copy.93
  14.5 0.1 copy.94
  14.7 0.1 copy.95
  14.8 0.1 copy.96
  14.9 0.1 copy.97
  15.0 0.1 copy.98
  15.3 0.3 multiply_add_fusion
  15.6 0.1 fusion.17
  15.8 4.0 %collective-permute-start.1 = (bf16[1,144,128]{2,1,0:T(8,128)(2,1)S(1)}, bf16[1,144,128]{2,1,0:T(8,128)(2,1)S(1)}, u32[]{:S(2)}, u32[]{:S(2)}) collective-permute-start(bf16[1,144,128]{2,1,0:T(8,128)(2,1)S(1)} %maximum_bitcast_fusion), channel_id=1, source_target_pairs={{0,2},{2,0},{4,6},{6,4},{1,3},{3,1},{5,7},{7,5},{8,10},{10,8},{12,... | collective-permute-start | bytes 110600 | tf_op jit(solution)/shard_map/ppermute | solution.py:46
  19.8 1.9 %collective-permute-done.1 = bf16[1,144,128]{2,1,0:T(8,128)(2,1)S(1)} collective-permute-done((bf16[1,144,128]{2,1,0:T(8,128)(2,1)S(1)}, bf16[1,144,128]{2,1,0:T(8,128)(2,1)S(1)}, u32[]{:S(2)}, u32[]{:S(2)}) %collective-permute-start.1) | collective-permute-done | bytes 36896 | tf_op jit(solution)/shard_map/ppermute | solution.py:46
  21.7 1.9 %collective-permute-start.2 = (bf16[2,144,128]{2,1,0:T(8,128)(2,1)S(1)}, bf16[2,144,128]{2,1,0:T(8,128)(2,1)S(1)}, u32[]{:S(2)}, u32[]{:S(2)}) collective-permute-start(bf16[2,144,128]{2,1,0:T(8,128)(2,1)S(1)} %pad_maximum_fusion.8), channel_id=1, source_target_pairs={{0,4},{2,6},{4,0},{6,2},{1,5},{3,7},{5,1},{7,3},{8,12},{10,14},{12... | collective-permute-start | bytes 221192 | tf_op jit(solution)/shard_map/ppermute | solution.py:46
  23.7 0.1 copy.76
  23.8 1.9 %collective-permute-start.3 = (bf16[512,128]{1,0:T(8,128)(2,1)S(1)}, bf16[512,128]{1,0:T(8,128)(2,1)S(1)}, u32[]{:S(2)}, u32[]{:S(2)}) collective-permute-start(bf16[512,128]{1,0:T(8,128)(2,1)S(1)} %bitcast.139), channel_id=1, source_target_pairs={{0,384},{128,256},{256,128},{384,0},{1,385},{129,257},{257,129},{3... | collective-permute-start | bytes 393224 | tf_op jit(solution)/shard_map/ppermute | solution.py:46
  25.8 3.1 %collective-permute-done.2 = bf16[2,144,128]{2,1,0:T(8,128)(2,1)S(1)} collective-permute-done((bf16[2,144,128]{2,1,0:T(8,128)(2,1)S(1)}, bf16[2,144,128]{2,1,0:T(8,128)(2,1)S(1)}, u32[]{:S(2)}, u32[]{:S(2)}) %collective-permute-start.2) | collective-permute-done | bytes 73760 | tf_op jit(solution)/shard_map/ppermute | solution.py:46
  28.9 3.0 %collective-permute-done.3 = bf16[512,128]{1,0:T(8,128)(2,1)S(1)} collective-permute-done((bf16[512,128]{1,0:T(8,128)(2,1)S(1)}, bf16[512,128]{1,0:T(8,128)(2,1)S(1)}, u32[]{:S(2)}, u32[]{:S(2)}) %collective-permute-start.3) | collective-permute-done | bytes 131104 | tf_op jit(solution)/shard_map/ppermute | solution.py:46
  31.9 0.1 copy.77
  32.1 0.1 copy.78
  32.2 0.1 copy.79
  32.3 0.9 broadcast_in_dim.31
  33.2 14.2 %all-to-all-start = ((bf16[16,128,128]{1,2,0:T(8,128)(2,1)}), bf16[16,128,128]{1,2,0:T(8,128)(2,1)S(1)}, u32[]{:S(2)}, u32[]{:S(2)}) async-start(bf16[16,128,128]{1,2,0:T(8,128)(2,1)} %broadcast_in_dim.31), calls=%async_computation | async-start | bytes 1048576 | tf_op jit(solution)/shard_map/all_to_all | solution.py:41
  47.4 1.9 %collective-permute-start.4 = (bf16[1088,128]{1,0:T(8,128)(2,1)S(1)}, bf16[1088,128]{1,0:T(8,128)(2,1)S(1)}, u32[]{:S(2)}, u32[]{:S(2)}) collective-permute-start(bf16[1088,128]{1,0:T(8,128)(2,1)S(1)} %pad_maximum_fusion.3), channel_id=1, source_target_pairs={{0,128},{128,0},{256,384},{384,256},{1,129},{129,1},{257,385},{385... | collective-permute-start | bytes 835592 | tf_op jit(solution)/shard_map/ppermute | solution.py:46
  49.4 6.5 %collective-permute-done.4 = bf16[1088,128]{1,0:T(8,128)(2,1)S(1)} collective-permute-done((bf16[1088,128]{1,0:T(8,128)(2,1)S(1)}, bf16[1088,128]{1,0:T(8,128)(2,1)S(1)}, u32[]{:S(2)}, u32[]{:S(2)}) %collective-permute-start.4) | collective-permute-done | bytes 278560 | tf_op jit(solution)/shard_map/ppermute | solution.py:46
  55.9 5.1 %collective-permute-start.5 = (bf16[2,4,144,128]{3,2,1,0:T(8,128)(2,1)S(1)}, bf16[2,4,144,128]{3,2,1,0:T(8,128)(2,1)S(1)}, u32[]{:S(2)}, u32[]{:S(2)}) collective-permute-start(bf16[2,4,144,128]{3,2,1,0:T(8,128)(2,1)S(1)} %pad_maximum_fusion.2), channel_id=1, source_target_pairs={{0,384},{128,256},{256,128},{384,0},{1,385},{129,257},{257,129},{3... | collective-permute-start | bytes 884744 | tf_op jit(solution)/shard_map/ppermute | solution.py:46
  61.1 4.7 %collective-permute-done.5 = bf16[2,4,144,128]{3,2,1,0:T(8,128)(2,1)S(1)} collective-permute-done((bf16[2,4,144,128]{3,2,1,0:T(8,128)(2,1)S(1)}, bf16[2,4,144,128]{3,2,1,0:T(8,128)(2,1)S(1)}, u32[]{:S(2)}, u32[]{:S(2)}) %collective-permute-start.5) | collective-permute-done | bytes 294944 | tf_op jit(solution)/shard_map/ppermute | solution.py:46
  65.8 1.9 %collective-permute-start.6 = (bf16[4,4,144,128]{3,2,1,0:T(8,128)(2,1)S(1)}, bf16[4,4,144,128]{3,2,1,0:T(8,128)(2,1)S(1)}, u32[]{:S(2)}, u32[]{:S(2)}) collective-permute-start(bf16[4,4,144,128]{3,2,1,0:T(8,128)(2,1)S(1)} %pad_maximum_fusion.1), channel_id=1, source_target_pairs={{0,1},{1,0},{2,3},{3,2},{4,5},{5,4},{6,7},{7,6},{8,9},{9,8},{10,11... | collective-permute-start | bytes 1769480 | tf_op jit(solution)/shard_map/ppermute | solution.py:46
  67.8 0.1 dynamic-slice_bitcast_fusion
  67.9 0.1 copy.85
  68.0 0.1 copy.84
  68.2 0.1 copy.86
  68.3 1.4 %collective-permute-done.6 = bf16[4,4,144,128]{3,2,1,0:T(8,128)(2,1)S(1)} collective-permute-done((bf16[4,4,144,128]{3,2,1,0:T(8,128)(2,1)S(1)}, bf16[4,4,144,128]{3,2,1,0:T(8,128)(2,1)S(1)}, u32[]{:S(2)}, u32[]{:S(2)}) %collective-permute-start.6) | collective-permute-done | bytes 589856 | tf_op jit(solution)/shard_map/ppermute | solution.py:46
  69.8 0.1 fusion.1
  69.9 0.1 copy.80
  70.0 0.7 convert_reduce_fusion
  70.8 0.2 fusion.10
  71.0 0.1 copy.83
  71.2 5.1 %collective-permute-start.7 = (bf16[528,128]{1,0:T(8,128)(2,1)S(1)}, bf16[528,128]{1,0:T(8,128)(2,1)S(1)}, u32[]{:S(2)}, u32[]{:S(2)}) collective-permute-start(bf16[528,128]{1,0:T(8,128)(2,1)S(1)} %fusion.16), channel_id=1, source_target_pairs={{0,384},{128,256},{256,128},{384,0},{1,385},{129,257},{257,129},{3... | collective-permute-start | bytes 405512 | tf_op jit(solution)/shard_map/ppermute | solution.py:46
  76.3 0.1 copy.82
  76.4 0.5 fusion
  76.9 1.0 copy.87
  77.9 12.0 %all-to-all-start.1 = ((bf16[16,128,128]{2,1,0:T(8,128)(2,1)}), bf16[16,128,128]{2,1,0:T(8,128)(2,1)S(1)}, u32[]{:S(2)}, u32[]{:S(2)}) async-start(bf16[16,128,128]{2,1,0:T(8,128)(2,1)} %bitcast.49), calls=%async_computation.1 | async-start | bytes 1048576 | tf_op jit(solution)/shard_map/all_to_all | solution.py:41
  90.0 0.2 concatenate.51
  90.2 1.9 %collective-permute-start.8 = (bf16[528,128]{1,0:T(8,128)(2,1)S(1)}, bf16[528,128]{1,0:T(8,128)(2,1)S(1)}, u32[]{:S(2)}, u32[]{:S(2)}) collective-permute-start(bf16[528,128]{1,0:T(8,128)(2,1)S(1)} %concatenate.51), channel_id=1, source_target_pairs={{0,128},{128,0},{256,384},{384,256},{1,129},{129,1},{257,385},{385... | collective-permute-start | bytes 405512 | tf_op jit(solution)/shard_map/ppermute | solution.py:46
  92.1 0.1 copy.81
  92.3 4.8 %collective-permute-done.8 = bf16[528,128]{1,0:T(8,128)(2,1)S(1)} collective-permute-done((bf16[528,128]{1,0:T(8,128)(2,1)S(1)}, bf16[528,128]{1,0:T(8,128)(2,1)S(1)}, u32[]{:S(2)}, u32[]{:S(2)}) %collective-permute-start.8) | collective-permute-done | bytes 135200 | tf_op jit(solution)/shard_map/ppermute | solution.py:46
  97.4 0.2 fusion.4
  97.6 1.9 %collective-permute-start.9 = (f32[128]{0:T(128)S(1)}, f32[128]{0:T(128)S(1)}, u32[]{:S(2)}, u32[]{:S(2)}) collective-permute-start(f32[128]{0:T(128)S(1)} %fusion.4), channel_id=1, source_target_pairs={{0,1},{1,0},{2,3},{3,2},{4,5},{5,4},{6,7},{7,6},{8,9},{9,8},{10,11... | collective-permute-start | bytes 1544 | tf_op jit(solution)/shard_map/ppermute | solution.py:46
  99.5 1.1 collective-permute-done.9
  100.6 3.4 %collective-permute-start.10 = (f32[128]{0:T(128)S(1)}, f32[128]{0:T(128)S(1)}, u32[]{:S(2)}, u32[]{:S(2)}) collective-permute-start(f32[128]{0:T(128)S(1)} %add.56), channel_id=1, source_target_pairs={{0,2},{2,0},{4,6},{6,4},{1,3},{3,1},{5,7},{7,5},{8,10},{10,8},{12,... | collective-permute-start | bytes 1544 | tf_op jit(solution)/shard_map/ppermute | solution.py:46
  104.1 2.0 %collective-permute-done.10 = f32[128]{0:T(128)S(1)} collective-permute-done((f32[128]{0:T(128)S(1)}, f32[128]{0:T(128)S(1)}, u32[]{:S(2)}, u32[]{:S(2)}) %collective-permute-start.10) | collective-permute-done | bytes 544 | tf_op jit(solution)/shard_map/ppermute | solution.py:46
  106.0 1.9 %collective-permute-start.11 = (f32[128]{0:T(128)S(1)}, f32[128]{0:T(128)S(1)}, u32[]{:S(2)}, u32[]{:S(2)}) collective-permute-start(f32[128]{0:T(128)S(1)} %add.57), channel_id=1, source_target_pairs={{0,4},{2,6},{4,0},{6,2},{1,5},{3,7},{5,1},{7,3},{8,12},{10,14},{12... | collective-permute-start | bytes 1544 | tf_op jit(solution)/shard_map/ppermute | solution.py:46
  108.0 0.1 select_reduce_fusion
  108.1 4.3 %collective-permute-done.11 = f32[128]{0:T(128)S(1)} collective-permute-done((f32[128]{0:T(128)S(1)}, f32[128]{0:T(128)S(1)}, u32[]{:S(2)}, u32[]{:S(2)}) %collective-permute-start.11) | collective-permute-done | bytes 544 | tf_op jit(solution)/shard_map/ppermute | solution.py:46
  112.4 5.1 %collective-permute-start.12 = (f32[128,128]{1,0:T(8,128)S(1)}, f32[128,128]{1,0:T(8,128)S(1)}, u32[]{:S(2)}, u32[]{:S(2)}) collective-permute-start(f32[128,128]{1,0:T(8,128)S(1)} %convert_reduce_fusion.1), channel_id=1, source_target_pairs={{0,0},{16,1},{32,2},{48,3},{64,4},{80,5},{96,6},{112,7},{8,8},{24,... | collective-permute-start | bytes 196616 | tf_op jit(solution)/shard_map/ppermute | solution.py:114
  117.5 0.6 broadcast_in_dim.55
  118.2 11.1 %all-to-all-start.2 = ((f32[16,8,128]{2,1,0:T(8,128)}), f32[16,8,128]{2,1,0:T(8,128)S(1)}, u32[]{:S(2)}, u32[]{:S(2)}) async-start(f32[16,8,128]{2,1,0:T(8,128)} %broadcast_in_dim.55), calls=%async_computation.2 | async-start | bytes 131072 | tf_op jit(solution)/shard_map/all_to_all | solution.py:41
  129.3 1.0 fusion.8
  130.2 12.0 %all-to-all-done.2 = f32[16,8,128]{2,1,0:T(8,128)S(1)} async-done(((f32[16,8,128]{2,1,0:T(8,128)}), f32[16,8,128]{2,1,0:T(8,128)S(1)}, u32[]{:S(2)}, u32[]{:S(2)}) %all-to-all-start.2) | async-done | bytes 65568 | tf_op jit(solution)/shard_map/all_to_all | solution.py:41
  142.2 0.6 reduce_sum.98
  142.8 0.6 copy.118
  (77 shorter events, 0.9 us)
Async XLA Ops:
  0.6 14.5 %copy-start.2 = (bf16[128,128]{1,0:T(8,128)(2,1)S(1)}, bf16[128,128]{1,0:T(8,128)(2,1)}, u32[]{:S(2)}) copy-start(bf16[128,128]{1,0:T(8,128)(2,1)} %param.8) | copy-start | bytes 98308
  0.6 15.1 %collective-permute-start = (bf16[128,128]{1,0:T(8,128)(2,1)}, bf16[128,128]{1,0:T(8,128)(2,1)S(1)}, u32[]{:S(2)}, u32[]{:S(2)}) collective-permute-start(bf16[128,128]{1,0:T(8,128)(2,1)} %param.9), channel_id=1, source_target_pairs={{0,0},{1,16},{2,32},{3,48},{4,64},{5,80},{6,96},{7,112},{8,8},{9,2... | collective-permute-start | bytes 98312 | tf_op jit(solution)/shard_map/ppermute | solution.py:67
  15.8 6.0 %collective-permute-start.1 = (bf16[1,144,128]{2,1,0:T(8,128)(2,1)S(1)}, bf16[1,144,128]{2,1,0:T(8,128)(2,1)S(1)}, u32[]{:S(2)}, u32[]{:S(2)}) collective-permute-start(bf16[1,144,128]{2,1,0:T(8,128)(2,1)S(1)} %maximum_bitcast_fusion), channel_id=1, source_target_pairs={{0,2},{2,0},{4,6},{6,4},{1,3},{3,1},{5,7},{7,5},{8,10},{10,8},{12,... | collective-permute-start | bytes 110600 | tf_op jit(solution)/shard_map/ppermute | solution.py:46
  21.7 7.1 %collective-permute-start.2 = (bf16[2,144,128]{2,1,0:T(8,128)(2,1)S(1)}, bf16[2,144,128]{2,1,0:T(8,128)(2,1)S(1)}, u32[]{:S(2)}, u32[]{:S(2)}) collective-permute-start(bf16[2,144,128]{2,1,0:T(8,128)(2,1)S(1)} %pad_maximum_fusion.8), channel_id=1, source_target_pairs={{0,4},{2,6},{4,0},{6,2},{1,5},{3,7},{5,1},{7,3},{8,12},{10,14},{12... | collective-permute-start | bytes 221192 | tf_op jit(solution)/shard_map/ppermute | solution.py:46
  23.8 8.1 %collective-permute-start.3 = (bf16[512,128]{1,0:T(8,128)(2,1)S(1)}, bf16[512,128]{1,0:T(8,128)(2,1)S(1)}, u32[]{:S(2)}, u32[]{:S(2)}) collective-permute-start(bf16[512,128]{1,0:T(8,128)(2,1)S(1)} %bitcast.139), channel_id=1, source_target_pairs={{0,384},{128,256},{256,128},{384,0},{1,385},{129,257},{257,129},{3... | collective-permute-start | bytes 393224 | tf_op jit(solution)/shard_map/ppermute | solution.py:46
  33.2 32.6 %all-to-all-start = ((bf16[16,128,128]{1,2,0:T(8,128)(2,1)}), bf16[16,128,128]{1,2,0:T(8,128)(2,1)S(1)}, u32[]{:S(2)}, u32[]{:S(2)}) async-start(bf16[16,128,128]{1,2,0:T(8,128)(2,1)} %broadcast_in_dim.31), calls=%async_computation | async-start | bytes 1048576 | tf_op jit(solution)/shard_map/all_to_all | solution.py:41
  47.4 20.4 %copy-start.4 = (s32[4]{0:T(128)S(1)}, s32[4]{0:T(128)}, u32[]{:S(2)}) copy-start(s32[4]{0:T(128)} %constant.46.clone) | copy-start | bytes 52
  47.4 20.4 %copy-start.3 = (f32[1024]{0:T(1024)S(1)}, f32[1024]{0:T(1024)}, u32[]{:S(2)}) copy-start(f32[1024]{0:T(1024)} %param.10) | copy-start | bytes 12292
  47.4 8.4 %collective-permute-start.4 = (bf16[1088,128]{1,0:T(8,128)(2,1)S(1)}, bf16[1088,128]{1,0:T(8,128)(2,1)S(1)}, u32[]{:S(2)}, u32[]{:S(2)}) collective-permute-start(bf16[1088,128]{1,0:T(8,128)(2,1)S(1)} %pad_maximum_fusion.3), channel_id=1, source_target_pairs={{0,128},{128,0},{256,384},{384,256},{1,129},{129,1},{257,385},{385... | collective-permute-start | bytes 835592 | tf_op jit(solution)/shard_map/ppermute | solution.py:46
  55.9 9.8 %collective-permute-start.5 = (bf16[2,4,144,128]{3,2,1,0:T(8,128)(2,1)S(1)}, bf16[2,4,144,128]{3,2,1,0:T(8,128)(2,1)S(1)}, u32[]{:S(2)}, u32[]{:S(2)}) collective-permute-start(bf16[2,4,144,128]{3,2,1,0:T(8,128)(2,1)S(1)} %pad_maximum_fusion.2), channel_id=1, source_target_pairs={{0,384},{128,256},{256,128},{384,0},{1,385},{129,257},{257,129},{3... | collective-permute-start | bytes 884744 | tf_op jit(solution)/shard_map/ppermute | solution.py:46
  65.8 3.9 %collective-permute-start.6 = (bf16[4,4,144,128]{3,2,1,0:T(8,128)(2,1)S(1)}, bf16[4,4,144,128]{3,2,1,0:T(8,128)(2,1)S(1)}, u32[]{:S(2)}, u32[]{:S(2)}) collective-permute-start(bf16[4,4,144,128]{3,2,1,0:T(8,128)(2,1)S(1)} %pad_maximum_fusion.1), channel_id=1, source_target_pairs={{0,1},{1,0},{2,3},{3,2},{4,5},{5,4},{6,7},{7,6},{8,9},{9,8},{10,11... | collective-permute-start | bytes 1769480 | tf_op jit(solution)/shard_map/ppermute | solution.py:46
  71.2 18.8 %collective-permute-start.7 = (bf16[528,128]{1,0:T(8,128)(2,1)S(1)}, bf16[528,128]{1,0:T(8,128)(2,1)S(1)}, u32[]{:S(2)}, u32[]{:S(2)}) collective-permute-start(bf16[528,128]{1,0:T(8,128)(2,1)S(1)} %fusion.16), channel_id=1, source_target_pairs={{0,384},{128,256},{256,128},{384,0},{1,385},{129,257},{257,129},{3... | collective-permute-start | bytes 405512 | tf_op jit(solution)/shard_map/ppermute | solution.py:46
  77.9 34.4 %all-to-all-start.1 = ((bf16[16,128,128]{2,1,0:T(8,128)(2,1)}), bf16[16,128,128]{2,1,0:T(8,128)(2,1)S(1)}, u32[]{:S(2)}, u32[]{:S(2)}) async-start(bf16[16,128,128]{2,1,0:T(8,128)(2,1)} %bitcast.49), calls=%async_computation.1 | async-start | bytes 1048576 | tf_op jit(solution)/shard_map/all_to_all | solution.py:41
  90.0 7.4 %copy-start = (bf16[128,1024]{1,0:T(8,128)(2,1)S(1)}, bf16[128,1024]{1,0:T(8,128)(2,1)}, u32[]{:S(2)}) copy-start(bf16[128,1024]{1,0:T(8,128)(2,1)} %param.6) | copy-start | bytes 786436
  90.2 6.9 %collective-permute-start.8 = (bf16[528,128]{1,0:T(8,128)(2,1)S(1)}, bf16[528,128]{1,0:T(8,128)(2,1)S(1)}, u32[]{:S(2)}, u32[]{:S(2)}) collective-permute-start(bf16[528,128]{1,0:T(8,128)(2,1)S(1)} %concatenate.51), channel_id=1, source_target_pairs={{0,128},{128,0},{256,384},{384,256},{1,129},{129,1},{257,385},{385... | collective-permute-start | bytes 405512 | tf_op jit(solution)/shard_map/ppermute | solution.py:46
  97.2 32.1 %copy-start.1 = (bf16[128,1024]{1,0:T(8,128)(2,1)S(1)}, bf16[128,1024]{1,0:T(8,128)(2,1)}, u32[]{:S(2)}) copy-start(bf16[128,1024]{1,0:T(8,128)(2,1)} %param.7) | copy-start | bytes 786436
  97.6 3.0 %collective-permute-start.9 = (f32[128]{0:T(128)S(1)}, f32[128]{0:T(128)S(1)}, u32[]{:S(2)}, u32[]{:S(2)}) collective-permute-start(f32[128]{0:T(128)S(1)} %fusion.4), channel_id=1, source_target_pairs={{0,1},{1,0},{2,3},{3,2},{4,5},{5,4},{6,7},{7,6},{8,9},{9,8},{10,11... | collective-permute-start | bytes 1544 | tf_op jit(solution)/shard_map/ppermute | solution.py:46
  100.6 5.4 %collective-permute-start.10 = (f32[128]{0:T(128)S(1)}, f32[128]{0:T(128)S(1)}, u32[]{:S(2)}, u32[]{:S(2)}) collective-permute-start(f32[128]{0:T(128)S(1)} %add.56), channel_id=1, source_target_pairs={{0,2},{2,0},{4,6},{6,4},{1,3},{3,1},{5,7},{7,5},{8,10},{10,8},{12,... | collective-permute-start | bytes 1544 | tf_op jit(solution)/shard_map/ppermute | solution.py:46
  106.0 6.3 %collective-permute-start.11 = (f32[128]{0:T(128)S(1)}, f32[128]{0:T(128)S(1)}, u32[]{:S(2)}, u32[]{:S(2)}) collective-permute-start(f32[128]{0:T(128)S(1)} %add.57), channel_id=1, source_target_pairs={{0,4},{2,6},{4,0},{6,2},{1,5},{3,7},{5,1},{7,3},{8,12},{10,14},{12... | collective-permute-start | bytes 1544 | tf_op jit(solution)/shard_map/ppermute | solution.py:46
  112.4 17.8 %collective-permute-start.12 = (f32[128,128]{1,0:T(8,128)S(1)}, f32[128,128]{1,0:T(8,128)S(1)}, u32[]{:S(2)}, u32[]{:S(2)}) collective-permute-start(f32[128,128]{1,0:T(8,128)S(1)} %convert_reduce_fusion.1), channel_id=1, source_target_pairs={{0,0},{16,1},{32,2},{48,3},{64,4},{80,5},{96,6},{112,7},{8,8},{24,... | collective-permute-start | bytes 196616 | tf_op jit(solution)/shard_map/ppermute | solution.py:114
  118.2 24.0 %all-to-all-start.2 = ((f32[16,8,128]{2,1,0:T(8,128)}), f32[16,8,128]{2,1,0:T(8,128)S(1)}, u32[]{:S(2)}, u32[]{:S(2)}) async-start(f32[16,8,128]{2,1,0:T(8,128)} %broadcast_in_dim.55), calls=%async_computation.2 | async-start | bytes 131072 | tf_op jit(solution)/shard_map/all_to_all | solution.py:41

commit v7 on v6

--- a/solution.py
+++ b/solution.py
@@ -81,12 +81,17 @@
         return lax.dynamic_slice_in_dim(blocks, (mine ^ r) * 2, 2, axis=0)
 
     packet, moved = lax.optimization_barrier((packet, moved))
+    other = swap(moved, "zh", 1)
+    first = lax.axis_index("zh") == 0
+    wide = jnp.stack([jnp.where(first, moved, other), jnp.where(first, other, moved)])
     packet = jnp.concatenate([packet, swap(packet, "zl", 1)])
+    packet, wide = lax.optimization_barrier((packet, wide))
+    wide = jnp.stack([wide, swap(wide, "core", 1)])
+    weights = lax.all_gather(wide, "y", axis=0)[:, 0]
     given = jnp.concatenate([quarter(3), quarter(2)]).reshape(4 * TOK, HD)
     near = swap(given, "x", 3)
     packet = jnp.concatenate([packet, swap(packet, "zl", 2)])
-    packet, moved, near = lax.optimization_barrier((packet, moved, near))
-    weights = exchange(jnp.broadcast_to(moved[None], (16, HD, HD)), ROW)
+    packet, near = lax.optimization_barrier((packet, near))
 
     near = near.reshape(2, 2, TOK, HD)
     given = jnp.concatenate([quarter(1), near[1]]).reshape(4 * TOK, HD)
@@ -106,47 +111,31 @@
     normal = rows.astype(jnp.float32) * inv_all.reshape(1, 4 * TOK, 1)
     normed = (normal * gain_quarter).astype(jnp.bfloat16)
 
-    pieces = jnp.einsum(
-        "ktc,btf->kbcf", kv, normed, preferred_element_type=jnp.float32
-    ).astype(jnp.bfloat16)
-    arrived = exchange(pieces.reshape(16, HD, HD), ROW)
-    block = jnp.sum(arrived.astype(jnp.float32), axis=0)
-    weight_grad = lax.ppermute(block, AXES, [(b, a) for a, b in moves])
-
     products = jnp.einsum(
         "ktc,kbcf->kbtf",
         kv,
-        weights.reshape(8, 2, HD, HD),
+        weights,
         preferred_element_type=jnp.float32,
     ).astype(jnp.bfloat16)
     norm_grad = jnp.sum(products.astype(jnp.float32), axis=0)
     gain_part = terms_of(jnp.sum(norm_grad * normal, axis=1)).reshape(6, HD)
 
+    pieces = jnp.einsum(
+        "ktc,btf->kbcf", kv, normed, preferred_element_type=jnp.float32
+    ).astype(jnp.bfloat16)
+    gain_rows = jnp.broadcast_to(jnp.pad(gain_part, ((0, 10), (0, 0)))[None], (16, 16, HD))
+    arrived = exchange(jnp.concatenate([pieces.reshape(16, HD, HD), gain_rows], axis=1), ROW)
+    block = jnp.sum(arrived[:, :HD].astype(jnp.float32), axis=0)
+    weight_grad = lax.ppermute(block, AXES, [(b, a) for a, b in moves])
+    gains = jnp.sum(arrived[:, HD : HD + 6].astype(jnp.float32), axis=0)
+    gains = jnp.sum(gains.reshape(3, 2, HD), axis=0)
+    gains = exchange(jnp.broadcast_to(gains[None], (4, 2, HD)), "x")
+    gain_grad = gains.reshape(4 * QUARTER)
+
     back = norm_grad.astype(jnp.bfloat16)
-    given = jnp.concatenate(
-        [back[:, 2 * TOK :].reshape(4 * TOK, HD), jnp.pad(gain_part, ((0, 10), (0, 0)))]
-    )
-    came = swap(given, "x", 3)
-    near, gain_near = came[: 4 * TOK].reshape(2, 2 * TOK, HD), came[4 * TOK : 4 * TOK + 6]
-    given = jnp.concatenate(
-        [
-            back[:, TOK : 2 * TOK].reshape(2 * TOK, HD),
-            near[:, TOK:].reshape(2 * TOK, HD),
-            gain_part,
-            gain_near,
-            jnp.zeros((4, HD), jnp.bfloat16),
-        ]
-    )
-    came = swap(given, "x", 1)
-    far, gain_far = came[: 4 * TOK].reshape(2, 2, TOK, HD), came[4 * TOK : 4 * TOK + 12]
-    gains = jnp.concatenate([gain_part, gain_near, gain_far]).astype(jnp.float32)
-    gains = jnp.sum(gains.reshape(4, 3, 2, HD), axis=1)
-    place = mine ^ jnp.array([0, 3, 1, 2])
-    chosen = place[None, :, None, None] == jnp.arange(4)[:, None, None, None]
-    gains = jnp.sum(jnp.where(chosen, gains[None], 0.0), axis=1).reshape(8, HD)
-    gains, block = lax.optimization_barrier((gains, block))
-    gain_parts = exchange(jnp.broadcast_to(gains[None], (16, 8, HD)), ROW)
-    gain_grad = jnp.sum(gain_parts, axis=0).reshape(4 * QUARTER)
+    near = swap(back[:, 2 * TOK :].reshape(4 * TOK, HD), "x", 3).reshape(2, 2 * TOK, HD)
+    given = jnp.concatenate([back[:, TOK : 2 * TOK], near[:, TOK:]]).reshape(4 * TOK, HD)
+    far = swap(given, "x", 1).reshape(2, 2, TOK, HD)
 
     full = jnp.zeros((8, TOK, HD), jnp.bfloat16)
     for part, r in ((back[:, :TOK], 0), (far[0], 1), (near[:, :TOK], 3), (far[1], 2)):

time: 145 us -> 153 us (1.055)
  starting transfers between devices: 85 us -> 69.7 us
  between operations: 1.38 us -> 14.7 us
  waiting for transfers between devices: 44.8 us -> 53.1 us
    all_to_all x3 -> x2, starting transfers between devices: 37.2 us -> 14.5 us  [exchange(): return lax.all_to_all(value, axes, split_axis=0, concat_axis=0, tiled=True)]
    ppermute x11 -> x13, waiting for transfers between devices: 32.8 us -> 42.7 us  [swap(): return lax.ppermute(value, axis, [(i, i ^ mask) for i in range(count)])]
    all_to_all x3 -> x2, waiting for transfers between devices: 12 us -> 2.27 us  [exchange(): return lax.all_to_all(value, axes, split_axis=0, concat_axis=0, tiled=True)]
    all_gather x0 -> x1, waiting for transfers between devices: none -> 8.19 us  [shards(): weights = lax.all_gather(wide, 'y', axis=0)[:, 0]]
    ppermute x11 -> x13, starting transfers between devices: 31.1 us -> 38.4 us  [swap(): return lax.ppermute(value, axis, [(i, i ^ mask) for i in range(count)])]
  transfers between devices with their start and end apart: 16 -> 18, of which waited for: 11 -> 14; matrix products, arithmetic and copies ran while one was open for 6% -> 5% of each run, Pallas kernels for 0% -> 0%
where the time goes in v7:
time: 153 us; the launch traced here: 151 us
  starting transfers between devices  69.7 us (46%)
  waiting for transfers between devices  53.1 us (35%)
  between operations  14.7 us (10%)
  local copies, waits for them, and re-layouts  6.92 us (5%)
  other arithmetic  4.87 us (3%)
    ppermute x13, waiting for transfers between devices, swap(): return lax.ppermute(value, axis, [(i, i ^ mask) for i in range(count)])  42.7 us
    ppermute x13, starting transfers between devices, swap(): return lax.ppermute(value, axis, [(i, i ^ mask) for i in range(count)])  38.4 us
    all_to_all x2, starting transfers between devices, exchange(): return lax.all_to_all(value, axes, split_axis=0, concat_axis=0, tiled=True)  14.5 us
    ppermute x1, starting transfers between devices, shards(): moved = lax.ppermute(kv_weight, AXES, moves)  11.5 us
    all_gather x1, waiting for transfers between devices, shards(): weights = lax.all_gather(wide, 'y', axis=0)[:, 0]  8.19 us
    ppermute x1, starting transfers between devices, shards(): weight_grad = lax.ppermute(block, AXES, [(b, a) for a, b in moves])  5.34 us
  transfers between devices with their start and end apart: 18, of which 14 were waited for; matrix products, arithmetic and copies ran while one was open for 5% of the time, Pallas kernels for 0%

profile of v7, /device:TPU:6, one launch (start us, length us, event | category | flops | bytes accessed | tf_op | source)
XLA Modules:
  0.0 150.7 jit_solution(13664367532869156999)
XLA Ops:
  7.2 11.5 %collective-permute-start = (bf16[128,128]{1,0:T(8,128)(2,1)}, bf16[128,128]{1,0:T(8,128)(2,1)S(1)}, u32[]{:S(2)}, u32[]{:S(2)}) collective-permute-start(bf16[128,128]{1,0:T(8,128)(2,1)} %param.8), channel_id=1, source_target_pairs={{0,0},{1,16},{2,32},{3,48},{4,64},{5,80},{6,96},{7,112},{8,8},{9,2... | collective-permute-start | bytes 98312 | tf_op jit(solution)/shard_map/ppermute | solution.py:67
  18.7 0.9 fusion.29
  19.6 1.1 fusion.9
  20.7 0.1 copy.82
  20.9 0.1 copy.83
  21.0 0.1 copy.84
  21.1 0.1 copy.85
  21.2 0.1 copy.86
  21.5 0.3 multiply_add_fusion
  21.9 0.1 copy.87
  22.0 8.2 %collective-permute-start.2 = (bf16[128,128]{1,0:T(8,128)(2,1)S(1)}, bf16[128,128]{1,0:T(8,128)(2,1)S(1)}, u32[]{:S(2)}, u32[]{:S(2)}) collective-permute-start(bf16[128,128]{1,0:T(8,128)(2,1)S(1)} %collective-permute-done), channel_id=1, source_target_pairs={{0,8},{8,0},{1,9},{9,1},{2,10},{10,2},{3,11},{11,3},{4,12},{12,4},... | collective-permute-start | bytes 98312 | tf_op jit(solution)/shard_map/ppermute | solution.py:46
  30.2 0.1 copy.88
  30.4 4.0 %collective-permute-start.1 = (bf16[1,144,128]{2,1,0:T(8,128)(2,1)S(1)}, bf16[1,144,128]{2,1,0:T(8,128)(2,1)S(1)}, u32[]{:S(2)}, u32[]{:S(2)}) collective-permute-start(bf16[1,144,128]{2,1,0:T(8,128)(2,1)S(1)} %maximum_bitcast_fusion), channel_id=1, source_target_pairs={{0,2},{2,0},{4,6},{6,4},{1,3},{3,1},{5,7},{7,5},{8,10},{10,8},{12,... | collective-permute-start | bytes 110600 | tf_op jit(solution)/shard_map/ppermute | solution.py:46
  34.5 1.9 %collective-permute-done.1 = bf16[1,144,128]{2,1,0:T(8,128)(2,1)S(1)} collective-permute-done((bf16[1,144,128]{2,1,0:T(8,128)(2,1)S(1)}, bf16[1,144,128]{2,1,0:T(8,128)(2,1)S(1)}, u32[]{:S(2)}, u32[]{:S(2)}) %collective-permute-start.1) | collective-permute-done | bytes 36896 | tf_op jit(solution)/shard_map/ppermute | solution.py:46
  36.4 1.9 %collective-permute-start.7 = (bf16[2,128,128]{2,1,0:T(8,128)(2,1)S(1)}, bf16[2,128,128]{2,1,0:T(8,128)(2,1)S(1)}, u32[]{:S(2)}, u32[]{:S(2)}) collective-permute-start(bf16[2,128,128]{2,1,0:T(8,128)(2,1)S(1)} %pad_maximum_fusion.12), channel_id=1, source_target_pairs={{0,1},{1,0},{2,3},{3,2},{4,5},{5,4},{6,7},{7,6},{8,9},{9,8},{10,11... | collective-permute-start | bytes 196616 | tf_op jit(solution)/shard_map/ppermute | solution.py:46
  38.3 0.1 copy.89
  38.4 1.1 collective-permute-done.7
  39.5 0.7 pad_maximum_fusion.9
  40.3 1.9 %collective-permute-start.3 = (bf16[2,144,128]{2,1,0:T(8,128)(2,1)S(1)}, bf16[2,144,128]{2,1,0:T(8,128)(2,1)S(1)}, u32[]{:S(2)}, u32[]{:S(2)}) collective-permute-start(bf16[2,144,128]{2,1,0:T(8,128)(2,1)S(1)} %pad_maximum_fusion.11), channel_id=1, source_target_pairs={{0,4},{2,6},{4,0},{6,2},{1,5},{3,7},{5,1},{7,3},{8,12},{10,14},{12... | collective-permute-start | bytes 221192 | tf_op jit(solution)/shard_map/ppermute | solution.py:46
  42.2 0.1 copy.61
  42.4 3.5 %collective-permute-start.4 = (bf16[512,128]{1,0:T(8,128)(2,1)S(1)}, bf16[512,128]{1,0:T(8,128)(2,1)S(1)}, u32[]{:S(2)}, u32[]{:S(2)}) collective-permute-start(bf16[512,128]{1,0:T(8,128)(2,1)S(1)} %bitcast.144), channel_id=1, source_target_pairs={{0,384},{128,256},{256,128},{384,0},{1,385},{129,257},{257,129},{3... | collective-permute-start | bytes 393224 | tf_op jit(solution)/shard_map/ppermute | solution.py:46
  45.9 3.1 %collective-permute-done.3 = bf16[2,144,128]{2,1,0:T(8,128)(2,1)S(1)} collective-permute-done((bf16[2,144,128]{2,1,0:T(8,128)(2,1)S(1)}, bf16[2,144,128]{2,1,0:T(8,128)(2,1)S(1)}, u32[]{:S(2)}, u32[]{:S(2)}) %collective-permute-start.3) | collective-permute-done | bytes 73760 | tf_op jit(solution)/shard_map/ppermute | solution.py:46
  49.0 2.0 %collective-permute-done.4 = bf16[512,128]{1,0:T(8,128)(2,1)S(1)} collective-permute-done((bf16[512,128]{1,0:T(8,128)(2,1)S(1)}, bf16[512,128]{1,0:T(8,128)(2,1)S(1)}, u32[]{:S(2)}, u32[]{:S(2)}) %collective-permute-start.4) | collective-permute-done | bytes 131104 | tf_op jit(solution)/shard_map/ppermute | solution.py:46
  51.0 0.1 copy.62
  51.2 0.1 copy.63
  51.3 2.1 %collective-permute-start.5 = (bf16[1088,128]{1,0:T(8,128)(2,1)S(1)}, bf16[1088,128]{1,0:T(8,128)(2,1)S(1)}, u32[]{:S(2)}, u32[]{:S(2)}) collective-permute-start(bf16[1088,128]{1,0:T(8,128)(2,1)S(1)} %pad_maximum_fusion.4), channel_id=1, source_target_pairs={{0,128},{128,0},{256,384},{384,256},{1,129},{129,1},{257,385},{385... | collective-permute-start | bytes 835592 | tf_op jit(solution)/shard_map/ppermute | solution.py:46
  53.5 7.7 %collective-permute-done.5 = bf16[1088,128]{1,0:T(8,128)(2,1)S(1)} collective-permute-done((bf16[1088,128]{1,0:T(8,128)(2,1)S(1)}, bf16[1088,128]{1,0:T(8,128)(2,1)S(1)}, u32[]{:S(2)}, u32[]{:S(2)}) %collective-permute-start.5) | collective-permute-done | bytes 278560 | tf_op jit(solution)/shard_map/ppermute | solution.py:46
  61.2 2.9 %collective-permute-start.6 = (bf16[2,4,144,128]{3,2,1,0:T(8,128)(2,1)S(1)}, bf16[2,4,144,128]{3,2,1,0:T(8,128)(2,1)S(1)}, u32[]{:S(2)}, u32[]{:S(2)}) collective-permute-start(bf16[2,4,144,128]{3,2,1,0:T(8,128)(2,1)S(1)} %pad_maximum_fusion.3), channel_id=1, source_target_pairs={{0,384},{128,256},{256,128},{384,0},{1,385},{129,257},{257,129},{3... | collective-permute-start | bytes 884744 | tf_op jit(solution)/shard_map/ppermute | solution.py:46
  64.1 7.5 %collective-permute-done.6 = bf16[2,4,144,128]{3,2,1,0:T(8,128)(2,1)S(1)} collective-permute-done((bf16[2,4,144,128]{3,2,1,0:T(8,128)(2,1)S(1)}, bf16[2,4,144,128]{3,2,1,0:T(8,128)(2,1)S(1)}, u32[]{:S(2)}, u32[]{:S(2)}) %collective-permute-start.6) | collective-permute-done | bytes 294944 | tf_op jit(solution)/shard_map/ppermute | solution.py:46
  71.7 8.2 %all-gather.3.cloned.1.call-done = bf16[16,2,128,128]{3,2,1,0:T(8,128)(2,1)} async-done(((bf16[2,2,128,128]{3,2,1,0:T(8,128)(2,1)}), bf16[16,2,128,128]{3,2,1,0:T(8,128)(2,1)}) %all-gather.3.cloned.1.call-update) | async-done | bytes 1048592 | tf_op jit(solution)/shard_map/all_gather | solution.py:90
  79.9 1.1 slice.156
  81.0 0.3 copy.90
  81.3 1.9 %collective-permute-start.8 = (bf16[4,4,144,128]{3,2,1,0:T(8,128)(2,1)S(1)}, bf16[4,4,144,128]{3,2,1,0:T(8,128)(2,1)S(1)}, u32[]{:S(2)}, u32[]{:S(2)}) collective-permute-start(bf16[4,4,144,128]{3,2,1,0:T(8,128)(2,1)S(1)} %pad_maximum_fusion.1), channel_id=1, source_target_pairs={{0,1},{1,0},{2,3},{3,2},{4,5},{5,4},{6,7},{7,6},{8,9},{9,8},{10,11... | collective-permute-start | bytes 1769480 | tf_op jit(solution)/shard_map/ppermute | solution.py:46
  83.3 0.1 copy.71
  83.5 0.1 copy.70
  83.6 0.1 copy.72
  83.7 1.5 collective-permute-done.8
  85.5 0.7 convert_reduce_fusion
  86.2 0.2 fusion.10
  86.4 0.6 fusion
  87.1 0.9 pad_maximum_fusion.2
  88.0 10.0 %all-to-all-start = ((bf16[16,144,128]{2,1,0:T(8,128)(2,1)}), bf16[16,144,128]{2,1,0:T(8,128)(2,1)S(1)}, u32[]{:S(2)}, u32[]{:S(2)}) async-start(bf16[16,144,128]{2,1,0:T(8,128)(2,1)} %pad_maximum_fusion.2), calls=%async_computation | async-start | bytes 1179648 | tf_op jit(solution)/shard_map/all_to_all | solution.py:41
  97.9 0.1 copy.67
  98.1 2.5 %collective-permute-start.9 = (bf16[512,128]{1,0:T(8,128)(2,1)S(1)}, bf16[512,128]{1,0:T(8,128)(2,1)S(1)}, u32[]{:S(2)}, u32[]{:S(2)}) collective-permute-start(bf16[512,128]{1,0:T(8,128)(2,1)S(1)} %bitcast.145), channel_id=1, source_target_pairs={{0,384},{128,256},{256,128},{384,0},{1,385},{129,257},{257,129},{3... | collective-permute-start | bytes 393224 | tf_op jit(solution)/shard_map/ppermute | solution.py:46
  100.6 5.9 %collective-permute-done.9 = bf16[512,128]{1,0:T(8,128)(2,1)S(1)} collective-permute-done((bf16[512,128]{1,0:T(8,128)(2,1)S(1)}, bf16[512,128]{1,0:T(8,128)(2,1)S(1)}, u32[]{:S(2)}, u32[]{:S(2)}) %collective-permute-start.9) | collective-permute-done | bytes 131104 | tf_op jit(solution)/shard_map/ppermute | solution.py:46
  106.4 0.1 copy.91
  106.6 0.1 copy.69
  106.7 1.9 %collective-permute-start.10 = (bf16[512,128]{1,0:T(8,128)(2,1)S(1)}, bf16[512,128]{1,0:T(8,128)(2,1)S(1)}, u32[]{:S(2)}, u32[]{:S(2)}) collective-permute-start(bf16[512,128]{1,0:T(8,128)(2,1)S(1)} %bitcast.143), channel_id=1, source_target_pairs={{0,128},{128,0},{256,384},{384,256},{1,129},{129,1},{257,385},{385... | collective-permute-start | bytes 393224 | tf_op jit(solution)/shard_map/ppermute | solution.py:46
  108.7 0.1 copy.66
  108.9 4.7 %collective-permute-done.10 = bf16[512,128]{1,0:T(8,128)(2,1)S(1)} collective-permute-done((bf16[512,128]{1,0:T(8,128)(2,1)S(1)}, bf16[512,128]{1,0:T(8,128)(2,1)S(1)}, u32[]{:S(2)}, u32[]{:S(2)}) %collective-permute-start.10) | collective-permute-done | bytes 131104 | tf_op jit(solution)/shard_map/ppermute | solution.py:46
  113.8 0.2 fusion.4
  114.1 1.9 %collective-permute-start.11 = (f32[128]{0:T(128)S(1)}, f32[128]{0:T(128)S(1)}, u32[]{:S(2)}, u32[]{:S(2)}) collective-permute-start(f32[128]{0:T(128)S(1)} %fusion.4), channel_id=1, source_target_pairs={{0,1},{1,0},{2,3},{3,2},{4,5},{5,4},{6,7},{7,6},{8,9},{9,8},{10,11... | collective-permute-start | bytes 1544 | tf_op jit(solution)/shard_map/ppermute | solution.py:46
  116.0 1.1 collective-permute-done.11
  117.1 2.6 %collective-permute-start.12 = (f32[128]{0:T(128)S(1)}, f32[128]{0:T(128)S(1)}, u32[]{:S(2)}, u32[]{:S(2)}) collective-permute-start(f32[128]{0:T(128)S(1)} %add.56), channel_id=1, source_target_pairs={{0,2},{2,0},{4,6},{6,4},{1,3},{3,1},{5,7},{7,5},{8,10},{10,8},{12,... | collective-permute-start | bytes 1544 | tf_op jit(solution)/shard_map/ppermute | solution.py:46
  119.7 2.8 %collective-permute-done.12 = f32[128]{0:T(128)S(1)} collective-permute-done((f32[128]{0:T(128)S(1)}, f32[128]{0:T(128)S(1)}, u32[]{:S(2)}, u32[]{:S(2)}) %collective-permute-start.12) | collective-permute-done | bytes 544 | tf_op jit(solution)/shard_map/ppermute | solution.py:46
  122.5 2.9 %collective-permute-start.13 = (f32[128]{0:T(128)S(1)}, f32[128]{0:T(128)S(1)}, u32[]{:S(2)}, u32[]{:S(2)}) collective-permute-start(f32[128]{0:T(128)S(1)} %add.57), channel_id=1, source_target_pairs={{0,4},{2,6},{4,0},{6,2},{1,5},{3,7},{5,1},{7,3},{8,12},{10,14},{12... | collective-permute-start | bytes 1544 | tf_op jit(solution)/shard_map/ppermute | solution.py:46
  125.4 3.5 %collective-permute-done.13 = f32[128]{0:T(128)S(1)} collective-permute-done((f32[128]{0:T(128)S(1)}, f32[128]{0:T(128)S(1)}, u32[]{:S(2)}, u32[]{:S(2)}) %collective-permute-start.13) | collective-permute-done | bytes 544 | tf_op jit(solution)/shard_map/ppermute | solution.py:46
  128.9 5.3 %collective-permute-start.14 = (f32[128,128]{1,0:T(8,128)S(1)}, f32[128,128]{1,0:T(8,128)S(1)}, u32[]{:S(2)}, u32[]{:S(2)}) collective-permute-start(f32[128,128]{1,0:T(8,128)S(1)} %convert_reduce_fusion.1), channel_id=1, source_target_pairs={{0,0},{16,1},{32,2},{48,3},{64,4},{80,5},{96,6},{112,7},{8,8},{24,... | collective-permute-start | bytes 196616 | tf_op jit(solution)/shard_map/ppermute | solution.py:129
  134.3 0.6 broadcast_in_dim.11
  134.9 4.5 %all-to-all-start.1 = ((f32[4,2,128]{2,1,0:T(2,128)}), f32[4,2,128]{2,1,0:T(2,128)S(1)}, u32[]{:S(2)}, u32[]{:S(2)}) async-start(f32[4,2,128]{2,1,0:T(2,128)} %broadcast_in_dim.11), calls=%async_computation.1 | async-start | bytes 8192 | tf_op jit(solution)/shard_map/all_to_all | solution.py:41
  139.4 1.0 fusion.8
  140.4 2.3 %all-to-all-done.1 = f32[4,2,128]{2,1,0:T(2,128)S(1)} async-done(((f32[4,2,128]{2,1,0:T(2,128)}), f32[4,2,128]{2,1,0:T(2,128)S(1)}, u32[]{:S(2)}, u32[]{:S(2)}) %all-to-all-start.1) | async-done | bytes 4128 | tf_op jit(solution)/shard_map/all_to_all | solution.py:41
  142.6 0.6 copy.112
  143.3 0.6 copy.113
  (79 shorter events, 1.4 us)
Async XLA Ops:
  7.2 14.2 %copy-start.2 = (bf16[128,128]{1,0:T(8,128)(2,1)S(1)}, bf16[128,128]{1,0:T(8,128)(2,1)}, u32[]{:S(2)}) copy-start(bf16[128,128]{1,0:T(8,128)(2,1)} %param.7) | copy-start | bytes 98308
  7.2 72.8 %all-gather.3.cloned.1.call-start = ((), (), s32[]{:S(2)}) async-start(), calls=%async_computation.2 | async-start | bytes 1179648 | tf_op jit(solution)/shard_map/all_gather | solution.py:90
  7.2 14.8 %collective-permute-start = (bf16[128,128]{1,0:T(8,128)(2,1)}, bf16[128,128]{1,0:T(8,128)(2,1)S(1)}, u32[]{:S(2)}, u32[]{:S(2)}) collective-permute-start(bf16[128,128]{1,0:T(8,128)(2,1)} %param.8), channel_id=1, source_target_pairs={{0,0},{1,16},{2,32},{3,48},{4,64},{5,80},{6,96},{7,112},{8,8},{9,2... | collective-permute-start | bytes 98312 | tf_op jit(solution)/shard_map/ppermute | solution.py:67
  22.0 12.4 %collective-permute-start.2 = (bf16[128,128]{1,0:T(8,128)(2,1)S(1)}, bf16[128,128]{1,0:T(8,128)(2,1)S(1)}, u32[]{:S(2)}, u32[]{:S(2)}) collective-permute-start(bf16[128,128]{1,0:T(8,128)(2,1)S(1)} %collective-permute-done), channel_id=1, source_target_pairs={{0,8},{8,0},{1,9},{9,1},{2,10},{10,2},{3,11},{11,3},{4,12},{12,4},... | collective-permute-start | bytes 98312 | tf_op jit(solution)/shard_map/ppermute | solution.py:46
  30.4 6.0 %collective-permute-start.1 = (bf16[1,144,128]{2,1,0:T(8,128)(2,1)S(1)}, bf16[1,144,128]{2,1,0:T(8,128)(2,1)S(1)}, u32[]{:S(2)}, u32[]{:S(2)}) collective-permute-start(bf16[1,144,128]{2,1,0:T(8,128)(2,1)S(1)} %maximum_bitcast_fusion), channel_id=1, source_target_pairs={{0,2},{2,0},{4,6},{6,4},{1,3},{3,1},{5,7},{7,5},{8,10},{10,8},{12,... | collective-permute-start | bytes 110600 | tf_op jit(solution)/shard_map/ppermute | solution.py:46
  36.4 3.1 %collective-permute-start.7 = (bf16[2,128,128]{2,1,0:T(8,128)(2,1)S(1)}, bf16[2,128,128]{2,1,0:T(8,128)(2,1)S(1)}, u32[]{:S(2)}, u32[]{:S(2)}) collective-permute-start(bf16[2,128,128]{2,1,0:T(8,128)(2,1)S(1)} %pad_maximum_fusion.12), channel_id=1, source_target_pairs={{0,1},{1,0},{2,3},{3,2},{4,5},{5,4},{6,7},{7,6},{8,9},{9,8},{10,11... | collective-permute-start | bytes 196616 | tf_op jit(solution)/shard_map/ppermute | solution.py:46
  40.3 8.7 %collective-permute-start.3 = (bf16[2,144,128]{2,1,0:T(8,128)(2,1)S(1)}, bf16[2,144,128]{2,1,0:T(8,128)(2,1)S(1)}, u32[]{:S(2)}, u32[]{:S(2)}) collective-permute-start(bf16[2,144,128]{2,1,0:T(8,128)(2,1)S(1)} %pad_maximum_fusion.11), channel_id=1, source_target_pairs={{0,4},{2,6},{4,0},{6,2},{1,5},{3,7},{5,1},{7,3},{8,12},{10,14},{12... | collective-permute-start | bytes 221192 | tf_op jit(solution)/shard_map/ppermute | solution.py:46
  42.4 8.7 %collective-permute-start.4 = (bf16[512,128]{1,0:T(8,128)(2,1)S(1)}, bf16[512,128]{1,0:T(8,128)(2,1)S(1)}, u32[]{:S(2)}, u32[]{:S(2)}) collective-permute-start(bf16[512,128]{1,0:T(8,128)(2,1)S(1)} %bitcast.144), channel_id=1, source_target_pairs={{0,384},{128,256},{256,128},{384,0},{1,385},{129,257},{257,129},{3... | collective-permute-start | bytes 393224 | tf_op jit(solution)/shard_map/ppermute | solution.py:46
  51.3 9.8 %collective-permute-start.5 = (bf16[1088,128]{1,0:T(8,128)(2,1)S(1)}, bf16[1088,128]{1,0:T(8,128)(2,1)S(1)}, u32[]{:S(2)}, u32[]{:S(2)}) collective-permute-start(bf16[1088,128]{1,0:T(8,128)(2,1)S(1)} %pad_maximum_fusion.4), channel_id=1, source_target_pairs={{0,128},{128,0},{256,384},{384,256},{1,129},{129,1},{257,385},{385... | collective-permute-start | bytes 835592 | tf_op jit(solution)/shard_map/ppermute | solution.py:46
  61.2 10.5 %collective-permute-start.6 = (bf16[2,4,144,128]{3,2,1,0:T(8,128)(2,1)S(1)}, bf16[2,4,144,128]{3,2,1,0:T(8,128)(2,1)S(1)}, u32[]{:S(2)}, u32[]{:S(2)}) collective-permute-start(bf16[2,4,144,128]{3,2,1,0:T(8,128)(2,1)S(1)} %pad_maximum_fusion.3), channel_id=1, source_target_pairs={{0,384},{128,256},{256,128},{384,0},{1,385},{129,257},{257,129},{3... | collective-permute-start | bytes 884744 | tf_op jit(solution)/shard_map/ppermute | solution.py:46
  79.9 3.3 %copy-start.3 = (f32[1024]{0:T(1024)S(1)}, f32[1024]{0:T(1024)}, u32[]{:S(2)}) copy-start(f32[1024]{0:T(1024)} %param.9) | copy-start | bytes 12292
  81.3 3.9 %collective-permute-start.8 = (bf16[4,4,144,128]{3,2,1,0:T(8,128)(2,1)S(1)}, bf16[4,4,144,128]{3,2,1,0:T(8,128)(2,1)S(1)}, u32[]{:S(2)}, u32[]{:S(2)}) collective-permute-start(bf16[4,4,144,128]{3,2,1,0:T(8,128)(2,1)S(1)} %pad_maximum_fusion.1), channel_id=1, source_target_pairs={{0,1},{1,0},{2,3},{3,2},{4,5},{5,4},{6,7},{7,6},{8,9},{9,8},{10,11... | collective-permute-start | bytes 1769480 | tf_op jit(solution)/shard_map/ppermute | solution.py:46
  88.0 40.9 %all-to-all-start = ((bf16[16,144,128]{2,1,0:T(8,128)(2,1)}), bf16[16,144,128]{2,1,0:T(8,128)(2,1)S(1)}, u32[]{:S(2)}, u32[]{:S(2)}) async-start(bf16[16,144,128]{2,1,0:T(8,128)(2,1)} %pad_maximum_fusion.2), calls=%async_computation | async-start | bytes 1179648 | tf_op jit(solution)/shard_map/all_to_all | solution.py:41
  98.1 8.4 %collective-permute-start.9 = (bf16[512,128]{1,0:T(8,128)(2,1)S(1)}, bf16[512,128]{1,0:T(8,128)(2,1)S(1)}, u32[]{:S(2)}, u32[]{:S(2)}) collective-permute-start(bf16[512,128]{1,0:T(8,128)(2,1)S(1)} %bitcast.145), channel_id=1, source_target_pairs={{0,384},{128,256},{256,128},{384,0},{1,385},{129,257},{257,129},{3... | collective-permute-start | bytes 393224 | tf_op jit(solution)/shard_map/ppermute | solution.py:46
  106.6 7.3 %copy-start = (bf16[128,1024]{1,0:T(8,128)(2,1)S(1)}, bf16[128,1024]{1,0:T(8,128)(2,1)}, u32[]{:S(2)}) copy-start(bf16[128,1024]{1,0:T(8,128)(2,1)} %param.5) | copy-start | bytes 786436
  106.7 6.9 %collective-permute-start.10 = (bf16[512,128]{1,0:T(8,128)(2,1)S(1)}, bf16[512,128]{1,0:T(8,128)(2,1)S(1)}, u32[]{:S(2)}, u32[]{:S(2)}) collective-permute-start(bf16[512,128]{1,0:T(8,128)(2,1)S(1)} %bitcast.143), channel_id=1, source_target_pairs={{0,128},{128,0},{256,384},{384,256},{1,129},{129,1},{257,385},{385... | collective-permute-start | bytes 393224 | tf_op jit(solution)/shard_map/ppermute | solution.py:46
  113.6 25.8 %copy-start.1 = (bf16[128,1024]{1,0:T(8,128)(2,1)S(1)}, bf16[128,1024]{1,0:T(8,128)(2,1)}, u32[]{:S(2)}) copy-start(bf16[128,1024]{1,0:T(8,128)(2,1)} %param.6) | copy-start | bytes 786436
  114.1 3.0 %collective-permute-start.11 = (f32[128]{0:T(128)S(1)}, f32[128]{0:T(128)S(1)}, u32[]{:S(2)}, u32[]{:S(2)}) collective-permute-start(f32[128]{0:T(128)S(1)} %fusion.4), channel_id=1, source_target_pairs={{0,1},{1,0},{2,3},{3,2},{4,5},{5,4},{6,7},{7,6},{8,9},{9,8},{10,11... | collective-permute-start | bytes 1544 | tf_op jit(solution)/shard_map/ppermute | solution.py:46
  117.1 5.4 %collective-permute-start.12 = (f32[128]{0:T(128)S(1)}, f32[128]{0:T(128)S(1)}, u32[]{:S(2)}, u32[]{:S(2)}) collective-permute-start(f32[128]{0:T(128)S(1)} %add.56), channel_id=1, source_target_pairs={{0,2},{2,0},{4,6},{6,4},{1,3},{3,1},{5,7},{7,5},{8,10},{10,8},{12,... | collective-permute-start | bytes 1544 | tf_op jit(solution)/shard_map/ppermute | solution.py:46
  122.5 6.3 %collective-permute-start.13 = (f32[128]{0:T(128)S(1)}, f32[128]{0:T(128)S(1)}, u32[]{:S(2)}, u32[]{:S(2)}) collective-permute-start(f32[128]{0:T(128)S(1)} %add.57), channel_id=1, source_target_pairs={{0,4},{2,6},{4,0},{6,2},{1,5},{3,7},{5,1},{7,3},{8,12},{10,14},{12... | collective-permute-start | bytes 1544 | tf_op jit(solution)/shard_map/ppermute | solution.py:46
  128.9 13.7 %collective-permute-start.14 = (f32[128,128]{1,0:T(8,128)S(1)}, f32[128,128]{1,0:T(8,128)S(1)}, u32[]{:S(2)}, u32[]{:S(2)}) collective-permute-start(f32[128,128]{1,0:T(8,128)S(1)} %convert_reduce_fusion.1), channel_id=1, source_target_pairs={{0,0},{16,1},{32,2},{48,3},{64,4},{80,5},{96,6},{112,7},{8,8},{24,... | collective-permute-start | bytes 196616 | tf_op jit(solution)/shard_map/ppermute | solution.py:129
  134.9 7.7 %all-to-all-start.1 = ((f32[4,2,128]{2,1,0:T(2,128)}), f32[4,2,128]{2,1,0:T(2,128)S(1)}, u32[]{:S(2)}, u32[]{:S(2)}) async-start(f32[4,2,128]{2,1,0:T(2,128)} %broadcast_in_dim.11), calls=%async_computation.1 | async-start | bytes 8192 | tf_op jit(solution)/shard_map/all_to_all | solution.py:41
Sparse Core Ops, SparseCore 0:
  40.3 39.5 all-gather.2

commit v8 on v7

--- a/solution.py
+++ b/solution.py
@@ -81,13 +81,14 @@
         return lax.dynamic_slice_in_dim(blocks, (mine ^ r) * 2, 2, axis=0)
 
     packet, moved = lax.optimization_barrier((packet, moved))
-    other = swap(moved, "zh", 1)
-    first = lax.axis_index("zh") == 0
-    wide = jnp.stack([jnp.where(first, moved, other), jnp.where(first, other, moved)])
     packet = jnp.concatenate([packet, swap(packet, "zl", 1)])
-    packet, wide = lax.optimization_barrier((packet, wide))
-    wide = jnp.stack([wide, swap(wide, "core", 1)])
-    weights = lax.all_gather(wide, "y", axis=0)[:, 0]
+    weights = moved
+    for axis, mask, place in (("zh", 1, 0), ("y", 4, 0), ("y", 2, 1), ("y", 1, 2)):
+        other = swap(weights, axis, mask)
+        first = (lax.axis_index(axis) & mask) == 0
+        pair = [jnp.where(first, weights, other), jnp.where(first, other, weights)]
+        weights = jnp.stack(pair, axis=place)
+    weights = weights.reshape(8, 2, HD, HD)
     given = jnp.concatenate([quarter(3), quarter(2)]).reshape(4 * TOK, HD)
     near = swap(given, "x", 3)
     packet = jnp.concatenate([packet, swap(packet, "zl", 2)])
@@ -100,7 +101,6 @@
     rows = jnp.concatenate([quarter(0), far[0], near[0], far[1]], axis=1)
     packet = jnp.stack([packet, came[: 4 * (TOK + 16)].reshape(4, TOK + 16, HD)])
     packet = jnp.concatenate([packet, swap(packet, "x", 3)])
-    packet, weights = lax.optimization_barrier((packet, weights))
     packet = jnp.stack([packet, swap(packet, "core", 1)])
 
     kv = packet[:, :, :, :TOK].transpose(2, 0, 1, 3, 4).reshape(8, 4 * TOK, HD)

time: 153 us -> 125 us (0.82)
  the two profiles are of different devices: /device:TPU:6 before, /device:TPU:48 now
where the time goes in v8:
time: 125 us; the launch traced here: 124 us
  starting transfers between devices  78.3 us (63%)
  waiting for transfers between devices  32.4 us (26%)
  local copies, waits for them, and re-layouts  5.87 us (5%)
  other arithmetic  4.41 us (4%)
  between operations  1.41 us (1%)
  matrix products  1.32 us (1%)
    ppermute x15, starting transfers between devices, swap(): return lax.ppermute(value, axis, [(i, i ^ mask) for i in range(count)])  57.8 us
    ppermute x15, waiting for transfers between devices, swap(): return lax.ppermute(value, axis, [(i, i ^ mask) for i in range(count)])  25.3 us
    all_to_all x2, starting transfers between devices, exchange(): return lax.all_to_all(value, axes, split_axis=0, concat_axis=0, tiled=True)  11.8 us
    ppermute x1, starting transfers between devices, shards(): moved = lax.ppermute(kv_weight, AXES, moves)  4.7 us
    all_to_all x2, waiting for transfers between devices, exchange(): return lax.all_to_all(value, axes, split_axis=0, concat_axis=0, tiled=True)  4.34 us
    ppermute x1, starting transfers between devices, shards(): weight_grad = lax.ppermute(block, AXES, [(b, a) for a, b in moves])  4.09 us
    ppermute x1, waiting for transfers between devices, shards(): moved = lax.ppermute(kv_weight, AXES, moves)  2.71 us
  transfers between devices with their start and end apart: 19, of which 13 were waited for; matrix products, arithmetic and copies ran while one was open for 6% of the time, Pallas kernels for 0%

profile of v8, /device:TPU:48, one launch (start us, length us, event | category | flops | bytes accessed | tf_op | source)
XLA Modules:
  0.0 123.7 jit_solution(1335478173144753970)
XLA Ops:
  0.6 4.7 %collective-permute-start = (bf16[128,128]{1,0:T(8,128)(2,1)}, bf16[128,128]{1,0:T(8,128)(2,1)S(1)}, u32[]{:S(2)}, u32[]{:S(2)}) collective-permute-start(bf16[128,128]{1,0:T(8,128)(2,1)} %param.8), channel_id=1, source_target_pairs={{0,0},{1,16},{2,32},{3,48},{4,64},{5,80},{6,96},{7,112},{8,8},{9,2... | collective-permute-start | bytes 98312 | tf_op jit(solution)/shard_map/ppermute | solution.py:67
  5.4 0.9 fusion.30
  6.3 1.1 fusion.9
  7.4 0.1 copy.82
  7.5 0.1 copy.83
  7.6 0.1 copy.84
  7.7 0.1 copy.85
  7.9 0.1 copy.86
  8.0 0.1 copy.87
  8.1 0.1 copy.88
  8.2 0.1 copy.89
  8.5 0.3 multiply_add_fusion
  9.0 2.7 %collective-permute-done = bf16[128,128]{1,0:T(8,128)(2,1)S(1)} collective-permute-done((bf16[128,128]{1,0:T(8,128)(2,1)}, bf16[128,128]{1,0:T(8,128)(2,1)S(1)}, u32[]{:S(2)}, u32[]{:S(2)}) %collective-permute-start) | collective-permute-done | bytes 32800 | tf_op jit(solution)/shard_map/ppermute | solution.py:67
  11.7 10.7 %collective-permute-start.7 = (bf16[128,128]{1,0:T(8,128)(2,1)S(1)}, bf16[128,128]{1,0:T(8,128)(2,1)S(1)}, u32[]{:S(2)}, u32[]{:S(2)}) collective-permute-start(bf16[128,128]{1,0:T(8,128)(2,1)S(1)} %collective-permute-done), channel_id=1, source_target_pairs={{0,8},{8,0},{1,9},{9,1},{2,10},{10,2},{3,11},{11,3},{4,12},{12,4},... | collective-permute-start | bytes 98312 | tf_op jit(solution)/shard_map/ppermute | solution.py:46
  22.4 0.1 copy.61
  22.5 7.7 %collective-permute-start.3 = (bf16[512,128]{1,0:T(8,128)(2,1)S(1)}, bf16[512,128]{1,0:T(8,128)(2,1)S(1)}, u32[]{:S(2)}, u32[]{:S(2)}) collective-permute-start(bf16[512,128]{1,0:T(8,128)(2,1)S(1)} %bitcast.147), channel_id=1, source_target_pairs={{0,384},{128,256},{256,128},{384,0},{1,385},{129,257},{257,129},{3... | collective-permute-start | bytes 393224 | tf_op jit(solution)/shard_map/ppermute | solution.py:46
  30.3 1.9 %collective-permute-start.1 = (bf16[1,144,128]{2,1,0:T(8,128)(2,1)S(1)}, bf16[1,144,128]{2,1,0:T(8,128)(2,1)S(1)}, u32[]{:S(2)}, u32[]{:S(2)}) collective-permute-start(bf16[1,144,128]{2,1,0:T(8,128)(2,1)S(1)} %maximum_bitcast_fusion), channel_id=1, source_target_pairs={{0,2},{2,0},{4,6},{6,4},{1,3},{3,1},{5,7},{7,5},{8,10},{10,8},{12,... | collective-permute-start | bytes 110600 | tf_op jit(solution)/shard_map/ppermute | solution.py:46
  32.2 4.4 %collective-permute-done.1 = bf16[1,144,128]{2,1,0:T(8,128)(2,1)S(1)} collective-permute-done((bf16[1,144,128]{2,1,0:T(8,128)(2,1)S(1)}, bf16[1,144,128]{2,1,0:T(8,128)(2,1)S(1)}, u32[]{:S(2)}, u32[]{:S(2)}) %collective-permute-start.1) | collective-permute-done | bytes 36896 | tf_op jit(solution)/shard_map/ppermute | solution.py:46
  36.6 1.9 %collective-permute-start.2 = (bf16[2,144,128]{2,1,0:T(8,128)(2,1)S(1)}, bf16[2,144,128]{2,1,0:T(8,128)(2,1)S(1)}, u32[]{:S(2)}, u32[]{:S(2)}) collective-permute-start(bf16[2,144,128]{2,1,0:T(8,128)(2,1)S(1)} %pad_maximum_fusion.13), channel_id=1, source_target_pairs={{0,4},{2,6},{4,0},{6,2},{1,5},{3,7},{5,1},{7,3},{8,12},{10,14},{12... | collective-permute-start | bytes 221192 | tf_op jit(solution)/shard_map/ppermute | solution.py:46
  38.6 2.0 %collective-permute-start.8 = (bf16[2,128,128]{2,1,0:T(8,128)(2,1)S(1)}, bf16[2,128,128]{2,1,0:T(8,128)(2,1)S(1)}, u32[]{:S(2)}, u32[]{:S(2)}) collective-permute-start(bf16[2,128,128]{2,1,0:T(8,128)(2,1)S(1)} %pad_maximum_fusion.14), channel_id=1, source_target_pairs={{0,64},{16,80},{32,96},{48,112},{64,0},{80,16},{96,32},{112,48},{1... | collective-permute-start | bytes 196616 | tf_op jit(solution)/shard_map/ppermute | solution.py:46
  40.6 3.3 %collective-permute-done.2 = bf16[2,144,128]{2,1,0:T(8,128)(2,1)S(1)} collective-permute-done((bf16[2,144,128]{2,1,0:T(8,128)(2,1)S(1)}, bf16[2,144,128]{2,1,0:T(8,128)(2,1)S(1)}, u32[]{:S(2)}, u32[]{:S(2)}) %collective-permute-start.2) | collective-permute-done | bytes 73760 | tf_op jit(solution)/shard_map/ppermute | solution.py:46
  44.0 0.1 copy.62
  44.1 0.1 copy.63
  44.3 3.3 %collective-permute-start.4 = (bf16[1088,128]{1,0:T(8,128)(2,1)S(1)}, bf16[1088,128]{1,0:T(8,128)(2,1)S(1)}, u32[]{:S(2)}, u32[]{:S(2)}) collective-permute-start(bf16[1088,128]{1,0:T(8,128)(2,1)S(1)} %pad_maximum_fusion.5), channel_id=1, source_target_pairs={{0,128},{128,0},{256,384},{384,256},{1,129},{129,1},{257,385},{385... | collective-permute-start | bytes 835592 | tf_op jit(solution)/shard_map/ppermute | solution.py:46
  47.6 1.2 collective-permute-done.8
  48.8 3.3 %collective-permute-start.9 = (bf16[2,2,128,128]{3,2,1,0:T(8,128)(2,1)S(1)}, bf16[2,2,128,128]{3,2,1,0:T(8,128)(2,1)S(1)}, u32[]{:S(2)}, u32[]{:S(2)}) collective-permute-start(bf16[2,2,128,128]{3,2,1,0:T(8,128)(2,1)S(1)} %pad_maximum_fusion.11), channel_id=1, source_target_pairs={{0,32},{16,48},{32,0},{48,16},{64,96},{80,112},{96,64},{112,80},{1... | collective-permute-start | bytes 393224 | tf_op jit(solution)/shard_map/ppermute | solution.py:46
  52.2 0.1 copy.71
  52.3 0.4 collective-permute-done.4
  52.8 5.6 %collective-permute-start.5 = (bf16[2,4,144,128]{3,2,1,0:T(8,128)(2,1)S(1)}, bf16[2,4,144,128]{3,2,1,0:T(8,128)(2,1)S(1)}, u32[]{:S(2)}, u32[]{:S(2)}) collective-permute-start(bf16[2,4,144,128]{3,2,1,0:T(8,128)(2,1)S(1)} %pad_maximum_fusion.4), channel_id=1, source_target_pairs={{0,384},{128,256},{256,128},{384,0},{1,385},{129,257},{257,129},{3... | collective-permute-start | bytes 884744 | tf_op jit(solution)/shard_map/ppermute | solution.py:46
  58.4 1.9 %collective-permute-start.10 = (bf16[2,2,2,128,128]{4,3,2,0,1:T(8,128)(2,1)S(1)}, bf16[2,2,2,128,128]{4,3,2,0,1:T(8,128)(2,1)S(1)}, u32[]{:S(2)}, u32[]{:S(2)}) collective-permute-start(bf16[2,2,2,128,128]{4,3,2,0,1:T(8,128)(2,1)S(1)} %pad_maximum_fusion.6), channel_id=1, source_target_pairs={{0,16},{16,0},{32,48},{48,32},{64,80},{80,64},{96,112},{112,96},{1... | collective-permute-start | bytes 786440 | tf_op jit(solution)/shard_map/ppermute | solution.py:46
  60.3 2.7 %collective-permute-done.5 = bf16[2,4,144,128]{3,2,1,0:T(8,128)(2,1)S(1)} collective-permute-done((bf16[2,4,144,128]{3,2,1,0:T(8,128)(2,1)S(1)}, bf16[2,4,144,128]{3,2,1,0:T(8,128)(2,1)S(1)}, u32[]{:S(2)}, u32[]{:S(2)}) %collective-permute-start.5) | collective-permute-done | bytes 294944 | tf_op jit(solution)/shard_map/ppermute | solution.py:46
  63.1 1.9 %collective-permute-start.6 = (bf16[4,4,144,128]{3,2,1,0:T(8,128)(2,1)S(1)}, bf16[4,4,144,128]{3,2,1,0:T(8,128)(2,1)S(1)}, u32[]{:S(2)}, u32[]{:S(2)}) collective-permute-start(bf16[4,4,144,128]{3,2,1,0:T(8,128)(2,1)S(1)} %get-tuple-element.12), channel_id=1, source_target_pairs={{0,1},{1,0},{2,3},{3,2},{4,5},{5,4},{6,7},{7,6},{8,9},{9,8},{10,11... | collective-permute-start | bytes 1769480 | tf_op jit(solution)/shard_map/ppermute | solution.py:46
  65.1 0.1 copy.70
  65.2 0.1 copy.72
  65.3 1.4 %collective-permute-done.10 = bf16[2,2,2,128,128]{4,3,2,0,1:T(8,128)(2,1)S(1)} collective-permute-done((bf16[2,2,2,128,128]{4,3,2,0,1:T(8,128)(2,1)S(1)}, bf16[2,2,2,128,128]{4,3,2,0,1:T(8,128)(2,1)S(1)}, u32[]{:S(2)}, u32[]{:S(2)}) %collective-permute-start.10) | collective-permute-done | bytes 262176 | tf_op jit(solution)/shard_map/ppermute | solution.py:46
  66.8 0.3 copy.64
  67.1 0.1 fusion.1
  67.3 0.7 convert_reduce_fusion
  68.1 0.2 fusion.10
  68.2 0.6 fusion
  69.0 0.9 pad_maximum_fusion.2
  69.8 5.6 %all-to-all-start = ((bf16[16,144,128]{2,1,0:T(8,128)(2,1)}), bf16[16,144,128]{2,1,0:T(8,128)(2,1)S(1)}, u32[]{:S(2)}, u32[]{:S(2)}) async-start(bf16[16,144,128]{2,1,0:T(8,128)(2,1)} %pad_maximum_fusion.2), calls=%async_computation | async-start | bytes 1179648 | tf_op jit(solution)/shard_map/all_to_all | solution.py:41
  75.4 0.1 copy.67
  75.5 5.2 %collective-permute-start.11 = (bf16[512,128]{1,0:T(8,128)(2,1)S(1)}, bf16[512,128]{1,0:T(8,128)(2,1)S(1)}, u32[]{:S(2)}, u32[]{:S(2)}) collective-permute-start(bf16[512,128]{1,0:T(8,128)(2,1)S(1)} %bitcast.151), channel_id=1, source_target_pairs={{0,384},{128,256},{256,128},{384,0},{1,385},{129,257},{257,129},{3... | collective-permute-start | bytes 393224 | tf_op jit(solution)/shard_map/ppermute | solution.py:46
  80.8 2.9 %collective-permute-done.11 = bf16[512,128]{1,0:T(8,128)(2,1)S(1)} collective-permute-done((bf16[512,128]{1,0:T(8,128)(2,1)S(1)}, bf16[512,128]{1,0:T(8,128)(2,1)S(1)}, u32[]{:S(2)}, u32[]{:S(2)}) %collective-permute-start.11) | collective-permute-done | bytes 131104 | tf_op jit(solution)/shard_map/ppermute | solution.py:46
  83.7 0.1 copy.90
  83.9 0.1 copy.69
  84.0 2.3 %collective-permute-start.12 = (bf16[512,128]{1,0:T(8,128)(2,1)S(1)}, bf16[512,128]{1,0:T(8,128)(2,1)S(1)}, u32[]{:S(2)}, u32[]{:S(2)}) collective-permute-start(bf16[512,128]{1,0:T(8,128)(2,1)S(1)} %bitcast.150), channel_id=1, source_target_pairs={{0,128},{128,0},{256,384},{384,256},{1,129},{129,1},{257,385},{385... | collective-permute-start | bytes 393224 | tf_op jit(solution)/shard_map/ppermute | solution.py:46
  86.3 0.1 copy.66
  86.5 4.4 %collective-permute-done.12 = bf16[512,128]{1,0:T(8,128)(2,1)S(1)} collective-permute-done((bf16[512,128]{1,0:T(8,128)(2,1)S(1)}, bf16[512,128]{1,0:T(8,128)(2,1)S(1)}, u32[]{:S(2)}, u32[]{:S(2)}) %collective-permute-start.12) | collective-permute-done | bytes 131104 | tf_op jit(solution)/shard_map/ppermute | solution.py:46
  91.1 0.2 fusion.4
  91.3 1.9 %collective-permute-start.13 = (f32[128]{0:T(128)S(1)}, f32[128]{0:T(128)S(1)}, u32[]{:S(2)}, u32[]{:S(2)}) collective-permute-start(f32[128]{0:T(128)S(1)} %fusion.4), channel_id=1, source_target_pairs={{0,1},{1,0},{2,3},{3,2},{4,5},{5,4},{6,7},{7,6},{8,9},{9,8},{10,11... | collective-permute-start | bytes 1544 | tf_op jit(solution)/shard_map/ppermute | solution.py:46
  93.2 1.1 collective-permute-done.13
  94.3 3.3 %collective-permute-start.14 = (f32[128]{0:T(128)S(1)}, f32[128]{0:T(128)S(1)}, u32[]{:S(2)}, u32[]{:S(2)}) collective-permute-start(f32[128]{0:T(128)S(1)} %add.56), channel_id=1, source_target_pairs={{0,2},{2,0},{4,6},{6,4},{1,3},{3,1},{5,7},{7,5},{8,10},{10,8},{12,... | collective-permute-start | bytes 1544 | tf_op jit(solution)/shard_map/ppermute | solution.py:46
  97.6 2.1 %collective-permute-done.14 = f32[128]{0:T(128)S(1)} collective-permute-done((f32[128]{0:T(128)S(1)}, f32[128]{0:T(128)S(1)}, u32[]{:S(2)}, u32[]{:S(2)}) %collective-permute-start.14) | collective-permute-done | bytes 544 | tf_op jit(solution)/shard_map/ppermute | solution.py:46
  99.8 4.9 %collective-permute-start.15 = (f32[128]{0:T(128)S(1)}, f32[128]{0:T(128)S(1)}, u32[]{:S(2)}, u32[]{:S(2)}) collective-permute-start(f32[128]{0:T(128)S(1)} %add.57), channel_id=1, source_target_pairs={{0,4},{2,6},{4,0},{6,2},{1,5},{3,7},{5,1},{7,3},{8,12},{10,14},{12... | collective-permute-start | bytes 1544 | tf_op jit(solution)/shard_map/ppermute | solution.py:46
  104.6 1.5 %collective-permute-done.15 = f32[128]{0:T(128)S(1)} collective-permute-done((f32[128]{0:T(128)S(1)}, f32[128]{0:T(128)S(1)}, u32[]{:S(2)}, u32[]{:S(2)}) %collective-permute-start.15) | collective-permute-done | bytes 544 | tf_op jit(solution)/shard_map/ppermute | solution.py:46
  106.2 4.1 %collective-permute-start.16 = (f32[128,128]{1,0:T(8,128)S(1)}, f32[128,128]{1,0:T(8,128)S(1)}, u32[]{:S(2)}, u32[]{:S(2)}) collective-permute-start(f32[128,128]{1,0:T(8,128)S(1)} %convert_reduce_fusion.1), channel_id=1, source_target_pairs={{0,0},{16,1},{32,2},{48,3},{64,4},{80,5},{96,6},{112,7},{8,8},{24,... | collective-permute-start | bytes 196616 | tf_op jit(solution)/shard_map/ppermute | solution.py:129
  110.4 0.6 broadcast_in_dim.11
  111.0 6.2 %all-to-all-start.1 = ((f32[4,2,128]{2,1,0:T(2,128)}), f32[4,2,128]{2,1,0:T(2,128)S(1)}, u32[]{:S(2)}, u32[]{:S(2)}) async-start(f32[4,2,128]{2,1,0:T(2,128)} %broadcast_in_dim.11), calls=%async_computation.1 | async-start | bytes 8192 | tf_op jit(solution)/shard_map/all_to_all | solution.py:41
  117.2 1.0 fusion.8
  118.1 4.3 %all-to-all-done.1 = f32[4,2,128]{2,1,0:T(2,128)S(1)} async-done(((f32[4,2,128]{2,1,0:T(2,128)}), f32[4,2,128]{2,1,0:T(2,128)S(1)}, u32[]{:S(2)}, u32[]{:S(2)}) %all-to-all-start.1) | async-done | bytes 4128 | tf_op jit(solution)/shard_map/all_to_all | solution.py:41
  122.5 0.6 copy.111
  123.1 0.6 copy.112
  (84 shorter events, 1.4 us)
Async XLA Ops:
  0.6 7.8 %copy-start.2 = (bf16[128,128]{1,0:T(8,128)(2,1)S(1)}, bf16[128,128]{1,0:T(8,128)(2,1)}, u32[]{:S(2)}) copy-start(bf16[128,128]{1,0:T(8,128)(2,1)} %param.7) | copy-start | bytes 98308
  0.6 11.1 %collective-permute-start = (bf16[128,128]{1,0:T(8,128)(2,1)}, bf16[128,128]{1,0:T(8,128)(2,1)S(1)}, u32[]{:S(2)}, u32[]{:S(2)}) collective-permute-start(bf16[128,128]{1,0:T(8,128)(2,1)} %param.8), channel_id=1, source_target_pairs={{0,0},{1,16},{2,32},{3,48},{4,64},{5,80},{6,96},{7,112},{8,8},{9,2... | collective-permute-start | bytes 98312 | tf_op jit(solution)/shard_map/ppermute | solution.py:67
  11.7 20.5 %collective-permute-start.7 = (bf16[128,128]{1,0:T(8,128)(2,1)S(1)}, bf16[128,128]{1,0:T(8,128)(2,1)S(1)}, u32[]{:S(2)}, u32[]{:S(2)}) collective-permute-start(bf16[128,128]{1,0:T(8,128)(2,1)S(1)} %collective-permute-done), channel_id=1, source_target_pairs={{0,8},{8,0},{1,9},{9,1},{2,10},{10,2},{3,11},{11,3},{4,12},{12,4},... | collective-permute-start | bytes 98312 | tf_op jit(solution)/shard_map/ppermute | solution.py:46
  22.5 21.4 %collective-permute-start.3 = (bf16[512,128]{1,0:T(8,128)(2,1)S(1)}, bf16[512,128]{1,0:T(8,128)(2,1)S(1)}, u32[]{:S(2)}, u32[]{:S(2)}) collective-permute-start(bf16[512,128]{1,0:T(8,128)(2,1)S(1)} %bitcast.147), channel_id=1, source_target_pairs={{0,384},{128,256},{256,128},{384,0},{1,385},{129,257},{257,129},{3... | collective-permute-start | bytes 393224 | tf_op jit(solution)/shard_map/ppermute | solution.py:46
  30.3 6.4 %collective-permute-start.1 = (bf16[1,144,128]{2,1,0:T(8,128)(2,1)S(1)}, bf16[1,144,128]{2,1,0:T(8,128)(2,1)S(1)}, u32[]{:S(2)}, u32[]{:S(2)}) collective-permute-start(bf16[1,144,128]{2,1,0:T(8,128)(2,1)S(1)} %maximum_bitcast_fusion), channel_id=1, source_target_pairs={{0,2},{2,0},{4,6},{6,4},{1,3},{3,1},{5,7},{7,5},{8,10},{10,8},{12,... | collective-permute-start | bytes 110600 | tf_op jit(solution)/shard_map/ppermute | solution.py:46
  36.6 7.2 %collective-permute-start.2 = (bf16[2,144,128]{2,1,0:T(8,128)(2,1)S(1)}, bf16[2,144,128]{2,1,0:T(8,128)(2,1)S(1)}, u32[]{:S(2)}, u32[]{:S(2)}) collective-permute-start(bf16[2,144,128]{2,1,0:T(8,128)(2,1)S(1)} %pad_maximum_fusion.13), channel_id=1, source_target_pairs={{0,4},{2,6},{4,0},{6,2},{1,5},{3,7},{5,1},{7,3},{8,12},{10,14},{12... | collective-permute-start | bytes 221192 | tf_op jit(solution)/shard_map/ppermute | solution.py:46
  38.6 10.2 %collective-permute-start.8 = (bf16[2,128,128]{2,1,0:T(8,128)(2,1)S(1)}, bf16[2,128,128]{2,1,0:T(8,128)(2,1)S(1)}, u32[]{:S(2)}, u32[]{:S(2)}) collective-permute-start(bf16[2,128,128]{2,1,0:T(8,128)(2,1)S(1)} %pad_maximum_fusion.14), channel_id=1, source_target_pairs={{0,64},{16,80},{32,96},{48,112},{64,0},{80,16},{96,32},{112,48},{1... | collective-permute-start | bytes 196616 | tf_op jit(solution)/shard_map/ppermute | solution.py:46
  43.9 8.2 %copy-start.3 = (f32[1024]{0:T(1024)S(1)}, f32[1024]{0:T(1024)}, u32[]{:S(2)}) copy-start(f32[1024]{0:T(1024)} %param.9) | copy-start | bytes 12292
  44.3 8.4 %collective-permute-start.4 = (bf16[1088,128]{1,0:T(8,128)(2,1)S(1)}, bf16[1088,128]{1,0:T(8,128)(2,1)S(1)}, u32[]{:S(2)}, u32[]{:S(2)}) collective-permute-start(bf16[1088,128]{1,0:T(8,128)(2,1)S(1)} %pad_maximum_fusion.5), channel_id=1, source_target_pairs={{0,128},{128,0},{256,384},{384,256},{1,129},{129,1},{257,385},{385... | collective-permute-start | bytes 835592 | tf_op jit(solution)/shard_map/ppermute | solution.py:46
  48.8 9.5 %collective-permute-start.9 = (bf16[2,2,128,128]{3,2,1,0:T(8,128)(2,1)S(1)}, bf16[2,2,128,128]{3,2,1,0:T(8,128)(2,1)S(1)}, u32[]{:S(2)}, u32[]{:S(2)}) collective-permute-start(bf16[2,2,128,128]{3,2,1,0:T(8,128)(2,1)S(1)} %pad_maximum_fusion.11), channel_id=1, source_target_pairs={{0,32},{16,48},{32,0},{48,16},{64,96},{80,112},{96,64},{112,80},{1... | collective-permute-start | bytes 393224 | tf_op jit(solution)/shard_map/ppermute | solution.py:46
  52.8 10.2 %collective-permute-start.5 = (bf16[2,4,144,128]{3,2,1,0:T(8,128)(2,1)S(1)}, bf16[2,4,144,128]{3,2,1,0:T(8,128)(2,1)S(1)}, u32[]{:S(2)}, u32[]{:S(2)}) collective-permute-start(bf16[2,4,144,128]{3,2,1,0:T(8,128)(2,1)S(1)} %pad_maximum_fusion.4), channel_id=1, source_target_pairs={{0,384},{128,256},{256,128},{384,0},{1,385},{129,257},{257,129},{3... | collective-permute-start | bytes 884744 | tf_op jit(solution)/shard_map/ppermute | solution.py:46
  58.4 8.3 %collective-permute-start.10 = (bf16[2,2,2,128,128]{4,3,2,0,1:T(8,128)(2,1)S(1)}, bf16[2,2,2,128,128]{4,3,2,0,1:T(8,128)(2,1)S(1)}, u32[]{:S(2)}, u32[]{:S(2)}) collective-permute-start(bf16[2,2,2,128,128]{4,3,2,0,1:T(8,128)(2,1)S(1)} %pad_maximum_fusion.6), channel_id=1, source_target_pairs={{0,16},{16,0},{32,48},{48,32},{64,80},{80,64},{96,112},{112,96},{1... | collective-permute-start | bytes 786440 | tf_op jit(solution)/shard_map/ppermute | solution.py:46
  63.1 4.0 %collective-permute-start.6 = (bf16[4,4,144,128]{3,2,1,0:T(8,128)(2,1)S(1)}, bf16[4,4,144,128]{3,2,1,0:T(8,128)(2,1)S(1)}, u32[]{:S(2)}, u32[]{:S(2)}) collective-permute-start(bf16[4,4,144,128]{3,2,1,0:T(8,128)(2,1)S(1)} %get-tuple-element.12), channel_id=1, source_target_pairs={{0,1},{1,0},{2,3},{3,2},{4,5},{5,4},{6,7},{7,6},{8,9},{9,8},{10,11... | collective-permute-start | bytes 1769480 | tf_op jit(solution)/shard_map/ppermute | solution.py:46
  69.8 36.3 %all-to-all-start = ((bf16[16,144,128]{2,1,0:T(8,128)(2,1)}), bf16[16,144,128]{2,1,0:T(8,128)(2,1)S(1)}, u32[]{:S(2)}, u32[]{:S(2)}) async-start(bf16[16,144,128]{2,1,0:T(8,128)(2,1)} %pad_maximum_fusion.2), calls=%async_computation | async-start | bytes 1179648 | tf_op jit(solution)/shard_map/all_to_all | solution.py:41
  75.5 8.1 %collective-permute-start.11 = (bf16[512,128]{1,0:T(8,128)(2,1)S(1)}, bf16[512,128]{1,0:T(8,128)(2,1)S(1)}, u32[]{:S(2)}, u32[]{:S(2)}) collective-permute-start(bf16[512,128]{1,0:T(8,128)(2,1)S(1)} %bitcast.151), channel_id=1, source_target_pairs={{0,384},{128,256},{256,128},{384,0},{1,385},{129,257},{257,129},{3... | collective-permute-start | bytes 393224 | tf_op jit(solution)/shard_map/ppermute | solution.py:46
  83.8 7.3 %copy-start = (bf16[128,1024]{1,0:T(8,128)(2,1)S(1)}, bf16[128,1024]{1,0:T(8,128)(2,1)}, u32[]{:S(2)}) copy-start(bf16[128,1024]{1,0:T(8,128)(2,1)} %param.5) | copy-start | bytes 786436
  84.0 6.9 %collective-permute-start.12 = (bf16[512,128]{1,0:T(8,128)(2,1)S(1)}, bf16[512,128]{1,0:T(8,128)(2,1)S(1)}, u32[]{:S(2)}, u32[]{:S(2)}) collective-permute-start(bf16[512,128]{1,0:T(8,128)(2,1)S(1)} %bitcast.150), channel_id=1, source_target_pairs={{0,128},{128,0},{256,384},{384,256},{1,129},{129,1},{257,385},{385... | collective-permute-start | bytes 393224 | tf_op jit(solution)/shard_map/ppermute | solution.py:46
  90.9 26.3 %copy-start.1 = (bf16[128,1024]{1,0:T(8,128)(2,1)S(1)}, bf16[128,1024]{1,0:T(8,128)(2,1)}, u32[]{:S(2)}) copy-start(bf16[128,1024]{1,0:T(8,128)(2,1)} %param.6) | copy-start | bytes 786436
  91.3 3.0 %collective-permute-start.13 = (f32[128]{0:T(128)S(1)}, f32[128]{0:T(128)S(1)}, u32[]{:S(2)}, u32[]{:S(2)}) collective-permute-start(f32[128]{0:T(128)S(1)} %fusion.4), channel_id=1, source_target_pairs={{0,1},{1,0},{2,3},{3,2},{4,5},{5,4},{6,7},{7,6},{8,9},{9,8},{10,11... | collective-permute-start | bytes 1544 | tf_op jit(solution)/shard_map/ppermute | solution.py:46
  94.3 5.4 %collective-permute-start.14 = (f32[128]{0:T(128)S(1)}, f32[128]{0:T(128)S(1)}, u32[]{:S(2)}, u32[]{:S(2)}) collective-permute-start(f32[128]{0:T(128)S(1)} %add.56), channel_id=1, source_target_pairs={{0,2},{2,0},{4,6},{6,4},{1,3},{3,1},{5,7},{7,5},{8,10},{10,8},{12,... | collective-permute-start | bytes 1544 | tf_op jit(solution)/shard_map/ppermute | solution.py:46
  99.8 6.4 %collective-permute-start.15 = (f32[128]{0:T(128)S(1)}, f32[128]{0:T(128)S(1)}, u32[]{:S(2)}, u32[]{:S(2)}) collective-permute-start(f32[128]{0:T(128)S(1)} %add.57), channel_id=1, source_target_pairs={{0,4},{2,6},{4,0},{6,2},{1,5},{3,7},{5,1},{7,3},{8,12},{10,14},{12... | collective-permute-start | bytes 1544 | tf_op jit(solution)/shard_map/ppermute | solution.py:46
  106.2 16.2 %collective-permute-start.16 = (f32[128,128]{1,0:T(8,128)S(1)}, f32[128,128]{1,0:T(8,128)S(1)}, u32[]{:S(2)}, u32[]{:S(2)}) collective-permute-start(f32[128,128]{1,0:T(8,128)S(1)} %convert_reduce_fusion.1), channel_id=1, source_target_pairs={{0,0},{16,1},{32,2},{48,3},{64,4},{80,5},{96,6},{112,7},{8,8},{24,... | collective-permute-start | bytes 196616 | tf_op jit(solution)/shard_map/ppermute | solution.py:129
  111.0 11.5 %all-to-all-start.1 = ((f32[4,2,128]{2,1,0:T(2,128)}), f32[4,2,128]{2,1,0:T(2,128)S(1)}, u32[]{:S(2)}, u32[]{:S(2)}) async-start(f32[4,2,128]{2,1,0:T(2,128)} %broadcast_in_dim.11), calls=%async_computation.1 | async-start | bytes 8192 | tf_op jit(solution)/shard_map/all_to_all | solution.py:41

commit v9 on v8

--- a/solution.py
+++ b/solution.py
@@ -51,6 +51,11 @@
     second = lax.reduce_precision(value - first, 8, 7)
     third = value - first - second
     return jnp.stack([first, second, third]).astype(jnp.bfloat16)
+
+
+def whole_of(terms):
+    first, second, third = terms.astype(jnp.float32).reshape(3, 2, HD)
+    return first + second + third
 
 
 def rope_tables(positions_count, head_size):
@@ -118,22 +123,35 @@
         preferred_element_type=jnp.float32,
     ).astype(jnp.bfloat16)
     norm_grad = jnp.sum(products.astype(jnp.float32), axis=0)
-    gain_part = terms_of(jnp.sum(norm_grad * normal, axis=1)).reshape(6, HD)
+    gain_sum = jnp.sum(norm_grad * normal, axis=1)
 
-    pieces = jnp.einsum(
-        "ktc,btf->kbcf", kv, normed, preferred_element_type=jnp.float32
-    ).astype(jnp.bfloat16)
-    gain_rows = jnp.broadcast_to(jnp.pad(gain_part, ((0, 10), (0, 0)))[None], (16, 16, HD))
-    arrived = exchange(jnp.concatenate([pieces.reshape(16, HD, HD), gain_rows], axis=1), ROW)
-    block = jnp.sum(arrived[:, :HD].astype(jnp.float32), axis=0)
+    back = norm_grad.astype(jnp.bfloat16)
+    near = swap(back[:, 2 * TOK :].reshape(4 * TOK, HD), "x", 3)
+
+    sums = jnp.einsum("ktc,btf->kbcf", kv, normed, preferred_element_type=jnp.float32)
+    sums = sums.reshape(2, 2, 2, 2, HD, HD)
+    for mask, place in ((1, 2), (2, 1), (4, 0)):
+        first = (lax.axis_index("y") & mask) == 0
+        low, high = (lax.index_in_dim(sums, i, place, keepdims=False) for i in range(2))
+        given = jnp.where(first, high, low).astype(jnp.bfloat16).reshape(-1, HD)
+        terms = terms_of(gain_sum).reshape(6, HD)
+        came = swap(jnp.concatenate([given, jnp.pad(terms, ((0, 10), (0, 0)))]), "y", mask)
+        if mask == 1:
+            near, came = lax.optimization_barrier((near, came))
+        kept = jnp.where(first, low, high)
+        sums = kept + came[:-16].astype(jnp.float32).reshape(kept.shape)
+        gain_sum = whole_of(terms) + whole_of(came[-16:-10])
+    first = lax.axis_index("zh") == 0
+    given = jnp.where(first, sums[1], sums[0])
+    came = swap(jnp.concatenate([given, jnp.pad(gain_sum, ((0, 6), (0, 0)))]), "zh", 1)
+    block = jnp.where(first, sums[0], sums[1]) + came[:HD]
+    gain_sum = gain_sum + came[HD : HD + 2]
     weight_grad = lax.ppermute(block, AXES, [(b, a) for a, b in moves])
-    gains = jnp.sum(arrived[:, HD : HD + 6].astype(jnp.float32), axis=0)
-    gains = jnp.sum(gains.reshape(3, 2, HD), axis=0)
-    gains = exchange(jnp.broadcast_to(gains[None], (4, 2, HD)), "x")
+    gain_sum, block = lax.optimization_barrier((gain_sum, block))
+    gains = exchange(jnp.broadcast_to(gain_sum[None], (4, 2, HD)), "x")
     gain_grad = gains.reshape(4 * QUARTER)
 
-    back = norm_grad.astype(jnp.bfloat16)
-    near = swap(back[:, 2 * TOK :].reshape(4 * TOK, HD), "x", 3).reshape(2, 2 * TOK, HD)
+    near = near.reshape(2, 2 * TOK, HD)
     given = jnp.concatenate([back[:, TOK : 2 * TOK], near[:, TOK:]]).reshape(4 * TOK, HD)
     far = swap(given, "x", 1).reshape(2, 2, TOK, HD)
 

time: 125 us -> 143 us (1.14)
  the two profiles are of different devices: /device:TPU:48 before, /device:TPU:6 now
where the time goes in v9:
time: 143 us; the launch traced here: 140 us
  starting transfers between devices  83.4 us (58%)
  waiting for transfers between devices  42.5 us (30%)
  local copies, waits for them, and re-layouts  6.7 us (5%)
  other arithmetic  4.59 us (3%)
  between operations  1.69 us (1%)
    ppermute x19, starting transfers between devices, swap(): return lax.ppermute(value, axis, [(i, i ^ mask) for i in range(count)])  63.4 us
    ppermute x19, waiting for transfers between devices, swap(): return lax.ppermute(value, axis, [(i, i ^ mask) for i in range(count)])  39.2 us
    ppermute x1, starting transfers between devices, shards(): moved = lax.ppermute(kv_weight, AXES, moves)  11.5 us
    all_to_all x1, starting transfers between devices, exchange(): return lax.all_to_all(value, axes, split_axis=0, concat_axis=0, tiled=True)  4.5 us
    ppermute x1, starting transfers between devices, shards(): weight_grad = lax.ppermute(block, AXES, [(b, a) for a, b in moves])  4.07 us
  transfers between devices with their start and end apart: 22, of which 14 were waited for; matrix products, arithmetic and copies ran while one was open for 6% of the time, Pallas kernels for 0%

profile of v9, /device:TPU:6, one launch (start us, length us, event | category | flops | bytes accessed | tf_op | source)
XLA Modules:
  0.0 140.2 jit_solution(10388285716820762335)
XLA Ops:
  0.6 11.5 %collective-permute-start = (bf16[128,128]{1,0:T(8,128)(2,1)}, bf16[128,128]{1,0:T(8,128)(2,1)S(1)}, u32[]{:S(2)}, u32[]{:S(2)}) collective-permute-start(bf16[128,128]{1,0:T(8,128)(2,1)} %param.8), channel_id=1, source_target_pairs={{0,0},{1,16},{2,32},{3,48},{4,64},{5,80},{6,96},{7,112},{8,8},{9,2... | collective-permute-start | bytes 98312 | tf_op jit(solution)/shard_map/ppermute | solution.py:72
  12.2 1.1 fusion.9
  13.3 0.9 fusion.45
  14.2 0.8 convert_element_type.105
  15.1 0.1 copy.70
  15.2 0.1 copy.69
  15.3 0.1 copy.68
  15.5 0.1 copy.67
  15.6 0.1 copy.66
  15.7 0.1 copy.65
  15.8 0.1 copy.64
  16.0 0.3 multiply_add_fusion
  16.6 8.2 %collective-permute-start.7 = (bf16[128,128]{1,0:T(8,128)(2,1)S(1)}, bf16[128,128]{1,0:T(8,128)(2,1)S(1)}, u32[]{:S(2)}, u32[]{:S(2)}) collective-permute-start(bf16[128,128]{1,0:T(8,128)(2,1)S(1)} %collective-permute-done), channel_id=1, source_target_pairs={{0,8},{8,0},{1,9},{9,1},{2,10},{10,2},{3,11},{11,3},{4,12},{12,4},... | collective-permute-start | bytes 98312 | tf_op jit(solution)/shard_map/ppermute | solution.py:46
  24.8 0.1 copy.42
  24.9 1.9 %collective-permute-start.3 = (bf16[512,128]{1,0:T(8,128)(2,1)S(1)}, bf16[512,128]{1,0:T(8,128)(2,1)S(1)}, u32[]{:S(2)}, u32[]{:S(2)}) collective-permute-start(bf16[512,128]{1,0:T(8,128)(2,1)S(1)} %bitcast.186), channel_id=1, source_target_pairs={{0,384},{128,256},{256,128},{384,0},{1,385},{129,257},{257,129},{3... | collective-permute-start | bytes 393224 | tf_op jit(solution)/shard_map/ppermute | solution.py:46
  26.9 4.0 %collective-permute-start.1 = (bf16[1,144,128]{2,1,0:T(8,128)(2,1)S(1)}, bf16[1,144,128]{2,1,0:T(8,128)(2,1)S(1)}, u32[]{:S(2)}, u32[]{:S(2)}) collective-permute-start(bf16[1,144,128]{2,1,0:T(8,128)(2,1)S(1)} %maximum_bitcast_fusion), channel_id=1, source_target_pairs={{0,2},{2,0},{4,6},{6,4},{1,3},{3,1},{5,7},{7,5},{8,10},{10,8},{12,... | collective-permute-start | bytes 110600 | tf_op jit(solution)/shard_map/ppermute | solution.py:46
  31.0 1.9 %collective-permute-done.1 = bf16[1,144,128]{2,1,0:T(8,128)(2,1)S(1)} collective-permute-done((bf16[1,144,128]{2,1,0:T(8,128)(2,1)S(1)}, bf16[1,144,128]{2,1,0:T(8,128)(2,1)S(1)}, u32[]{:S(2)}, u32[]{:S(2)}) %collective-permute-start.1) | collective-permute-done | bytes 36896 | tf_op jit(solution)/shard_map/ppermute | solution.py:46
  32.9 3.5 %collective-permute-start.2 = (bf16[2,144,128]{2,1,0:T(8,128)(2,1)S(1)}, bf16[2,144,128]{2,1,0:T(8,128)(2,1)S(1)}, u32[]{:S(2)}, u32[]{:S(2)}) collective-permute-start(bf16[2,144,128]{2,1,0:T(8,128)(2,1)S(1)} %pad_maximum_fusion.12), channel_id=1, source_target_pairs={{0,4},{2,6},{4,0},{6,2},{1,5},{3,7},{5,1},{7,3},{8,12},{10,14},{12... | collective-permute-start | bytes 221192 | tf_op jit(solution)/shard_map/ppermute | solution.py:46
  36.4 10.0 %collective-permute-start.8 = (bf16[2,128,128]{2,1,0:T(8,128)(2,1)S(1)}, bf16[2,128,128]{2,1,0:T(8,128)(2,1)S(1)}, u32[]{:S(2)}, u32[]{:S(2)}) collective-permute-start(bf16[2,128,128]{2,1,0:T(8,128)(2,1)S(1)} %pad_maximum_fusion.13), channel_id=1, source_target_pairs={{0,64},{16,80},{32,96},{48,112},{64,0},{80,16},{96,32},{112,48},{1... | collective-permute-start | bytes 196616 | tf_op jit(solution)/shard_map/ppermute | solution.py:46
  46.5 0.1 copy.43
  46.7 0.1 copy.44
  46.8 1.9 %collective-permute-start.4 = (bf16[1088,128]{1,0:T(8,128)(2,1)S(1)}, bf16[1088,128]{1,0:T(8,128)(2,1)S(1)}, u32[]{:S(2)}, u32[]{:S(2)}) collective-permute-start(bf16[1088,128]{1,0:T(8,128)(2,1)S(1)} %pad_maximum_fusion.4), channel_id=1, source_target_pairs={{0,128},{128,0},{256,384},{384,256},{1,129},{129,1},{257,385},{385... | collective-permute-start | bytes 835592 | tf_op jit(solution)/shard_map/ppermute | solution.py:46
  48.8 3.1 %collective-permute-start.9 = (bf16[2,2,128,128]{3,2,1,0:T(8,128)(2,1)S(1)}, bf16[2,2,128,128]{3,2,1,0:T(8,128)(2,1)S(1)}, u32[]{:S(2)}, u32[]{:S(2)}) collective-permute-start(bf16[2,2,128,128]{3,2,1,0:T(8,128)(2,1)S(1)} %pad_maximum_fusion.10), channel_id=1, source_target_pairs={{0,32},{16,48},{32,0},{48,16},{64,96},{80,112},{96,64},{112,80},{1... | collective-permute-start | bytes 393224 | tf_op jit(solution)/shard_map/ppermute | solution.py:46
  52.1 3.2 %collective-permute-done.4 = bf16[1088,128]{1,0:T(8,128)(2,1)S(1)} collective-permute-done((bf16[1088,128]{1,0:T(8,128)(2,1)S(1)}, bf16[1088,128]{1,0:T(8,128)(2,1)S(1)}, u32[]{:S(2)}, u32[]{:S(2)}) %collective-permute-start.4) | collective-permute-done | bytes 278560 | tf_op jit(solution)/shard_map/ppermute | solution.py:46
  55.3 1.9 %collective-permute-start.5 = (bf16[2,4,144,128]{3,2,1,0:T(8,128)(2,1)S(1)}, bf16[2,4,144,128]{3,2,1,0:T(8,128)(2,1)S(1)}, u32[]{:S(2)}, u32[]{:S(2)}) collective-permute-start(bf16[2,4,144,128]{3,2,1,0:T(8,128)(2,1)S(1)} %pad_maximum_fusion.3), channel_id=1, source_target_pairs={{0,384},{128,256},{256,128},{384,0},{1,385},{129,257},{257,129},{3... | collective-permute-start | bytes 884744 | tf_op jit(solution)/shard_map/ppermute | solution.py:46
  57.3 0.4 collective-permute-done.9
  57.7 1.9 %collective-permute-start.10 = (bf16[2,2,2,128,128]{4,3,2,0,1:T(8,128)(2,1)S(1)}, bf16[2,2,2,128,128]{4,3,2,0,1:T(8,128)(2,1)S(1)}, u32[]{:S(2)}, u32[]{:S(2)}) collective-permute-start(bf16[2,2,2,128,128]{4,3,2,0,1:T(8,128)(2,1)S(1)} %pad_maximum_fusion.5), channel_id=1, source_target_pairs={{0,16},{16,0},{32,48},{48,32},{64,80},{80,64},{96,112},{112,96},{1... | collective-permute-start | bytes 786440 | tf_op jit(solution)/shard_map/ppermute | solution.py:46
  59.7 5.5 %collective-permute-done.5 = bf16[2,4,144,128]{3,2,1,0:T(8,128)(2,1)S(1)} collective-permute-done((bf16[2,4,144,128]{3,2,1,0:T(8,128)(2,1)S(1)}, bf16[2,4,144,128]{3,2,1,0:T(8,128)(2,1)S(1)}, u32[]{:S(2)}, u32[]{:S(2)}) %collective-permute-start.5) | collective-permute-done | bytes 294944 | tf_op jit(solution)/shard_map/ppermute | solution.py:46
  65.3 1.9 %collective-permute-start.6 = (bf16[4,4,144,128]{3,2,1,0:T(8,128)(2,1)S(1)}, bf16[4,4,144,128]{3,2,1,0:T(8,128)(2,1)S(1)}, u32[]{:S(2)}, u32[]{:S(2)}) collective-permute-start(bf16[4,4,144,128]{3,2,1,0:T(8,128)(2,1)S(1)} %get-tuple-element.24), channel_id=1, source_target_pairs={{0,1},{1,0},{2,3},{3,2},{4,5},{5,4},{6,7},{7,6},{8,9},{9,8},{10,11... | collective-permute-start | bytes 1769480 | tf_op jit(solution)/shard_map/ppermute | solution.py:46
  67.3 0.1 copy.51
  67.6 0.3 copy.45
  67.9 1.3 collective-permute-done.6
  69.4 0.7 convert_reduce_fusion
  70.2 0.2 fusion.10
  70.3 0.6 fusion.14
  71.1 0.8 slice-done
  71.9 0.1 copy.48
  72.0 2.0 %collective-permute-start.11 = (bf16[512,128]{1,0:T(8,128)(2,1)S(1)}, bf16[512,128]{1,0:T(8,128)(2,1)S(1)}, u32[]{:S(2)}, u32[]{:S(2)}) collective-permute-start(bf16[512,128]{1,0:T(8,128)(2,1)S(1)} %bitcast.187), channel_id=1, source_target_pairs={{0,384},{128,256},{256,128},{384,0},{1,385},{129,257},{257,129},{3... | collective-permute-start | bytes 393224 | tf_op jit(solution)/shard_map/ppermute | solution.py:46
  74.1 1.9 %collective-permute-start.12 = (bf16[1040,128]{1,0:T(8,128)(2,1)S(1)}, bf16[1040,128]{1,0:T(8,128)(2,1)S(1)}, u32[]{:S(2)}, u32[]{:S(2)}) collective-permute-start(bf16[1040,128]{1,0:T(8,128)(2,1)S(1)} %fusion.12), channel_id=1, source_target_pairs={{0,16},{16,0},{32,48},{48,32},{64,80},{80,64},{96,112},{112,96},{1... | collective-permute-start | bytes 798728 | tf_op jit(solution)/shard_map/ppermute | solution.py:46
  76.0 0.1 copy.47
  76.2 4.4 %collective-permute-done.11 = bf16[512,128]{1,0:T(8,128)(2,1)S(1)} collective-permute-done((bf16[512,128]{1,0:T(8,128)(2,1)S(1)}, bf16[512,128]{1,0:T(8,128)(2,1)S(1)}, u32[]{:S(2)}, u32[]{:S(2)}) %collective-permute-start.11) | collective-permute-done | bytes 131104 | tf_op jit(solution)/shard_map/ppermute | solution.py:46
  80.7 3.7 %collective-permute-done.12 = bf16[1040,128]{1,0:T(8,128)(2,1)S(1)} collective-permute-done((bf16[1040,128]{1,0:T(8,128)(2,1)S(1)}, bf16[1040,128]{1,0:T(8,128)(2,1)S(1)}, u32[]{:S(2)}, u32[]{:S(2)}) %collective-permute-start.12) | collective-permute-done | bytes 266272 | tf_op jit(solution)/shard_map/ppermute | solution.py:46
  84.7 0.1 copy.57
  84.8 1.9 %collective-permute-start.13 = (bf16[512,128]{1,0:T(8,128)(2,1)S(1)}, bf16[512,128]{1,0:T(8,128)(2,1)S(1)}, u32[]{:S(2)}, u32[]{:S(2)}) collective-permute-start(bf16[512,128]{1,0:T(8,128)(2,1)S(1)} %bitcast.188), channel_id=1, source_target_pairs={{0,128},{128,0},{256,384},{384,256},{1,129},{129,1},{257,385},{385... | collective-permute-start | bytes 393224 | tf_op jit(solution)/shard_map/ppermute | solution.py:46
  86.8 3.0 %collective-permute-start.17 = (bf16[528,128]{1,0:T(8,128)(2,1)S(1)}, bf16[528,128]{1,0:T(8,128)(2,1)S(1)}, u32[]{:S(2)}, u32[]{:S(2)}) collective-permute-start(bf16[528,128]{1,0:T(8,128)(2,1)S(1)} %fusion.19), channel_id=1, source_target_pairs={{0,32},{16,48},{32,0},{48,16},{64,96},{80,112},{96,64},{112,80},{1... | collective-permute-start | bytes 405512 | tf_op jit(solution)/shard_map/ppermute | solution.py:46
  89.8 1.9 %collective-permute-done.13 = bf16[512,128]{1,0:T(8,128)(2,1)S(1)} collective-permute-done((bf16[512,128]{1,0:T(8,128)(2,1)S(1)}, bf16[512,128]{1,0:T(8,128)(2,1)S(1)}, u32[]{:S(2)}, u32[]{:S(2)}) %collective-permute-start.13) | collective-permute-done | bytes 131104 | tf_op jit(solution)/shard_map/ppermute | solution.py:46
  91.9 5.3 %collective-permute-done.17 = bf16[528,128]{1,0:T(8,128)(2,1)S(1)} collective-permute-done((bf16[528,128]{1,0:T(8,128)(2,1)S(1)}, bf16[528,128]{1,0:T(8,128)(2,1)S(1)}, u32[]{:S(2)}, u32[]{:S(2)}) %collective-permute-start.17) | collective-permute-done | bytes 135200 | tf_op jit(solution)/shard_map/ppermute | solution.py:46
  97.4 4.5 %collective-permute-start.18 = (bf16[272,128]{1,0:T(8,128)(2,1)S(1)}, bf16[272,128]{1,0:T(8,128)(2,1)S(1)}, u32[]{:S(2)}, u32[]{:S(2)}) collective-permute-start(bf16[272,128]{1,0:T(8,128)(2,1)S(1)} %fusion.20), channel_id=1, source_target_pairs={{0,64},{16,80},{32,96},{48,112},{64,0},{80,16},{96,32},{112,48},{1... | collective-permute-start | bytes 208904 | tf_op jit(solution)/shard_map/ppermute | solution.py:46
  101.9 0.2 fusion.4
  102.1 1.9 %collective-permute-start.14 = (f32[128]{0:T(128)S(1)}, f32[128]{0:T(128)S(1)}, u32[]{:S(2)}, u32[]{:S(2)}) collective-permute-start(f32[128]{0:T(128)S(1)} %fusion.4), channel_id=1, source_target_pairs={{0,1},{1,0},{2,3},{3,2},{4,5},{5,4},{6,7},{7,6},{8,9},{9,8},{10,11... | collective-permute-start | bytes 1544 | tf_op jit(solution)/shard_map/ppermute | solution.py:46
  104.0 1.1 collective-permute-done.14
  105.1 3.0 %collective-permute-start.15 = (f32[128]{0:T(128)S(1)}, f32[128]{0:T(128)S(1)}, u32[]{:S(2)}, u32[]{:S(2)}) collective-permute-start(f32[128]{0:T(128)S(1)} %add.163), channel_id=1, source_target_pairs={{0,2},{2,0},{4,6},{6,4},{1,3},{3,1},{5,7},{7,5},{8,10},{10,8},{12,... | collective-permute-start | bytes 1544 | tf_op jit(solution)/shard_map/ppermute | solution.py:46
  108.1 2.5 %collective-permute-done.15 = f32[128]{0:T(128)S(1)} collective-permute-done((f32[128]{0:T(128)S(1)}, f32[128]{0:T(128)S(1)}, u32[]{:S(2)}, u32[]{:S(2)}) %collective-permute-start.15) | collective-permute-done | bytes 544 | tf_op jit(solution)/shard_map/ppermute | solution.py:46
  110.5 4.8 %collective-permute-start.16 = (f32[128]{0:T(128)S(1)}, f32[128]{0:T(128)S(1)}, u32[]{:S(2)}, u32[]{:S(2)}) collective-permute-start(f32[128]{0:T(128)S(1)} %add.164), channel_id=1, source_target_pairs={{0,4},{2,6},{4,0},{6,2},{1,5},{3,7},{5,1},{7,3},{8,12},{10,14},{12... | collective-permute-start | bytes 1544 | tf_op jit(solution)/shard_map/ppermute | solution.py:46
  115.5 1.9 %collective-permute-start.19 = (f32[136,128]{1,0:T(8,128)S(1)}, f32[136,128]{1,0:T(8,128)S(1)}, u32[]{:S(2)}, u32[]{:S(2)}) collective-permute-start(f32[136,128]{1,0:T(8,128)S(1)} %select_maximum_fusion), channel_id=1, source_target_pairs={{0,8},{8,0},{1,9},{9,1},{2,10},{10,2},{3,11},{11,3},{4,12},{12,4},... | collective-permute-start | bytes 208904 | tf_op jit(solution)/shard_map/ppermute | solution.py:46
  117.4 8.2 %collective-permute-done.19 = f32[136,128]{1,0:T(8,128)S(1)} collective-permute-done((f32[136,128]{1,0:T(8,128)S(1)}, f32[136,128]{1,0:T(8,128)S(1)}, u32[]{:S(2)}, u32[]{:S(2)}) %collective-permute-start.19) | collective-permute-done | bytes 69664 | tf_op jit(solution)/shard_map/ppermute | solution.py:46
  125.6 4.1 %collective-permute-start.20 = (f32[128,128]{1,0:T(8,128)S(1)}, f32[128,128]{1,0:T(8,128)S(1)}, u32[]{:S(2)}, u32[]{:S(2)}) collective-permute-start(f32[128,128]{1,0:T(8,128)S(1)} %slice_add_fusion), channel_id=1, source_target_pairs={{0,0},{16,1},{32,2},{48,3},{64,4},{80,5},{96,6},{112,7},{8,8},{24,... | collective-permute-start | bytes 196616 | tf_op jit(solution)/shard_map/ppermute | solution.py:149
  129.7 0.6 broadcast_in_dim.8
  130.3 4.5 %all-to-all-start = ((f32[4,2,128]{2,1,0:T(2,128)}), f32[4,2,128]{2,1,0:T(2,128)S(1)}, u32[]{:S(2)}, u32[]{:S(2)}) async-start(f32[4,2,128]{2,1,0:T(2,128)} %broadcast_in_dim.8), calls=%async_computation | async-start | bytes 8192 | tf_op jit(solution)/shard_map/all_to_all | solution.py:41
  134.8 1.0 fusion.8
  135.7 2.3 %all-to-all-done = f32[4,2,128]{2,1,0:T(2,128)S(1)} async-done(((f32[4,2,128]{2,1,0:T(2,128)}), f32[4,2,128]{2,1,0:T(2,128)S(1)}, u32[]{:S(2)}, u32[]{:S(2)}) %all-to-all-start) | async-done | bytes 4128 | tf_op jit(solution)/shard_map/all_to_all | solution.py:41
  138.0 0.9 collective-permute-done.20
  139.0 0.6 copy.99
  139.6 0.6 copy.100
  (117 shorter events, 2.4 us)
Async XLA Ops:
  0.6 15.9 %collective-permute-start = (bf16[128,128]{1,0:T(8,128)(2,1)}, bf16[128,128]{1,0:T(8,128)(2,1)S(1)}, u32[]{:S(2)}, u32[]{:S(2)}) collective-permute-start(bf16[128,128]{1,0:T(8,128)(2,1)} %param.8), channel_id=1, source_target_pairs={{0,0},{1,16},{2,32},{3,48},{4,64},{5,80},{6,96},{7,112},{8,8},{9,2... | collective-permute-start | bytes 98312 | tf_op jit(solution)/shard_map/ppermute | solution.py:72
  12.2 4.2 %copy-start.3 = (bf16[128,128]{1,0:T(8,128)(2,1)S(1)}, bf16[128,128]{1,0:T(8,128)(2,1)}, u32[]{:S(2)}) copy-start(bf16[128,128]{1,0:T(8,128)(2,1)} %param.7) | copy-start | bytes 98308
  16.6 14.4 %collective-permute-start.7 = (bf16[128,128]{1,0:T(8,128)(2,1)S(1)}, bf16[128,128]{1,0:T(8,128)(2,1)S(1)}, u32[]{:S(2)}, u32[]{:S(2)}) collective-permute-start(bf16[128,128]{1,0:T(8,128)(2,1)S(1)} %collective-permute-done), channel_id=1, source_target_pairs={{0,8},{8,0},{1,9},{9,1},{2,10},{10,2},{3,11},{11,3},{4,12},{12,4},... | collective-permute-start | bytes 98312 | tf_op jit(solution)/shard_map/ppermute | solution.py:46
  24.9 21.6 %collective-permute-start.3 = (bf16[512,128]{1,0:T(8,128)(2,1)S(1)}, bf16[512,128]{1,0:T(8,128)(2,1)S(1)}, u32[]{:S(2)}, u32[]{:S(2)}) collective-permute-start(bf16[512,128]{1,0:T(8,128)(2,1)S(1)} %bitcast.186), channel_id=1, source_target_pairs={{0,384},{128,256},{256,128},{384,0},{1,385},{129,257},{257,129},{3... | collective-permute-start | bytes 393224 | tf_op jit(solution)/shard_map/ppermute | solution.py:46
  26.9 6.0 %collective-permute-start.1 = (bf16[1,144,128]{2,1,0:T(8,128)(2,1)S(1)}, bf16[1,144,128]{2,1,0:T(8,128)(2,1)S(1)}, u32[]{:S(2)}, u32[]{:S(2)}) collective-permute-start(bf16[1,144,128]{2,1,0:T(8,128)(2,1)S(1)} %maximum_bitcast_fusion), channel_id=1, source_target_pairs={{0,2},{2,0},{4,6},{6,4},{1,3},{3,1},{5,7},{7,5},{8,10},{10,8},{12,... | collective-permute-start | bytes 110600 | tf_op jit(solution)/shard_map/ppermute | solution.py:46
  32.9 13.6 %collective-permute-start.2 = (bf16[2,144,128]{2,1,0:T(8,128)(2,1)S(1)}, bf16[2,144,128]{2,1,0:T(8,128)(2,1)S(1)}, u32[]{:S(2)}, u32[]{:S(2)}) collective-permute-start(bf16[2,144,128]{2,1,0:T(8,128)(2,1)S(1)} %pad_maximum_fusion.12), channel_id=1, source_target_pairs={{0,4},{2,6},{4,0},{6,2},{1,5},{3,7},{5,1},{7,3},{8,12},{10,14},{12... | collective-permute-start | bytes 221192 | tf_op jit(solution)/shard_map/ppermute | solution.py:46
  36.4 12.3 %collective-permute-start.8 = (bf16[2,128,128]{2,1,0:T(8,128)(2,1)S(1)}, bf16[2,128,128]{2,1,0:T(8,128)(2,1)S(1)}, u32[]{:S(2)}, u32[]{:S(2)}) collective-permute-start(bf16[2,128,128]{2,1,0:T(8,128)(2,1)S(1)} %pad_maximum_fusion.13), channel_id=1, source_target_pairs={{0,64},{16,80},{32,96},{48,112},{64,0},{80,16},{96,32},{112,48},{1... | collective-permute-start | bytes 196616 | tf_op jit(solution)/shard_map/ppermute | solution.py:46
  46.5 5.4 %copy-start.4 = (f32[1024]{0:T(1024)S(1)}, f32[1024]{0:T(1024)}, u32[]{:S(2)}) copy-start(f32[1024]{0:T(1024)} %param.9) | copy-start | bytes 12292
  46.8 8.4 %collective-permute-start.4 = (bf16[1088,128]{1,0:T(8,128)(2,1)S(1)}, bf16[1088,128]{1,0:T(8,128)(2,1)S(1)}, u32[]{:S(2)}, u32[]{:S(2)}) collective-permute-start(bf16[1088,128]{1,0:T(8,128)(2,1)S(1)} %pad_maximum_fusion.4), channel_id=1, source_target_pairs={{0,128},{128,0},{256,384},{384,256},{1,129},{129,1},{257,385},{385... | collective-permute-start | bytes 835592 | tf_op jit(solution)/shard_map/ppermute | solution.py:46
  48.8 8.9 %collective-permute-start.9 = (bf16[2,2,128,128]{3,2,1,0:T(8,128)(2,1)S(1)}, bf16[2,2,128,128]{3,2,1,0:T(8,128)(2,1)S(1)}, u32[]{:S(2)}, u32[]{:S(2)}) collective-permute-start(bf16[2,2,128,128]{3,2,1,0:T(8,128)(2,1)S(1)} %pad_maximum_fusion.10), channel_id=1, source_target_pairs={{0,32},{16,48},{32,0},{48,16},{64,96},{80,112},{96,64},{112,80},{1... | collective-permute-start | bytes 393224 | tf_op jit(solution)/shard_map/ppermute | solution.py:46
  55.3 9.8 %collective-permute-start.5 = (bf16[2,4,144,128]{3,2,1,0:T(8,128)(2,1)S(1)}, bf16[2,4,144,128]{3,2,1,0:T(8,128)(2,1)S(1)}, u32[]{:S(2)}, u32[]{:S(2)}) collective-permute-start(bf16[2,4,144,128]{3,2,1,0:T(8,128)(2,1)S(1)} %pad_maximum_fusion.3), channel_id=1, source_target_pairs={{0,384},{128,256},{256,128},{384,0},{1,385},{129,257},{257,129},{3... | collective-permute-start | bytes 884744 | tf_op jit(solution)/shard_map/ppermute | solution.py:46
  57.7 9.7 %collective-permute-start.10 = (bf16[2,2,2,128,128]{4,3,2,0,1:T(8,128)(2,1)S(1)}, bf16[2,2,2,128,128]{4,3,2,0,1:T(8,128)(2,1)S(1)}, u32[]{:S(2)}, u32[]{:S(2)}) collective-permute-start(bf16[2,2,2,128,128]{4,3,2,0,1:T(8,128)(2,1)S(1)} %pad_maximum_fusion.5), channel_id=1, source_target_pairs={{0,16},{16,0},{32,48},{48,32},{64,80},{80,64},{96,112},{112,96},{1... | collective-permute-start | bytes 786440 | tf_op jit(solution)/shard_map/ppermute | solution.py:46
  65.3 3.9 %collective-permute-start.6 = (bf16[4,4,144,128]{3,2,1,0:T(8,128)(2,1)S(1)}, bf16[4,4,144,128]{3,2,1,0:T(8,128)(2,1)S(1)}, u32[]{:S(2)}, u32[]{:S(2)}) collective-permute-start(bf16[4,4,144,128]{3,2,1,0:T(8,128)(2,1)S(1)} %get-tuple-element.24), channel_id=1, source_target_pairs={{0,1},{1,0},{2,3},{3,2},{4,5},{5,4},{6,7},{7,6},{8,9},{9,8},{10,11... | collective-permute-start | bytes 1769480 | tf_op jit(solution)/shard_map/ppermute | solution.py:46
  70.1 0.8 copy-start.1
  71.0 0.9 slice-start
  72.0 8.6 %collective-permute-start.11 = (bf16[512,128]{1,0:T(8,128)(2,1)S(1)}, bf16[512,128]{1,0:T(8,128)(2,1)S(1)}, u32[]{:S(2)}, u32[]{:S(2)}) collective-permute-start(bf16[512,128]{1,0:T(8,128)(2,1)S(1)} %bitcast.187), channel_id=1, source_target_pairs={{0,384},{128,256},{256,128},{384,0},{1,385},{129,257},{257,129},{3... | collective-permute-start | bytes 393224 | tf_op jit(solution)/shard_map/ppermute | solution.py:46
  74.1 10.3 %collective-permute-start.12 = (bf16[1040,128]{1,0:T(8,128)(2,1)S(1)}, bf16[1040,128]{1,0:T(8,128)(2,1)S(1)}, u32[]{:S(2)}, u32[]{:S(2)}) collective-permute-start(bf16[1040,128]{1,0:T(8,128)(2,1)S(1)} %fusion.12), channel_id=1, source_target_pairs={{0,16},{16,0},{32,48},{48,32},{64,80},{80,64},{96,112},{112,96},{1... | collective-permute-start | bytes 798728 | tf_op jit(solution)/shard_map/ppermute | solution.py:46
  84.8 6.9 %collective-permute-start.13 = (bf16[512,128]{1,0:T(8,128)(2,1)S(1)}, bf16[512,128]{1,0:T(8,128)(2,1)S(1)}, u32[]{:S(2)}, u32[]{:S(2)}) collective-permute-start(bf16[512,128]{1,0:T(8,128)(2,1)S(1)} %bitcast.188), channel_id=1, source_target_pairs={{0,128},{128,0},{256,384},{384,256},{1,129},{129,1},{257,385},{385... | collective-permute-start | bytes 393224 | tf_op jit(solution)/shard_map/ppermute | solution.py:46
  86.8 10.4 %collective-permute-start.17 = (bf16[528,128]{1,0:T(8,128)(2,1)S(1)}, bf16[528,128]{1,0:T(8,128)(2,1)S(1)}, u32[]{:S(2)}, u32[]{:S(2)}) collective-permute-start(bf16[528,128]{1,0:T(8,128)(2,1)S(1)} %fusion.19), channel_id=1, source_target_pairs={{0,32},{16,48},{32,0},{48,16},{64,96},{80,112},{96,64},{112,80},{1... | collective-permute-start | bytes 405512 | tf_op jit(solution)/shard_map/ppermute | solution.py:46
  91.8 10.1 %copy-start = (bf16[128,1024]{1,0:T(8,128)(2,1)S(1)}, bf16[128,1024]{1,0:T(8,128)(2,1)}, u32[]{:S(2)}) copy-start(bf16[128,1024]{1,0:T(8,128)(2,1)} %param.5) | copy-start | bytes 786436
  97.4 37.4 %copy-start.2 = (bf16[128,1024]{1,0:T(8,128)(2,1)S(1)}, bf16[128,1024]{1,0:T(8,128)(2,1)}, u32[]{:S(2)}) copy-start(bf16[128,1024]{1,0:T(8,128)(2,1)} %param.6) | copy-start | bytes 786436
  97.4 18.0 %collective-permute-start.18 = (bf16[272,128]{1,0:T(8,128)(2,1)S(1)}, bf16[272,128]{1,0:T(8,128)(2,1)S(1)}, u32[]{:S(2)}, u32[]{:S(2)}) collective-permute-start(bf16[272,128]{1,0:T(8,128)(2,1)S(1)} %fusion.20), channel_id=1, source_target_pairs={{0,64},{16,80},{32,96},{48,112},{64,0},{80,16},{96,32},{112,48},{1... | collective-permute-start | bytes 208904 | tf_op jit(solution)/shard_map/ppermute | solution.py:46
  102.1 3.0 %collective-permute-start.14 = (f32[128]{0:T(128)S(1)}, f32[128]{0:T(128)S(1)}, u32[]{:S(2)}, u32[]{:S(2)}) collective-permute-start(f32[128]{0:T(128)S(1)} %fusion.4), channel_id=1, source_target_pairs={{0,1},{1,0},{2,3},{3,2},{4,5},{5,4},{6,7},{7,6},{8,9},{9,8},{10,11... | collective-permute-start | bytes 1544 | tf_op jit(solution)/shard_map/ppermute | solution.py:46
  105.1 5.4 %collective-permute-start.15 = (f32[128]{0:T(128)S(1)}, f32[128]{0:T(128)S(1)}, u32[]{:S(2)}, u32[]{:S(2)}) collective-permute-start(f32[128]{0:T(128)S(1)} %add.163), channel_id=1, source_target_pairs={{0,2},{2,0},{4,6},{6,4},{1,3},{3,1},{5,7},{7,5},{8,10},{10,8},{12,... | collective-permute-start | bytes 1544 | tf_op jit(solution)/shard_map/ppermute | solution.py:46
  110.5 6.9 %collective-permute-start.16 = (f32[128]{0:T(128)S(1)}, f32[128]{0:T(128)S(1)}, u32[]{:S(2)}, u32[]{:S(2)}) collective-permute-start(f32[128]{0:T(128)S(1)} %add.164), channel_id=1, source_target_pairs={{0,4},{2,6},{4,0},{6,2},{1,5},{3,7},{5,1},{7,3},{8,12},{10,14},{12... | collective-permute-start | bytes 1544 | tf_op jit(solution)/shard_map/ppermute | solution.py:46
  115.5 10.1 %collective-permute-start.19 = (f32[136,128]{1,0:T(8,128)S(1)}, f32[136,128]{1,0:T(8,128)S(1)}, u32[]{:S(2)}, u32[]{:S(2)}) collective-permute-start(f32[136,128]{1,0:T(8,128)S(1)} %select_maximum_fusion), channel_id=1, source_target_pairs={{0,8},{8,0},{1,9},{9,1},{2,10},{10,2},{3,11},{11,3},{4,12},{12,4},... | collective-permute-start | bytes 208904 | tf_op jit(solution)/shard_map/ppermute | solution.py:46
  125.6 13.4 %collective-permute-start.20 = (f32[128,128]{1,0:T(8,128)S(1)}, f32[128,128]{1,0:T(8,128)S(1)}, u32[]{:S(2)}, u32[]{:S(2)}) collective-permute-start(f32[128,128]{1,0:T(8,128)S(1)} %slice_add_fusion), channel_id=1, source_target_pairs={{0,0},{16,1},{32,2},{48,3},{64,4},{80,5},{96,6},{112,7},{8,8},{24,... | collective-permute-start | bytes 196616 | tf_op jit(solution)/shard_map/ppermute | solution.py:149
  130.3 7.7 %all-to-all-start = ((f32[4,2,128]{2,1,0:T(2,128)}), f32[4,2,128]{2,1,0:T(2,128)S(1)}, u32[]{:S(2)}, u32[]{:S(2)}) async-start(f32[4,2,128]{2,1,0:T(2,128)} %broadcast_in_dim.8), calls=%async_computation | async-start | bytes 8192 | tf_op jit(solution)/shard_map/all_to_all | solution.py:41

commit v10 on v8

--- a/solution.py
+++ b/solution.py
@@ -80,7 +80,9 @@
     def quarter(r):
         return lax.dynamic_slice_in_dim(blocks, (mine ^ r) * 2, 2, axis=0)
 
-    packet, moved = lax.optimization_barrier((packet, moved))
+    given = jnp.concatenate([quarter(3), quarter(2)]).reshape(4 * TOK, HD)
+    near = swap(given, "x", 3)
+    packet, moved, near = lax.optimization_barrier((packet, moved, near))
     packet = jnp.concatenate([packet, swap(packet, "zl", 1)])
     weights = moved
     for axis, mask, place in (("zh", 1, 0), ("y", 4, 0), ("y", 2, 1), ("y", 1, 2)):
@@ -89,10 +91,7 @@
         pair = [jnp.where(first, weights, other), jnp.where(first, other, weights)]
         weights = jnp.stack(pair, axis=place)
     weights = weights.reshape(8, 2, HD, HD)
-    given = jnp.concatenate([quarter(3), quarter(2)]).reshape(4 * TOK, HD)
-    near = swap(given, "x", 3)
     packet = jnp.concatenate([packet, swap(packet, "zl", 2)])
-    packet, near = lax.optimization_barrier((packet, near))
 
     near = near.reshape(2, 2, TOK, HD)
     given = jnp.concatenate([quarter(1), near[1]]).reshape(4 * TOK, HD)
@@ -125,13 +124,6 @@
     ).astype(jnp.bfloat16)
     gain_rows = jnp.broadcast_to(jnp.pad(gain_part, ((0, 10), (0, 0)))[None], (16, 16, HD))
     arrived = exchange(jnp.concatenate([pieces.reshape(16, HD, HD), gain_rows], axis=1), ROW)
-    block = jnp.sum(arrived[:, :HD].astype(jnp.float32), axis=0)
-    weight_grad = lax.ppermute(block, AXES, [(b, a) for a, b in moves])
-    gains = jnp.sum(arrived[:, HD : HD + 6].astype(jnp.float32), axis=0)
-    gains = jnp.sum(gains.reshape(3, 2, HD), axis=0)
-    gains = exchange(jnp.broadcast_to(gains[None], (4, 2, HD)), "x")
-    gain_grad = gains.reshape(4 * QUARTER)
-
     back = norm_grad.astype(jnp.bfloat16)
     near = swap(back[:, 2 * TOK :].reshape(4 * TOK, HD), "x", 3).reshape(2, 2 * TOK, HD)
     given = jnp.concatenate([back[:, TOK : 2 * TOK], near[:, TOK:]]).reshape(4 * TOK, HD)
@@ -144,9 +136,19 @@
     scaled = full.astype(jnp.float32) * norm_gain[None, :]
     normal = widened * inv_scale
     inner = jnp.sum(scaled * normal, axis=1)
-    for axis, mask in (("core", 1), ("zl", 1), ("zl", 2)):
-        inner = inner + swap(inner, axis, mask)
-    inner = inner[:, None] / D
+    block = jnp.sum(arrived[:, :HD].astype(jnp.float32), axis=0)
+    gains = jnp.sum(arrived[:, HD : HD + 6].astype(jnp.float32), axis=0)
+    gains = jnp.sum(gains.reshape(3, 2, HD), axis=0)
+    inner, gains, block = lax.optimization_barrier((inner, gains, block))
+    weight_grad = lax.ppermute(block, AXES, [(b, a) for a, b in moves])
+    inner = inner + swap(inner, "core", 1)
+    both = jnp.concatenate([inner[None], gains])
+    both = exchange(jnp.broadcast_to(both[None], (16, 3, HD)), ("x", "zl")).reshape(4, 4, 3, HD)
+    both, weight_grad = lax.optimization_barrier((both, weight_grad))
+    inner = lax.dynamic_index_in_dim(both[:, :, 0], mine, 0, keepdims=False)
+    inner = jnp.sum(inner, axis=0)[:, None] / D
+    gains = lax.dynamic_index_in_dim(both[:, :, 1:], lax.axis_index("zl"), 1, keepdims=False)
+    gain_grad = gains.reshape(4 * QUARTER)
     input_grad = (
         residual_grad.astype(jnp.float32) + inv_scale * (scaled - normal * inner)
     ).astype(jnp.bfloat16)

time: 125 us -> 135 us (1.080)
  the two profiles are of different devices: /device:TPU:48 before, /device:TPU:1 now
where the time goes in v10:
time: 135 us; the launch traced here: 134 us
  starting transfers between devices  83.2 us (62%)
  waiting for transfers between devices  37.6 us (28%)
  local copies, waits for them, and re-layouts  6.64 us (5%)
  other arithmetic  3.48 us (3%)
  between operations  1.48 us (1%)
    ppermute x13, starting transfers between devices, swap(): return lax.ppermute(value, axis, [(i, i ^ mask) for i in range(count)])  60.8 us
    ppermute x13, waiting for transfers between devices, swap(): return lax.ppermute(value, axis, [(i, i ^ mask) for i in range(count)])  18.4 us
    all_to_all x2, waiting for transfers between devices, exchange(): return lax.all_to_all(value, axes, split_axis=0, concat_axis=0, tiled=True)  15.1 us
    all_to_all x2, starting transfers between devices, exchange(): return lax.all_to_all(value, axes, split_axis=0, concat_axis=0, tiled=True)  10.5 us
    ppermute x1, starting transfers between devices, shards(): weight_grad = lax.ppermute(block, AXES, [(b, a) for a, b in moves])  7.78 us
    ppermute x1, waiting for transfers between devices, shards(): moved = lax.ppermute(kv_weight, AXES, moves)  4.18 us
    ppermute x1, starting transfers between devices, shards(): moved = lax.ppermute(kv_weight, AXES, moves)  4.05 us
  transfers between devices with their start and end apart: 17, of which 10 were waited for; matrix products, arithmetic and copies ran while one was open for 3% of the time, Pallas kernels for 0%

profile of v10, /device:TPU:1, one launch (start us, length us, event | category | flops | bytes accessed | tf_op | source)
XLA Modules:
  0.0 133.8 jit_solution(2926712575792504919)
XLA Ops:
  0.7 0.9 fusion.32
  1.6 0.1 copy.157
  1.7 0.1 copy.158
  1.8 0.1 copy.159
  2.0 0.1 copy.160
  2.1 0.1 copy.161
  2.2 0.1 copy.162
  2.3 0.1 copy.163
  2.5 0.1 copy.164
  2.7 0.7 constant_dynamic-slice_fusion.2
  3.4 0.1 copy.133
  3.5 5.2 %collective-permute-start.1 = (bf16[512,128]{1,0:T(8,128)(2,1)S(1)}, bf16[512,128]{1,0:T(8,128)(2,1)S(1)}, u32[]{:S(2)}, u32[]{:S(2)}) collective-permute-start(bf16[512,128]{1,0:T(8,128)(2,1)S(1)} %bitcast.154), channel_id=1, source_target_pairs={{0,384},{128,256},{256,128},{384,0},{1,385},{129,257},{257,129},{3... | collective-permute-start | bytes 393224 | tf_op jit(solution)/shard_map/ppermute | solution.py:46
  8.8 4.0 %collective-permute-start = (bf16[128,128]{1,0:T(8,128)(2,1)S(1)}, bf16[128,128]{1,0:T(8,128)(2,1)S(1)}, u32[]{:S(2)}, u32[]{:S(2)}) collective-permute-start(bf16[128,128]{1,0:T(8,128)(2,1)S(1)} %copy-done.5), channel_id=1, source_target_pairs={{0,0},{1,16},{2,32},{3,48},{4,64},{5,80},{6,96},{7,112},{8,8},{9,2... | collective-permute-start | bytes 98312 | tf_op jit(solution)/shard_map/ppermute | solution.py:67
  12.8 0.1 fusion.9
  13.0 0.3 multiply_add_fusion
  13.3 0.1 fusion.15
  13.4 4.2 %collective-permute-done = bf16[128,128]{1,0:T(8,128)(2,1)S(1)} collective-permute-done((bf16[128,128]{1,0:T(8,128)(2,1)S(1)}, bf16[128,128]{1,0:T(8,128)(2,1)S(1)}, u32[]{:S(2)}, u32[]{:S(2)}) %collective-permute-start) | collective-permute-done | bytes 32800 | tf_op jit(solution)/shard_map/ppermute | solution.py:67
  17.6 4.6 %collective-permute-start.2 = (bf16[1,144,128]{2,1,0:T(8,128)(2,1)S(1)}, bf16[1,144,128]{2,1,0:T(8,128)(2,1)S(1)}, u32[]{:S(2)}, u32[]{:S(2)}) collective-permute-start(bf16[1,144,128]{2,1,0:T(8,128)(2,1)S(1)} %maximum_bitcast_fusion), channel_id=1, source_target_pairs={{0,2},{2,0},{4,6},{6,4},{1,3},{3,1},{5,7},{7,5},{8,10},{10,8},{12,... | collective-permute-start | bytes 110600 | tf_op jit(solution)/shard_map/ppermute | solution.py:46
  22.2 0.1 copy.134
  22.4 9.7 %collective-permute-start.7 = (bf16[128,128]{1,0:T(8,128)(2,1)S(1)}, bf16[128,128]{1,0:T(8,128)(2,1)S(1)}, u32[]{:S(2)}, u32[]{:S(2)}) collective-permute-start(bf16[128,128]{1,0:T(8,128)(2,1)S(1)} %collective-permute-done), channel_id=1, source_target_pairs={{0,8},{8,0},{1,9},{9,1},{2,10},{10,2},{3,11},{11,3},{4,12},{12,4},... | collective-permute-start | bytes 98312 | tf_op jit(solution)/shard_map/ppermute | solution.py:46
  32.2 0.1 copy.135
  32.3 1.2 collective-permute-done.7
  33.5 4.4 %collective-permute-start.8 = (bf16[2,128,128]{2,1,0:T(8,128)(2,1)S(1)}, bf16[2,128,128]{2,1,0:T(8,128)(2,1)S(1)}, u32[]{:S(2)}, u32[]{:S(2)}) collective-permute-start(bf16[2,128,128]{2,1,0:T(8,128)(2,1)S(1)} %pad_maximum_fusion.13), channel_id=1, source_target_pairs={{0,64},{16,80},{32,96},{48,112},{64,0},{80,16},{96,32},{112,48},{1... | collective-permute-start | bytes 196616 | tf_op jit(solution)/shard_map/ppermute | solution.py:46
  37.9 6.6 %collective-permute-start.3 = (bf16[2,144,128]{2,1,0:T(8,128)(2,1)S(1)}, bf16[2,144,128]{2,1,0:T(8,128)(2,1)S(1)}, u32[]{:S(2)}, u32[]{:S(2)}) collective-permute-start(bf16[2,144,128]{2,1,0:T(8,128)(2,1)S(1)} %pad_maximum_fusion.12), channel_id=1, source_target_pairs={{0,4},{2,6},{4,0},{6,2},{1,5},{3,7},{5,1},{7,3},{8,12},{10,14},{12... | collective-permute-start | bytes 221192 | tf_op jit(solution)/shard_map/ppermute | solution.py:46
  44.5 2.5 %collective-permute-done.3 = bf16[2,144,128]{2,1,0:T(8,128)(2,1)S(1)} collective-permute-done((bf16[2,144,128]{2,1,0:T(8,128)(2,1)S(1)}, bf16[2,144,128]{2,1,0:T(8,128)(2,1)S(1)}, u32[]{:S(2)}, u32[]{:S(2)}) %collective-permute-start.3) | collective-permute-done | bytes 73760 | tf_op jit(solution)/shard_map/ppermute | solution.py:46
  47.1 1.9 %collective-permute-start.4 = (bf16[1088,128]{1,0:T(8,128)(2,1)S(1)}, bf16[1088,128]{1,0:T(8,128)(2,1)S(1)}, u32[]{:S(2)}, u32[]{:S(2)}) collective-permute-start(bf16[1088,128]{1,0:T(8,128)(2,1)S(1)} %pad_maximum_fusion.5), channel_id=1, source_target_pairs={{0,128},{128,0},{256,384},{384,256},{1,129},{129,1},{257,385},{385... | collective-permute-start | bytes 835592 | tf_op jit(solution)/shard_map/ppermute | solution.py:46
  49.1 3.5 %collective-permute-start.9 = (bf16[2,2,128,128]{3,2,1,0:T(8,128)(2,1)S(1)}, bf16[2,2,128,128]{3,2,1,0:T(8,128)(2,1)S(1)}, u32[]{:S(2)}, u32[]{:S(2)}) collective-permute-start(bf16[2,2,128,128]{3,2,1,0:T(8,128)(2,1)S(1)} %pad_maximum_fusion.10), channel_id=1, source_target_pairs={{0,32},{16,48},{32,0},{48,16},{64,96},{80,112},{96,64},{112,80},{1... | collective-permute-start | bytes 393224 | tf_op jit(solution)/shard_map/ppermute | solution.py:46
  52.6 0.1 dynamic-slice_bitcast_fusion
  52.7 0.1 copy.143
  52.8 1.7 %collective-permute-done.4 = bf16[1088,128]{1,0:T(8,128)(2,1)S(1)} collective-permute-done((bf16[1088,128]{1,0:T(8,128)(2,1)S(1)}, bf16[1088,128]{1,0:T(8,128)(2,1)S(1)}, u32[]{:S(2)}, u32[]{:S(2)}) %collective-permute-start.4) | collective-permute-done | bytes 278560 | tf_op jit(solution)/shard_map/ppermute | solution.py:46
  54.5 4.2 %collective-permute-start.5 = (bf16[2,4,144,128]{3,2,1,0:T(8,128)(2,1)S(1)}, bf16[2,4,144,128]{3,2,1,0:T(8,128)(2,1)S(1)}, u32[]{:S(2)}, u32[]{:S(2)}) collective-permute-start(bf16[2,4,144,128]{3,2,1,0:T(8,128)(2,1)S(1)} %pad_maximum_fusion.4), channel_id=1, source_target_pairs={{0,384},{128,256},{256,128},{384,0},{1,385},{129,257},{257,129},{3... | collective-permute-start | bytes 884744 | tf_op jit(solution)/shard_map/ppermute | solution.py:46
  58.8 2.0 %collective-permute-start.10 = (bf16[2,2,2,128,128]{4,3,2,0,1:T(8,128)(2,1)S(1)}, bf16[2,2,2,128,128]{4,3,2,0,1:T(8,128)(2,1)S(1)}, u32[]{:S(2)}, u32[]{:S(2)}) collective-permute-start(bf16[2,2,2,128,128]{4,3,2,0,1:T(8,128)(2,1)S(1)} %pad_maximum_fusion.6), channel_id=1, source_target_pairs={{0,16},{16,0},{32,48},{48,32},{64,80},{80,64},{96,112},{112,96},{1... | collective-permute-start | bytes 786440 | tf_op jit(solution)/shard_map/ppermute | solution.py:46
  60.7 2.6 %collective-permute-done.5 = bf16[2,4,144,128]{3,2,1,0:T(8,128)(2,1)S(1)} collective-permute-done((bf16[2,4,144,128]{3,2,1,0:T(8,128)(2,1)S(1)}, bf16[2,4,144,128]{3,2,1,0:T(8,128)(2,1)S(1)}, u32[]{:S(2)}, u32[]{:S(2)}) %collective-permute-start.5) | collective-permute-done | bytes 294944 | tf_op jit(solution)/shard_map/ppermute | solution.py:46
  63.3 0.1 fusion.29
  63.4 11.8 %collective-permute-start.6 = (bf16[4,4,144,128]{3,2,1,0:T(8,128)(2,1)S(1)}, bf16[4,4,144,128]{3,2,1,0:T(8,128)(2,1)S(1)}, u32[]{:S(2)}, u32[]{:S(2)}) collective-permute-start(bf16[4,4,144,128]{3,2,1,0:T(8,128)(2,1)S(1)} %get-tuple-element.20), channel_id=1, source_target_pairs={{0,1},{1,0},{2,3},{3,2},{4,5},{5,4},{6,7},{7,6},{8,9},{9,8},{10,11... | collective-permute-start | bytes 1769480 | tf_op jit(solution)/shard_map/ppermute | solution.py:46
  75.3 0.1 copy.142
  75.4 0.1 copy.144
  75.6 0.3 copy.136
  75.9 0.9 collective-permute-done.6
  76.9 0.1 fusion.1
  77.1 0.7 convert_reduce_fusion
  77.9 0.1 copy-done.2
  77.9 0.2 fusion.10
  78.1 0.6 fusion
  78.8 0.9 pad_maximum_fusion.2
  79.7 7.0 %all-to-all-start = ((bf16[16,144,128]{2,1,0:T(8,128)(2,1)}), bf16[16,144,128]{2,1,0:T(8,128)(2,1)S(1)}, u32[]{:S(2)}, u32[]{:S(2)}) async-start(bf16[16,144,128]{2,1,0:T(8,128)(2,1)} %pad_maximum_fusion.2), calls=%async_computation | async-start | bytes 1179648 | tf_op jit(solution)/shard_map/all_to_all | solution.py:41
  86.7 0.1 copy.139
  86.9 1.9 %collective-permute-start.11 = (bf16[512,128]{1,0:T(8,128)(2,1)S(1)}, bf16[512,128]{1,0:T(8,128)(2,1)S(1)}, u32[]{:S(2)}, u32[]{:S(2)}) collective-permute-start(bf16[512,128]{1,0:T(8,128)(2,1)S(1)} %bitcast.158), channel_id=1, source_target_pairs={{0,384},{128,256},{256,128},{384,0},{1,385},{129,257},{257,129},{3... | collective-permute-start | bytes 393224 | tf_op jit(solution)/shard_map/ppermute | solution.py:46
  88.8 5.5 %collective-permute-done.11 = bf16[512,128]{1,0:T(8,128)(2,1)S(1)} collective-permute-done((bf16[512,128]{1,0:T(8,128)(2,1)S(1)}, bf16[512,128]{1,0:T(8,128)(2,1)S(1)}, u32[]{:S(2)}, u32[]{:S(2)}) %collective-permute-start.11) | collective-permute-done | bytes 131104 | tf_op jit(solution)/shard_map/ppermute | solution.py:46
  94.4 0.1 copy.165
  94.5 0.1 copy.141
  94.6 1.9 %collective-permute-start.12 = (bf16[512,128]{1,0:T(8,128)(2,1)S(1)}, bf16[512,128]{1,0:T(8,128)(2,1)S(1)}, u32[]{:S(2)}, u32[]{:S(2)}) collective-permute-start(bf16[512,128]{1,0:T(8,128)(2,1)S(1)} %bitcast.157), channel_id=1, source_target_pairs={{0,128},{128,0},{256,384},{384,256},{1,129},{129,1},{257,385},{385... | collective-permute-start | bytes 393224 | tf_op jit(solution)/shard_map/ppermute | solution.py:46
  96.6 0.1 copy.138
  96.8 3.9 %collective-permute-done.12 = bf16[512,128]{1,0:T(8,128)(2,1)S(1)} collective-permute-done((bf16[512,128]{1,0:T(8,128)(2,1)S(1)}, bf16[512,128]{1,0:T(8,128)(2,1)S(1)}, u32[]{:S(2)}, u32[]{:S(2)}) %collective-permute-start.12) | collective-permute-done | bytes 131104 | tf_op jit(solution)/shard_map/ppermute | solution.py:46
  100.9 0.2 fusion.4
  101.1 8.3 %all-to-all-done = bf16[16,144,128]{2,1,0:T(8,128)(2,1)S(1)} async-done(((bf16[16,144,128]{2,1,0:T(8,128)(2,1)}), bf16[16,144,128]{2,1,0:T(8,128)(2,1)S(1)}, u32[]{:S(2)}, u32[]{:S(2)}) %all-to-all-start) | async-done | bytes 589856 | tf_op jit(solution)/shard_map/all_to_all | solution.py:41
  109.5 3.2 %collective-permute-start.13 = (f32[128]{0:T(128)S(1)}, f32[128]{0:T(128)S(1)}, u32[]{:S(2)}, u32[]{:S(2)}) collective-permute-start(f32[128]{0:T(128)S(1)} %fusion.4), channel_id=1, source_target_pairs={{0,1},{1,0},{2,3},{3,2},{4,5},{5,4},{6,7},{7,6},{8,9},{9,8},{10,11... | collective-permute-start | bytes 1544 | tf_op jit(solution)/shard_map/ppermute | solution.py:46
  112.7 7.8 %collective-permute-start.14 = (f32[128,128]{1,0:T(8,128)S(1)}, f32[128,128]{1,0:T(8,128)S(1)}, u32[]{:S(2)}, u32[]{:S(2)}) collective-permute-start(f32[128,128]{1,0:T(8,128)S(1)} %convert_reduce_fusion.1), channel_id=1, source_target_pairs={{0,0},{16,1},{32,2},{48,3},{64,4},{80,5},{96,6},{112,7},{8,8},{24,... | collective-permute-start | bytes 196616 | tf_op jit(solution)/shard_map/ppermute | solution.py:143
  120.6 0.6 broadcast_in_dim.14
  121.2 3.5 %all-to-all-start.1 = ((f32[16,3,128]{2,1,0:T(4,128)}), f32[16,3,128]{2,1,0:T(4,128)S(1)}, u32[]{:S(2)}, u32[]{:S(2)}) async-start(f32[16,3,128]{2,1,0:T(4,128)} %broadcast_in_dim.14), calls=%async_computation.1 | async-start | bytes 65536 | tf_op jit(solution)/shard_map/all_to_all | solution.py:41
  124.7 6.8 %all-to-all-done.1 = f32[16,3,128]{2,1,0:T(4,128)S(1)} async-done(((f32[16,3,128]{2,1,0:T(4,128)}), f32[16,3,128]{2,1,0:T(4,128)S(1)}, u32[]{:S(2)}, u32[]{:S(2)}) %all-to-all-start.1) | async-done | bytes 24608 | tf_op jit(solution)/shard_map/all_to_all | solution.py:41
  131.6 0.6 copy.150
  132.2 1.0 fusion.8
  133.1 0.6 copy.187
  (91 shorter events, 1.2 us)
Async XLA Ops:
  1.6 7.2 %copy-start.5 = (bf16[128,128]{1,0:T(8,128)(2,1)S(1)}, bf16[128,128]{1,0:T(8,128)(2,1)}, u32[]{:S(2)}) copy-start(bf16[128,128]{1,0:T(8,128)(2,1)} %param.8) | copy-start | bytes 98308
  1.6 11.3 %copy-start = (bf16[128,1024]{1,0:T(8,128)(2,1)S(1)}, bf16[128,1024]{1,0:T(8,128)(2,1)}, u32[]{:S(2)}) copy-start(bf16[128,1024]{1,0:T(8,128)(2,1)} %param.5) | copy-start | bytes 786436
  2.0 11.0 %copy-start.3 = (bf16[128,128]{1,0:T(8,128)(2,1)S(1)}, bf16[128,128]{1,0:T(8,128)(2,1)}, u32[]{:S(2)}) copy-start(bf16[128,128]{1,0:T(8,128)(2,1)} %param.7) | copy-start | bytes 98308
  3.5 14.1 %collective-permute-start.1 = (bf16[512,128]{1,0:T(8,128)(2,1)S(1)}, bf16[512,128]{1,0:T(8,128)(2,1)S(1)}, u32[]{:S(2)}, u32[]{:S(2)}) collective-permute-start(bf16[512,128]{1,0:T(8,128)(2,1)S(1)} %bitcast.154), channel_id=1, source_target_pairs={{0,384},{128,256},{256,128},{384,0},{1,385},{129,257},{257,129},{3... | collective-permute-start | bytes 393224 | tf_op jit(solution)/shard_map/ppermute | solution.py:46
  8.8 8.8 %collective-permute-start = (bf16[128,128]{1,0:T(8,128)(2,1)S(1)}, bf16[128,128]{1,0:T(8,128)(2,1)S(1)}, u32[]{:S(2)}, u32[]{:S(2)}) collective-permute-start(bf16[128,128]{1,0:T(8,128)(2,1)S(1)} %copy-done.5), channel_id=1, source_target_pairs={{0,0},{1,16},{2,32},{3,48},{4,64},{5,80},{6,96},{7,112},{8,8},{9,2... | collective-permute-start | bytes 98312 | tf_op jit(solution)/shard_map/ppermute | solution.py:67
  17.6 20.3 %collective-permute-start.2 = (bf16[1,144,128]{2,1,0:T(8,128)(2,1)S(1)}, bf16[1,144,128]{2,1,0:T(8,128)(2,1)S(1)}, u32[]{:S(2)}, u32[]{:S(2)}) collective-permute-start(bf16[1,144,128]{2,1,0:T(8,128)(2,1)S(1)} %maximum_bitcast_fusion), channel_id=1, source_target_pairs={{0,2},{2,0},{4,6},{6,4},{1,3},{3,1},{5,7},{7,5},{8,10},{10,8},{12,... | collective-permute-start | bytes 110600 | tf_op jit(solution)/shard_map/ppermute | solution.py:46
  22.4 11.1 %collective-permute-start.7 = (bf16[128,128]{1,0:T(8,128)(2,1)S(1)}, bf16[128,128]{1,0:T(8,128)(2,1)S(1)}, u32[]{:S(2)}, u32[]{:S(2)}) collective-permute-start(bf16[128,128]{1,0:T(8,128)(2,1)S(1)} %collective-permute-done), channel_id=1, source_target_pairs={{0,8},{8,0},{1,9},{9,1},{2,10},{10,2},{3,11},{11,3},{4,12},{12,4},... | collective-permute-start | bytes 98312 | tf_op jit(solution)/shard_map/ppermute | solution.py:46
  32.1 20.4 %copy-start.4 = (f32[1024]{0:T(1024)S(1)}, f32[1024]{0:T(1024)}, u32[]{:S(2)}) copy-start(f32[1024]{0:T(1024)} %param.9) | copy-start | bytes 12292
  33.5 15.5 %collective-permute-start.8 = (bf16[2,128,128]{2,1,0:T(8,128)(2,1)S(1)}, bf16[2,128,128]{2,1,0:T(8,128)(2,1)S(1)}, u32[]{:S(2)}, u32[]{:S(2)}) collective-permute-start(bf16[2,128,128]{2,1,0:T(8,128)(2,1)S(1)} %pad_maximum_fusion.13), channel_id=1, source_target_pairs={{0,64},{16,80},{32,96},{48,112},{64,0},{80,16},{96,32},{112,48},{1... | collective-permute-start | bytes 196616 | tf_op jit(solution)/shard_map/ppermute | solution.py:46
  37.9 9.1 %collective-permute-start.3 = (bf16[2,144,128]{2,1,0:T(8,128)(2,1)S(1)}, bf16[2,144,128]{2,1,0:T(8,128)(2,1)S(1)}, u32[]{:S(2)}, u32[]{:S(2)}) collective-permute-start(bf16[2,144,128]{2,1,0:T(8,128)(2,1)S(1)} %pad_maximum_fusion.12), channel_id=1, source_target_pairs={{0,4},{2,6},{4,0},{6,2},{1,5},{3,7},{5,1},{7,3},{8,12},{10,14},{12... | collective-permute-start | bytes 221192 | tf_op jit(solution)/shard_map/ppermute | solution.py:46
  47.1 7.4 %collective-permute-start.4 = (bf16[1088,128]{1,0:T(8,128)(2,1)S(1)}, bf16[1088,128]{1,0:T(8,128)(2,1)S(1)}, u32[]{:S(2)}, u32[]{:S(2)}) collective-permute-start(bf16[1088,128]{1,0:T(8,128)(2,1)S(1)} %pad_maximum_fusion.5), channel_id=1, source_target_pairs={{0,128},{128,0},{256,384},{384,256},{1,129},{129,1},{257,385},{385... | collective-permute-start | bytes 835592 | tf_op jit(solution)/shard_map/ppermute | solution.py:46
  49.1 9.6 %collective-permute-start.9 = (bf16[2,2,128,128]{3,2,1,0:T(8,128)(2,1)S(1)}, bf16[2,2,128,128]{3,2,1,0:T(8,128)(2,1)S(1)}, u32[]{:S(2)}, u32[]{:S(2)}) collective-permute-start(bf16[2,2,128,128]{3,2,1,0:T(8,128)(2,1)S(1)} %pad_maximum_fusion.10), channel_id=1, source_target_pairs={{0,32},{16,48},{32,0},{48,16},{64,96},{80,112},{96,64},{112,80},{1... | collective-permute-start | bytes 393224 | tf_op jit(solution)/shard_map/ppermute | solution.py:46
  54.5 8.8 %collective-permute-start.5 = (bf16[2,4,144,128]{3,2,1,0:T(8,128)(2,1)S(1)}, bf16[2,4,144,128]{3,2,1,0:T(8,128)(2,1)S(1)}, u32[]{:S(2)}, u32[]{:S(2)}) collective-permute-start(bf16[2,4,144,128]{3,2,1,0:T(8,128)(2,1)S(1)} %pad_maximum_fusion.4), channel_id=1, source_target_pairs={{0,384},{128,256},{256,128},{384,0},{1,385},{129,257},{257,129},{3... | collective-permute-start | bytes 884744 | tf_op jit(solution)/shard_map/ppermute | solution.py:46
  58.8 16.7 %collective-permute-start.10 = (bf16[2,2,2,128,128]{4,3,2,0,1:T(8,128)(2,1)S(1)}, bf16[2,2,2,128,128]{4,3,2,0,1:T(8,128)(2,1)S(1)}, u32[]{:S(2)}, u32[]{:S(2)}) collective-permute-start(bf16[2,2,2,128,128]{4,3,2,0,1:T(8,128)(2,1)S(1)} %pad_maximum_fusion.6), channel_id=1, source_target_pairs={{0,16},{16,0},{32,48},{48,32},{64,80},{80,64},{96,112},{112,96},{1... | collective-permute-start | bytes 786440 | tf_op jit(solution)/shard_map/ppermute | solution.py:46
  63.4 13.4 %collective-permute-start.6 = (bf16[4,4,144,128]{3,2,1,0:T(8,128)(2,1)S(1)}, bf16[4,4,144,128]{3,2,1,0:T(8,128)(2,1)S(1)}, u32[]{:S(2)}, u32[]{:S(2)}) collective-permute-start(bf16[4,4,144,128]{3,2,1,0:T(8,128)(2,1)S(1)} %get-tuple-element.20), channel_id=1, source_target_pairs={{0,1},{1,0},{2,3},{3,2},{4,5},{5,4},{6,7},{7,6},{8,9},{9,8},{10,11... | collective-permute-start | bytes 1769480 | tf_op jit(solution)/shard_map/ppermute | solution.py:46
  77.1 0.8 copy-start.2
  79.7 29.7 %all-to-all-start = ((bf16[16,144,128]{2,1,0:T(8,128)(2,1)}), bf16[16,144,128]{2,1,0:T(8,128)(2,1)S(1)}, u32[]{:S(2)}, u32[]{:S(2)}) async-start(bf16[16,144,128]{2,1,0:T(8,128)(2,1)} %pad_maximum_fusion.2), calls=%async_computation | async-start | bytes 1179648 | tf_op jit(solution)/shard_map/all_to_all | solution.py:41
  86.9 7.5 %collective-permute-start.11 = (bf16[512,128]{1,0:T(8,128)(2,1)S(1)}, bf16[512,128]{1,0:T(8,128)(2,1)S(1)}, u32[]{:S(2)}, u32[]{:S(2)}) collective-permute-start(bf16[512,128]{1,0:T(8,128)(2,1)S(1)} %bitcast.158), channel_id=1, source_target_pairs={{0,384},{128,256},{256,128},{384,0},{1,385},{129,257},{257,129},{3... | collective-permute-start | bytes 393224 | tf_op jit(solution)/shard_map/ppermute | solution.py:46
  94.6 6.0 %collective-permute-start.12 = (bf16[512,128]{1,0:T(8,128)(2,1)S(1)}, bf16[512,128]{1,0:T(8,128)(2,1)S(1)}, u32[]{:S(2)}, u32[]{:S(2)}) collective-permute-start(bf16[512,128]{1,0:T(8,128)(2,1)S(1)} %bitcast.157), channel_id=1, source_target_pairs={{0,128},{128,0},{256,384},{384,256},{1,129},{129,1},{257,385},{385... | collective-permute-start | bytes 393224 | tf_op jit(solution)/shard_map/ppermute | solution.py:46
  100.7 31.5 %copy-start.1 = (bf16[128,1024]{1,0:T(8,128)(2,1)S(1)}, bf16[128,1024]{1,0:T(8,128)(2,1)}, u32[]{:S(2)}) copy-start(bf16[128,1024]{1,0:T(8,128)(2,1)} %param.6) | copy-start | bytes 786436
  109.5 11.0 %collective-permute-start.13 = (f32[128]{0:T(128)S(1)}, f32[128]{0:T(128)S(1)}, u32[]{:S(2)}, u32[]{:S(2)}) collective-permute-start(f32[128]{0:T(128)S(1)} %fusion.4), channel_id=1, source_target_pairs={{0,1},{1,0},{2,3},{3,2},{4,5},{5,4},{6,7},{7,6},{8,9},{9,8},{10,11... | collective-permute-start | bytes 1544 | tf_op jit(solution)/shard_map/ppermute | solution.py:46
  112.7 18.8 %collective-permute-start.14 = (f32[128,128]{1,0:T(8,128)S(1)}, f32[128,128]{1,0:T(8,128)S(1)}, u32[]{:S(2)}, u32[]{:S(2)}) collective-permute-start(f32[128,128]{1,0:T(8,128)S(1)} %convert_reduce_fusion.1), channel_id=1, source_target_pairs={{0,0},{16,1},{32,2},{48,3},{64,4},{80,5},{96,6},{112,7},{8,8},{24,... | collective-permute-start | bytes 196616 | tf_op jit(solution)/shard_map/ppermute | solution.py:143
  121.2 10.3 %all-to-all-start.1 = ((f32[16,3,128]{2,1,0:T(4,128)}), f32[16,3,128]{2,1,0:T(4,128)S(1)}, u32[]{:S(2)}, u32[]{:S(2)}) async-start(f32[16,3,128]{2,1,0:T(4,128)} %broadcast_in_dim.14), calls=%async_computation.1 | async-start | bytes 65536 | tf_op jit(solution)/shard_map/all_to_all | solution.py:41

commit v11 on v10

--- a/solution.py
+++ b/solution.py
@@ -65,6 +65,7 @@
     mine = lax.axis_index("x")
 
     moved = lax.ppermute(kv_weight, AXES, moves)
+    other = lax.ppermute(kv_weight, AXES, [(a, b ^ 8) for a, b in moves])
 
     cosine, sine = rope_tables(TOK, HD)
     grads = key_value_grad.astype(jnp.float32)
@@ -80,18 +81,20 @@
     def quarter(r):
         return lax.dynamic_slice_in_dim(blocks, (mine ^ r) * 2, 2, axis=0)
 
-    given = jnp.concatenate([quarter(3), quarter(2)]).reshape(4 * TOK, HD)
-    near = swap(given, "x", 3)
-    packet, moved, near = lax.optimization_barrier((packet, moved, near))
+    packet, moved, other = lax.optimization_barrier((packet, moved, other))
     packet = jnp.concatenate([packet, swap(packet, "zl", 1)])
-    weights = moved
-    for axis, mask, place in (("zh", 1, 0), ("y", 4, 0), ("y", 2, 1), ("y", 1, 2)):
-        other = swap(weights, axis, mask)
-        first = (lax.axis_index(axis) & mask) == 0
+    first = lax.axis_index("zh") == 0
+    weights = jnp.stack([jnp.where(first, moved, other), jnp.where(first, other, moved)])
+    for mask, place in ((4, 0), (2, 1), (1, 2)):
+        other = swap(weights, "y", mask)
+        first = (lax.axis_index("y") & mask) == 0
         pair = [jnp.where(first, weights, other), jnp.where(first, other, weights)]
         weights = jnp.stack(pair, axis=place)
     weights = weights.reshape(8, 2, HD, HD)
+    given = jnp.concatenate([quarter(3), quarter(2)]).reshape(4 * TOK, HD)
+    near = swap(given, "x", 3)
     packet = jnp.concatenate([packet, swap(packet, "zl", 2)])
+    packet, near = lax.optimization_barrier((packet, near))
 
     near = near.reshape(2, 2, TOK, HD)
     given = jnp.concatenate([quarter(1), near[1]]).reshape(4 * TOK, HD)
@@ -122,7 +125,7 @@
     pieces = jnp.einsum(
         "ktc,btf->kbcf", kv, normed, preferred_element_type=jnp.float32
     ).astype(jnp.bfloat16)
-    gain_rows = jnp.broadcast_to(jnp.pad(gain_part, ((0, 10), (0, 0)))[None], (16, 16, HD))
+    gain_rows = jnp.broadcast_to(jnp.pad(gain_part, ((0, 2), (0, 0)))[None], (16, 8, HD))
     arrived = exchange(jnp.concatenate([pieces.reshape(16, HD, HD), gain_rows], axis=1), ROW)
     back = norm_grad.astype(jnp.bfloat16)
     near = swap(back[:, 2 * TOK :].reshape(4 * TOK, HD), "x", 3).reshape(2, 2 * TOK, HD)

time: 135 us -> 127 us (0.941)
  waiting for transfers between devices: 37.6 us -> 30.3 us
    ppermute x13 -> x12, starting transfers between devices: 60.8 us -> 47 us  [swap(): return lax.ppermute(value, axis, [(i, i ^ mask) for i in range(count)])]
    ppermute x0 -> x1, starting transfers between devices: none -> 11.7 us  [shards(): other = lax.ppermute(kv_weight, AXES, [(a, b ^ 8) for a, b in moves])]
    ppermute x1, waiting for transfers between devices: 4.18 us -> 0.01 us  [shards(): moved = lax.ppermute(kv_weight, AXES, moves)]
    all_to_all x2, starting transfers between devices: 10.5 us -> 13.1 us  [exchange(): return lax.all_to_all(value, axes, split_axis=0, concat_axis=0, tiled=True)]
    all_to_all x2, waiting for transfers between devices: 15.1 us -> 13.4 us  [exchange(): return lax.all_to_all(value, axes, split_axis=0, concat_axis=0, tiled=True)]
    ppermute x13 -> x12, waiting for transfers between devices: 18.4 us -> 16.8 us  [swap(): return lax.ppermute(value, axis, [(i, i ^ mask) for i in range(count)])]
  transfers between devices with their start and end apart: 17 -> 17, of which waited for: 10 -> 10; matrix products, arithmetic and copies ran while one was open for 3% -> 5% of each run, Pallas kernels for 0% -> 0%
where the time goes in v11:
time: 127 us; the launch traced here: 126 us
  starting transfers between devices  82.9 us (65%)
  waiting for transfers between devices  30.3 us (24%)
  local copies, waits for them, and re-layouts  6.61 us (5%)
  other arithmetic  3.48 us (3%)
  between operations  1.46 us (1%)
  matrix products  1.32 us (1%)
    ppermute x12, starting transfers between devices, swap(): return lax.ppermute(value, axis, [(i, i ^ mask) for i in range(count)])  47 us
    ppermute x12, waiting for transfers between devices, swap(): return lax.ppermute(value, axis, [(i, i ^ mask) for i in range(count)])  16.8 us
    all_to_all x2, waiting for transfers between devices, exchange(): return lax.all_to_all(value, axes, split_axis=0, concat_axis=0, tiled=True)  13.4 us
    all_to_all x2, starting transfers between devices, exchange(): return lax.all_to_all(value, axes, split_axis=0, concat_axis=0, tiled=True)  13.1 us
    ppermute x1, starting transfers between devices, shards(): other = lax.ppermute(kv_weight, AXES, [(a, b ^ 8) for a, b in moves])  11.7 us
    ppermute x1, starting transfers between devices, shards(): weight_grad = lax.ppermute(block, AXES, [(b, a) for a, b in moves])  6.46 us
    ppermute x1, starting transfers between devices, shards(): moved = lax.ppermute(kv_weight, AXES, moves)  4.59 us
  transfers between devices with their start and end apart: 17, of which 10 were waited for; matrix products, arithmetic and copies ran while one was open for 5% of the time, Pallas kernels for 0%

profile of v11, /device:TPU:1, one launch (start us, length us, event | category | flops | bytes accessed | tf_op | source)
XLA Modules:
  0.0 126.0 jit_solution(17468071996022000311)
XLA Ops:
  0.6 4.6 %collective-permute-start = (bf16[128,128]{1,0:T(8,128)(2,1)}, bf16[128,128]{1,0:T(8,128)(2,1)S(1)}, u32[]{:S(2)}, u32[]{:S(2)}) collective-permute-start(bf16[128,128]{1,0:T(8,128)(2,1)} %param.8), channel_id=1, source_target_pairs={{0,0},{1,16},{2,32},{3,48},{4,64},{5,80},{6,96},{7,112},{8,8},{9,2... | collective-permute-start | bytes 98312 | tf_op jit(solution)/shard_map/ppermute | solution.py:67
  5.2 11.7 %collective-permute-start.1 = (bf16[128,128]{1,0:T(8,128)(2,1)}, bf16[128,128]{1,0:T(8,128)(2,1)S(1)}, u32[]{:S(2)}, u32[]{:S(2)}) collective-permute-start(bf16[128,128]{1,0:T(8,128)(2,1)} %param.8), channel_id=1, source_target_pairs={{0,8},{1,24},{2,40},{3,56},{4,72},{5,88},{6,104},{7,120},{8,0},{9,... | collective-permute-start | bytes 98312 | tf_op jit(solution)/shard_map/ppermute | solution.py:68
  17.0 0.9 fusion.32
  17.9 0.1 copy.157
  18.0 0.1 copy.158
  18.2 0.1 copy.159
  18.3 0.1 copy.160
  18.4 0.1 copy.161
  18.5 0.1 copy.162
  18.7 0.1 copy.163
  18.8 0.1 copy.164
  19.0 0.7 constant_dynamic-slice_fusion.2
  19.7 0.1 copy.133
  19.9 7.0 %collective-permute-start.4 = (bf16[512,128]{1,0:T(8,128)(2,1)S(1)}, bf16[512,128]{1,0:T(8,128)(2,1)S(1)}, u32[]{:S(2)}, u32[]{:S(2)}) collective-permute-start(bf16[512,128]{1,0:T(8,128)(2,1)S(1)} %bitcast.154), channel_id=1, source_target_pairs={{0,384},{128,256},{256,128},{384,0},{1,385},{129,257},{257,129},{3... | collective-permute-start | bytes 393224 | tf_op jit(solution)/shard_map/ppermute | solution.py:46
  26.9 0.1 fusion.9
  27.1 0.3 multiply_add_fusion
  27.4 0.1 fusion.15
  27.5 3.6 %collective-permute-start.2 = (bf16[1,144,128]{2,1,0:T(8,128)(2,1)S(1)}, bf16[1,144,128]{2,1,0:T(8,128)(2,1)S(1)}, u32[]{:S(2)}, u32[]{:S(2)}) collective-permute-start(bf16[1,144,128]{2,1,0:T(8,128)(2,1)S(1)} %maximum_bitcast_fusion), channel_id=1, source_target_pairs={{0,2},{2,0},{4,6},{6,4},{1,3},{3,1},{5,7},{7,5},{8,10},{10,8},{12,... | collective-permute-start | bytes 110600 | tf_op jit(solution)/shard_map/ppermute | solution.py:46
  31.2 1.3 %collective-permute-done.2 = bf16[1,144,128]{2,1,0:T(8,128)(2,1)S(1)} collective-permute-done((bf16[1,144,128]{2,1,0:T(8,128)(2,1)S(1)}, bf16[1,144,128]{2,1,0:T(8,128)(2,1)S(1)}, u32[]{:S(2)}, u32[]{:S(2)}) %collective-permute-start.2) | collective-permute-done | bytes 36896 | tf_op jit(solution)/shard_map/ppermute | solution.py:46
  32.5 6.9 %collective-permute-start.3 = (bf16[2,144,128]{2,1,0:T(8,128)(2,1)S(1)}, bf16[2,144,128]{2,1,0:T(8,128)(2,1)S(1)}, u32[]{:S(2)}, u32[]{:S(2)}) collective-permute-start(bf16[2,144,128]{2,1,0:T(8,128)(2,1)S(1)} %pad_maximum_fusion.13), channel_id=1, source_target_pairs={{0,4},{2,6},{4,0},{6,2},{1,5},{3,7},{5,1},{7,3},{8,12},{10,14},{12... | collective-permute-start | bytes 221192 | tf_op jit(solution)/shard_map/ppermute | solution.py:46
  39.4 4.4 %collective-permute-start.8 = (bf16[2,128,128]{2,1,0:T(8,128)(2,1)S(1)}, bf16[2,128,128]{2,1,0:T(8,128)(2,1)S(1)}, u32[]{:S(2)}, u32[]{:S(2)}) collective-permute-start(bf16[2,128,128]{2,1,0:T(8,128)(2,1)S(1)} %pad_maximum_fusion.14), channel_id=1, source_target_pairs={{0,64},{16,80},{32,96},{48,112},{64,0},{80,16},{96,32},{112,48},{1... | collective-permute-start | bytes 196616 | tf_op jit(solution)/shard_map/ppermute | solution.py:46
  43.9 0.1 copy.134
  44.0 0.1 copy.135
  44.2 1.9 %collective-permute-start.5 = (bf16[1088,128]{1,0:T(8,128)(2,1)S(1)}, bf16[1088,128]{1,0:T(8,128)(2,1)S(1)}, u32[]{:S(2)}, u32[]{:S(2)}) collective-permute-start(bf16[1088,128]{1,0:T(8,128)(2,1)S(1)} %pad_maximum_fusion.5), channel_id=1, source_target_pairs={{0,128},{128,0},{256,384},{384,256},{1,129},{129,1},{257,385},{385... | collective-permute-start | bytes 835592 | tf_op jit(solution)/shard_map/ppermute | solution.py:46
  46.1 2.2 %collective-permute-done.8 = bf16[2,128,128]{2,1,0:T(8,128)(2,1)S(1)} collective-permute-done((bf16[2,128,128]{2,1,0:T(8,128)(2,1)S(1)}, bf16[2,128,128]{2,1,0:T(8,128)(2,1)S(1)}, u32[]{:S(2)}, u32[]{:S(2)}) %collective-permute-start.8) | collective-permute-done | bytes 65568 | tf_op jit(solution)/shard_map/ppermute | solution.py:46
  48.4 1.9 %collective-permute-start.9 = (bf16[2,2,128,128]{3,2,1,0:T(8,128)(2,1)S(1)}, bf16[2,2,128,128]{3,2,1,0:T(8,128)(2,1)S(1)}, u32[]{:S(2)}, u32[]{:S(2)}) collective-permute-start(bf16[2,2,128,128]{3,2,1,0:T(8,128)(2,1)S(1)} %pad_maximum_fusion.11), channel_id=1, source_target_pairs={{0,32},{16,48},{32,0},{48,16},{64,96},{80,112},{96,64},{112,80},{1... | collective-permute-start | bytes 393224 | tf_op jit(solution)/shard_map/ppermute | solution.py:46
  50.3 0.1 dynamic-slice_bitcast_fusion
  50.4 0.1 copy.143
  50.5 1.5 %collective-permute-done.5 = bf16[1088,128]{1,0:T(8,128)(2,1)S(1)} collective-permute-done((bf16[1088,128]{1,0:T(8,128)(2,1)S(1)}, bf16[1088,128]{1,0:T(8,128)(2,1)S(1)}, u32[]{:S(2)}, u32[]{:S(2)}) %collective-permute-start.5) | collective-permute-done | bytes 278560 | tf_op jit(solution)/shard_map/ppermute | solution.py:46
  52.1 2.8 %collective-permute-start.6 = (bf16[2,4,144,128]{3,2,1,0:T(8,128)(2,1)S(1)}, bf16[2,4,144,128]{3,2,1,0:T(8,128)(2,1)S(1)}, u32[]{:S(2)}, u32[]{:S(2)}) collective-permute-start(bf16[2,4,144,128]{3,2,1,0:T(8,128)(2,1)S(1)} %pad_maximum_fusion.4), channel_id=1, source_target_pairs={{0,384},{128,256},{256,128},{384,0},{1,385},{129,257},{257,129},{3... | collective-permute-start | bytes 884744 | tf_op jit(solution)/shard_map/ppermute | solution.py:46
  55.1 3.8 %collective-permute-start.10 = (bf16[2,2,2,128,128]{4,3,2,0,1:T(8,128)(2,1)S(1)}, bf16[2,2,2,128,128]{4,3,2,0,1:T(8,128)(2,1)S(1)}, u32[]{:S(2)}, u32[]{:S(2)}) collective-permute-start(bf16[2,2,2,128,128]{4,3,2,0,1:T(8,128)(2,1)S(1)} %pad_maximum_fusion.6), channel_id=1, source_target_pairs={{0,16},{16,0},{32,48},{48,32},{64,80},{80,64},{96,112},{112,96},{1... | collective-permute-start | bytes 786440 | tf_op jit(solution)/shard_map/ppermute | solution.py:46
  58.9 1.9 %collective-permute-done.6 = bf16[2,4,144,128]{3,2,1,0:T(8,128)(2,1)S(1)} collective-permute-done((bf16[2,4,144,128]{3,2,1,0:T(8,128)(2,1)S(1)}, bf16[2,4,144,128]{3,2,1,0:T(8,128)(2,1)S(1)}, u32[]{:S(2)}, u32[]{:S(2)}) %collective-permute-start.6) | collective-permute-done | bytes 294944 | tf_op jit(solution)/shard_map/ppermute | solution.py:46
  60.8 0.1 fusion.29
  60.9 6.1 %collective-permute-start.7 = (bf16[4,4,144,128]{3,2,1,0:T(8,128)(2,1)S(1)}, bf16[4,4,144,128]{3,2,1,0:T(8,128)(2,1)S(1)}, u32[]{:S(2)}, u32[]{:S(2)}) collective-permute-start(bf16[4,4,144,128]{3,2,1,0:T(8,128)(2,1)S(1)} %get-tuple-element.24), channel_id=1, source_target_pairs={{0,1},{1,0},{2,3},{3,2},{4,5},{5,4},{6,7},{7,6},{8,9},{9,8},{10,11... | collective-permute-start | bytes 1769480 | tf_op jit(solution)/shard_map/ppermute | solution.py:46
  67.1 0.1 copy.142
  67.2 0.1 copy.144
  67.4 0.3 copy.136
  67.7 0.9 collective-permute-done.7
  68.7 0.1 fusion.1
  68.9 0.7 convert_reduce_fusion
  69.6 0.1 copy-done.2
  69.7 0.2 fusion.10
  69.9 0.6 fusion
  70.6 0.8 pad_maximum_fusion.2
  71.5 9.2 %all-to-all-start = ((bf16[16,136,128]{2,1,0:T(8,128)(2,1)}), bf16[16,136,128]{2,1,0:T(8,128)(2,1)S(1)}, u32[]{:S(2)}, u32[]{:S(2)}) async-start(bf16[16,136,128]{2,1,0:T(8,128)(2,1)} %pad_maximum_fusion.2), calls=%async_computation | async-start | bytes 1114112 | tf_op jit(solution)/shard_map/all_to_all | solution.py:41
  80.7 0.1 copy.139
  80.8 2.6 %collective-permute-start.11 = (bf16[512,128]{1,0:T(8,128)(2,1)S(1)}, bf16[512,128]{1,0:T(8,128)(2,1)S(1)}, u32[]{:S(2)}, u32[]{:S(2)}) collective-permute-start(bf16[512,128]{1,0:T(8,128)(2,1)S(1)} %bitcast.158), channel_id=1, source_target_pairs={{0,384},{128,256},{256,128},{384,0},{1,385},{129,257},{257,129},{3... | collective-permute-start | bytes 393224 | tf_op jit(solution)/shard_map/ppermute | solution.py:46
  83.4 4.9 %collective-permute-done.11 = bf16[512,128]{1,0:T(8,128)(2,1)S(1)} collective-permute-done((bf16[512,128]{1,0:T(8,128)(2,1)S(1)}, bf16[512,128]{1,0:T(8,128)(2,1)S(1)}, u32[]{:S(2)}, u32[]{:S(2)}) %collective-permute-start.11) | collective-permute-done | bytes 131104 | tf_op jit(solution)/shard_map/ppermute | solution.py:46
  88.3 0.1 copy.165
  88.5 0.1 copy.141
  88.6 1.9 %collective-permute-start.12 = (bf16[512,128]{1,0:T(8,128)(2,1)S(1)}, bf16[512,128]{1,0:T(8,128)(2,1)S(1)}, u32[]{:S(2)}, u32[]{:S(2)}) collective-permute-start(bf16[512,128]{1,0:T(8,128)(2,1)S(1)} %bitcast.157), channel_id=1, source_target_pairs={{0,128},{128,0},{256,384},{384,256},{1,129},{129,1},{257,385},{385... | collective-permute-start | bytes 393224 | tf_op jit(solution)/shard_map/ppermute | solution.py:46
  90.5 0.1 copy.138
  90.7 3.9 %collective-permute-done.12 = bf16[512,128]{1,0:T(8,128)(2,1)S(1)} collective-permute-done((bf16[512,128]{1,0:T(8,128)(2,1)S(1)}, bf16[512,128]{1,0:T(8,128)(2,1)S(1)}, u32[]{:S(2)}, u32[]{:S(2)}) %collective-permute-start.12) | collective-permute-done | bytes 131104 | tf_op jit(solution)/shard_map/ppermute | solution.py:46
  94.8 0.2 fusion.4
  95.1 6.6 %all-to-all-done = bf16[16,136,128]{2,1,0:T(8,128)(2,1)S(1)} async-done(((bf16[16,136,128]{2,1,0:T(8,128)(2,1)}), bf16[16,136,128]{2,1,0:T(8,128)(2,1)S(1)}, u32[]{:S(2)}, u32[]{:S(2)}) %all-to-all-start) | async-done | bytes 557088 | tf_op jit(solution)/shard_map/all_to_all | solution.py:41
  101.7 0.1 convert_reduce_fusion.1
  101.8 4.1 %collective-permute-start.13 = (f32[128]{0:T(128)S(1)}, f32[128]{0:T(128)S(1)}, u32[]{:S(2)}, u32[]{:S(2)}) collective-permute-start(f32[128]{0:T(128)S(1)} %fusion.4), channel_id=1, source_target_pairs={{0,1},{1,0},{2,3},{3,2},{4,5},{5,4},{6,7},{7,6},{8,9},{9,8},{10,11... | collective-permute-start | bytes 1544 | tf_op jit(solution)/shard_map/ppermute | solution.py:46
  105.9 6.5 %collective-permute-start.14 = (f32[128,128]{1,0:T(8,128)S(1)}, f32[128,128]{1,0:T(8,128)S(1)}, u32[]{:S(2)}, u32[]{:S(2)}) collective-permute-start(f32[128,128]{1,0:T(8,128)S(1)} %convert_reduce_fusion.1), channel_id=1, source_target_pairs={{0,0},{16,1},{32,2},{48,3},{64,4},{80,5},{96,6},{112,7},{8,8},{24,... | collective-permute-start | bytes 196616 | tf_op jit(solution)/shard_map/ppermute | solution.py:146
  112.4 0.6 broadcast_in_dim.14
  113.0 3.9 %all-to-all-start.1 = ((f32[16,3,128]{2,1,0:T(4,128)}), f32[16,3,128]{2,1,0:T(4,128)S(1)}, u32[]{:S(2)}, u32[]{:S(2)}) async-start(f32[16,3,128]{2,1,0:T(4,128)} %broadcast_in_dim.14), calls=%async_computation.1 | async-start | bytes 65536 | tf_op jit(solution)/shard_map/all_to_all | solution.py:41
  116.9 6.9 %all-to-all-done.1 = f32[16,3,128]{2,1,0:T(4,128)S(1)} async-done(((f32[16,3,128]{2,1,0:T(4,128)}), f32[16,3,128]{2,1,0:T(4,128)S(1)}, u32[]{:S(2)}, u32[]{:S(2)}) %all-to-all-start.1) | async-done | bytes 24608 | tf_op jit(solution)/shard_map/all_to_all | solution.py:41
  123.8 0.6 copy.150
  124.4 1.0 fusion.8
  125.4 0.6 copy.185
  (87 shorter events, 1.2 us)
Async XLA Ops:
  0.6 26.9 %collective-permute-start = (bf16[128,128]{1,0:T(8,128)(2,1)}, bf16[128,128]{1,0:T(8,128)(2,1)S(1)}, u32[]{:S(2)}, u32[]{:S(2)}) collective-permute-start(bf16[128,128]{1,0:T(8,128)(2,1)} %param.8), channel_id=1, source_target_pairs={{0,0},{1,16},{2,32},{3,48},{4,64},{5,80},{6,96},{7,112},{8,8},{9,2... | collective-permute-start | bytes 98312 | tf_op jit(solution)/shard_map/ppermute | solution.py:67
  5.2 22.3 %collective-permute-start.1 = (bf16[128,128]{1,0:T(8,128)(2,1)}, bf16[128,128]{1,0:T(8,128)(2,1)S(1)}, u32[]{:S(2)}, u32[]{:S(2)}) collective-permute-start(bf16[128,128]{1,0:T(8,128)(2,1)} %param.8), channel_id=1, source_target_pairs={{0,8},{1,24},{2,40},{3,56},{4,72},{5,88},{6,104},{7,120},{8,0},{9,... | collective-permute-start | bytes 98312 | tf_op jit(solution)/shard_map/ppermute | solution.py:68
  17.9 9.0 %copy-start = (bf16[128,1024]{1,0:T(8,128)(2,1)S(1)}, bf16[128,1024]{1,0:T(8,128)(2,1)}, u32[]{:S(2)}) copy-start(bf16[128,1024]{1,0:T(8,128)(2,1)} %param.5) | copy-start | bytes 786436
  18.3 8.8 %copy-start.3 = (bf16[128,128]{1,0:T(8,128)(2,1)S(1)}, bf16[128,128]{1,0:T(8,128)(2,1)}, u32[]{:S(2)}) copy-start(bf16[128,128]{1,0:T(8,128)(2,1)} %param.7) | copy-start | bytes 98308
  19.9 24.0 %collective-permute-start.4 = (bf16[512,128]{1,0:T(8,128)(2,1)S(1)}, bf16[512,128]{1,0:T(8,128)(2,1)S(1)}, u32[]{:S(2)}, u32[]{:S(2)}) collective-permute-start(bf16[512,128]{1,0:T(8,128)(2,1)S(1)} %bitcast.154), channel_id=1, source_target_pairs={{0,384},{128,256},{256,128},{384,0},{1,385},{129,257},{257,129},{3... | collective-permute-start | bytes 393224 | tf_op jit(solution)/shard_map/ppermute | solution.py:46
  27.5 5.0 %collective-permute-start.2 = (bf16[1,144,128]{2,1,0:T(8,128)(2,1)S(1)}, bf16[1,144,128]{2,1,0:T(8,128)(2,1)S(1)}, u32[]{:S(2)}, u32[]{:S(2)}) collective-permute-start(bf16[1,144,128]{2,1,0:T(8,128)(2,1)S(1)} %maximum_bitcast_fusion), channel_id=1, source_target_pairs={{0,2},{2,0},{4,6},{6,4},{1,3},{3,1},{5,7},{7,5},{8,10},{10,8},{12,... | collective-permute-start | bytes 110600 | tf_op jit(solution)/shard_map/ppermute | solution.py:46
  32.5 11.3 %collective-permute-start.3 = (bf16[2,144,128]{2,1,0:T(8,128)(2,1)S(1)}, bf16[2,144,128]{2,1,0:T(8,128)(2,1)S(1)}, u32[]{:S(2)}, u32[]{:S(2)}) collective-permute-start(bf16[2,144,128]{2,1,0:T(8,128)(2,1)S(1)} %pad_maximum_fusion.13), channel_id=1, source_target_pairs={{0,4},{2,6},{4,0},{6,2},{1,5},{3,7},{5,1},{7,3},{8,12},{10,14},{12... | collective-permute-start | bytes 221192 | tf_op jit(solution)/shard_map/ppermute | solution.py:46
  39.4 9.0 %collective-permute-start.8 = (bf16[2,128,128]{2,1,0:T(8,128)(2,1)S(1)}, bf16[2,128,128]{2,1,0:T(8,128)(2,1)S(1)}, u32[]{:S(2)}, u32[]{:S(2)}) collective-permute-start(bf16[2,128,128]{2,1,0:T(8,128)(2,1)S(1)} %pad_maximum_fusion.14), channel_id=1, source_target_pairs={{0,64},{16,80},{32,96},{48,112},{64,0},{80,16},{96,32},{112,48},{1... | collective-permute-start | bytes 196616 | tf_op jit(solution)/shard_map/ppermute | solution.py:46
  43.8 6.5 %copy-start.4 = (f32[1024]{0:T(1024)S(1)}, f32[1024]{0:T(1024)}, u32[]{:S(2)}) copy-start(f32[1024]{0:T(1024)} %param.9) | copy-start | bytes 12292
  44.2 7.9 %collective-permute-start.5 = (bf16[1088,128]{1,0:T(8,128)(2,1)S(1)}, bf16[1088,128]{1,0:T(8,128)(2,1)S(1)}, u32[]{:S(2)}, u32[]{:S(2)}) collective-permute-start(bf16[1088,128]{1,0:T(8,128)(2,1)S(1)} %pad_maximum_fusion.5), channel_id=1, source_target_pairs={{0,128},{128,0},{256,384},{384,256},{1,129},{129,1},{257,385},{385... | collective-permute-start | bytes 835592 | tf_op jit(solution)/shard_map/ppermute | solution.py:46
  48.4 6.6 %collective-permute-start.9 = (bf16[2,2,128,128]{3,2,1,0:T(8,128)(2,1)S(1)}, bf16[2,2,128,128]{3,2,1,0:T(8,128)(2,1)S(1)}, u32[]{:S(2)}, u32[]{:S(2)}) collective-permute-start(bf16[2,2,128,128]{3,2,1,0:T(8,128)(2,1)S(1)} %pad_maximum_fusion.11), channel_id=1, source_target_pairs={{0,32},{16,48},{32,0},{48,16},{64,96},{80,112},{96,64},{112,80},{1... | collective-permute-start | bytes 393224 | tf_op jit(solution)/shard_map/ppermute | solution.py:46
  52.1 8.7 %collective-permute-start.6 = (bf16[2,4,144,128]{3,2,1,0:T(8,128)(2,1)S(1)}, bf16[2,4,144,128]{3,2,1,0:T(8,128)(2,1)S(1)}, u32[]{:S(2)}, u32[]{:S(2)}) collective-permute-start(bf16[2,4,144,128]{3,2,1,0:T(8,128)(2,1)S(1)} %pad_maximum_fusion.4), channel_id=1, source_target_pairs={{0,384},{128,256},{256,128},{384,0},{1,385},{129,257},{257,129},{3... | collective-permute-start | bytes 884744 | tf_op jit(solution)/shard_map/ppermute | solution.py:46
  55.1 12.2 %collective-permute-start.10 = (bf16[2,2,2,128,128]{4,3,2,0,1:T(8,128)(2,1)S(1)}, bf16[2,2,2,128,128]{4,3,2,0,1:T(8,128)(2,1)S(1)}, u32[]{:S(2)}, u32[]{:S(2)}) collective-permute-start(bf16[2,2,2,128,128]{4,3,2,0,1:T(8,128)(2,1)S(1)} %pad_maximum_fusion.6), channel_id=1, source_target_pairs={{0,16},{16,0},{32,48},{48,32},{64,80},{80,64},{96,112},{112,96},{1... | collective-permute-start | bytes 786440 | tf_op jit(solution)/shard_map/ppermute | solution.py:46
  60.9 7.7 %collective-permute-start.7 = (bf16[4,4,144,128]{3,2,1,0:T(8,128)(2,1)S(1)}, bf16[4,4,144,128]{3,2,1,0:T(8,128)(2,1)S(1)}, u32[]{:S(2)}, u32[]{:S(2)}) collective-permute-start(bf16[4,4,144,128]{3,2,1,0:T(8,128)(2,1)S(1)} %get-tuple-element.24), channel_id=1, source_target_pairs={{0,1},{1,0},{2,3},{3,2},{4,5},{5,4},{6,7},{7,6},{8,9},{9,8},{10,11... | collective-permute-start | bytes 1769480 | tf_op jit(solution)/shard_map/ppermute | solution.py:46
  68.9 0.8 copy-start.2
  71.5 30.2 %all-to-all-start = ((bf16[16,136,128]{2,1,0:T(8,128)(2,1)}), bf16[16,136,128]{2,1,0:T(8,128)(2,1)S(1)}, u32[]{:S(2)}, u32[]{:S(2)}) async-start(bf16[16,136,128]{2,1,0:T(8,128)(2,1)} %pad_maximum_fusion.2), calls=%async_computation | async-start | bytes 1114112 | tf_op jit(solution)/shard_map/all_to_all | solution.py:41
  80.8 7.5 %collective-permute-start.11 = (bf16[512,128]{1,0:T(8,128)(2,1)S(1)}, bf16[512,128]{1,0:T(8,128)(2,1)S(1)}, u32[]{:S(2)}, u32[]{:S(2)}) collective-permute-start(bf16[512,128]{1,0:T(8,128)(2,1)S(1)} %bitcast.158), channel_id=1, source_target_pairs={{0,384},{128,256},{256,128},{384,0},{1,385},{129,257},{257,129},{3... | collective-permute-start | bytes 393224 | tf_op jit(solution)/shard_map/ppermute | solution.py:46
  88.6 6.0 %collective-permute-start.12 = (bf16[512,128]{1,0:T(8,128)(2,1)S(1)}, bf16[512,128]{1,0:T(8,128)(2,1)S(1)}, u32[]{:S(2)}, u32[]{:S(2)}) collective-permute-start(bf16[512,128]{1,0:T(8,128)(2,1)S(1)} %bitcast.157), channel_id=1, source_target_pairs={{0,128},{128,0},{256,384},{384,256},{1,129},{129,1},{257,385},{385... | collective-permute-start | bytes 393224 | tf_op jit(solution)/shard_map/ppermute | solution.py:46
  94.7 29.7 %copy-start.1 = (bf16[128,1024]{1,0:T(8,128)(2,1)S(1)}, bf16[128,1024]{1,0:T(8,128)(2,1)}, u32[]{:S(2)}) copy-start(bf16[128,1024]{1,0:T(8,128)(2,1)} %param.6) | copy-start | bytes 786436
  101.8 10.6 %collective-permute-start.13 = (f32[128]{0:T(128)S(1)}, f32[128]{0:T(128)S(1)}, u32[]{:S(2)}, u32[]{:S(2)}) collective-permute-start(f32[128]{0:T(128)S(1)} %fusion.4), channel_id=1, source_target_pairs={{0,1},{1,0},{2,3},{3,2},{4,5},{5,4},{6,7},{7,6},{8,9},{9,8},{10,11... | collective-permute-start | bytes 1544 | tf_op jit(solution)/shard_map/ppermute | solution.py:46
  105.9 17.9 %collective-permute-start.14 = (f32[128,128]{1,0:T(8,128)S(1)}, f32[128,128]{1,0:T(8,128)S(1)}, u32[]{:S(2)}, u32[]{:S(2)}) collective-permute-start(f32[128,128]{1,0:T(8,128)S(1)} %convert_reduce_fusion.1), channel_id=1, source_target_pairs={{0,0},{16,1},{32,2},{48,3},{64,4},{80,5},{96,6},{112,7},{8,8},{24,... | collective-permute-start | bytes 196616 | tf_op jit(solution)/shard_map/ppermute | solution.py:146
  113.0 10.7 %all-to-all-start.1 = ((f32[16,3,128]{2,1,0:T(4,128)}), f32[16,3,128]{2,1,0:T(4,128)S(1)}, u32[]{:S(2)}, u32[]{:S(2)}) async-start(f32[16,3,128]{2,1,0:T(4,128)} %broadcast_in_dim.14), calls=%async_computation.1 | async-start | bytes 65536 | tf_op jit(solution)/shard_map/all_to_all | solution.py:41

commit v12 on v8

--- a/solution.py
+++ b/solution.py
@@ -65,6 +65,7 @@
     mine = lax.axis_index("x")
 
     moved = lax.ppermute(kv_weight, AXES, moves)
+    other = lax.ppermute(kv_weight, AXES, [(a, b ^ 8) for a, b in moves])
 
     cosine, sine = rope_tables(TOK, HD)
     grads = key_value_grad.astype(jnp.float32)
@@ -80,12 +81,13 @@
     def quarter(r):
         return lax.dynamic_slice_in_dim(blocks, (mine ^ r) * 2, 2, axis=0)
 
-    packet, moved = lax.optimization_barrier((packet, moved))
     packet = jnp.concatenate([packet, swap(packet, "zl", 1)])
-    weights = moved
-    for axis, mask, place in (("zh", 1, 0), ("y", 4, 0), ("y", 2, 1), ("y", 1, 2)):
-        other = swap(weights, axis, mask)
-        first = (lax.axis_index(axis) & mask) == 0
+    packet, moved, other = lax.optimization_barrier((packet, moved, other))
+    first = lax.axis_index("zh") == 0
+    weights = jnp.stack([jnp.where(first, moved, other), jnp.where(first, other, moved)])
+    for mask, place in ((4, 0), (2, 1), (1, 2)):
+        other = swap(weights, "y", mask)
+        first = (lax.axis_index("y") & mask) == 0
         pair = [jnp.where(first, weights, other), jnp.where(first, other, weights)]
         weights = jnp.stack(pair, axis=place)
     weights = weights.reshape(8, 2, HD, HD)
@@ -123,7 +125,7 @@
     pieces = jnp.einsum(
         "ktc,btf->kbcf", kv, normed, preferred_element_type=jnp.float32
     ).astype(jnp.bfloat16)
-    gain_rows = jnp.broadcast_to(jnp.pad(gain_part, ((0, 10), (0, 0)))[None], (16, 16, HD))
+    gain_rows = jnp.broadcast_to(jnp.pad(gain_part, ((0, 2), (0, 0)))[None], (16, 8, HD))
     arrived = exchange(jnp.concatenate([pieces.reshape(16, HD, HD), gain_rows], axis=1), ROW)
     block = jnp.sum(arrived[:, :HD].astype(jnp.float32), axis=0)
     weight_grad = lax.ppermute(block, AXES, [(b, a) for a, b in moves])

time: 125 us -> 124 us (level)
  other arithmetic: 4.41 us -> 5.92 us
  starting transfers between devices: 78.3 us -> 76.8 us
    ppermute x15 -> x14, starting transfers between devices: 57.8 us -> 38.6 us  [swap(): return lax.ppermute(value, axis, [(i, i ^ mask) for i in range(count)])]
    ppermute x0 -> x1, starting transfers between devices: none -> 17.3 us  [shards(): other = lax.ppermute(kv_weight, AXES, [(a, b ^ 8) for a, b in moves])]
    ppermute x1, waiting for transfers between devices: 2.71 us -> 0.01 us  [shards(): moved = lax.ppermute(kv_weight, AXES, moves)]
    ppermute x15 -> x14, waiting for transfers between devices: 25.3 us -> 27.9 us  [swap(): return lax.ppermute(value, axis, [(i, i ^ mask) for i in range(count)])]
  transfers between devices with their start and end apart: 19 -> 19, of which waited for: 13 -> 11; matrix products, arithmetic and copies ran while one was open for 6% -> 7% of each run, Pallas kernels for 0% -> 0%
where the time goes in v12:
time: 124 us; the launch traced here: 123 us
  starting transfers between devices  76.8 us (62%)
  waiting for transfers between devices  32.2 us (26%)
  other arithmetic  5.92 us (5%)
  local copies, waits for them, and re-layouts  5.85 us (5%)
  between operations  1.4 us (1%)
  matrix products  1.32 us (1%)
    ppermute x14, starting transfers between devices, swap(): return lax.ppermute(value, axis, [(i, i ^ mask) for i in range(count)])  38.6 us
    ppermute x14, waiting for transfers between devices, swap(): return lax.ppermute(value, axis, [(i, i ^ mask) for i in range(count)])  27.9 us
    ppermute x1, starting transfers between devices, shards(): other = lax.ppermute(kv_weight, AXES, [(a, b ^ 8) for a, b in moves])  17.3 us
    all_to_all x2, starting transfers between devices, exchange(): return lax.all_to_all(value, axes, split_axis=0, concat_axis=0, tiled=True)  11.8 us
    ppermute x1, starting transfers between devices, shards(): moved = lax.ppermute(kv_weight, AXES, moves)  4.7 us
    all_to_all x2, waiting for transfers between devices, exchange(): return lax.all_to_all(value, axes, split_axis=0, concat_axis=0, tiled=True)  4.34 us
    ppermute x1, starting transfers between devices, shards(): weight_grad = lax.ppermute(block, AXES, [(b, a) for a, b in moves])  4.27 us
  transfers between devices with their start and end apart: 19, of which 11 were waited for; matrix products, arithmetic and copies ran while one was open for 7% of the time, Pallas kernels for 0%

profile of v12, /device:TPU:48, one launch (start us, length us, event | category | flops | bytes accessed | tf_op | source)
XLA Modules:
  0.0 123.4 jit_solution(8502586160470400683)
XLA Ops:
  0.6 4.7 %collective-permute-start.1 = (bf16[128,128]{1,0:T(8,128)(2,1)}, bf16[128,128]{1,0:T(8,128)(2,1)S(1)}, u32[]{:S(2)}, u32[]{:S(2)}) collective-permute-start(bf16[128,128]{1,0:T(8,128)(2,1)} %param.8), channel_id=1, source_target_pairs={{0,0},{1,16},{2,32},{3,48},{4,64},{5,80},{6,96},{7,112},{8,8},{9,2... | collective-permute-start | bytes 98312 | tf_op jit(solution)/shard_map/ppermute | solution.py:67
  5.3 17.3 %collective-permute-start.2 = (bf16[128,128]{1,0:T(8,128)(2,1)}, bf16[128,128]{1,0:T(8,128)(2,1)S(1)}, u32[]{:S(2)}, u32[]{:S(2)}) collective-permute-start(bf16[128,128]{1,0:T(8,128)(2,1)} %param.8), channel_id=1, source_target_pairs={{0,8},{1,24},{2,40},{3,56},{4,72},{5,88},{6,104},{7,120},{8,0},{9,... | collective-permute-start | bytes 98312 | tf_op jit(solution)/shard_map/ppermute | solution.py:68
  22.7 1.1 fusion.9
  23.8 0.8 convert_element_type.61
  24.6 0.3 multiply_add_fusion
  24.9 0.9 fusion.15
  25.7 2.3 %collective-permute-start = (bf16[1,144,128]{2,1,0:T(8,128)(2,1)S(1)}, bf16[1,144,128]{2,1,0:T(8,128)(2,1)S(1)}, u32[]{:S(2)}, u32[]{:S(2)}) collective-permute-start(bf16[1,144,128]{2,1,0:T(8,128)(2,1)S(1)} %maximum_bitcast_fusion), channel_id=1, source_target_pairs={{0,2},{2,0},{4,6},{6,4},{1,3},{3,1},{5,7},{7,5},{8,10},{10,8},{12,... | collective-permute-start | bytes 110600 | tf_op jit(solution)/shard_map/ppermute | solution.py:46
  28.0 0.9 fusion.30
  28.9 0.1 copy.82
  29.1 0.1 copy.83
  29.2 0.1 copy.84
  29.3 0.1 copy.85
  29.4 0.1 copy.86
  29.6 0.1 copy.87
  29.7 0.1 copy.88
  29.8 0.1 copy.89
  30.1 0.1 copy.61
  30.3 1.9 %collective-permute-start.4 = (bf16[512,128]{1,0:T(8,128)(2,1)S(1)}, bf16[512,128]{1,0:T(8,128)(2,1)S(1)}, u32[]{:S(2)}, u32[]{:S(2)}) collective-permute-start(bf16[512,128]{1,0:T(8,128)(2,1)S(1)} %bitcast.147), channel_id=1, source_target_pairs={{0,384},{128,256},{256,128},{384,0},{1,385},{129,257},{257,129},{3... | collective-permute-start | bytes 393224 | tf_op jit(solution)/shard_map/ppermute | solution.py:46
  32.2 1.9 %collective-permute-start.3 = (bf16[2,144,128]{2,1,0:T(8,128)(2,1)S(1)}, bf16[2,144,128]{2,1,0:T(8,128)(2,1)S(1)}, u32[]{:S(2)}, u32[]{:S(2)}) collective-permute-start(bf16[2,144,128]{2,1,0:T(8,128)(2,1)S(1)} %pad_maximum_fusion.13), channel_id=1, source_target_pairs={{0,4},{2,6},{4,0},{6,2},{1,5},{3,7},{5,1},{7,3},{8,12},{10,14},{12... | collective-permute-start | bytes 221192 | tf_op jit(solution)/shard_map/ppermute | solution.py:46
  34.2 4.1 %collective-permute-start.8 = (bf16[2,128,128]{2,1,0:T(8,128)(2,1)S(1)}, bf16[2,128,128]{2,1,0:T(8,128)(2,1)S(1)}, u32[]{:S(2)}, u32[]{:S(2)}) collective-permute-start(bf16[2,128,128]{2,1,0:T(8,128)(2,1)S(1)} %pad_maximum_fusion.14), channel_id=1, source_target_pairs={{0,64},{16,80},{32,96},{48,112},{64,0},{80,16},{96,32},{112,48},{1... | collective-permute-start | bytes 196616 | tf_op jit(solution)/shard_map/ppermute | solution.py:46
  38.3 2.5 %collective-permute-done.3 = bf16[2,144,128]{2,1,0:T(8,128)(2,1)S(1)} collective-permute-done((bf16[2,144,128]{2,1,0:T(8,128)(2,1)S(1)}, bf16[2,144,128]{2,1,0:T(8,128)(2,1)S(1)}, u32[]{:S(2)}, u32[]{:S(2)}) %collective-permute-start.3) | collective-permute-done | bytes 73760 | tf_op jit(solution)/shard_map/ppermute | solution.py:46
  40.9 0.1 copy.62
  41.0 0.1 copy.63
  41.2 1.9 %collective-permute-start.5 = (bf16[1088,128]{1,0:T(8,128)(2,1)S(1)}, bf16[1088,128]{1,0:T(8,128)(2,1)S(1)}, u32[]{:S(2)}, u32[]{:S(2)}) collective-permute-start(bf16[1088,128]{1,0:T(8,128)(2,1)S(1)} %pad_maximum_fusion.5), channel_id=1, source_target_pairs={{0,128},{128,0},{256,384},{384,256},{1,129},{129,1},{257,385},{385... | collective-permute-start | bytes 835592 | tf_op jit(solution)/shard_map/ppermute | solution.py:46
  43.1 1.2 collective-permute-done.8
  44.3 5.2 %collective-permute-start.9 = (bf16[2,2,128,128]{3,2,1,0:T(8,128)(2,1)S(1)}, bf16[2,2,128,128]{3,2,1,0:T(8,128)(2,1)S(1)}, u32[]{:S(2)}, u32[]{:S(2)}) collective-permute-start(bf16[2,2,128,128]{3,2,1,0:T(8,128)(2,1)S(1)} %pad_maximum_fusion.11), channel_id=1, source_target_pairs={{0,32},{16,48},{32,0},{48,16},{64,96},{80,112},{96,64},{112,80},{1... | collective-permute-start | bytes 393224 | tf_op jit(solution)/shard_map/ppermute | solution.py:46
  49.6 0.1 copy.71
  49.7 1.8 %collective-permute-done.5 = bf16[1088,128]{1,0:T(8,128)(2,1)S(1)} collective-permute-done((bf16[1088,128]{1,0:T(8,128)(2,1)S(1)}, bf16[1088,128]{1,0:T(8,128)(2,1)S(1)}, u32[]{:S(2)}, u32[]{:S(2)}) %collective-permute-start.5) | collective-permute-done | bytes 278560 | tf_op jit(solution)/shard_map/ppermute | solution.py:46
  51.7 3.8 %collective-permute-start.6 = (bf16[2,4,144,128]{3,2,1,0:T(8,128)(2,1)S(1)}, bf16[2,4,144,128]{3,2,1,0:T(8,128)(2,1)S(1)}, u32[]{:S(2)}, u32[]{:S(2)}) collective-permute-start(bf16[2,4,144,128]{3,2,1,0:T(8,128)(2,1)S(1)} %pad_maximum_fusion.4), channel_id=1, source_target_pairs={{0,384},{128,256},{256,128},{384,0},{1,385},{129,257},{257,129},{3... | collective-permute-start | bytes 884744 | tf_op jit(solution)/shard_map/ppermute | solution.py:46
  55.5 2.4 %collective-permute-start.10 = (bf16[2,2,2,128,128]{4,3,2,0,1:T(8,128)(2,1)S(1)}, bf16[2,2,2,128,128]{4,3,2,0,1:T(8,128)(2,1)S(1)}, u32[]{:S(2)}, u32[]{:S(2)}) collective-permute-start(bf16[2,2,2,128,128]{4,3,2,0,1:T(8,128)(2,1)S(1)} %pad_maximum_fusion.6), channel_id=1, source_target_pairs={{0,16},{16,0},{32,48},{48,32},{64,80},{80,64},{96,112},{112,96},{1... | collective-permute-start | bytes 786440 | tf_op jit(solution)/shard_map/ppermute | solution.py:46
  57.9 4.9 %collective-permute-done.6 = bf16[2,4,144,128]{3,2,1,0:T(8,128)(2,1)S(1)} collective-permute-done((bf16[2,4,144,128]{3,2,1,0:T(8,128)(2,1)S(1)}, bf16[2,4,144,128]{3,2,1,0:T(8,128)(2,1)S(1)}, u32[]{:S(2)}, u32[]{:S(2)}) %collective-permute-start.6) | collective-permute-done | bytes 294944 | tf_op jit(solution)/shard_map/ppermute | solution.py:46
  62.9 1.9 %collective-permute-start.7 = (bf16[4,4,144,128]{3,2,1,0:T(8,128)(2,1)S(1)}, bf16[4,4,144,128]{3,2,1,0:T(8,128)(2,1)S(1)}, u32[]{:S(2)}, u32[]{:S(2)}) collective-permute-start(bf16[4,4,144,128]{3,2,1,0:T(8,128)(2,1)S(1)} %get-tuple-element.14), channel_id=1, source_target_pairs={{0,1},{1,0},{2,3},{3,2},{4,5},{5,4},{6,7},{7,6},{8,9},{9,8},{10,11... | collective-permute-start | bytes 1769480 | tf_op jit(solution)/shard_map/ppermute | solution.py:46
  64.8 0.1 copy.70
  64.9 0.1 copy.72
  65.2 0.3 copy.64
  65.5 1.3 %collective-permute-done.7 = bf16[4,4,144,128]{3,2,1,0:T(8,128)(2,1)S(1)} collective-permute-done((bf16[4,4,144,128]{3,2,1,0:T(8,128)(2,1)S(1)}, bf16[4,4,144,128]{3,2,1,0:T(8,128)(2,1)S(1)}, u32[]{:S(2)}, u32[]{:S(2)}) %collective-permute-start.7) | collective-permute-done | bytes 589856 | tf_op jit(solution)/shard_map/ppermute | solution.py:46
  66.8 0.1 fusion.1
  67.0 0.7 convert_reduce_fusion
  67.7 0.2 fusion.10
  67.9 0.6 fusion
  68.6 0.8 pad_maximum_fusion.2
  69.5 5.6 %all-to-all-start = ((bf16[16,136,128]{2,1,0:T(8,128)(2,1)}), bf16[16,136,128]{2,1,0:T(8,128)(2,1)S(1)}, u32[]{:S(2)}, u32[]{:S(2)}) async-start(bf16[16,136,128]{2,1,0:T(8,128)(2,1)} %pad_maximum_fusion.2), calls=%async_computation | async-start | bytes 1114112 | tf_op jit(solution)/shard_map/all_to_all | solution.py:41
  75.1 0.1 copy.67
  75.2 3.3 %collective-permute-start.11 = (bf16[512,128]{1,0:T(8,128)(2,1)S(1)}, bf16[512,128]{1,0:T(8,128)(2,1)S(1)}, u32[]{:S(2)}, u32[]{:S(2)}) collective-permute-start(bf16[512,128]{1,0:T(8,128)(2,1)S(1)} %bitcast.151), channel_id=1, source_target_pairs={{0,384},{128,256},{256,128},{384,0},{1,385},{129,257},{257,129},{3... | collective-permute-start | bytes 393224 | tf_op jit(solution)/shard_map/ppermute | solution.py:46
  78.6 4.7 %collective-permute-done.11 = bf16[512,128]{1,0:T(8,128)(2,1)S(1)} collective-permute-done((bf16[512,128]{1,0:T(8,128)(2,1)S(1)}, bf16[512,128]{1,0:T(8,128)(2,1)S(1)}, u32[]{:S(2)}, u32[]{:S(2)}) %collective-permute-start.11) | collective-permute-done | bytes 131104 | tf_op jit(solution)/shard_map/ppermute | solution.py:46
  83.3 0.1 copy.90
  83.5 0.1 copy.69
  83.6 1.9 %collective-permute-start.12 = (bf16[512,128]{1,0:T(8,128)(2,1)S(1)}, bf16[512,128]{1,0:T(8,128)(2,1)S(1)}, u32[]{:S(2)}, u32[]{:S(2)}) collective-permute-start(bf16[512,128]{1,0:T(8,128)(2,1)S(1)} %bitcast.150), channel_id=1, source_target_pairs={{0,128},{128,0},{256,384},{384,256},{1,129},{129,1},{257,385},{385... | collective-permute-start | bytes 393224 | tf_op jit(solution)/shard_map/ppermute | solution.py:46
  85.6 0.1 copy.66
  85.8 4.7 %collective-permute-done.12 = bf16[512,128]{1,0:T(8,128)(2,1)S(1)} collective-permute-done((bf16[512,128]{1,0:T(8,128)(2,1)S(1)}, bf16[512,128]{1,0:T(8,128)(2,1)S(1)}, u32[]{:S(2)}, u32[]{:S(2)}) %collective-permute-start.12) | collective-permute-done | bytes 131104 | tf_op jit(solution)/shard_map/ppermute | solution.py:46
  90.7 0.2 fusion.4
  90.9 1.9 %collective-permute-start.13 = (f32[128]{0:T(128)S(1)}, f32[128]{0:T(128)S(1)}, u32[]{:S(2)}, u32[]{:S(2)}) collective-permute-start(f32[128]{0:T(128)S(1)} %fusion.4), channel_id=1, source_target_pairs={{0,1},{1,0},{2,3},{3,2},{4,5},{5,4},{6,7},{7,6},{8,9},{9,8},{10,11... | collective-permute-start | bytes 1544 | tf_op jit(solution)/shard_map/ppermute | solution.py:46
  92.9 1.1 collective-permute-done.13
  94.0 3.1 %collective-permute-start.14 = (f32[128]{0:T(128)S(1)}, f32[128]{0:T(128)S(1)}, u32[]{:S(2)}, u32[]{:S(2)}) collective-permute-start(f32[128]{0:T(128)S(1)} %add.56), channel_id=1, source_target_pairs={{0,2},{2,0},{4,6},{6,4},{1,3},{3,1},{5,7},{7,5},{8,10},{10,8},{12,... | collective-permute-start | bytes 1544 | tf_op jit(solution)/shard_map/ppermute | solution.py:46
  97.1 2.3 %collective-permute-done.14 = f32[128]{0:T(128)S(1)} collective-permute-done((f32[128]{0:T(128)S(1)}, f32[128]{0:T(128)S(1)}, u32[]{:S(2)}, u32[]{:S(2)}) %collective-permute-start.14) | collective-permute-done | bytes 544 | tf_op jit(solution)/shard_map/ppermute | solution.py:46
  99.4 3.0 %collective-permute-start.15 = (f32[128]{0:T(128)S(1)}, f32[128]{0:T(128)S(1)}, u32[]{:S(2)}, u32[]{:S(2)}) collective-permute-start(f32[128]{0:T(128)S(1)} %add.57), channel_id=1, source_target_pairs={{0,4},{2,6},{4,0},{6,2},{1,5},{3,7},{5,1},{7,3},{8,12},{10,14},{12... | collective-permute-start | bytes 1544 | tf_op jit(solution)/shard_map/ppermute | solution.py:46
  102.4 3.3 %collective-permute-done.15 = f32[128]{0:T(128)S(1)} collective-permute-done((f32[128]{0:T(128)S(1)}, f32[128]{0:T(128)S(1)}, u32[]{:S(2)}, u32[]{:S(2)}) %collective-permute-start.15) | collective-permute-done | bytes 544 | tf_op jit(solution)/shard_map/ppermute | solution.py:46
  105.8 4.3 %collective-permute-start.16 = (f32[128,128]{1,0:T(8,128)S(1)}, f32[128,128]{1,0:T(8,128)S(1)}, u32[]{:S(2)}, u32[]{:S(2)}) collective-permute-start(f32[128,128]{1,0:T(8,128)S(1)} %convert_reduce_fusion.1), channel_id=1, source_target_pairs={{0,0},{16,1},{32,2},{48,3},{64,4},{80,5},{96,6},{112,7},{8,8},{24,... | collective-permute-start | bytes 196616 | tf_op jit(solution)/shard_map/ppermute | solution.py:131
  110.1 0.6 broadcast_in_dim.11
  110.7 6.2 %all-to-all-start.1 = ((f32[4,2,128]{2,1,0:T(2,128)}), f32[4,2,128]{2,1,0:T(2,128)S(1)}, u32[]{:S(2)}, u32[]{:S(2)}) async-start(f32[4,2,128]{2,1,0:T(2,128)} %broadcast_in_dim.11), calls=%async_computation.1 | async-start | bytes 8192 | tf_op jit(solution)/shard_map/all_to_all | solution.py:41
  116.9 1.0 fusion.8
  117.9 4.3 %all-to-all-done.1 = f32[4,2,128]{2,1,0:T(2,128)S(1)} async-done(((f32[4,2,128]{2,1,0:T(2,128)}), f32[4,2,128]{2,1,0:T(2,128)S(1)}, u32[]{:S(2)}, u32[]{:S(2)}) %all-to-all-start.1) | async-done | bytes 4128 | tf_op jit(solution)/shard_map/all_to_all | solution.py:41
  122.2 0.6 copy.111
  122.9 0.6 copy.112
  (82 shorter events, 1.3 us)
Async XLA Ops:
  0.6 31.6 %collective-permute-start.1 = (bf16[128,128]{1,0:T(8,128)(2,1)}, bf16[128,128]{1,0:T(8,128)(2,1)S(1)}, u32[]{:S(2)}, u32[]{:S(2)}) collective-permute-start(bf16[128,128]{1,0:T(8,128)(2,1)} %param.8), channel_id=1, source_target_pairs={{0,0},{1,16},{2,32},{3,48},{4,64},{5,80},{6,96},{7,112},{8,8},{9,2... | collective-permute-start | bytes 98312 | tf_op jit(solution)/shard_map/ppermute | solution.py:67
  5.3 26.9 %collective-permute-start.2 = (bf16[128,128]{1,0:T(8,128)(2,1)}, bf16[128,128]{1,0:T(8,128)(2,1)S(1)}, u32[]{:S(2)}, u32[]{:S(2)}) collective-permute-start(bf16[128,128]{1,0:T(8,128)(2,1)} %param.8), channel_id=1, source_target_pairs={{0,8},{1,24},{2,40},{3,56},{4,72},{5,88},{6,104},{7,120},{8,0},{9,... | collective-permute-start | bytes 98312 | tf_op jit(solution)/shard_map/ppermute | solution.py:68
  25.7 6.5 %collective-permute-start = (bf16[1,144,128]{2,1,0:T(8,128)(2,1)S(1)}, bf16[1,144,128]{2,1,0:T(8,128)(2,1)S(1)}, u32[]{:S(2)}, u32[]{:S(2)}) collective-permute-start(bf16[1,144,128]{2,1,0:T(8,128)(2,1)S(1)} %maximum_bitcast_fusion), channel_id=1, source_target_pairs={{0,2},{2,0},{4,6},{6,4},{1,3},{3,1},{5,7},{7,5},{8,10},{10,8},{12,... | collective-permute-start | bytes 110600 | tf_op jit(solution)/shard_map/ppermute | solution.py:46
  30.3 10.6 %collective-permute-start.4 = (bf16[512,128]{1,0:T(8,128)(2,1)S(1)}, bf16[512,128]{1,0:T(8,128)(2,1)S(1)}, u32[]{:S(2)}, u32[]{:S(2)}) collective-permute-start(bf16[512,128]{1,0:T(8,128)(2,1)S(1)} %bitcast.147), channel_id=1, source_target_pairs={{0,384},{128,256},{256,128},{384,0},{1,385},{129,257},{257,129},{3... | collective-permute-start | bytes 393224 | tf_op jit(solution)/shard_map/ppermute | solution.py:46
  32.2 8.6 %collective-permute-start.3 = (bf16[2,144,128]{2,1,0:T(8,128)(2,1)S(1)}, bf16[2,144,128]{2,1,0:T(8,128)(2,1)S(1)}, u32[]{:S(2)}, u32[]{:S(2)}) collective-permute-start(bf16[2,144,128]{2,1,0:T(8,128)(2,1)S(1)} %pad_maximum_fusion.13), channel_id=1, source_target_pairs={{0,4},{2,6},{4,0},{6,2},{1,5},{3,7},{5,1},{7,3},{8,12},{10,14},{12... | collective-permute-start | bytes 221192 | tf_op jit(solution)/shard_map/ppermute | solution.py:46
  34.2 10.1 %collective-permute-start.8 = (bf16[2,128,128]{2,1,0:T(8,128)(2,1)S(1)}, bf16[2,128,128]{2,1,0:T(8,128)(2,1)S(1)}, u32[]{:S(2)}, u32[]{:S(2)}) collective-permute-start(bf16[2,128,128]{2,1,0:T(8,128)(2,1)S(1)} %pad_maximum_fusion.14), channel_id=1, source_target_pairs={{0,64},{16,80},{32,96},{48,112},{64,0},{80,16},{96,32},{112,48},{1... | collective-permute-start | bytes 196616 | tf_op jit(solution)/shard_map/ppermute | solution.py:46
  40.8 8.7 %copy-start.2 = (f32[1024]{0:T(1024)S(1)}, f32[1024]{0:T(1024)}, u32[]{:S(2)}) copy-start(f32[1024]{0:T(1024)} %param.9) | copy-start | bytes 12292
  41.2 10.4 %collective-permute-start.5 = (bf16[1088,128]{1,0:T(8,128)(2,1)S(1)}, bf16[1088,128]{1,0:T(8,128)(2,1)S(1)}, u32[]{:S(2)}, u32[]{:S(2)}) collective-permute-start(bf16[1088,128]{1,0:T(8,128)(2,1)S(1)} %pad_maximum_fusion.5), channel_id=1, source_target_pairs={{0,128},{128,0},{256,384},{384,256},{1,129},{129,1},{257,385},{385... | collective-permute-start | bytes 835592 | tf_op jit(solution)/shard_map/ppermute | solution.py:46
  44.3 11.1 %collective-permute-start.9 = (bf16[2,2,128,128]{3,2,1,0:T(8,128)(2,1)S(1)}, bf16[2,2,128,128]{3,2,1,0:T(8,128)(2,1)S(1)}, u32[]{:S(2)}, u32[]{:S(2)}) collective-permute-start(bf16[2,2,128,128]{3,2,1,0:T(8,128)(2,1)S(1)} %pad_maximum_fusion.11), channel_id=1, source_target_pairs={{0,32},{16,48},{32,0},{48,16},{64,96},{80,112},{96,64},{112,80},{1... | collective-permute-start | bytes 393224 | tf_op jit(solution)/shard_map/ppermute | solution.py:46
  51.7 11.1 %collective-permute-start.6 = (bf16[2,4,144,128]{3,2,1,0:T(8,128)(2,1)S(1)}, bf16[2,4,144,128]{3,2,1,0:T(8,128)(2,1)S(1)}, u32[]{:S(2)}, u32[]{:S(2)}) collective-permute-start(bf16[2,4,144,128]{3,2,1,0:T(8,128)(2,1)S(1)} %pad_maximum_fusion.4), channel_id=1, source_target_pairs={{0,384},{128,256},{256,128},{384,0},{1,385},{129,257},{257,129},{3... | collective-permute-start | bytes 884744 | tf_op jit(solution)/shard_map/ppermute | solution.py:46
  55.5 9.6 %collective-permute-start.10 = (bf16[2,2,2,128,128]{4,3,2,0,1:T(8,128)(2,1)S(1)}, bf16[2,2,2,128,128]{4,3,2,0,1:T(8,128)(2,1)S(1)}, u32[]{:S(2)}, u32[]{:S(2)}) collective-permute-start(bf16[2,2,2,128,128]{4,3,2,0,1:T(8,128)(2,1)S(1)} %pad_maximum_fusion.6), channel_id=1, source_target_pairs={{0,16},{16,0},{32,48},{48,32},{64,80},{80,64},{96,112},{112,96},{1... | collective-permute-start | bytes 786440 | tf_op jit(solution)/shard_map/ppermute | solution.py:46
  62.9 3.9 %collective-permute-start.7 = (bf16[4,4,144,128]{3,2,1,0:T(8,128)(2,1)S(1)}, bf16[4,4,144,128]{3,2,1,0:T(8,128)(2,1)S(1)}, u32[]{:S(2)}, u32[]{:S(2)}) collective-permute-start(bf16[4,4,144,128]{3,2,1,0:T(8,128)(2,1)S(1)} %get-tuple-element.14), channel_id=1, source_target_pairs={{0,1},{1,0},{2,3},{3,2},{4,5},{5,4},{6,7},{7,6},{8,9},{9,8},{10,11... | collective-permute-start | bytes 1769480 | tf_op jit(solution)/shard_map/ppermute | solution.py:46
  69.5 36.2 %all-to-all-start = ((bf16[16,136,128]{2,1,0:T(8,128)(2,1)}), bf16[16,136,128]{2,1,0:T(8,128)(2,1)S(1)}, u32[]{:S(2)}, u32[]{:S(2)}) async-start(bf16[16,136,128]{2,1,0:T(8,128)(2,1)} %pad_maximum_fusion.2), calls=%async_computation | async-start | bytes 1114112 | tf_op jit(solution)/shard_map/all_to_all | solution.py:41
  75.2 8.1 %collective-permute-start.11 = (bf16[512,128]{1,0:T(8,128)(2,1)S(1)}, bf16[512,128]{1,0:T(8,128)(2,1)S(1)}, u32[]{:S(2)}, u32[]{:S(2)}) collective-permute-start(bf16[512,128]{1,0:T(8,128)(2,1)S(1)} %bitcast.151), channel_id=1, source_target_pairs={{0,384},{128,256},{256,128},{384,0},{1,385},{129,257},{257,129},{3... | collective-permute-start | bytes 393224 | tf_op jit(solution)/shard_map/ppermute | solution.py:46
  83.5 7.3 %copy-start = (bf16[128,1024]{1,0:T(8,128)(2,1)S(1)}, bf16[128,1024]{1,0:T(8,128)(2,1)}, u32[]{:S(2)}) copy-start(bf16[128,1024]{1,0:T(8,128)(2,1)} %param.5) | copy-start | bytes 786436
  83.6 6.9 %collective-permute-start.12 = (bf16[512,128]{1,0:T(8,128)(2,1)S(1)}, bf16[512,128]{1,0:T(8,128)(2,1)S(1)}, u32[]{:S(2)}, u32[]{:S(2)}) collective-permute-start(bf16[512,128]{1,0:T(8,128)(2,1)S(1)} %bitcast.150), channel_id=1, source_target_pairs={{0,128},{128,0},{256,384},{384,256},{1,129},{129,1},{257,385},{385... | collective-permute-start | bytes 393224 | tf_op jit(solution)/shard_map/ppermute | solution.py:46
  90.5 26.4 %copy-start.1 = (bf16[128,1024]{1,0:T(8,128)(2,1)S(1)}, bf16[128,1024]{1,0:T(8,128)(2,1)}, u32[]{:S(2)}) copy-start(bf16[128,1024]{1,0:T(8,128)(2,1)} %param.6) | copy-start | bytes 786436
  90.9 3.0 %collective-permute-start.13 = (f32[128]{0:T(128)S(1)}, f32[128]{0:T(128)S(1)}, u32[]{:S(2)}, u32[]{:S(2)}) collective-permute-start(f32[128]{0:T(128)S(1)} %fusion.4), channel_id=1, source_target_pairs={{0,1},{1,0},{2,3},{3,2},{4,5},{5,4},{6,7},{7,6},{8,9},{9,8},{10,11... | collective-permute-start | bytes 1544 | tf_op jit(solution)/shard_map/ppermute | solution.py:46
  94.0 5.4 %collective-permute-start.14 = (f32[128]{0:T(128)S(1)}, f32[128]{0:T(128)S(1)}, u32[]{:S(2)}, u32[]{:S(2)}) collective-permute-start(f32[128]{0:T(128)S(1)} %add.56), channel_id=1, source_target_pairs={{0,2},{2,0},{4,6},{6,4},{1,3},{3,1},{5,7},{7,5},{8,10},{10,8},{12,... | collective-permute-start | bytes 1544 | tf_op jit(solution)/shard_map/ppermute | solution.py:46
  99.4 6.3 %collective-permute-start.15 = (f32[128]{0:T(128)S(1)}, f32[128]{0:T(128)S(1)}, u32[]{:S(2)}, u32[]{:S(2)}) collective-permute-start(f32[128]{0:T(128)S(1)} %add.57), channel_id=1, source_target_pairs={{0,4},{2,6},{4,0},{6,2},{1,5},{3,7},{5,1},{7,3},{8,12},{10,14},{12... | collective-permute-start | bytes 1544 | tf_op jit(solution)/shard_map/ppermute | solution.py:46
  105.8 16.4 %collective-permute-start.16 = (f32[128,128]{1,0:T(8,128)S(1)}, f32[128,128]{1,0:T(8,128)S(1)}, u32[]{:S(2)}, u32[]{:S(2)}) collective-permute-start(f32[128,128]{1,0:T(8,128)S(1)} %convert_reduce_fusion.1), channel_id=1, source_target_pairs={{0,0},{16,1},{32,2},{48,3},{64,4},{80,5},{96,6},{112,7},{8,8},{24,... | collective-permute-start | bytes 196616 | tf_op jit(solution)/shard_map/ppermute | solution.py:131
  110.7 11.5 %all-to-all-start.1 = ((f32[4,2,128]{2,1,0:T(2,128)}), f32[4,2,128]{2,1,0:T(2,128)S(1)}, u32[]{:S(2)}, u32[]{:S(2)}) async-start(f32[4,2,128]{2,1,0:T(2,128)} %broadcast_in_dim.11), calls=%async_computation.1 | async-start | bytes 8192 | tf_op jit(solution)/shard_map/all_to_all | solution.py:41

commit v13 on v11

--- a/solution.py
+++ b/solution.py
@@ -16,7 +16,6 @@
 AXES = ("x", "y", "zh", "zl", "core")
 DP = ("x", "y", "zh")
 TENSOR = ("zl", "core")
-ROW = ("y", "zh")
 
 
 def flat_index(x, y, zh, zl, core):
@@ -53,6 +52,11 @@
     return jnp.stack([first, second, third]).astype(jnp.bfloat16)
 
 
+def whole_of(terms):
+    first, second, third = terms.astype(jnp.float32).reshape(3, 2, HD)
+    return first + second + third
+
+
 def rope_tables(positions_count, head_size):
     half_head = head_size // 2
     frequency = rope_theta ** (-(jnp.arange(half_head, dtype=jnp.float32) * 2.0 / head_size))
@@ -81,8 +85,8 @@
     def quarter(r):
         return lax.dynamic_slice_in_dim(blocks, (mine ^ r) * 2, 2, axis=0)
 
+    packet = jnp.concatenate([packet, swap(packet, "zl", 1)])
     packet, moved, other = lax.optimization_barrier((packet, moved, other))
-    packet = jnp.concatenate([packet, swap(packet, "zl", 1)])
     first = lax.axis_index("zh") == 0
     weights = jnp.stack([jnp.where(first, moved, other), jnp.where(first, other, moved)])
     for mask, place in ((4, 0), (2, 1), (1, 2)):
@@ -120,15 +124,27 @@
         preferred_element_type=jnp.float32,
     ).astype(jnp.bfloat16)
     norm_grad = jnp.sum(products.astype(jnp.float32), axis=0)
-    gain_part = terms_of(jnp.sum(norm_grad * normal, axis=1)).reshape(6, HD)
+    gain_part = jnp.sum(norm_grad * normal, axis=1)
 
-    pieces = jnp.einsum(
-        "ktc,btf->kbcf", kv, normed, preferred_element_type=jnp.float32
-    ).astype(jnp.bfloat16)
-    gain_rows = jnp.broadcast_to(jnp.pad(gain_part, ((0, 2), (0, 0)))[None], (16, 8, HD))
-    arrived = exchange(jnp.concatenate([pieces.reshape(16, HD, HD), gain_rows], axis=1), ROW)
+    sums = jnp.einsum("ktc,btf->kbcf", kv, normed, preferred_element_type=jnp.float32)
+    first = lax.axis_index("zh") == 0
+    given = jnp.where(first, sums[:, 1], sums[:, 0]).astype(jnp.bfloat16).reshape(8 * HD, HD)
+    terms = terms_of(gain_part).reshape(6, HD)
+    came = swap(jnp.concatenate([given, jnp.pad(terms, ((0, 10), (0, 0)))]), "zh", 1)
+    kept = jnp.where(first, sums[:, 0], sums[:, 1])
+    kept = kept + came[: 8 * HD].astype(jnp.float32).reshape(8, HD, HD)
+    gain_part = whole_of(terms) + whole_of(came[8 * HD : 8 * HD + 6])
+
     back = norm_grad.astype(jnp.bfloat16)
-    near = swap(back[:, 2 * TOK :].reshape(4 * TOK, HD), "x", 3).reshape(2, 2 * TOK, HD)
+    near = swap(back[:, 2 * TOK :].reshape(4 * TOK, HD), "x", 3)
+    near, kept, gain_part = lax.optimization_barrier((near, kept, gain_part))
+    near = near.reshape(2, 2 * TOK, HD)
+
+    gain_rows = jnp.pad(terms_of(gain_part).reshape(6, HD), ((0, 2), (0, 0)))
+    gain_rows = jnp.broadcast_to(gain_rows[None], (8, 8, HD))
+    pieces = jnp.concatenate([kept.astype(jnp.bfloat16), gain_rows], axis=1)
+    arrived = exchange(pieces, "y")
+
     given = jnp.concatenate([back[:, TOK : 2 * TOK], near[:, TOK:]]).reshape(4 * TOK, HD)
     far = swap(given, "x", 1).reshape(2, 2, TOK, HD)
 

time: 127 us -> 130 us (1.024)
  the two profiles are of different devices: /device:TPU:1 before, /device:TPU:6 now
where the time goes in v13:
time: 130 us; the launch traced here: 127 us
  starting transfers between devices  70.9 us (55%)
  waiting for transfers between devices  41.7 us (32%)
  other arithmetic  5.96 us (5%)
  local copies, waits for them, and re-layouts  5.93 us (5%)
  between operations  1.51 us (1%)
  matrix products  1.31 us (1%)
    ppermute x13, starting transfers between devices, swap(): return lax.ppermute(value, axis, [(i, i ^ mask) for i in range(count)])  35.9 us
    ppermute x13, waiting for transfers between devices, swap(): return lax.ppermute(value, axis, [(i, i ^ mask) for i in range(count)])  25.1 us
    all_to_all x2, waiting for transfers between devices, exchange(): return lax.all_to_all(value, axes, split_axis=0, concat_axis=0, tiled=True)  16.6 us
    ppermute x1, starting transfers between devices, shards(): other = lax.ppermute(kv_weight, AXES, [(a, b ^ 8) for a, b in moves])  14.6 us
    all_to_all x2, starting transfers between devices, exchange(): return lax.all_to_all(value, axes, split_axis=0, concat_axis=0, tiled=True)  12.1 us
    ppermute x1, starting transfers between devices, shards(): moved = lax.ppermute(kv_weight, AXES, moves)  4.45 us
    ppermute x1, starting transfers between devices, shards(): weight_grad = lax.ppermute(block, AXES, [(b, a) for a, b in moves])  3.81 us
  transfers between devices with their start and end apart: 18, of which 8 were waited for; matrix products, arithmetic and copies ran while one was open for 7% of the time, Pallas kernels for 0%

profile of v13, /device:TPU:6, one launch (start us, length us, event | category | flops | bytes accessed | tf_op | source)
XLA Modules:
  0.0 127.3 jit_solution(694716161043077872)
XLA Ops:
  0.6 14.6 %collective-permute-start.2 = (bf16[128,128]{1,0:T(8,128)(2,1)}, bf16[128,128]{1,0:T(8,128)(2,1)S(1)}, u32[]{:S(2)}, u32[]{:S(2)}) collective-permute-start(bf16[128,128]{1,0:T(8,128)(2,1)} %param.8), channel_id=1, source_target_pairs={{0,8},{1,24},{2,40},{3,56},{4,72},{5,88},{6,104},{7,120},{8,0},{9,... | collective-permute-start | bytes 98312 | tf_op jit(solution)/shard_map/ppermute | solution.py:72
  15.2 4.5 %collective-permute-start.1 = (bf16[128,128]{1,0:T(8,128)(2,1)}, bf16[128,128]{1,0:T(8,128)(2,1)S(1)}, u32[]{:S(2)}, u32[]{:S(2)}) collective-permute-start(bf16[128,128]{1,0:T(8,128)(2,1)} %param.8), channel_id=1, source_target_pairs={{0,0},{1,16},{2,32},{3,48},{4,64},{5,80},{6,96},{7,112},{8,8},{9,2... | collective-permute-start | bytes 98312 | tf_op jit(solution)/shard_map/ppermute | solution.py:71
  19.7 1.1 fusion.9
  20.8 0.8 convert_element_type.79
  21.5 0.3 multiply_add_fusion
  21.8 0.9 fusion.16
  22.7 2.4 %collective-permute-start = (bf16[1,144,128]{2,1,0:T(8,128)(2,1)S(1)}, bf16[1,144,128]{2,1,0:T(8,128)(2,1)S(1)}, u32[]{:S(2)}, u32[]{:S(2)}) collective-permute-start(bf16[1,144,128]{2,1,0:T(8,128)(2,1)S(1)} %maximum_bitcast_fusion), channel_id=1, source_target_pairs={{0,2},{2,0},{4,6},{6,4},{1,3},{3,1},{5,7},{7,5},{8,10},{10,8},{12,... | collective-permute-start | bytes 110600 | tf_op jit(solution)/shard_map/ppermute | solution.py:45
  25.1 0.9 fusion.37
  26.0 0.1 copy.154
  26.2 0.1 copy.153
  26.3 0.1 copy.152
  26.4 0.1 copy.151
  26.5 0.1 copy.150
  26.7 0.1 copy.149
  26.8 0.1 copy.148
  26.9 0.1 copy.147
  27.2 0.1 copy.124
  27.4 2.0 %collective-permute-start.4 = (bf16[512,128]{1,0:T(8,128)(2,1)S(1)}, bf16[512,128]{1,0:T(8,128)(2,1)S(1)}, u32[]{:S(2)}, u32[]{:S(2)}) collective-permute-start(bf16[512,128]{1,0:T(8,128)(2,1)S(1)} %bitcast.167), channel_id=1, source_target_pairs={{0,384},{128,256},{256,128},{384,0},{1,385},{129,257},{257,129},{3... | collective-permute-start | bytes 393224 | tf_op jit(solution)/shard_map/ppermute | solution.py:45
  29.4 5.9 %collective-permute-start.3 = (bf16[2,144,128]{2,1,0:T(8,128)(2,1)S(1)}, bf16[2,144,128]{2,1,0:T(8,128)(2,1)S(1)}, u32[]{:S(2)}, u32[]{:S(2)}) collective-permute-start(bf16[2,144,128]{2,1,0:T(8,128)(2,1)S(1)} %pad_maximum_fusion.13), channel_id=1, source_target_pairs={{0,4},{2,6},{4,0},{6,2},{1,5},{3,7},{5,1},{7,3},{8,12},{10,14},{12... | collective-permute-start | bytes 221192 | tf_op jit(solution)/shard_map/ppermute | solution.py:45
  35.4 2.7 %collective-permute-start.8 = (bf16[2,128,128]{2,1,0:T(8,128)(2,1)S(1)}, bf16[2,128,128]{2,1,0:T(8,128)(2,1)S(1)}, u32[]{:S(2)}, u32[]{:S(2)}) collective-permute-start(bf16[2,128,128]{2,1,0:T(8,128)(2,1)S(1)} %pad_maximum_fusion.14), channel_id=1, source_target_pairs={{0,64},{16,80},{32,96},{48,112},{64,0},{80,16},{96,32},{112,48},{1... | collective-permute-start | bytes 196616 | tf_op jit(solution)/shard_map/ppermute | solution.py:45
  38.1 0.1 collective-permute-done.3
  38.3 0.1 copy.125
  38.5 0.1 copy.126
  38.6 3.5 %collective-permute-start.5 = (bf16[1088,128]{1,0:T(8,128)(2,1)S(1)}, bf16[1088,128]{1,0:T(8,128)(2,1)S(1)}, u32[]{:S(2)}, u32[]{:S(2)}) collective-permute-start(bf16[1088,128]{1,0:T(8,128)(2,1)S(1)} %pad_maximum_fusion.4), channel_id=1, source_target_pairs={{0,128},{128,0},{256,384},{384,256},{1,129},{129,1},{257,385},{385... | collective-permute-start | bytes 835592 | tf_op jit(solution)/shard_map/ppermute | solution.py:45
  42.2 3.4 %collective-permute-done.8 = bf16[2,128,128]{2,1,0:T(8,128)(2,1)S(1)} collective-permute-done((bf16[2,128,128]{2,1,0:T(8,128)(2,1)S(1)}, bf16[2,128,128]{2,1,0:T(8,128)(2,1)S(1)}, u32[]{:S(2)}, u32[]{:S(2)}) %collective-permute-start.8) | collective-permute-done | bytes 65568 | tf_op jit(solution)/shard_map/ppermute | solution.py:45
  45.6 5.0 %collective-permute-start.9 = (bf16[2,2,128,128]{3,2,1,0:T(8,128)(2,1)S(1)}, bf16[2,2,128,128]{3,2,1,0:T(8,128)(2,1)S(1)}, u32[]{:S(2)}, u32[]{:S(2)}) collective-permute-start(bf16[2,2,128,128]{3,2,1,0:T(8,128)(2,1)S(1)} %pad_maximum_fusion.11), channel_id=1, source_target_pairs={{0,32},{16,48},{32,0},{48,16},{64,96},{80,112},{96,64},{112,80},{1... | collective-permute-start | bytes 393224 | tf_op jit(solution)/shard_map/ppermute | solution.py:45
  50.6 0.1 dynamic-slice_bitcast_fusion
  50.7 0.1 copy.132
  50.9 2.8 %collective-permute-start.6 = (bf16[2,4,144,128]{3,2,1,0:T(8,128)(2,1)S(1)}, bf16[2,4,144,128]{3,2,1,0:T(8,128)(2,1)S(1)}, u32[]{:S(2)}, u32[]{:S(2)}) collective-permute-start(bf16[2,4,144,128]{3,2,1,0:T(8,128)(2,1)S(1)} %pad_maximum_fusion.3), channel_id=1, source_target_pairs={{0,384},{128,256},{256,128},{384,0},{1,385},{129,257},{257,129},{3... | collective-permute-start | bytes 884744 | tf_op jit(solution)/shard_map/ppermute | solution.py:45
  53.7 2.8 %collective-permute-done.9 = bf16[2,2,128,128]{3,2,1,0:T(8,128)(2,1)S(1)} collective-permute-done((bf16[2,2,128,128]{3,2,1,0:T(8,128)(2,1)S(1)}, bf16[2,2,128,128]{3,2,1,0:T(8,128)(2,1)S(1)}, u32[]{:S(2)}, u32[]{:S(2)}) %collective-permute-start.9) | collective-permute-done | bytes 131104 | tf_op jit(solution)/shard_map/ppermute | solution.py:45
  56.5 1.9 %collective-permute-start.10 = (bf16[2,2,2,128,128]{4,3,2,0,1:T(8,128)(2,1)S(1)}, bf16[2,2,2,128,128]{4,3,2,0,1:T(8,128)(2,1)S(1)}, u32[]{:S(2)}, u32[]{:S(2)}) collective-permute-start(bf16[2,2,2,128,128]{4,3,2,0,1:T(8,128)(2,1)S(1)} %pad_maximum_fusion.6), channel_id=1, source_target_pairs={{0,16},{16,0},{32,48},{48,32},{64,80},{80,64},{96,112},{112,96},{1... | collective-permute-start | bytes 786440 | tf_op jit(solution)/shard_map/ppermute | solution.py:45
  58.5 3.6 %collective-permute-done.6 = bf16[2,4,144,128]{3,2,1,0:T(8,128)(2,1)S(1)} collective-permute-done((bf16[2,4,144,128]{3,2,1,0:T(8,128)(2,1)S(1)}, bf16[2,4,144,128]{3,2,1,0:T(8,128)(2,1)S(1)}, u32[]{:S(2)}, u32[]{:S(2)}) %collective-permute-start.6) | collective-permute-done | bytes 294944 | tf_op jit(solution)/shard_map/ppermute | solution.py:45
  62.1 0.1 fusion.34
  62.1 1.9 %collective-permute-start.7 = (bf16[4,4,144,128]{3,2,1,0:T(8,128)(2,1)S(1)}, bf16[4,4,144,128]{3,2,1,0:T(8,128)(2,1)S(1)}, u32[]{:S(2)}, u32[]{:S(2)}) collective-permute-start(bf16[4,4,144,128]{3,2,1,0:T(8,128)(2,1)S(1)} %get-tuple-element.30), channel_id=1, source_target_pairs={{0,1},{1,0},{2,3},{3,2},{4,5},{5,4},{6,7},{7,6},{8,9},{9,8},{10,11... | collective-permute-start | bytes 1769480 | tf_op jit(solution)/shard_map/ppermute | solution.py:45
  64.1 0.1 copy.131
  64.2 0.1 copy.133
  64.3 2.1 %collective-permute-done.10 = bf16[2,2,2,128,128]{4,3,2,0,1:T(8,128)(2,1)S(1)} collective-permute-done((bf16[2,2,2,128,128]{4,3,2,0,1:T(8,128)(2,1)S(1)}, bf16[2,2,2,128,128]{4,3,2,0,1:T(8,128)(2,1)S(1)}, u32[]{:S(2)}, u32[]{:S(2)}) %collective-permute-start.10) | collective-permute-done | bytes 262176 | tf_op jit(solution)/shard_map/ppermute | solution.py:45
  66.5 0.3 copy.127
  66.9 0.1 fusion
  67.0 0.1 copy.128
  67.1 0.7 convert_reduce_fusion
  67.9 0.2 fusion.10
  68.1 0.1 copy.129
  68.2 0.6 convolution_bitcast_fusion
  68.9 1.9 %collective-permute-start.12 = (bf16[1040,128]{1,0:T(8,128)(2,1)S(1)}, bf16[1040,128]{1,0:T(8,128)(2,1)S(1)}, u32[]{:S(2)}, u32[]{:S(2)}) collective-permute-start(bf16[1040,128]{1,0:T(8,128)(2,1)S(1)} %fusion.11), channel_id=1, source_target_pairs={{0,8},{8,0},{1,9},{9,1},{2,10},{10,2},{3,11},{11,3},{4,12},{12,4},... | collective-permute-start | bytes 798728 | tf_op jit(solution)/shard_map/ppermute | solution.py:45
  71.0 0.1 copy.130
  71.1 1.9 %collective-permute-start.11 = (bf16[512,128]{1,0:T(8,128)(2,1)S(1)}, bf16[512,128]{1,0:T(8,128)(2,1)S(1)}, u32[]{:S(2)}, u32[]{:S(2)}) collective-permute-start(bf16[512,128]{1,0:T(8,128)(2,1)S(1)} %bitcast.169), channel_id=1, source_target_pairs={{0,384},{128,256},{256,128},{384,0},{1,385},{129,257},{257,129},{3... | collective-permute-start | bytes 393224 | tf_op jit(solution)/shard_map/ppermute | solution.py:45
  73.0 13.2 %collective-permute-done.12 = bf16[1040,128]{1,0:T(8,128)(2,1)S(1)} collective-permute-done((bf16[1040,128]{1,0:T(8,128)(2,1)S(1)}, bf16[1040,128]{1,0:T(8,128)(2,1)S(1)}, u32[]{:S(2)}, u32[]{:S(2)}) %collective-permute-start.12) | collective-permute-done | bytes 266272 | tf_op jit(solution)/shard_map/ppermute | solution.py:45
  86.2 0.1 convert_add_fusion
  86.4 0.1 copy.155
  86.5 0.1 copy.137
  86.6 1.9 %collective-permute-start.13 = (bf16[512,128]{1,0:T(8,128)(2,1)S(1)}, bf16[512,128]{1,0:T(8,128)(2,1)S(1)}, u32[]{:S(2)}, u32[]{:S(2)}) collective-permute-start(bf16[512,128]{1,0:T(8,128)(2,1)S(1)} %bitcast.168), channel_id=1, source_target_pairs={{0,128},{128,0},{256,384},{384,256},{1,129},{129,1},{257,385},{385... | collective-permute-start | bytes 393224 | tf_op jit(solution)/shard_map/ppermute | solution.py:45
  88.6 0.7 pad_maximum_fusion.5
  89.4 4.4 %all-to-all-start = ((bf16[8,136,128]{2,1,0:T(8,128)(2,1)}), bf16[8,136,128]{2,1,0:T(8,128)(2,1)S(1)}, u32[]{:S(2)}, u32[]{:S(2)}) async-start(bf16[8,136,128]{2,1,0:T(8,128)(2,1)} %pad_maximum_fusion.5), calls=%async_computation | async-start | bytes 557056 | tf_op jit(solution)/shard_map/all_to_all | solution.py:40
  94.0 0.2 fusion.4
  94.3 10.2 %all-to-all-done = bf16[8,136,128]{2,1,0:T(8,128)(2,1)S(1)} async-done(((bf16[8,136,128]{2,1,0:T(8,128)(2,1)}), bf16[8,136,128]{2,1,0:T(8,128)(2,1)S(1)}, u32[]{:S(2)}, u32[]{:S(2)}) %all-to-all-start) | async-done | bytes 278560 | tf_op jit(solution)/shard_map/all_to_all | solution.py:40
  104.5 1.9 %collective-permute-start.14 = (f32[128]{0:T(128)S(1)}, f32[128]{0:T(128)S(1)}, u32[]{:S(2)}, u32[]{:S(2)}) collective-permute-start(f32[128]{0:T(128)S(1)} %fusion.4), channel_id=1, source_target_pairs={{0,1},{1,0},{2,3},{3,2},{4,5},{5,4},{6,7},{7,6},{8,9},{9,8},{10,11... | collective-permute-start | bytes 1544 | tf_op jit(solution)/shard_map/ppermute | solution.py:45
  106.4 3.8 %collective-permute-start.15 = (f32[128,128]{1,0:T(8,128)S(1)}, f32[128,128]{1,0:T(8,128)S(1)}, u32[]{:S(2)}, u32[]{:S(2)}) collective-permute-start(f32[128,128]{1,0:T(8,128)S(1)} %convert_reduce_fusion.1), channel_id=1, source_target_pairs={{0,0},{16,1},{32,2},{48,3},{64,4},{80,5},{96,6},{112,7},{8,8},{24,... | collective-permute-start | bytes 196616 | tf_op jit(solution)/shard_map/ppermute | solution.py:162
  110.3 0.6 broadcast_in_dim.14
  110.9 7.7 %all-to-all-start.1 = ((f32[16,3,128]{2,1,0:T(4,128)}), f32[16,3,128]{2,1,0:T(4,128)S(1)}, u32[]{:S(2)}, u32[]{:S(2)}) async-start(f32[16,3,128]{2,1,0:T(4,128)} %broadcast_in_dim.14), calls=%async_computation.1 | async-start | bytes 65536 | tf_op jit(solution)/shard_map/all_to_all | solution.py:40
  118.6 6.4 %all-to-all-done.1 = f32[16,3,128]{2,1,0:T(4,128)S(1)} async-done(((f32[16,3,128]{2,1,0:T(4,128)}), f32[16,3,128]{2,1,0:T(4,128)S(1)}, u32[]{:S(2)}, u32[]{:S(2)}) %all-to-all-start.1) | async-done | bytes 24608 | tf_op jit(solution)/shard_map/all_to_all | solution.py:40
  125.1 0.6 copy.140
  125.7 1.0 fusion.8
  126.7 0.6 copy.175
  (94 shorter events, 1.2 us)
Async XLA Ops:
  0.6 28.8 %collective-permute-start.2 = (bf16[128,128]{1,0:T(8,128)(2,1)}, bf16[128,128]{1,0:T(8,128)(2,1)S(1)}, u32[]{:S(2)}, u32[]{:S(2)}) collective-permute-start(bf16[128,128]{1,0:T(8,128)(2,1)} %param.8), channel_id=1, source_target_pairs={{0,8},{1,24},{2,40},{3,56},{4,72},{5,88},{6,104},{7,120},{8,0},{9,... | collective-permute-start | bytes 98312 | tf_op jit(solution)/shard_map/ppermute | solution.py:72
  15.2 14.2 %collective-permute-start.1 = (bf16[128,128]{1,0:T(8,128)(2,1)}, bf16[128,128]{1,0:T(8,128)(2,1)S(1)}, u32[]{:S(2)}, u32[]{:S(2)}) collective-permute-start(bf16[128,128]{1,0:T(8,128)(2,1)} %param.8), channel_id=1, source_target_pairs={{0,0},{1,16},{2,32},{3,48},{4,64},{5,80},{6,96},{7,112},{8,8},{9,2... | collective-permute-start | bytes 98312 | tf_op jit(solution)/shard_map/ppermute | solution.py:71
  22.7 6.7 %collective-permute-start = (bf16[1,144,128]{2,1,0:T(8,128)(2,1)S(1)}, bf16[1,144,128]{2,1,0:T(8,128)(2,1)S(1)}, u32[]{:S(2)}, u32[]{:S(2)}) collective-permute-start(bf16[1,144,128]{2,1,0:T(8,128)(2,1)S(1)} %maximum_bitcast_fusion), channel_id=1, source_target_pairs={{0,2},{2,0},{4,6},{6,4},{1,3},{3,1},{5,7},{7,5},{8,10},{10,8},{12,... | collective-permute-start | bytes 110600 | tf_op jit(solution)/shard_map/ppermute | solution.py:45
  27.4 10.9 %collective-permute-start.4 = (bf16[512,128]{1,0:T(8,128)(2,1)S(1)}, bf16[512,128]{1,0:T(8,128)(2,1)S(1)}, u32[]{:S(2)}, u32[]{:S(2)}) collective-permute-start(bf16[512,128]{1,0:T(8,128)(2,1)S(1)} %bitcast.167), channel_id=1, source_target_pairs={{0,384},{128,256},{256,128},{384,0},{1,385},{129,257},{257,129},{3... | collective-permute-start | bytes 393224 | tf_op jit(solution)/shard_map/ppermute | solution.py:45
  29.4 8.8 %collective-permute-start.3 = (bf16[2,144,128]{2,1,0:T(8,128)(2,1)S(1)}, bf16[2,144,128]{2,1,0:T(8,128)(2,1)S(1)}, u32[]{:S(2)}, u32[]{:S(2)}) collective-permute-start(bf16[2,144,128]{2,1,0:T(8,128)(2,1)S(1)} %pad_maximum_fusion.13), channel_id=1, source_target_pairs={{0,4},{2,6},{4,0},{6,2},{1,5},{3,7},{5,1},{7,3},{8,12},{10,14},{12... | collective-permute-start | bytes 221192 | tf_op jit(solution)/shard_map/ppermute | solution.py:45
  35.4 10.2 %collective-permute-start.8 = (bf16[2,128,128]{2,1,0:T(8,128)(2,1)S(1)}, bf16[2,128,128]{2,1,0:T(8,128)(2,1)S(1)}, u32[]{:S(2)}, u32[]{:S(2)}) collective-permute-start(bf16[2,128,128]{2,1,0:T(8,128)(2,1)S(1)} %pad_maximum_fusion.14), channel_id=1, source_target_pairs={{0,64},{16,80},{32,96},{48,112},{64,0},{80,16},{96,32},{112,48},{1... | collective-permute-start | bytes 196616 | tf_op jit(solution)/shard_map/ppermute | solution.py:45
  38.3 12.3 %copy-start.2 = (f32[1024]{0:T(1024)S(1)}, f32[1024]{0:T(1024)}, u32[]{:S(2)}) copy-start(f32[1024]{0:T(1024)} %param.9) | copy-start | bytes 12292
  38.6 12.2 %collective-permute-start.5 = (bf16[1088,128]{1,0:T(8,128)(2,1)S(1)}, bf16[1088,128]{1,0:T(8,128)(2,1)S(1)}, u32[]{:S(2)}, u32[]{:S(2)}) collective-permute-start(bf16[1088,128]{1,0:T(8,128)(2,1)S(1)} %pad_maximum_fusion.4), channel_id=1, source_target_pairs={{0,128},{128,0},{256,384},{384,256},{1,129},{129,1},{257,385},{385... | collective-permute-start | bytes 835592 | tf_op jit(solution)/shard_map/ppermute | solution.py:45
  45.6 10.9 %collective-permute-start.9 = (bf16[2,2,128,128]{3,2,1,0:T(8,128)(2,1)S(1)}, bf16[2,2,128,128]{3,2,1,0:T(8,128)(2,1)S(1)}, u32[]{:S(2)}, u32[]{:S(2)}) collective-permute-start(bf16[2,2,128,128]{3,2,1,0:T(8,128)(2,1)S(1)} %pad_maximum_fusion.11), channel_id=1, source_target_pairs={{0,32},{16,48},{32,0},{48,16},{64,96},{80,112},{96,64},{112,80},{1... | collective-permute-start | bytes 393224 | tf_op jit(solution)/shard_map/ppermute | solution.py:45
  50.9 11.2 %collective-permute-start.6 = (bf16[2,4,144,128]{3,2,1,0:T(8,128)(2,1)S(1)}, bf16[2,4,144,128]{3,2,1,0:T(8,128)(2,1)S(1)}, u32[]{:S(2)}, u32[]{:S(2)}) collective-permute-start(bf16[2,4,144,128]{3,2,1,0:T(8,128)(2,1)S(1)} %pad_maximum_fusion.3), channel_id=1, source_target_pairs={{0,384},{128,256},{256,128},{384,0},{1,385},{129,257},{257,129},{3... | collective-permute-start | bytes 884744 | tf_op jit(solution)/shard_map/ppermute | solution.py:45
  56.5 9.9 %collective-permute-start.10 = (bf16[2,2,2,128,128]{4,3,2,0,1:T(8,128)(2,1)S(1)}, bf16[2,2,2,128,128]{4,3,2,0,1:T(8,128)(2,1)S(1)}, u32[]{:S(2)}, u32[]{:S(2)}) collective-permute-start(bf16[2,2,2,128,128]{4,3,2,0,1:T(8,128)(2,1)S(1)} %pad_maximum_fusion.6), channel_id=1, source_target_pairs={{0,16},{16,0},{32,48},{48,32},{64,80},{80,64},{96,112},{112,96},{1... | collective-permute-start | bytes 786440 | tf_op jit(solution)/shard_map/ppermute | solution.py:45
  62.1 4.7 %collective-permute-start.7 = (bf16[4,4,144,128]{3,2,1,0:T(8,128)(2,1)S(1)}, bf16[4,4,144,128]{3,2,1,0:T(8,128)(2,1)S(1)}, u32[]{:S(2)}, u32[]{:S(2)}) collective-permute-start(bf16[4,4,144,128]{3,2,1,0:T(8,128)(2,1)S(1)} %get-tuple-element.30), channel_id=1, source_target_pairs={{0,1},{1,0},{2,3},{3,2},{4,5},{5,4},{6,7},{7,6},{8,9},{9,8},{10,11... | collective-permute-start | bytes 1769480 | tf_op jit(solution)/shard_map/ppermute | solution.py:45
  68.9 17.3 %collective-permute-start.12 = (bf16[1040,128]{1,0:T(8,128)(2,1)S(1)}, bf16[1040,128]{1,0:T(8,128)(2,1)S(1)}, u32[]{:S(2)}, u32[]{:S(2)}) collective-permute-start(bf16[1040,128]{1,0:T(8,128)(2,1)S(1)} %fusion.11), channel_id=1, source_target_pairs={{0,8},{8,0},{1,9},{9,1},{2,10},{10,2},{3,11},{11,3},{4,12},{12,4},... | collective-permute-start | bytes 798728 | tf_op jit(solution)/shard_map/ppermute | solution.py:45
  71.1 15.2 %collective-permute-start.11 = (bf16[512,128]{1,0:T(8,128)(2,1)S(1)}, bf16[512,128]{1,0:T(8,128)(2,1)S(1)}, u32[]{:S(2)}, u32[]{:S(2)}) collective-permute-start(bf16[512,128]{1,0:T(8,128)(2,1)S(1)} %bitcast.169), channel_id=1, source_target_pairs={{0,384},{128,256},{256,128},{384,0},{1,385},{129,257},{257,129},{3... | collective-permute-start | bytes 393224 | tf_op jit(solution)/shard_map/ppermute | solution.py:45
  86.6 7.1 %collective-permute-start.13 = (bf16[512,128]{1,0:T(8,128)(2,1)S(1)}, bf16[512,128]{1,0:T(8,128)(2,1)S(1)}, u32[]{:S(2)}, u32[]{:S(2)}) collective-permute-start(bf16[512,128]{1,0:T(8,128)(2,1)S(1)} %bitcast.168), channel_id=1, source_target_pairs={{0,128},{128,0},{256,384},{384,256},{1,129},{129,1},{257,385},{385... | collective-permute-start | bytes 393224 | tf_op jit(solution)/shard_map/ppermute | solution.py:45
  88.6 5.4 %copy-start = (bf16[128,1024]{1,0:T(8,128)(2,1)S(1)}, bf16[128,1024]{1,0:T(8,128)(2,1)}, u32[]{:S(2)}) copy-start(bf16[128,1024]{1,0:T(8,128)(2,1)} %param.5) | copy-start | bytes 786436
  89.4 15.1 %all-to-all-start = ((bf16[8,136,128]{2,1,0:T(8,128)(2,1)}), bf16[8,136,128]{2,1,0:T(8,128)(2,1)S(1)}, u32[]{:S(2)}, u32[]{:S(2)}) async-start(bf16[8,136,128]{2,1,0:T(8,128)(2,1)} %pad_maximum_fusion.5), calls=%async_computation | async-start | bytes 557056 | tf_op jit(solution)/shard_map/all_to_all | solution.py:40
  93.8 31.9 %copy-start.1 = (bf16[128,1024]{1,0:T(8,128)(2,1)S(1)}, bf16[128,1024]{1,0:T(8,128)(2,1)}, u32[]{:S(2)}) copy-start(bf16[128,1024]{1,0:T(8,128)(2,1)} %param.6) | copy-start | bytes 786436
  104.5 5.7 %collective-permute-start.14 = (f32[128]{0:T(128)S(1)}, f32[128]{0:T(128)S(1)}, u32[]{:S(2)}, u32[]{:S(2)}) collective-permute-start(f32[128]{0:T(128)S(1)} %fusion.4), channel_id=1, source_target_pairs={{0,1},{1,0},{2,3},{3,2},{4,5},{5,4},{6,7},{7,6},{8,9},{9,8},{10,11... | collective-permute-start | bytes 1544 | tf_op jit(solution)/shard_map/ppermute | solution.py:45
  106.4 18.6 %collective-permute-start.15 = (f32[128,128]{1,0:T(8,128)S(1)}, f32[128,128]{1,0:T(8,128)S(1)}, u32[]{:S(2)}, u32[]{:S(2)}) collective-permute-start(f32[128,128]{1,0:T(8,128)S(1)} %convert_reduce_fusion.1), channel_id=1, source_target_pairs={{0,0},{16,1},{32,2},{48,3},{64,4},{80,5},{96,6},{112,7},{8,8},{24,... | collective-permute-start | bytes 196616 | tf_op jit(solution)/shard_map/ppermute | solution.py:162
  110.9 14.1 %all-to-all-start.1 = ((f32[16,3,128]{2,1,0:T(4,128)}), f32[16,3,128]{2,1,0:T(4,128)S(1)}, u32[]{:S(2)}, u32[]{:S(2)}) async-start(f32[16,3,128]{2,1,0:T(4,128)} %broadcast_in_dim.14), calls=%async_computation.1 | async-start | bytes 65536 | tf_op jit(solution)/shard_map/all_to_all | solution.py:40

commit v14 on v12

--- a/solution.py
+++ b/solution.py
@@ -64,9 +64,6 @@
     moves = weight_moves()
     mine = lax.axis_index("x")
 
-    moved = lax.ppermute(kv_weight, AXES, moves)
-    other = lax.ppermute(kv_weight, AXES, [(a, b ^ 8) for a, b in moves])
-
     cosine, sine = rope_tables(TOK, HD)
     grads = key_value_grad.astype(jnp.float32)
     low, high = grads[:, : HD // 2], grads[:, HD // 2 :]
@@ -81,6 +78,12 @@
     def quarter(r):
         return lax.dynamic_slice_in_dim(blocks, (mine ^ r) * 2, 2, axis=0)
 
+    given = jnp.concatenate([quarter(3), quarter(2)]).reshape(4 * TOK, HD)
+    packet, given, kv_weight = lax.optimization_barrier((packet, given, kv_weight))
+
+    moved = lax.ppermute(kv_weight, AXES, moves)
+    other = lax.ppermute(kv_weight, AXES, [(a, b ^ 8) for a, b in moves])
+
     packet = jnp.concatenate([packet, swap(packet, "zl", 1)])
     packet, moved, other = lax.optimization_barrier((packet, moved, other))
     first = lax.axis_index("zh") == 0
@@ -91,7 +94,6 @@
         pair = [jnp.where(first, weights, other), jnp.where(first, other, weights)]
         weights = jnp.stack(pair, axis=place)
     weights = weights.reshape(8, 2, HD, HD)
-    given = jnp.concatenate([quarter(3), quarter(2)]).reshape(4 * TOK, HD)
     near = swap(given, "x", 3)
     packet = jnp.concatenate([packet, swap(packet, "zl", 2)])
     packet, near = lax.optimization_barrier((packet, near))

time: 124 us -> 130 us (1.048)
  starting transfers between devices: 76.8 us -> 88.2 us
  waiting for transfers between devices: 32.2 us -> 28.2 us
  other arithmetic: 5.92 us -> 4.41 us
    all_to_all x2, starting transfers between devices: 11.8 us -> 19.2 us  [exchange(): return lax.all_to_all(value, axes, split_axis=0, concat_axis=0, tiled=True)]
    ppermute x14, starting transfers between devices: 38.6 us -> 43.2 us  [swap(): return lax.ppermute(value, axis, [(i, i ^ mask) for i in range(count)])]
    ppermute x14, waiting for transfers between devices: 27.9 us -> 23.8 us  [swap(): return lax.ppermute(value, axis, [(i, i ^ mask) for i in range(count)])]
  transfers between devices with their start and end apart: 19 -> 19, of which waited for: 11 -> 10; matrix products, arithmetic and copies ran while one was open for 7% -> 3% of each run, Pallas kernels for 0% -> 0%
where the time goes in v14:
time: 130 us; the launch traced here: 129 us
  starting transfers between devices  88.2 us (68%)
  waiting for transfers between devices  28.2 us (22%)
  local copies, waits for them, and re-layouts  5.86 us (5%)
  other arithmetic  4.41 us (3%)
  between operations  1.46 us (1%)
  matrix products  1.31 us (1%)
    ppermute x14, starting transfers between devices, swap(): return lax.ppermute(value, axis, [(i, i ^ mask) for i in range(count)])  43.2 us
    ppermute x14, waiting for transfers between devices, swap(): return lax.ppermute(value, axis, [(i, i ^ mask) for i in range(count)])  23.8 us
    all_to_all x2, starting transfers between devices, exchange(): return lax.all_to_all(value, axes, split_axis=0, concat_axis=0, tiled=True)  19.2 us
    ppermute x1, starting transfers between devices, shards(): other = lax.ppermute(kv_weight, AXES, [(a, b ^ 8) for a, b in moves])  16.7 us
    ppermute x1, starting transfers between devices, shards(): weight_grad = lax.ppermute(block, AXES, [(b, a) for a, b in moves])  4.67 us
    ppermute x1, starting transfers between devices, shards(): moved = lax.ppermute(kv_weight, AXES, moves)  4.42 us
    all_to_all x2, waiting for transfers between devices, exchange(): return lax.all_to_all(value, axes, split_axis=0, concat_axis=0, tiled=True)  4.34 us
  transfers between devices with their start and end apart: 19, of which 10 were waited for; matrix products, arithmetic and copies ran while one was open for 3% of the time, Pallas kernels for 0%

profile of v14, /device:TPU:48, one launch (start us, length us, event | category | flops | bytes accessed | tf_op | source)
XLA Modules:
  0.0 129.4 jit_solution(7844573904658760944)
XLA Ops:
  0.7 0.9 fusion.30
  1.6 1.1 fusion.9
  2.7 0.1 copy.82
  2.8 0.1 copy.83
  2.9 0.1 copy.84
  3.0 0.1 copy.85
  3.2 0.1 copy.86
  3.3 0.1 copy.87
  3.4 0.1 copy.88
  3.6 0.1 copy.89
  3.9 0.1 copy.61
  4.0 0.3 multiply_add_fusion
  4.3 0.1 fusion.15
  4.4 4.3 %collective-permute-start = (bf16[1,144,128]{2,1,0:T(8,128)(2,1)S(1)}, bf16[1,144,128]{2,1,0:T(8,128)(2,1)S(1)}, u32[]{:S(2)}, u32[]{:S(2)}) collective-permute-start(bf16[1,144,128]{2,1,0:T(8,128)(2,1)S(1)} %maximum_bitcast_fusion), channel_id=1, source_target_pairs={{0,2},{2,0},{4,6},{6,4},{1,3},{3,1},{5,7},{7,5},{8,10},{10,8},{12,... | collective-permute-start | bytes 110600 | tf_op jit(solution)/shard_map/ppermute | solution.py:46
  8.7 4.4 %collective-permute-start.1 = (bf16[128,128]{1,0:T(8,128)(2,1)S(1)}, bf16[128,128]{1,0:T(8,128)(2,1)S(1)}, u32[]{:S(2)}, u32[]{:S(2)}) collective-permute-start(bf16[128,128]{1,0:T(8,128)(2,1)S(1)} %copy-done.4), channel_id=1, source_target_pairs={{0,0},{1,16},{2,32},{3,48},{4,64},{5,80},{6,96},{7,112},{8,8},{9,2... | collective-permute-start | bytes 98312 | tf_op jit(solution)/shard_map/ppermute | solution.py:84
  13.2 16.7 %collective-permute-start.2 = (bf16[128,128]{1,0:T(8,128)(2,1)S(1)}, bf16[128,128]{1,0:T(8,128)(2,1)S(1)}, u32[]{:S(2)}, u32[]{:S(2)}) collective-permute-start(bf16[128,128]{1,0:T(8,128)(2,1)S(1)} %copy-done.4), channel_id=1, source_target_pairs={{0,8},{1,24},{2,40},{3,56},{4,72},{5,88},{6,104},{7,120},{8,0},{9,... | collective-permute-start | bytes 98312 | tf_op jit(solution)/shard_map/ppermute | solution.py:85
  29.9 1.9 %collective-permute-start.4 = (bf16[512,128]{1,0:T(8,128)(2,1)S(1)}, bf16[512,128]{1,0:T(8,128)(2,1)S(1)}, u32[]{:S(2)}, u32[]{:S(2)}) collective-permute-start(bf16[512,128]{1,0:T(8,128)(2,1)S(1)} %bitcast.147), channel_id=1, source_target_pairs={{0,384},{128,256},{256,128},{384,0},{1,385},{129,257},{257,129},{3... | collective-permute-start | bytes 393224 | tf_op jit(solution)/shard_map/ppermute | solution.py:46
  31.9 2.0 %collective-permute-start.3 = (bf16[2,144,128]{2,1,0:T(8,128)(2,1)S(1)}, bf16[2,144,128]{2,1,0:T(8,128)(2,1)S(1)}, u32[]{:S(2)}, u32[]{:S(2)}) collective-permute-start(bf16[2,144,128]{2,1,0:T(8,128)(2,1)S(1)} %pad_maximum_fusion.13), channel_id=1, source_target_pairs={{0,4},{2,6},{4,0},{6,2},{1,5},{3,7},{5,1},{7,3},{8,12},{10,14},{12... | collective-permute-start | bytes 221192 | tf_op jit(solution)/shard_map/ppermute | solution.py:46
  33.9 4.4 %collective-permute-start.8 = (bf16[2,128,128]{2,1,0:T(8,128)(2,1)S(1)}, bf16[2,128,128]{2,1,0:T(8,128)(2,1)S(1)}, u32[]{:S(2)}, u32[]{:S(2)}) collective-permute-start(bf16[2,128,128]{2,1,0:T(8,128)(2,1)S(1)} %pad_maximum_fusion.14), channel_id=1, source_target_pairs={{0,64},{16,80},{32,96},{48,112},{64,0},{80,16},{96,32},{112,48},{1... | collective-permute-start | bytes 196616 | tf_op jit(solution)/shard_map/ppermute | solution.py:46
  38.3 1.5 %collective-permute-done.3 = bf16[2,144,128]{2,1,0:T(8,128)(2,1)S(1)} collective-permute-done((bf16[2,144,128]{2,1,0:T(8,128)(2,1)S(1)}, bf16[2,144,128]{2,1,0:T(8,128)(2,1)S(1)}, u32[]{:S(2)}, u32[]{:S(2)}) %collective-permute-start.3) | collective-permute-done | bytes 73760 | tf_op jit(solution)/shard_map/ppermute | solution.py:46
  39.9 0.1 copy.62
  40.0 0.1 copy.63
  40.2 1.9 %collective-permute-start.5 = (bf16[1088,128]{1,0:T(8,128)(2,1)S(1)}, bf16[1088,128]{1,0:T(8,128)(2,1)S(1)}, u32[]{:S(2)}, u32[]{:S(2)}) collective-permute-start(bf16[1088,128]{1,0:T(8,128)(2,1)S(1)} %pad_maximum_fusion.5), channel_id=1, source_target_pairs={{0,128},{128,0},{256,384},{384,256},{1,129},{129,1},{257,385},{385... | collective-permute-start | bytes 835592 | tf_op jit(solution)/shard_map/ppermute | solution.py:46
  42.1 1.9 %collective-permute-done.8 = bf16[2,128,128]{2,1,0:T(8,128)(2,1)S(1)} collective-permute-done((bf16[2,128,128]{2,1,0:T(8,128)(2,1)S(1)}, bf16[2,128,128]{2,1,0:T(8,128)(2,1)S(1)}, u32[]{:S(2)}, u32[]{:S(2)}) %collective-permute-start.8) | collective-permute-done | bytes 65568 | tf_op jit(solution)/shard_map/ppermute | solution.py:46
  44.0 5.3 %collective-permute-start.9 = (bf16[2,2,128,128]{3,2,1,0:T(8,128)(2,1)S(1)}, bf16[2,2,128,128]{3,2,1,0:T(8,128)(2,1)S(1)}, u32[]{:S(2)}, u32[]{:S(2)}) collective-permute-start(bf16[2,2,128,128]{3,2,1,0:T(8,128)(2,1)S(1)} %pad_maximum_fusion.11), channel_id=1, source_target_pairs={{0,32},{16,48},{32,0},{48,16},{64,96},{80,112},{96,64},{112,80},{1... | collective-permute-start | bytes 393224 | tf_op jit(solution)/shard_map/ppermute | solution.py:46
  49.3 0.1 dynamic-slice_bitcast_fusion
  49.4 0.1 copy.71
  49.6 4.0 %collective-permute-start.6 = (bf16[2,4,144,128]{3,2,1,0:T(8,128)(2,1)S(1)}, bf16[2,4,144,128]{3,2,1,0:T(8,128)(2,1)S(1)}, u32[]{:S(2)}, u32[]{:S(2)}) collective-permute-start(bf16[2,4,144,128]{3,2,1,0:T(8,128)(2,1)S(1)} %pad_maximum_fusion.4), channel_id=1, source_target_pairs={{0,384},{128,256},{256,128},{384,0},{1,385},{129,257},{257,129},{3... | collective-permute-start | bytes 884744 | tf_op jit(solution)/shard_map/ppermute | solution.py:46
  53.7 3.4 %collective-permute-start.10 = (bf16[2,2,2,128,128]{4,3,2,0,1:T(8,128)(2,1)S(1)}, bf16[2,2,2,128,128]{4,3,2,0,1:T(8,128)(2,1)S(1)}, u32[]{:S(2)}, u32[]{:S(2)}) collective-permute-start(bf16[2,2,2,128,128]{4,3,2,0,1:T(8,128)(2,1)S(1)} %pad_maximum_fusion.6), channel_id=1, source_target_pairs={{0,16},{16,0},{32,48},{48,32},{64,80},{80,64},{96,112},{112,96},{1... | collective-permute-start | bytes 786440 | tf_op jit(solution)/shard_map/ppermute | solution.py:46
  57.1 3.9 %collective-permute-done.6 = bf16[2,4,144,128]{3,2,1,0:T(8,128)(2,1)S(1)} collective-permute-done((bf16[2,4,144,128]{3,2,1,0:T(8,128)(2,1)S(1)}, bf16[2,4,144,128]{3,2,1,0:T(8,128)(2,1)S(1)}, u32[]{:S(2)}, u32[]{:S(2)}) %collective-permute-start.6) | collective-permute-done | bytes 294944 | tf_op jit(solution)/shard_map/ppermute | solution.py:46
  60.9 0.1 fusion.27
  61.0 1.9 %collective-permute-start.7 = (bf16[4,4,144,128]{3,2,1,0:T(8,128)(2,1)S(1)}, bf16[4,4,144,128]{3,2,1,0:T(8,128)(2,1)S(1)}, u32[]{:S(2)}, u32[]{:S(2)}) collective-permute-start(bf16[4,4,144,128]{3,2,1,0:T(8,128)(2,1)S(1)} %get-tuple-element.20), channel_id=1, source_target_pairs={{0,1},{1,0},{2,3},{3,2},{4,5},{5,4},{6,7},{7,6},{8,9},{9,8},{10,11... | collective-permute-start | bytes 1769480 | tf_op jit(solution)/shard_map/ppermute | solution.py:46
  63.0 0.1 copy.70
  63.1 0.1 copy.72
  63.4 0.3 copy.64
  63.6 1.3 collective-permute-done.7
  65.0 0.1 fusion.1
  65.2 0.7 convert_reduce_fusion
  65.9 0.2 fusion.10
  66.1 0.6 fusion
  66.8 0.9 pad_maximum_fusion.2
  67.7 12.9 %all-to-all-start = ((bf16[16,136,128]{2,1,0:T(8,128)(2,1)}), bf16[16,136,128]{2,1,0:T(8,128)(2,1)S(1)}, u32[]{:S(2)}, u32[]{:S(2)}) async-start(bf16[16,136,128]{2,1,0:T(8,128)(2,1)} %pad_maximum_fusion.2), calls=%async_computation | async-start | bytes 1114112 | tf_op jit(solution)/shard_map/all_to_all | solution.py:41
  80.6 0.1 copy.67
  80.8 3.9 %collective-permute-start.11 = (bf16[512,128]{1,0:T(8,128)(2,1)S(1)}, bf16[512,128]{1,0:T(8,128)(2,1)S(1)}, u32[]{:S(2)}, u32[]{:S(2)}) collective-permute-start(bf16[512,128]{1,0:T(8,128)(2,1)S(1)} %bitcast.151), channel_id=1, source_target_pairs={{0,384},{128,256},{256,128},{384,0},{1,385},{129,257},{257,129},{3... | collective-permute-start | bytes 393224 | tf_op jit(solution)/shard_map/ppermute | solution.py:46
  84.7 4.1 %collective-permute-done.11 = bf16[512,128]{1,0:T(8,128)(2,1)S(1)} collective-permute-done((bf16[512,128]{1,0:T(8,128)(2,1)S(1)}, bf16[512,128]{1,0:T(8,128)(2,1)S(1)}, u32[]{:S(2)}, u32[]{:S(2)}) %collective-permute-start.11) | collective-permute-done | bytes 131104 | tf_op jit(solution)/shard_map/ppermute | solution.py:46
  88.8 0.1 copy.90
  89.0 0.1 copy.69
  89.1 1.9 %collective-permute-start.12 = (bf16[512,128]{1,0:T(8,128)(2,1)S(1)}, bf16[512,128]{1,0:T(8,128)(2,1)S(1)}, u32[]{:S(2)}, u32[]{:S(2)}) collective-permute-start(bf16[512,128]{1,0:T(8,128)(2,1)S(1)} %bitcast.150), channel_id=1, source_target_pairs={{0,128},{128,0},{256,384},{384,256},{1,129},{129,1},{257,385},{385... | collective-permute-start | bytes 393224 | tf_op jit(solution)/shard_map/ppermute | solution.py:46
  91.1 0.1 copy.66
  91.3 4.7 %collective-permute-done.12 = bf16[512,128]{1,0:T(8,128)(2,1)S(1)} collective-permute-done((bf16[512,128]{1,0:T(8,128)(2,1)S(1)}, bf16[512,128]{1,0:T(8,128)(2,1)S(1)}, u32[]{:S(2)}, u32[]{:S(2)}) %collective-permute-start.12) | collective-permute-done | bytes 131104 | tf_op jit(solution)/shard_map/ppermute | solution.py:46
  96.3 0.2 fusion.4
  96.5 1.9 %collective-permute-start.13 = (f32[128]{0:T(128)S(1)}, f32[128]{0:T(128)S(1)}, u32[]{:S(2)}, u32[]{:S(2)}) collective-permute-start(f32[128]{0:T(128)S(1)} %fusion.4), channel_id=1, source_target_pairs={{0,1},{1,0},{2,3},{3,2},{4,5},{5,4},{6,7},{7,6},{8,9},{9,8},{10,11... | collective-permute-start | bytes 1544 | tf_op jit(solution)/shard_map/ppermute | solution.py:46
  98.4 1.1 collective-permute-done.13
  99.5 2.5 %collective-permute-start.14 = (f32[128]{0:T(128)S(1)}, f32[128]{0:T(128)S(1)}, u32[]{:S(2)}, u32[]{:S(2)}) collective-permute-start(f32[128]{0:T(128)S(1)} %add.56), channel_id=1, source_target_pairs={{0,2},{2,0},{4,6},{6,4},{1,3},{3,1},{5,7},{7,5},{8,10},{10,8},{12,... | collective-permute-start | bytes 1544 | tf_op jit(solution)/shard_map/ppermute | solution.py:46
  102.0 2.9 %collective-permute-done.14 = f32[128]{0:T(128)S(1)} collective-permute-done((f32[128]{0:T(128)S(1)}, f32[128]{0:T(128)S(1)}, u32[]{:S(2)}, u32[]{:S(2)}) %collective-permute-start.14) | collective-permute-done | bytes 544 | tf_op jit(solution)/shard_map/ppermute | solution.py:46
  104.9 3.9 %collective-permute-start.15 = (f32[128]{0:T(128)S(1)}, f32[128]{0:T(128)S(1)}, u32[]{:S(2)}, u32[]{:S(2)}) collective-permute-start(f32[128]{0:T(128)S(1)} %add.57), channel_id=1, source_target_pairs={{0,4},{2,6},{4,0},{6,2},{1,5},{3,7},{5,1},{7,3},{8,12},{10,14},{12... | collective-permute-start | bytes 1544 | tf_op jit(solution)/shard_map/ppermute | solution.py:46
  108.8 2.4 %collective-permute-done.15 = f32[128]{0:T(128)S(1)} collective-permute-done((f32[128]{0:T(128)S(1)}, f32[128]{0:T(128)S(1)}, u32[]{:S(2)}, u32[]{:S(2)}) %collective-permute-start.15) | collective-permute-done | bytes 544 | tf_op jit(solution)/shard_map/ppermute | solution.py:46
  111.3 4.7 %collective-permute-start.16 = (f32[128,128]{1,0:T(8,128)S(1)}, f32[128,128]{1,0:T(8,128)S(1)}, u32[]{:S(2)}, u32[]{:S(2)}) collective-permute-start(f32[128,128]{1,0:T(8,128)S(1)} %convert_reduce_fusion.1), channel_id=1, source_target_pairs={{0,0},{16,1},{32,2},{48,3},{64,4},{80,5},{96,6},{112,7},{8,8},{24,... | collective-permute-start | bytes 196616 | tf_op jit(solution)/shard_map/ppermute | solution.py:133
  116.0 0.6 broadcast_in_dim.11
  116.6 6.2 %all-to-all-start.1 = ((f32[4,2,128]{2,1,0:T(2,128)}), f32[4,2,128]{2,1,0:T(2,128)S(1)}, u32[]{:S(2)}, u32[]{:S(2)}) async-start(f32[4,2,128]{2,1,0:T(2,128)} %broadcast_in_dim.11), calls=%async_computation.1 | async-start | bytes 8192 | tf_op jit(solution)/shard_map/all_to_all | solution.py:41
  122.9 1.0 fusion.8
  123.8 4.3 %all-to-all-done.1 = f32[4,2,128]{2,1,0:T(2,128)S(1)} async-done(((f32[4,2,128]{2,1,0:T(2,128)}), f32[4,2,128]{2,1,0:T(2,128)S(1)}, u32[]{:S(2)}, u32[]{:S(2)}) %all-to-all-start.1) | async-done | bytes 4128 | tf_op jit(solution)/shard_map/all_to_all | solution.py:41
  128.2 0.6 copy.111
  128.8 0.6 copy.112
  (86 shorter events, 1.2 us)
Async XLA Ops:
  2.8 1.2 copy-start.2
  3.5 5.2 %copy-start.4 = (bf16[128,128]{1,0:T(8,128)(2,1)S(1)}, bf16[128,128]{1,0:T(8,128)(2,1)}, u32[]{:S(2)}) copy-start(bf16[128,128]{1,0:T(8,128)(2,1)} %param.8) | copy-start | bytes 98308
  4.4 27.4 %collective-permute-start = (bf16[1,144,128]{2,1,0:T(8,128)(2,1)S(1)}, bf16[1,144,128]{2,1,0:T(8,128)(2,1)S(1)}, u32[]{:S(2)}, u32[]{:S(2)}) collective-permute-start(bf16[1,144,128]{2,1,0:T(8,128)(2,1)S(1)} %maximum_bitcast_fusion), channel_id=1, source_target_pairs={{0,2},{2,0},{4,6},{6,4},{1,3},{3,1},{5,7},{7,5},{8,10},{10,8},{12,... | collective-permute-start | bytes 110600 | tf_op jit(solution)/shard_map/ppermute | solution.py:46
  8.7 23.1 %collective-permute-start.1 = (bf16[128,128]{1,0:T(8,128)(2,1)S(1)}, bf16[128,128]{1,0:T(8,128)(2,1)S(1)}, u32[]{:S(2)}, u32[]{:S(2)}) collective-permute-start(bf16[128,128]{1,0:T(8,128)(2,1)S(1)} %copy-done.4), channel_id=1, source_target_pairs={{0,0},{1,16},{2,32},{3,48},{4,64},{5,80},{6,96},{7,112},{8,8},{9,2... | collective-permute-start | bytes 98312 | tf_op jit(solution)/shard_map/ppermute | solution.py:84
  13.2 18.7 %collective-permute-start.2 = (bf16[128,128]{1,0:T(8,128)(2,1)S(1)}, bf16[128,128]{1,0:T(8,128)(2,1)S(1)}, u32[]{:S(2)}, u32[]{:S(2)}) collective-permute-start(bf16[128,128]{1,0:T(8,128)(2,1)S(1)} %copy-done.4), channel_id=1, source_target_pairs={{0,8},{1,24},{2,40},{3,56},{4,72},{5,88},{6,104},{7,120},{8,0},{9,... | collective-permute-start | bytes 98312 | tf_op jit(solution)/shard_map/ppermute | solution.py:85
  29.9 9.9 %collective-permute-start.4 = (bf16[512,128]{1,0:T(8,128)(2,1)S(1)}, bf16[512,128]{1,0:T(8,128)(2,1)S(1)}, u32[]{:S(2)}, u32[]{:S(2)}) collective-permute-start(bf16[512,128]{1,0:T(8,128)(2,1)S(1)} %bitcast.147), channel_id=1, source_target_pairs={{0,384},{128,256},{256,128},{384,0},{1,385},{129,257},{257,129},{3... | collective-permute-start | bytes 393224 | tf_op jit(solution)/shard_map/ppermute | solution.py:46
  31.9 7.9 %collective-permute-start.3 = (bf16[2,144,128]{2,1,0:T(8,128)(2,1)S(1)}, bf16[2,144,128]{2,1,0:T(8,128)(2,1)S(1)}, u32[]{:S(2)}, u32[]{:S(2)}) collective-permute-start(bf16[2,144,128]{2,1,0:T(8,128)(2,1)S(1)} %pad_maximum_fusion.13), channel_id=1, source_target_pairs={{0,4},{2,6},{4,0},{6,2},{1,5},{3,7},{5,1},{7,3},{8,12},{10,14},{12... | collective-permute-start | bytes 221192 | tf_op jit(solution)/shard_map/ppermute | solution.py:46
  33.9 10.1 %collective-permute-start.8 = (bf16[2,128,128]{2,1,0:T(8,128)(2,1)S(1)}, bf16[2,128,128]{2,1,0:T(8,128)(2,1)S(1)}, u32[]{:S(2)}, u32[]{:S(2)}) collective-permute-start(bf16[2,128,128]{2,1,0:T(8,128)(2,1)S(1)} %pad_maximum_fusion.14), channel_id=1, source_target_pairs={{0,64},{16,80},{32,96},{48,112},{64,0},{80,16},{96,32},{112,48},{1... | collective-permute-start | bytes 196616 | tf_op jit(solution)/shard_map/ppermute | solution.py:46
  39.8 9.5 %copy-start.3 = (f32[1024]{0:T(1024)S(1)}, f32[1024]{0:T(1024)}, u32[]{:S(2)}) copy-start(f32[1024]{0:T(1024)} %param.9) | copy-start | bytes 12292
  40.2 9.4 %collective-permute-start.5 = (bf16[1088,128]{1,0:T(8,128)(2,1)S(1)}, bf16[1088,128]{1,0:T(8,128)(2,1)S(1)}, u32[]{:S(2)}, u32[]{:S(2)}) collective-permute-start(bf16[1088,128]{1,0:T(8,128)(2,1)S(1)} %pad_maximum_fusion.5), channel_id=1, source_target_pairs={{0,128},{128,0},{256,384},{384,256},{1,129},{129,1},{257,385},{385... | collective-permute-start | bytes 835592 | tf_op jit(solution)/shard_map/ppermute | solution.py:46
  44.0 9.6 %collective-permute-start.9 = (bf16[2,2,128,128]{3,2,1,0:T(8,128)(2,1)S(1)}, bf16[2,2,128,128]{3,2,1,0:T(8,128)(2,1)S(1)}, u32[]{:S(2)}, u32[]{:S(2)}) collective-permute-start(bf16[2,2,128,128]{3,2,1,0:T(8,128)(2,1)S(1)} %pad_maximum_fusion.11), channel_id=1, source_target_pairs={{0,32},{16,48},{32,0},{48,16},{64,96},{80,112},{96,64},{112,80},{1... | collective-permute-start | bytes 393224 | tf_op jit(solution)/shard_map/ppermute | solution.py:46
  49.6 11.3 %collective-permute-start.6 = (bf16[2,4,144,128]{3,2,1,0:T(8,128)(2,1)S(1)}, bf16[2,4,144,128]{3,2,1,0:T(8,128)(2,1)S(1)}, u32[]{:S(2)}, u32[]{:S(2)}) collective-permute-start(bf16[2,4,144,128]{3,2,1,0:T(8,128)(2,1)S(1)} %pad_maximum_fusion.4), channel_id=1, source_target_pairs={{0,384},{128,256},{256,128},{384,0},{1,385},{129,257},{257,129},{3... | collective-permute-start | bytes 884744 | tf_op jit(solution)/shard_map/ppermute | solution.py:46
  53.7 9.5 %collective-permute-start.10 = (bf16[2,2,2,128,128]{4,3,2,0,1:T(8,128)(2,1)S(1)}, bf16[2,2,2,128,128]{4,3,2,0,1:T(8,128)(2,1)S(1)}, u32[]{:S(2)}, u32[]{:S(2)}) collective-permute-start(bf16[2,2,2,128,128]{4,3,2,0,1:T(8,128)(2,1)S(1)} %pad_maximum_fusion.6), channel_id=1, source_target_pairs={{0,16},{16,0},{32,48},{48,32},{64,80},{80,64},{96,112},{112,96},{1... | collective-permute-start | bytes 786440 | tf_op jit(solution)/shard_map/ppermute | solution.py:46
  61.0 3.9 %collective-permute-start.7 = (bf16[4,4,144,128]{3,2,1,0:T(8,128)(2,1)S(1)}, bf16[4,4,144,128]{3,2,1,0:T(8,128)(2,1)S(1)}, u32[]{:S(2)}, u32[]{:S(2)}) collective-permute-start(bf16[4,4,144,128]{3,2,1,0:T(8,128)(2,1)S(1)} %get-tuple-element.20), channel_id=1, source_target_pairs={{0,1},{1,0},{2,3},{3,2},{4,5},{5,4},{6,7},{7,6},{8,9},{9,8},{10,11... | collective-permute-start | bytes 1769480 | tf_op jit(solution)/shard_map/ppermute | solution.py:46
  67.7 43.6 %all-to-all-start = ((bf16[16,136,128]{2,1,0:T(8,128)(2,1)}), bf16[16,136,128]{2,1,0:T(8,128)(2,1)S(1)}, u32[]{:S(2)}, u32[]{:S(2)}) async-start(bf16[16,136,128]{2,1,0:T(8,128)(2,1)} %pad_maximum_fusion.2), calls=%async_computation | async-start | bytes 1114112 | tf_op jit(solution)/shard_map/all_to_all | solution.py:41
  80.8 8.1 %collective-permute-start.11 = (bf16[512,128]{1,0:T(8,128)(2,1)S(1)}, bf16[512,128]{1,0:T(8,128)(2,1)S(1)}, u32[]{:S(2)}, u32[]{:S(2)}) collective-permute-start(bf16[512,128]{1,0:T(8,128)(2,1)S(1)} %bitcast.151), channel_id=1, source_target_pairs={{0,384},{128,256},{256,128},{384,0},{1,385},{129,257},{257,129},{3... | collective-permute-start | bytes 393224 | tf_op jit(solution)/shard_map/ppermute | solution.py:46
  89.0 7.3 %copy-start = (bf16[128,1024]{1,0:T(8,128)(2,1)S(1)}, bf16[128,1024]{1,0:T(8,128)(2,1)}, u32[]{:S(2)}) copy-start(bf16[128,1024]{1,0:T(8,128)(2,1)} %param.5) | copy-start | bytes 786436
  89.1 6.9 %collective-permute-start.12 = (bf16[512,128]{1,0:T(8,128)(2,1)S(1)}, bf16[512,128]{1,0:T(8,128)(2,1)S(1)}, u32[]{:S(2)}, u32[]{:S(2)}) collective-permute-start(bf16[512,128]{1,0:T(8,128)(2,1)S(1)} %bitcast.150), channel_id=1, source_target_pairs={{0,128},{128,0},{256,384},{384,256},{1,129},{129,1},{257,385},{385... | collective-permute-start | bytes 393224 | tf_op jit(solution)/shard_map/ppermute | solution.py:46
  96.0 26.8 %copy-start.1 = (bf16[128,1024]{1,0:T(8,128)(2,1)S(1)}, bf16[128,1024]{1,0:T(8,128)(2,1)}, u32[]{:S(2)}) copy-start(bf16[128,1024]{1,0:T(8,128)(2,1)} %param.6) | copy-start | bytes 786436
  96.5 3.0 %collective-permute-start.13 = (f32[128]{0:T(128)S(1)}, f32[128]{0:T(128)S(1)}, u32[]{:S(2)}, u32[]{:S(2)}) collective-permute-start(f32[128]{0:T(128)S(1)} %fusion.4), channel_id=1, source_target_pairs={{0,1},{1,0},{2,3},{3,2},{4,5},{5,4},{6,7},{7,6},{8,9},{9,8},{10,11... | collective-permute-start | bytes 1544 | tf_op jit(solution)/shard_map/ppermute | solution.py:46
  99.5 5.4 %collective-permute-start.14 = (f32[128]{0:T(128)S(1)}, f32[128]{0:T(128)S(1)}, u32[]{:S(2)}, u32[]{:S(2)}) collective-permute-start(f32[128]{0:T(128)S(1)} %add.56), channel_id=1, source_target_pairs={{0,2},{2,0},{4,6},{6,4},{1,3},{3,1},{5,7},{7,5},{8,10},{10,8},{12,... | collective-permute-start | bytes 1544 | tf_op jit(solution)/shard_map/ppermute | solution.py:46
  104.9 6.3 %collective-permute-start.15 = (f32[128]{0:T(128)S(1)}, f32[128]{0:T(128)S(1)}, u32[]{:S(2)}, u32[]{:S(2)}) collective-permute-start(f32[128]{0:T(128)S(1)} %add.57), channel_id=1, source_target_pairs={{0,4},{2,6},{4,0},{6,2},{1,5},{3,7},{5,1},{7,3},{8,12},{10,14},{12... | collective-permute-start | bytes 1544 | tf_op jit(solution)/shard_map/ppermute | solution.py:46
  111.3 16.8 %collective-permute-start.16 = (f32[128,128]{1,0:T(8,128)S(1)}, f32[128,128]{1,0:T(8,128)S(1)}, u32[]{:S(2)}, u32[]{:S(2)}) collective-permute-start(f32[128,128]{1,0:T(8,128)S(1)} %convert_reduce_fusion.1), channel_id=1, source_target_pairs={{0,0},{16,1},{32,2},{48,3},{64,4},{80,5},{96,6},{112,7},{8,8},{24,... | collective-permute-start | bytes 196616 | tf_op jit(solution)/shard_map/ppermute | solution.py:133
  116.6 11.5 %all-to-all-start.1 = ((f32[4,2,128]{2,1,0:T(2,128)}), f32[4,2,128]{2,1,0:T(2,128)S(1)}, u32[]{:S(2)}, u32[]{:S(2)}) async-start(f32[4,2,128]{2,1,0:T(2,128)} %broadcast_in_dim.11), calls=%async_computation.1 | async-start | bytes 8192 | tf_op jit(solution)/shard_map/all_to_all | solution.py:41

commit v15 on v8

--- a/solution.py
+++ b/solution.py
@@ -80,8 +80,8 @@
     def quarter(r):
         return lax.dynamic_slice_in_dim(blocks, (mine ^ r) * 2, 2, axis=0)
 
+    packet = jnp.concatenate([packet, swap(packet, "zl", 1)])
     packet, moved = lax.optimization_barrier((packet, moved))
-    packet = jnp.concatenate([packet, swap(packet, "zl", 1)])
     weights = moved
     for axis, mask, place in (("zh", 1, 0), ("y", 4, 0), ("y", 2, 1), ("y", 1, 2)):
         other = swap(weights, axis, mask)
@@ -123,7 +123,7 @@
     pieces = jnp.einsum(
         "ktc,btf->kbcf", kv, normed, preferred_element_type=jnp.float32
     ).astype(jnp.bfloat16)
-    gain_rows = jnp.broadcast_to(jnp.pad(gain_part, ((0, 10), (0, 0)))[None], (16, 16, HD))
+    gain_rows = jnp.broadcast_to(jnp.pad(gain_part, ((0, 2), (0, 0)))[None], (16, 8, HD))
     arrived = exchange(jnp.concatenate([pieces.reshape(16, HD, HD), gain_rows], axis=1), ROW)
     block = jnp.sum(arrived[:, :HD].astype(jnp.float32), axis=0)
     weight_grad = lax.ppermute(block, AXES, [(b, a) for a, b in moves])

time: 125 us -> 125 us (level)
  waiting for transfers between devices: 32.4 us -> 28.9 us
  starting transfers between devices: 78.3 us -> 81 us
  other arithmetic: 4.41 us -> 5.92 us
    ppermute x15, waiting for transfers between devices: 25.3 us -> 20.3 us  [swap(): return lax.ppermute(value, axis, [(i, i ^ mask) for i in range(count)])]
    ppermute x15, starting transfers between devices: 57.8 us -> 60 us  [swap(): return lax.ppermute(value, axis, [(i, i ^ mask) for i in range(count)])]
    ppermute x1, waiting for transfers between devices: 2.71 us -> 4.28 us  [shards(): moved = lax.ppermute(kv_weight, AXES, moves)]
  transfers between devices with their start and end apart: 19 -> 19, of which waited for: 13 -> 11; matrix products, arithmetic and copies ran while one was open for 6% -> 5% of each run, Pallas kernels for 0% -> 0%
where the time goes in v15:
time: 125 us; the launch traced here: 124 us
  starting transfers between devices  81 us (65%)
  waiting for transfers between devices  28.9 us (23%)
  other arithmetic  5.92 us (5%)
  local copies, waits for them, and re-layouts  5.85 us (5%)
  between operations  1.41 us (1%)
  matrix products  1.32 us (1%)
    ppermute x15, starting transfers between devices, swap(): return lax.ppermute(value, axis, [(i, i ^ mask) for i in range(count)])  60 us
    ppermute x15, waiting for transfers between devices, swap(): return lax.ppermute(value, axis, [(i, i ^ mask) for i in range(count)])  20.3 us
    all_to_all x2, starting transfers between devices, exchange(): return lax.all_to_all(value, axes, split_axis=0, concat_axis=0, tiled=True)  12.4 us
    ppermute x1, starting transfers between devices, shards(): moved = lax.ppermute(kv_weight, AXES, moves)  4.42 us
    all_to_all x2, waiting for transfers between devices, exchange(): return lax.all_to_all(value, axes, split_axis=0, concat_axis=0, tiled=True)  4.34 us
    ppermute x1, waiting for transfers between devices, shards(): moved = lax.ppermute(kv_weight, AXES, moves)  4.28 us
    ppermute x1, starting transfers between devices, shards(): weight_grad = lax.ppermute(block, AXES, [(b, a) for a, b in moves])  4.27 us
  transfers between devices with their start and end apart: 19, of which 11 were waited for; matrix products, arithmetic and copies ran while one was open for 5% of the time, Pallas kernels for 0%

profile of v15, /device:TPU:48, one launch (start us, length us, event | category | flops | bytes accessed | tf_op | source)
XLA Modules:
  0.0 124.4 jit_solution(17032409067974888528)
XLA Ops:
  0.6 1.1 fusion.9
  1.7 0.8 convert_element_type.61
  2.5 0.3 multiply_add_fusion
  2.8 0.9 fusion.15
  3.7 4.3 %collective-permute-start = (bf16[1,144,128]{2,1,0:T(8,128)(2,1)S(1)}, bf16[1,144,128]{2,1,0:T(8,128)(2,1)S(1)}, u32[]{:S(2)}, u32[]{:S(2)}) collective-permute-start(bf16[1,144,128]{2,1,0:T(8,128)(2,1)S(1)} %maximum_bitcast_fusion), channel_id=1, source_target_pairs={{0,2},{2,0},{4,6},{6,4},{1,3},{3,1},{5,7},{7,5},{8,10},{10,8},{12,... | collective-permute-start | bytes 110600 | tf_op jit(solution)/shard_map/ppermute | solution.py:46
  8.0 4.4 %collective-permute-start.1 = (bf16[128,128]{1,0:T(8,128)(2,1)}, bf16[128,128]{1,0:T(8,128)(2,1)S(1)}, u32[]{:S(2)}, u32[]{:S(2)}) collective-permute-start(bf16[128,128]{1,0:T(8,128)(2,1)} %param.8), channel_id=1, source_target_pairs={{0,0},{1,16},{2,32},{3,48},{4,64},{5,80},{6,96},{7,112},{8,8},{9,2... | collective-permute-start | bytes 98312 | tf_op jit(solution)/shard_map/ppermute | solution.py:67
  12.4 0.9 fusion.30
  13.3 0.1 copy.82
  13.4 0.1 copy.83
  13.6 0.1 copy.84
  13.7 0.1 copy.85
  13.8 0.1 copy.86
  13.9 0.1 copy.87
  14.1 0.1 copy.88
  14.2 0.1 copy.89
  14.5 4.3 %collective-permute-done.1 = bf16[128,128]{1,0:T(8,128)(2,1)S(1)} collective-permute-done((bf16[128,128]{1,0:T(8,128)(2,1)}, bf16[128,128]{1,0:T(8,128)(2,1)S(1)}, u32[]{:S(2)}, u32[]{:S(2)}) %collective-permute-start.1) | collective-permute-done | bytes 32800 | tf_op jit(solution)/shard_map/ppermute | solution.py:67
  18.8 10.0 %collective-permute-start.7 = (bf16[128,128]{1,0:T(8,128)(2,1)S(1)}, bf16[128,128]{1,0:T(8,128)(2,1)S(1)}, u32[]{:S(2)}, u32[]{:S(2)}) collective-permute-start(bf16[128,128]{1,0:T(8,128)(2,1)S(1)} %collective-permute-done.1), channel_id=1, source_target_pairs={{0,8},{8,0},{1,9},{9,1},{2,10},{10,2},{3,11},{11,3},{4,12},{12,4},... | collective-permute-start | bytes 98312 | tf_op jit(solution)/shard_map/ppermute | solution.py:46
  28.8 0.1 copy.61
  29.0 7.7 %collective-permute-start.3 = (bf16[512,128]{1,0:T(8,128)(2,1)S(1)}, bf16[512,128]{1,0:T(8,128)(2,1)S(1)}, u32[]{:S(2)}, u32[]{:S(2)}) collective-permute-start(bf16[512,128]{1,0:T(8,128)(2,1)S(1)} %bitcast.147), channel_id=1, source_target_pairs={{0,384},{128,256},{256,128},{384,0},{1,385},{129,257},{257,129},{3... | collective-permute-start | bytes 393224 | tf_op jit(solution)/shard_map/ppermute | solution.py:46
  36.7 1.9 %collective-permute-start.2 = (bf16[2,144,128]{2,1,0:T(8,128)(2,1)S(1)}, bf16[2,144,128]{2,1,0:T(8,128)(2,1)S(1)}, u32[]{:S(2)}, u32[]{:S(2)}) collective-permute-start(bf16[2,144,128]{2,1,0:T(8,128)(2,1)S(1)} %pad_maximum_fusion.13), channel_id=1, source_target_pairs={{0,4},{2,6},{4,0},{6,2},{1,5},{3,7},{5,1},{7,3},{8,12},{10,14},{12... | collective-permute-start | bytes 221192 | tf_op jit(solution)/shard_map/ppermute | solution.py:46
  38.6 1.9 %collective-permute-start.8 = (bf16[2,128,128]{2,1,0:T(8,128)(2,1)S(1)}, bf16[2,128,128]{2,1,0:T(8,128)(2,1)S(1)}, u32[]{:S(2)}, u32[]{:S(2)}) collective-permute-start(bf16[2,128,128]{2,1,0:T(8,128)(2,1)S(1)} %pad_maximum_fusion.14), channel_id=1, source_target_pairs={{0,64},{16,80},{32,96},{48,112},{64,0},{80,16},{96,32},{112,48},{1... | collective-permute-start | bytes 196616 | tf_op jit(solution)/shard_map/ppermute | solution.py:46
  40.6 3.2 %collective-permute-done.2 = bf16[2,144,128]{2,1,0:T(8,128)(2,1)S(1)} collective-permute-done((bf16[2,144,128]{2,1,0:T(8,128)(2,1)S(1)}, bf16[2,144,128]{2,1,0:T(8,128)(2,1)S(1)}, u32[]{:S(2)}, u32[]{:S(2)}) %collective-permute-start.2) | collective-permute-done | bytes 73760 | tf_op jit(solution)/shard_map/ppermute | solution.py:46
  43.9 0.1 copy.62
  44.0 0.1 copy.63
  44.2 3.3 %collective-permute-start.4 = (bf16[1088,128]{1,0:T(8,128)(2,1)S(1)}, bf16[1088,128]{1,0:T(8,128)(2,1)S(1)}, u32[]{:S(2)}, u32[]{:S(2)}) collective-permute-start(bf16[1088,128]{1,0:T(8,128)(2,1)S(1)} %pad_maximum_fusion.5), channel_id=1, source_target_pairs={{0,128},{128,0},{256,384},{384,256},{1,129},{129,1},{257,385},{385... | collective-permute-start | bytes 835592 | tf_op jit(solution)/shard_map/ppermute | solution.py:46
  47.5 1.2 collective-permute-done.8
  48.7 4.0 %collective-permute-start.9 = (bf16[2,2,128,128]{3,2,1,0:T(8,128)(2,1)S(1)}, bf16[2,2,128,128]{3,2,1,0:T(8,128)(2,1)S(1)}, u32[]{:S(2)}, u32[]{:S(2)}) collective-permute-start(bf16[2,2,128,128]{3,2,1,0:T(8,128)(2,1)S(1)} %pad_maximum_fusion.11), channel_id=1, source_target_pairs={{0,32},{16,48},{32,0},{48,16},{64,96},{80,112},{96,64},{112,80},{1... | collective-permute-start | bytes 393224 | tf_op jit(solution)/shard_map/ppermute | solution.py:46
  52.8 0.1 copy.71
  53.0 5.2 %collective-permute-start.5 = (bf16[2,4,144,128]{3,2,1,0:T(8,128)(2,1)S(1)}, bf16[2,4,144,128]{3,2,1,0:T(8,128)(2,1)S(1)}, u32[]{:S(2)}, u32[]{:S(2)}) collective-permute-start(bf16[2,4,144,128]{3,2,1,0:T(8,128)(2,1)S(1)} %pad_maximum_fusion.4), channel_id=1, source_target_pairs={{0,384},{128,256},{256,128},{384,0},{1,385},{129,257},{257,129},{3... | collective-permute-start | bytes 884744 | tf_op jit(solution)/shard_map/ppermute | solution.py:46
  58.2 2.7 %collective-permute-start.10 = (bf16[2,2,2,128,128]{4,3,2,0,1:T(8,128)(2,1)S(1)}, bf16[2,2,2,128,128]{4,3,2,0,1:T(8,128)(2,1)S(1)}, u32[]{:S(2)}, u32[]{:S(2)}) collective-permute-start(bf16[2,2,2,128,128]{4,3,2,0,1:T(8,128)(2,1)S(1)} %pad_maximum_fusion.6), channel_id=1, source_target_pairs={{0,16},{16,0},{32,48},{48,32},{64,80},{80,64},{96,112},{112,96},{1... | collective-permute-start | bytes 786440 | tf_op jit(solution)/shard_map/ppermute | solution.py:46
  61.0 1.9 %collective-permute-done.5 = bf16[2,4,144,128]{3,2,1,0:T(8,128)(2,1)S(1)} collective-permute-done((bf16[2,4,144,128]{3,2,1,0:T(8,128)(2,1)S(1)}, bf16[2,4,144,128]{3,2,1,0:T(8,128)(2,1)S(1)}, u32[]{:S(2)}, u32[]{:S(2)}) %collective-permute-start.5) | collective-permute-done | bytes 294944 | tf_op jit(solution)/shard_map/ppermute | solution.py:46
  62.9 1.9 %collective-permute-start.6 = (bf16[4,4,144,128]{3,2,1,0:T(8,128)(2,1)S(1)}, bf16[4,4,144,128]{3,2,1,0:T(8,128)(2,1)S(1)}, u32[]{:S(2)}, u32[]{:S(2)}) collective-permute-start(bf16[4,4,144,128]{3,2,1,0:T(8,128)(2,1)S(1)} %get-tuple-element.12), channel_id=1, source_target_pairs={{0,1},{1,0},{2,3},{3,2},{4,5},{5,4},{6,7},{7,6},{8,9},{9,8},{10,11... | collective-permute-start | bytes 1769480 | tf_op jit(solution)/shard_map/ppermute | solution.py:46
  64.9 0.1 copy.70
  65.0 0.1 copy.72
  65.1 1.4 %collective-permute-done.10 = bf16[2,2,2,128,128]{4,3,2,0,1:T(8,128)(2,1)S(1)} collective-permute-done((bf16[2,2,2,128,128]{4,3,2,0,1:T(8,128)(2,1)S(1)}, bf16[2,2,2,128,128]{4,3,2,0,1:T(8,128)(2,1)S(1)}, u32[]{:S(2)}, u32[]{:S(2)}) %collective-permute-start.10) | collective-permute-done | bytes 262176 | tf_op jit(solution)/shard_map/ppermute | solution.py:46
  66.6 0.3 copy.64
  66.9 0.1 fusion.1
  67.1 0.7 convert_reduce_fusion
  67.9 0.2 fusion.10
  68.1 0.6 fusion
  68.8 0.8 pad_maximum_fusion.2
  69.6 5.9 %all-to-all-start = ((bf16[16,136,128]{2,1,0:T(8,128)(2,1)}), bf16[16,136,128]{2,1,0:T(8,128)(2,1)S(1)}, u32[]{:S(2)}, u32[]{:S(2)}) async-start(bf16[16,136,128]{2,1,0:T(8,128)(2,1)} %pad_maximum_fusion.2), calls=%async_computation | async-start | bytes 1114112 | tf_op jit(solution)/shard_map/all_to_all | solution.py:41
  75.6 0.1 copy.67
  75.7 5.1 %collective-permute-start.11 = (bf16[512,128]{1,0:T(8,128)(2,1)S(1)}, bf16[512,128]{1,0:T(8,128)(2,1)S(1)}, u32[]{:S(2)}, u32[]{:S(2)}) collective-permute-start(bf16[512,128]{1,0:T(8,128)(2,1)S(1)} %bitcast.151), channel_id=1, source_target_pairs={{0,384},{128,256},{256,128},{384,0},{1,385},{129,257},{257,129},{3... | collective-permute-start | bytes 393224 | tf_op jit(solution)/shard_map/ppermute | solution.py:46
  80.8 3.1 %collective-permute-done.11 = bf16[512,128]{1,0:T(8,128)(2,1)S(1)} collective-permute-done((bf16[512,128]{1,0:T(8,128)(2,1)S(1)}, bf16[512,128]{1,0:T(8,128)(2,1)S(1)}, u32[]{:S(2)}, u32[]{:S(2)}) %collective-permute-start.11) | collective-permute-done | bytes 131104 | tf_op jit(solution)/shard_map/ppermute | solution.py:46
  84.0 0.1 copy.90
  84.1 0.1 copy.69
  84.3 2.9 %collective-permute-start.12 = (bf16[512,128]{1,0:T(8,128)(2,1)S(1)}, bf16[512,128]{1,0:T(8,128)(2,1)S(1)}, u32[]{:S(2)}, u32[]{:S(2)}) collective-permute-start(bf16[512,128]{1,0:T(8,128)(2,1)S(1)} %bitcast.150), channel_id=1, source_target_pairs={{0,128},{128,0},{256,384},{384,256},{1,129},{129,1},{257,385},{385... | collective-permute-start | bytes 393224 | tf_op jit(solution)/shard_map/ppermute | solution.py:46
  87.2 0.1 copy.66
  87.4 3.8 %collective-permute-done.12 = bf16[512,128]{1,0:T(8,128)(2,1)S(1)} collective-permute-done((bf16[512,128]{1,0:T(8,128)(2,1)S(1)}, bf16[512,128]{1,0:T(8,128)(2,1)S(1)}, u32[]{:S(2)}, u32[]{:S(2)}) %collective-permute-start.12) | collective-permute-done | bytes 131104 | tf_op jit(solution)/shard_map/ppermute | solution.py:46
  91.4 0.2 fusion.4
  91.6 1.9 %collective-permute-start.13 = (f32[128]{0:T(128)S(1)}, f32[128]{0:T(128)S(1)}, u32[]{:S(2)}, u32[]{:S(2)}) collective-permute-start(f32[128]{0:T(128)S(1)} %fusion.4), channel_id=1, source_target_pairs={{0,1},{1,0},{2,3},{3,2},{4,5},{5,4},{6,7},{7,6},{8,9},{9,8},{10,11... | collective-permute-start | bytes 1544 | tf_op jit(solution)/shard_map/ppermute | solution.py:46
  93.5 1.1 collective-permute-done.13
  94.6 2.3 %collective-permute-start.14 = (f32[128]{0:T(128)S(1)}, f32[128]{0:T(128)S(1)}, u32[]{:S(2)}, u32[]{:S(2)}) collective-permute-start(f32[128]{0:T(128)S(1)} %add.56), channel_id=1, source_target_pairs={{0,2},{2,0},{4,6},{6,4},{1,3},{3,1},{5,7},{7,5},{8,10},{10,8},{12,... | collective-permute-start | bytes 1544 | tf_op jit(solution)/shard_map/ppermute | solution.py:46
  96.9 3.1 %collective-permute-done.14 = f32[128]{0:T(128)S(1)} collective-permute-done((f32[128]{0:T(128)S(1)}, f32[128]{0:T(128)S(1)}, u32[]{:S(2)}, u32[]{:S(2)}) %collective-permute-start.14) | collective-permute-done | bytes 544 | tf_op jit(solution)/shard_map/ppermute | solution.py:46
  100.0 4.9 %collective-permute-start.15 = (f32[128]{0:T(128)S(1)}, f32[128]{0:T(128)S(1)}, u32[]{:S(2)}, u32[]{:S(2)}) collective-permute-start(f32[128]{0:T(128)S(1)} %add.57), channel_id=1, source_target_pairs={{0,4},{2,6},{4,0},{6,2},{1,5},{3,7},{5,1},{7,3},{8,12},{10,14},{12... | collective-permute-start | bytes 1544 | tf_op jit(solution)/shard_map/ppermute | solution.py:46
  104.9 1.5 %collective-permute-done.15 = f32[128]{0:T(128)S(1)} collective-permute-done((f32[128]{0:T(128)S(1)}, f32[128]{0:T(128)S(1)}, u32[]{:S(2)}, u32[]{:S(2)}) %collective-permute-start.15) | collective-permute-done | bytes 544 | tf_op jit(solution)/shard_map/ppermute | solution.py:46
  106.5 4.3 %collective-permute-start.16 = (f32[128,128]{1,0:T(8,128)S(1)}, f32[128,128]{1,0:T(8,128)S(1)}, u32[]{:S(2)}, u32[]{:S(2)}) collective-permute-start(f32[128,128]{1,0:T(8,128)S(1)} %convert_reduce_fusion.1), channel_id=1, source_target_pairs={{0,0},{16,1},{32,2},{48,3},{64,4},{80,5},{96,6},{112,7},{8,8},{24,... | collective-permute-start | bytes 196616 | tf_op jit(solution)/shard_map/ppermute | solution.py:129
  110.8 0.6 broadcast_in_dim.11
  111.4 6.5 %all-to-all-start.1 = ((f32[4,2,128]{2,1,0:T(2,128)}), f32[4,2,128]{2,1,0:T(2,128)S(1)}, u32[]{:S(2)}, u32[]{:S(2)}) async-start(f32[4,2,128]{2,1,0:T(2,128)} %broadcast_in_dim.11), calls=%async_computation.1 | async-start | bytes 8192 | tf_op jit(solution)/shard_map/all_to_all | solution.py:41
  117.9 1.0 fusion.8
  118.9 4.3 %all-to-all-done.1 = f32[4,2,128]{2,1,0:T(2,128)S(1)} async-done(((f32[4,2,128]{2,1,0:T(2,128)}), f32[4,2,128]{2,1,0:T(2,128)S(1)}, u32[]{:S(2)}, u32[]{:S(2)}) %all-to-all-start.1) | async-done | bytes 4128 | tf_op jit(solution)/shard_map/all_to_all | solution.py:41
  123.2 0.6 copy.111
  123.8 0.6 copy.112
  (82 shorter events, 1.3 us)
Async XLA Ops:
  3.7 10.8 %collective-permute-start = (bf16[1,144,128]{2,1,0:T(8,128)(2,1)S(1)}, bf16[1,144,128]{2,1,0:T(8,128)(2,1)S(1)}, u32[]{:S(2)}, u32[]{:S(2)}) collective-permute-start(bf16[1,144,128]{2,1,0:T(8,128)(2,1)S(1)} %maximum_bitcast_fusion), channel_id=1, source_target_pairs={{0,2},{2,0},{4,6},{6,4},{1,3},{3,1},{5,7},{7,5},{8,10},{10,8},{12,... | collective-permute-start | bytes 110600 | tf_op jit(solution)/shard_map/ppermute | solution.py:46
  8.0 10.8 %collective-permute-start.1 = (bf16[128,128]{1,0:T(8,128)(2,1)}, bf16[128,128]{1,0:T(8,128)(2,1)S(1)}, u32[]{:S(2)}, u32[]{:S(2)}) collective-permute-start(bf16[128,128]{1,0:T(8,128)(2,1)} %param.8), channel_id=1, source_target_pairs={{0,0},{1,16},{2,32},{3,48},{4,64},{5,80},{6,96},{7,112},{8,8},{9,2... | collective-permute-start | bytes 98312 | tf_op jit(solution)/shard_map/ppermute | solution.py:67
  18.8 19.8 %collective-permute-start.7 = (bf16[128,128]{1,0:T(8,128)(2,1)S(1)}, bf16[128,128]{1,0:T(8,128)(2,1)S(1)}, u32[]{:S(2)}, u32[]{:S(2)}) collective-permute-start(bf16[128,128]{1,0:T(8,128)(2,1)S(1)} %collective-permute-done.1), channel_id=1, source_target_pairs={{0,8},{8,0},{1,9},{9,1},{2,10},{10,2},{3,11},{11,3},{4,12},{12,4},... | collective-permute-start | bytes 98312 | tf_op jit(solution)/shard_map/ppermute | solution.py:46
  29.0 14.9 %collective-permute-start.3 = (bf16[512,128]{1,0:T(8,128)(2,1)S(1)}, bf16[512,128]{1,0:T(8,128)(2,1)S(1)}, u32[]{:S(2)}, u32[]{:S(2)}) collective-permute-start(bf16[512,128]{1,0:T(8,128)(2,1)S(1)} %bitcast.147), channel_id=1, source_target_pairs={{0,384},{128,256},{256,128},{384,0},{1,385},{129,257},{257,129},{3... | collective-permute-start | bytes 393224 | tf_op jit(solution)/shard_map/ppermute | solution.py:46
  36.7 7.1 %collective-permute-start.2 = (bf16[2,144,128]{2,1,0:T(8,128)(2,1)S(1)}, bf16[2,144,128]{2,1,0:T(8,128)(2,1)S(1)}, u32[]{:S(2)}, u32[]{:S(2)}) collective-permute-start(bf16[2,144,128]{2,1,0:T(8,128)(2,1)S(1)} %pad_maximum_fusion.13), channel_id=1, source_target_pairs={{0,4},{2,6},{4,0},{6,2},{1,5},{3,7},{5,1},{7,3},{8,12},{10,14},{12... | collective-permute-start | bytes 221192 | tf_op jit(solution)/shard_map/ppermute | solution.py:46
  38.6 10.1 %collective-permute-start.8 = (bf16[2,128,128]{2,1,0:T(8,128)(2,1)S(1)}, bf16[2,128,128]{2,1,0:T(8,128)(2,1)S(1)}, u32[]{:S(2)}, u32[]{:S(2)}) collective-permute-start(bf16[2,128,128]{2,1,0:T(8,128)(2,1)S(1)} %pad_maximum_fusion.14), channel_id=1, source_target_pairs={{0,64},{16,80},{32,96},{48,112},{64,0},{80,16},{96,32},{112,48},{1... | collective-permute-start | bytes 196616 | tf_op jit(solution)/shard_map/ppermute | solution.py:46
  43.8 8.9 %copy-start.2 = (f32[1024]{0:T(1024)S(1)}, f32[1024]{0:T(1024)}, u32[]{:S(2)}) copy-start(f32[1024]{0:T(1024)} %param.9) | copy-start | bytes 12292
  44.2 8.7 %collective-permute-start.4 = (bf16[1088,128]{1,0:T(8,128)(2,1)S(1)}, bf16[1088,128]{1,0:T(8,128)(2,1)S(1)}, u32[]{:S(2)}, u32[]{:S(2)}) collective-permute-start(bf16[1088,128]{1,0:T(8,128)(2,1)S(1)} %pad_maximum_fusion.5), channel_id=1, source_target_pairs={{0,128},{128,0},{256,384},{384,256},{1,129},{129,1},{257,385},{385... | collective-permute-start | bytes 835592 | tf_op jit(solution)/shard_map/ppermute | solution.py:46
  48.7 9.4 %collective-permute-start.9 = (bf16[2,2,128,128]{3,2,1,0:T(8,128)(2,1)S(1)}, bf16[2,2,128,128]{3,2,1,0:T(8,128)(2,1)S(1)}, u32[]{:S(2)}, u32[]{:S(2)}) collective-permute-start(bf16[2,2,128,128]{3,2,1,0:T(8,128)(2,1)S(1)} %pad_maximum_fusion.11), channel_id=1, source_target_pairs={{0,32},{16,48},{32,0},{48,16},{64,96},{80,112},{96,64},{112,80},{1... | collective-permute-start | bytes 393224 | tf_op jit(solution)/shard_map/ppermute | solution.py:46
  53.0 9.9 %collective-permute-start.5 = (bf16[2,4,144,128]{3,2,1,0:T(8,128)(2,1)S(1)}, bf16[2,4,144,128]{3,2,1,0:T(8,128)(2,1)S(1)}, u32[]{:S(2)}, u32[]{:S(2)}) collective-permute-start(bf16[2,4,144,128]{3,2,1,0:T(8,128)(2,1)S(1)} %pad_maximum_fusion.4), channel_id=1, source_target_pairs={{0,384},{128,256},{256,128},{384,0},{1,385},{129,257},{257,129},{3... | collective-permute-start | bytes 884744 | tf_op jit(solution)/shard_map/ppermute | solution.py:46
  58.2 8.3 %collective-permute-start.10 = (bf16[2,2,2,128,128]{4,3,2,0,1:T(8,128)(2,1)S(1)}, bf16[2,2,2,128,128]{4,3,2,0,1:T(8,128)(2,1)S(1)}, u32[]{:S(2)}, u32[]{:S(2)}) collective-permute-start(bf16[2,2,2,128,128]{4,3,2,0,1:T(8,128)(2,1)S(1)} %pad_maximum_fusion.6), channel_id=1, source_target_pairs={{0,16},{16,0},{32,48},{48,32},{64,80},{80,64},{96,112},{112,96},{1... | collective-permute-start | bytes 786440 | tf_op jit(solution)/shard_map/ppermute | solution.py:46
  62.9 4.0 %collective-permute-start.6 = (bf16[4,4,144,128]{3,2,1,0:T(8,128)(2,1)S(1)}, bf16[4,4,144,128]{3,2,1,0:T(8,128)(2,1)S(1)}, u32[]{:S(2)}, u32[]{:S(2)}) collective-permute-start(bf16[4,4,144,128]{3,2,1,0:T(8,128)(2,1)S(1)} %get-tuple-element.12), channel_id=1, source_target_pairs={{0,1},{1,0},{2,3},{3,2},{4,5},{5,4},{6,7},{7,6},{8,9},{9,8},{10,11... | collective-permute-start | bytes 1769480 | tf_op jit(solution)/shard_map/ppermute | solution.py:46
  69.6 36.8 %all-to-all-start = ((bf16[16,136,128]{2,1,0:T(8,128)(2,1)}), bf16[16,136,128]{2,1,0:T(8,128)(2,1)S(1)}, u32[]{:S(2)}, u32[]{:S(2)}) async-start(bf16[16,136,128]{2,1,0:T(8,128)(2,1)} %pad_maximum_fusion.2), calls=%async_computation | async-start | bytes 1114112 | tf_op jit(solution)/shard_map/all_to_all | solution.py:41
  75.7 8.3 %collective-permute-start.11 = (bf16[512,128]{1,0:T(8,128)(2,1)S(1)}, bf16[512,128]{1,0:T(8,128)(2,1)S(1)}, u32[]{:S(2)}, u32[]{:S(2)}) collective-permute-start(bf16[512,128]{1,0:T(8,128)(2,1)S(1)} %bitcast.151), channel_id=1, source_target_pairs={{0,384},{128,256},{256,128},{384,0},{1,385},{129,257},{257,129},{3... | collective-permute-start | bytes 393224 | tf_op jit(solution)/shard_map/ppermute | solution.py:46
  84.1 7.3 %copy-start = (bf16[128,1024]{1,0:T(8,128)(2,1)S(1)}, bf16[128,1024]{1,0:T(8,128)(2,1)}, u32[]{:S(2)}) copy-start(bf16[128,1024]{1,0:T(8,128)(2,1)} %param.5) | copy-start | bytes 786436
  84.3 6.9 %collective-permute-start.12 = (bf16[512,128]{1,0:T(8,128)(2,1)S(1)}, bf16[512,128]{1,0:T(8,128)(2,1)S(1)}, u32[]{:S(2)}, u32[]{:S(2)}) collective-permute-start(bf16[512,128]{1,0:T(8,128)(2,1)S(1)} %bitcast.150), channel_id=1, source_target_pairs={{0,128},{128,0},{256,384},{384,256},{1,129},{129,1},{257,385},{385... | collective-permute-start | bytes 393224 | tf_op jit(solution)/shard_map/ppermute | solution.py:46
  91.1 26.8 %copy-start.1 = (bf16[128,1024]{1,0:T(8,128)(2,1)S(1)}, bf16[128,1024]{1,0:T(8,128)(2,1)}, u32[]{:S(2)}) copy-start(bf16[128,1024]{1,0:T(8,128)(2,1)} %param.6) | copy-start | bytes 786436
  91.6 3.0 %collective-permute-start.13 = (f32[128]{0:T(128)S(1)}, f32[128]{0:T(128)S(1)}, u32[]{:S(2)}, u32[]{:S(2)}) collective-permute-start(f32[128]{0:T(128)S(1)} %fusion.4), channel_id=1, source_target_pairs={{0,1},{1,0},{2,3},{3,2},{4,5},{5,4},{6,7},{7,6},{8,9},{9,8},{10,11... | collective-permute-start | bytes 1544 | tf_op jit(solution)/shard_map/ppermute | solution.py:46
  94.6 5.4 %collective-permute-start.14 = (f32[128]{0:T(128)S(1)}, f32[128]{0:T(128)S(1)}, u32[]{:S(2)}, u32[]{:S(2)}) collective-permute-start(f32[128]{0:T(128)S(1)} %add.56), channel_id=1, source_target_pairs={{0,2},{2,0},{4,6},{6,4},{1,3},{3,1},{5,7},{7,5},{8,10},{10,8},{12,... | collective-permute-start | bytes 1544 | tf_op jit(solution)/shard_map/ppermute | solution.py:46
  100.0 6.4 %collective-permute-start.15 = (f32[128]{0:T(128)S(1)}, f32[128]{0:T(128)S(1)}, u32[]{:S(2)}, u32[]{:S(2)}) collective-permute-start(f32[128]{0:T(128)S(1)} %add.57), channel_id=1, source_target_pairs={{0,4},{2,6},{4,0},{6,2},{1,5},{3,7},{5,1},{7,3},{8,12},{10,14},{12... | collective-permute-start | bytes 1544 | tf_op jit(solution)/shard_map/ppermute | solution.py:46
  106.5 16.7 %collective-permute-start.16 = (f32[128,128]{1,0:T(8,128)S(1)}, f32[128,128]{1,0:T(8,128)S(1)}, u32[]{:S(2)}, u32[]{:S(2)}) collective-permute-start(f32[128,128]{1,0:T(8,128)S(1)} %convert_reduce_fusion.1), channel_id=1, source_target_pairs={{0,0},{16,1},{32,2},{48,3},{64,4},{80,5},{96,6},{112,7},{8,8},{24,... | collective-permute-start | bytes 196616 | tf_op jit(solution)/shard_map/ppermute | solution.py:129
  111.4 11.8 %all-to-all-start.1 = ((f32[4,2,128]{2,1,0:T(2,128)}), f32[4,2,128]{2,1,0:T(2,128)S(1)}, u32[]{:S(2)}, u32[]{:S(2)}) async-start(f32[4,2,128]{2,1,0:T(2,128)} %broadcast_in_dim.11), calls=%async_computation.1 | async-start | bytes 8192 | tf_op jit(solution)/shard_map/all_to_all | solution.py:41

commit v16 on v12

--- a/solution.py
+++ b/solution.py
@@ -146,8 +146,8 @@
     scaled = full.astype(jnp.float32) * norm_gain[None, :]
     normal = widened * inv_scale
     inner = jnp.sum(scaled * normal, axis=1)
-    for axis, mask in (("core", 1), ("zl", 1), ("zl", 2)):
-        inner = inner + swap(inner, axis, mask)
+    inner = inner + swap(inner, "core", 1)
+    inner = inner + swap(inner, "zl", 1) + swap(inner, "zl", 2) + swap(inner, "zl", 3)
     inner = inner[:, None] / D
     input_grad = (
         residual_grad.astype(jnp.float32) + inv_scale * (scaled - normal * inner)

time: 124 us -> 126 us (1.016)
  the two profiles are of different devices: /device:TPU:48 before, /device:TPU:6 now
where the time goes in v16:
time: 126 us; the launch traced here: 124 us
  starting transfers between devices  83.9 us (67%)
  waiting for transfers between devices  25.2 us (20%)
  other arithmetic  5.93 us (5%)
  local copies, waits for them, and re-layouts  5.85 us (5%)
  between operations  1.45 us (1%)
  matrix products  1.32 us (1%)
    ppermute x15, starting transfers between devices, swap(): return lax.ppermute(value, axis, [(i, i ^ mask) for i in range(count)])  49.6 us
    ppermute x15, waiting for transfers between devices, swap(): return lax.ppermute(value, axis, [(i, i ^ mask) for i in range(count)])  22.9 us
    ppermute x1, starting transfers between devices, shards(): moved = lax.ppermute(kv_weight, AXES, moves)  11.5 us
    all_to_all x2, starting transfers between devices, exchange(): return lax.all_to_all(value, axes, split_axis=0, concat_axis=0, tiled=True)  9.89 us
    ppermute x1, starting transfers between devices, shards(): other = lax.ppermute(kv_weight, AXES, [(a, b ^ 8) for a, b in moves])  7.5 us
    ppermute x1, starting transfers between devices, shards(): weight_grad = lax.ppermute(block, AXES, [(b, a) for a, b in moves])  5.42 us
  transfers between devices with their start and end apart: 20, of which 9 were waited for; matrix products, arithmetic and copies ran while one was open for 7% of the time, Pallas kernels for 0%

profile of v16, /device:TPU:6, one launch (start us, length us, event | category | flops | bytes accessed | tf_op | source)
XLA Modules:
  0.0 123.6 jit_solution(2338726372230358975)
XLA Ops:
  0.6 11.5 %collective-permute-start.1 = (bf16[128,128]{1,0:T(8,128)(2,1)}, bf16[128,128]{1,0:T(8,128)(2,1)S(1)}, u32[]{:S(2)}, u32[]{:S(2)}) collective-permute-start(bf16[128,128]{1,0:T(8,128)(2,1)} %param.8), channel_id=1, source_target_pairs={{0,0},{1,16},{2,32},{3,48},{4,64},{5,80},{6,96},{7,112},{8,8},{9,2... | collective-permute-start | bytes 98312 | tf_op jit(solution)/shard_map/ppermute | solution.py:67
  12.1 7.5 %collective-permute-start.2 = (bf16[128,128]{1,0:T(8,128)(2,1)}, bf16[128,128]{1,0:T(8,128)(2,1)S(1)}, u32[]{:S(2)}, u32[]{:S(2)}) collective-permute-start(bf16[128,128]{1,0:T(8,128)(2,1)} %param.8), channel_id=1, source_target_pairs={{0,8},{1,24},{2,40},{3,56},{4,72},{5,88},{6,104},{7,120},{8,0},{9,... | collective-permute-start | bytes 98312 | tf_op jit(solution)/shard_map/ppermute | solution.py:68
  19.7 1.1 fusion.9
  20.8 0.8 convert_element_type.61
  21.5 0.3 multiply_add_fusion
  21.8 0.9 fusion.15
  22.7 2.7 %collective-permute-start = (bf16[1,144,128]{2,1,0:T(8,128)(2,1)S(1)}, bf16[1,144,128]{2,1,0:T(8,128)(2,1)S(1)}, u32[]{:S(2)}, u32[]{:S(2)}) collective-permute-start(bf16[1,144,128]{2,1,0:T(8,128)(2,1)S(1)} %maximum_bitcast_fusion), channel_id=1, source_target_pairs={{0,2},{2,0},{4,6},{6,4},{1,3},{3,1},{5,7},{7,5},{8,10},{10,8},{12,... | collective-permute-start | bytes 110600 | tf_op jit(solution)/shard_map/ppermute | solution.py:46
  25.4 0.9 fusion.30
  26.3 0.1 copy.82
  26.5 0.1 copy.83
  26.6 0.1 copy.84
  26.7 0.1 copy.85
  26.8 0.1 copy.86
  27.0 0.1 copy.87
  27.1 0.1 copy.88
  27.2 0.1 copy.89
  27.5 0.1 copy.61
  27.7 1.9 %collective-permute-start.4 = (bf16[512,128]{1,0:T(8,128)(2,1)S(1)}, bf16[512,128]{1,0:T(8,128)(2,1)S(1)}, u32[]{:S(2)}, u32[]{:S(2)}) collective-permute-start(bf16[512,128]{1,0:T(8,128)(2,1)S(1)} %bitcast.147), channel_id=1, source_target_pairs={{0,384},{128,256},{256,128},{384,0},{1,385},{129,257},{257,129},{3... | collective-permute-start | bytes 393224 | tf_op jit(solution)/shard_map/ppermute | solution.py:46
  29.7 5.7 %collective-permute-start.3 = (bf16[2,144,128]{2,1,0:T(8,128)(2,1)S(1)}, bf16[2,144,128]{2,1,0:T(8,128)(2,1)S(1)}, u32[]{:S(2)}, u32[]{:S(2)}) collective-permute-start(bf16[2,144,128]{2,1,0:T(8,128)(2,1)S(1)} %pad_maximum_fusion.13), channel_id=1, source_target_pairs={{0,4},{2,6},{4,0},{6,2},{1,5},{3,7},{5,1},{7,3},{8,12},{10,14},{12... | collective-permute-start | bytes 221192 | tf_op jit(solution)/shard_map/ppermute | solution.py:46
  35.4 4.3 %collective-permute-start.8 = (bf16[2,128,128]{2,1,0:T(8,128)(2,1)S(1)}, bf16[2,128,128]{2,1,0:T(8,128)(2,1)S(1)}, u32[]{:S(2)}, u32[]{:S(2)}) collective-permute-start(bf16[2,128,128]{2,1,0:T(8,128)(2,1)S(1)} %pad_maximum_fusion.14), channel_id=1, source_target_pairs={{0,64},{16,80},{32,96},{48,112},{64,0},{80,16},{96,32},{112,48},{1... | collective-permute-start | bytes 196616 | tf_op jit(solution)/shard_map/ppermute | solution.py:46
  39.8 0.1 copy.62
  40.0 0.1 copy.63
  40.2 2.9 %collective-permute-start.5 = (bf16[1088,128]{1,0:T(8,128)(2,1)S(1)}, bf16[1088,128]{1,0:T(8,128)(2,1)S(1)}, u32[]{:S(2)}, u32[]{:S(2)}) collective-permute-start(bf16[1088,128]{1,0:T(8,128)(2,1)S(1)} %pad_maximum_fusion.5), channel_id=1, source_target_pairs={{0,128},{128,0},{256,384},{384,256},{1,129},{129,1},{257,385},{385... | collective-permute-start | bytes 835592 | tf_op jit(solution)/shard_map/ppermute | solution.py:46
  43.1 2.5 %collective-permute-done.8 = bf16[2,128,128]{2,1,0:T(8,128)(2,1)S(1)} collective-permute-done((bf16[2,128,128]{2,1,0:T(8,128)(2,1)S(1)}, bf16[2,128,128]{2,1,0:T(8,128)(2,1)S(1)}, u32[]{:S(2)}, u32[]{:S(2)}) %collective-permute-start.8) | collective-permute-done | bytes 65568 | tf_op jit(solution)/shard_map/ppermute | solution.py:46
  45.6 4.8 %collective-permute-start.9 = (bf16[2,2,128,128]{3,2,1,0:T(8,128)(2,1)S(1)}, bf16[2,2,128,128]{3,2,1,0:T(8,128)(2,1)S(1)}, u32[]{:S(2)}, u32[]{:S(2)}) collective-permute-start(bf16[2,2,128,128]{3,2,1,0:T(8,128)(2,1)S(1)} %pad_maximum_fusion.11), channel_id=1, source_target_pairs={{0,32},{16,48},{32,0},{48,16},{64,96},{80,112},{96,64},{112,80},{1... | collective-permute-start | bytes 393224 | tf_op jit(solution)/shard_map/ppermute | solution.py:46
  50.5 0.1 copy.71
  50.7 4.5 %collective-permute-start.6 = (bf16[2,4,144,128]{3,2,1,0:T(8,128)(2,1)S(1)}, bf16[2,4,144,128]{3,2,1,0:T(8,128)(2,1)S(1)}, u32[]{:S(2)}, u32[]{:S(2)}) collective-permute-start(bf16[2,4,144,128]{3,2,1,0:T(8,128)(2,1)S(1)} %pad_maximum_fusion.4), channel_id=1, source_target_pairs={{0,384},{128,256},{256,128},{384,0},{1,385},{129,257},{257,129},{3... | collective-permute-start | bytes 884744 | tf_op jit(solution)/shard_map/ppermute | solution.py:46
  55.2 0.5 collective-permute-done.9
  55.8 3.1 %collective-permute-start.10 = (bf16[2,2,2,128,128]{4,3,2,0,1:T(8,128)(2,1)S(1)}, bf16[2,2,2,128,128]{4,3,2,0,1:T(8,128)(2,1)S(1)}, u32[]{:S(2)}, u32[]{:S(2)}) collective-permute-start(bf16[2,2,2,128,128]{4,3,2,0,1:T(8,128)(2,1)S(1)} %pad_maximum_fusion.6), channel_id=1, source_target_pairs={{0,16},{16,0},{32,48},{48,32},{64,80},{80,64},{96,112},{112,96},{1... | collective-permute-start | bytes 786440 | tf_op jit(solution)/shard_map/ppermute | solution.py:46
  58.9 2.4 %collective-permute-done.6 = bf16[2,4,144,128]{3,2,1,0:T(8,128)(2,1)S(1)} collective-permute-done((bf16[2,4,144,128]{3,2,1,0:T(8,128)(2,1)S(1)}, bf16[2,4,144,128]{3,2,1,0:T(8,128)(2,1)S(1)}, u32[]{:S(2)}, u32[]{:S(2)}) %collective-permute-start.6) | collective-permute-done | bytes 294944 | tf_op jit(solution)/shard_map/ppermute | solution.py:46
  61.3 0.1 fusion.27
  61.4 1.9 %collective-permute-start.7 = (bf16[4,4,144,128]{3,2,1,0:T(8,128)(2,1)S(1)}, bf16[4,4,144,128]{3,2,1,0:T(8,128)(2,1)S(1)}, u32[]{:S(2)}, u32[]{:S(2)}) collective-permute-start(bf16[4,4,144,128]{3,2,1,0:T(8,128)(2,1)S(1)} %get-tuple-element.14), channel_id=1, source_target_pairs={{0,1},{1,0},{2,3},{3,2},{4,5},{5,4},{6,7},{7,6},{8,9},{9,8},{10,11... | collective-permute-start | bytes 1769480 | tf_op jit(solution)/shard_map/ppermute | solution.py:46
  63.3 0.1 copy.70
  63.4 0.1 copy.72
  63.6 1.8 %collective-permute-done.10 = bf16[2,2,2,128,128]{4,3,2,0,1:T(8,128)(2,1)S(1)} collective-permute-done((bf16[2,2,2,128,128]{4,3,2,0,1:T(8,128)(2,1)S(1)}, bf16[2,2,2,128,128]{4,3,2,0,1:T(8,128)(2,1)S(1)}, u32[]{:S(2)}, u32[]{:S(2)}) %collective-permute-start.10) | collective-permute-done | bytes 262176 | tf_op jit(solution)/shard_map/ppermute | solution.py:46
  65.5 0.3 copy.64
  65.8 0.1 fusion.1
  66.1 0.7 convert_reduce_fusion
  66.8 0.2 fusion.10
  67.0 0.6 fusion
  67.7 0.9 pad_maximum_fusion.2
  68.6 5.4 %all-to-all-start = ((bf16[16,136,128]{2,1,0:T(8,128)(2,1)}), bf16[16,136,128]{2,1,0:T(8,128)(2,1)S(1)}, u32[]{:S(2)}, u32[]{:S(2)}) async-start(bf16[16,136,128]{2,1,0:T(8,128)(2,1)} %pad_maximum_fusion.2), calls=%async_computation | async-start | bytes 1114112 | tf_op jit(solution)/shard_map/all_to_all | solution.py:41
  74.0 0.1 copy.67
  74.1 3.7 %collective-permute-start.11 = (bf16[512,128]{1,0:T(8,128)(2,1)S(1)}, bf16[512,128]{1,0:T(8,128)(2,1)S(1)}, u32[]{:S(2)}, u32[]{:S(2)}) collective-permute-start(bf16[512,128]{1,0:T(8,128)(2,1)S(1)} %bitcast.151), channel_id=1, source_target_pairs={{0,384},{128,256},{256,128},{384,0},{1,385},{129,257},{257,129},{3... | collective-permute-start | bytes 393224 | tf_op jit(solution)/shard_map/ppermute | solution.py:46
  77.9 4.6 %collective-permute-done.11 = bf16[512,128]{1,0:T(8,128)(2,1)S(1)} collective-permute-done((bf16[512,128]{1,0:T(8,128)(2,1)S(1)}, bf16[512,128]{1,0:T(8,128)(2,1)S(1)}, u32[]{:S(2)}, u32[]{:S(2)}) %collective-permute-start.11) | collective-permute-done | bytes 131104 | tf_op jit(solution)/shard_map/ppermute | solution.py:46
  82.5 0.1 copy.90
  82.6 0.1 copy.69
  82.8 1.9 %collective-permute-start.12 = (bf16[512,128]{1,0:T(8,128)(2,1)S(1)}, bf16[512,128]{1,0:T(8,128)(2,1)S(1)}, u32[]{:S(2)}, u32[]{:S(2)}) collective-permute-start(bf16[512,128]{1,0:T(8,128)(2,1)S(1)} %bitcast.150), channel_id=1, source_target_pairs={{0,128},{128,0},{256,384},{384,256},{1,129},{129,1},{257,385},{385... | collective-permute-start | bytes 393224 | tf_op jit(solution)/shard_map/ppermute | solution.py:46
  84.7 0.1 copy.66
  84.9 4.7 %collective-permute-done.12 = bf16[512,128]{1,0:T(8,128)(2,1)S(1)} collective-permute-done((bf16[512,128]{1,0:T(8,128)(2,1)S(1)}, bf16[512,128]{1,0:T(8,128)(2,1)S(1)}, u32[]{:S(2)}, u32[]{:S(2)}) %collective-permute-start.12) | collective-permute-done | bytes 131104 | tf_op jit(solution)/shard_map/ppermute | solution.py:46
  89.9 0.2 fusion.4
  90.1 1.9 %collective-permute-start.13 = (f32[128]{0:T(128)S(1)}, f32[128]{0:T(128)S(1)}, u32[]{:S(2)}, u32[]{:S(2)}) collective-permute-start(f32[128]{0:T(128)S(1)} %fusion.4), channel_id=1, source_target_pairs={{0,1},{1,0},{2,3},{3,2},{4,5},{5,4},{6,7},{7,6},{8,9},{9,8},{10,11... | collective-permute-start | bytes 1544 | tf_op jit(solution)/shard_map/ppermute | solution.py:46
  92.0 1.1 collective-permute-done.13
  93.1 3.3 %collective-permute-start.14 = (f32[128]{0:T(128)S(1)}, f32[128]{0:T(128)S(1)}, u32[]{:S(2)}, u32[]{:S(2)}) collective-permute-start(f32[128]{0:T(128)S(1)} %add.59), channel_id=1, source_target_pairs={{0,2},{2,0},{4,6},{6,4},{1,3},{3,1},{5,7},{7,5},{8,10},{10,8},{12,... | collective-permute-start | bytes 1544 | tf_op jit(solution)/shard_map/ppermute | solution.py:46
  96.4 4.8 %collective-permute-start.15 = (f32[128]{0:T(128)S(1)}, f32[128]{0:T(128)S(1)}, u32[]{:S(2)}, u32[]{:S(2)}) collective-permute-start(f32[128]{0:T(128)S(1)} %add.59), channel_id=1, source_target_pairs={{0,4},{2,6},{4,0},{6,2},{1,5},{3,7},{5,1},{7,3},{8,12},{10,14},{12... | collective-permute-start | bytes 1544 | tf_op jit(solution)/shard_map/ppermute | solution.py:46
  101.2 2.0 %collective-permute-start.16 = (f32[128]{0:T(128)S(1)}, f32[128]{0:T(128)S(1)}, u32[]{:S(2)}, u32[]{:S(2)}) collective-permute-start(f32[128]{0:T(128)S(1)} %add.59), channel_id=1, source_target_pairs={{0,6},{2,4},{4,2},{6,0},{1,7},{3,5},{5,3},{7,1},{8,14},{10,12},{12... | collective-permute-start | bytes 1544 | tf_op jit(solution)/shard_map/ppermute | solution.py:46
  103.3 5.2 %collective-permute-done.16 = f32[128]{0:T(128)S(1)} collective-permute-done((f32[128]{0:T(128)S(1)}, f32[128]{0:T(128)S(1)}, u32[]{:S(2)}, u32[]{:S(2)}) %collective-permute-start.16) | collective-permute-done | bytes 544 | tf_op jit(solution)/shard_map/ppermute | solution.py:46
  108.6 5.4 %collective-permute-start.17 = (f32[128,128]{1,0:T(8,128)S(1)}, f32[128,128]{1,0:T(8,128)S(1)}, u32[]{:S(2)}, u32[]{:S(2)}) collective-permute-start(f32[128,128]{1,0:T(8,128)S(1)} %convert_reduce_fusion.1), channel_id=1, source_target_pairs={{0,0},{16,1},{32,2},{48,3},{64,4},{80,5},{96,6},{112,7},{8,8},{24,... | collective-permute-start | bytes 196616 | tf_op jit(solution)/shard_map/ppermute | solution.py:131
  114.0 0.6 broadcast_in_dim.11
  114.6 4.5 %all-to-all-start.1 = ((f32[4,2,128]{2,1,0:T(2,128)}), f32[4,2,128]{2,1,0:T(2,128)S(1)}, u32[]{:S(2)}, u32[]{:S(2)}) async-start(f32[4,2,128]{2,1,0:T(2,128)} %broadcast_in_dim.11), calls=%async_computation.1 | async-start | bytes 8192 | tf_op jit(solution)/shard_map/all_to_all | solution.py:41
  119.2 1.0 fusion.8
  120.1 2.3 %all-to-all-done.1 = f32[4,2,128]{2,1,0:T(2,128)S(1)} async-done(((f32[4,2,128]{2,1,0:T(2,128)}), f32[4,2,128]{2,1,0:T(2,128)S(1)}, u32[]{:S(2)}, u32[]{:S(2)}) %all-to-all-start.1) | async-done | bytes 4128 | tf_op jit(solution)/shard_map/all_to_all | solution.py:41
  122.4 0.6 copy.111
  123.0 0.6 copy.112
  (83 shorter events, 1.3 us)
Async XLA Ops:
  0.6 29.0 %collective-permute-start.1 = (bf16[128,128]{1,0:T(8,128)(2,1)}, bf16[128,128]{1,0:T(8,128)(2,1)S(1)}, u32[]{:S(2)}, u32[]{:S(2)}) collective-permute-start(bf16[128,128]{1,0:T(8,128)(2,1)} %param.8), channel_id=1, source_target_pairs={{0,0},{1,16},{2,32},{3,48},{4,64},{5,80},{6,96},{7,112},{8,8},{9,2... | collective-permute-start | bytes 98312 | tf_op jit(solution)/shard_map/ppermute | solution.py:67
  12.1 17.5 %collective-permute-start.2 = (bf16[128,128]{1,0:T(8,128)(2,1)}, bf16[128,128]{1,0:T(8,128)(2,1)S(1)}, u32[]{:S(2)}, u32[]{:S(2)}) collective-permute-start(bf16[128,128]{1,0:T(8,128)(2,1)} %param.8), channel_id=1, source_target_pairs={{0,8},{1,24},{2,40},{3,56},{4,72},{5,88},{6,104},{7,120},{8,0},{9,... | collective-permute-start | bytes 98312 | tf_op jit(solution)/shard_map/ppermute | solution.py:68
  22.7 6.9 %collective-permute-start = (bf16[1,144,128]{2,1,0:T(8,128)(2,1)S(1)}, bf16[1,144,128]{2,1,0:T(8,128)(2,1)S(1)}, u32[]{:S(2)}, u32[]{:S(2)}) collective-permute-start(bf16[1,144,128]{2,1,0:T(8,128)(2,1)S(1)} %maximum_bitcast_fusion), channel_id=1, source_target_pairs={{0,2},{2,0},{4,6},{6,4},{1,3},{3,1},{5,7},{7,5},{8,10},{10,8},{12,... | collective-permute-start | bytes 110600 | tf_op jit(solution)/shard_map/ppermute | solution.py:46
  27.7 12.1 %collective-permute-start.4 = (bf16[512,128]{1,0:T(8,128)(2,1)S(1)}, bf16[512,128]{1,0:T(8,128)(2,1)S(1)}, u32[]{:S(2)}, u32[]{:S(2)}) collective-permute-start(bf16[512,128]{1,0:T(8,128)(2,1)S(1)} %bitcast.147), channel_id=1, source_target_pairs={{0,384},{128,256},{256,128},{384,0},{1,385},{129,257},{257,129},{3... | collective-permute-start | bytes 393224 | tf_op jit(solution)/shard_map/ppermute | solution.py:46
  29.7 10.1 %collective-permute-start.3 = (bf16[2,144,128]{2,1,0:T(8,128)(2,1)S(1)}, bf16[2,144,128]{2,1,0:T(8,128)(2,1)S(1)}, u32[]{:S(2)}, u32[]{:S(2)}) collective-permute-start(bf16[2,144,128]{2,1,0:T(8,128)(2,1)S(1)} %pad_maximum_fusion.13), channel_id=1, source_target_pairs={{0,4},{2,6},{4,0},{6,2},{1,5},{3,7},{5,1},{7,3},{8,12},{10,14},{12... | collective-permute-start | bytes 221192 | tf_op jit(solution)/shard_map/ppermute | solution.py:46
  35.4 10.2 %collective-permute-start.8 = (bf16[2,128,128]{2,1,0:T(8,128)(2,1)S(1)}, bf16[2,128,128]{2,1,0:T(8,128)(2,1)S(1)}, u32[]{:S(2)}, u32[]{:S(2)}) collective-permute-start(bf16[2,128,128]{2,1,0:T(8,128)(2,1)S(1)} %pad_maximum_fusion.14), channel_id=1, source_target_pairs={{0,64},{16,80},{32,96},{48,112},{64,0},{80,16},{96,32},{112,48},{1... | collective-permute-start | bytes 196616 | tf_op jit(solution)/shard_map/ppermute | solution.py:46
  39.8 10.6 %copy-start.2 = (f32[1024]{0:T(1024)S(1)}, f32[1024]{0:T(1024)}, u32[]{:S(2)}) copy-start(f32[1024]{0:T(1024)} %param.9) | copy-start | bytes 12292
  40.2 10.5 %collective-permute-start.5 = (bf16[1088,128]{1,0:T(8,128)(2,1)S(1)}, bf16[1088,128]{1,0:T(8,128)(2,1)S(1)}, u32[]{:S(2)}, u32[]{:S(2)}) collective-permute-start(bf16[1088,128]{1,0:T(8,128)(2,1)S(1)} %pad_maximum_fusion.5), channel_id=1, source_target_pairs={{0,128},{128,0},{256,384},{384,256},{1,129},{129,1},{257,385},{385... | collective-permute-start | bytes 835592 | tf_op jit(solution)/shard_map/ppermute | solution.py:46
  45.6 10.1 %collective-permute-start.9 = (bf16[2,2,128,128]{3,2,1,0:T(8,128)(2,1)S(1)}, bf16[2,2,128,128]{3,2,1,0:T(8,128)(2,1)S(1)}, u32[]{:S(2)}, u32[]{:S(2)}) collective-permute-start(bf16[2,2,128,128]{3,2,1,0:T(8,128)(2,1)S(1)} %pad_maximum_fusion.11), channel_id=1, source_target_pairs={{0,32},{16,48},{32,0},{48,16},{64,96},{80,112},{96,64},{112,80},{1... | collective-permute-start | bytes 393224 | tf_op jit(solution)/shard_map/ppermute | solution.py:46
  50.7 10.6 %collective-permute-start.6 = (bf16[2,4,144,128]{3,2,1,0:T(8,128)(2,1)S(1)}, bf16[2,4,144,128]{3,2,1,0:T(8,128)(2,1)S(1)}, u32[]{:S(2)}, u32[]{:S(2)}) collective-permute-start(bf16[2,4,144,128]{3,2,1,0:T(8,128)(2,1)S(1)} %pad_maximum_fusion.4), channel_id=1, source_target_pairs={{0,384},{128,256},{256,128},{384,0},{1,385},{129,257},{257,129},{3... | collective-permute-start | bytes 884744 | tf_op jit(solution)/shard_map/ppermute | solution.py:46
  55.8 9.6 %collective-permute-start.10 = (bf16[2,2,2,128,128]{4,3,2,0,1:T(8,128)(2,1)S(1)}, bf16[2,2,2,128,128]{4,3,2,0,1:T(8,128)(2,1)S(1)}, u32[]{:S(2)}, u32[]{:S(2)}) collective-permute-start(bf16[2,2,2,128,128]{4,3,2,0,1:T(8,128)(2,1)S(1)} %pad_maximum_fusion.6), channel_id=1, source_target_pairs={{0,16},{16,0},{32,48},{48,32},{64,80},{80,64},{96,112},{112,96},{1... | collective-permute-start | bytes 786440 | tf_op jit(solution)/shard_map/ppermute | solution.py:46
  61.4 4.4 %collective-permute-start.7 = (bf16[4,4,144,128]{3,2,1,0:T(8,128)(2,1)S(1)}, bf16[4,4,144,128]{3,2,1,0:T(8,128)(2,1)S(1)}, u32[]{:S(2)}, u32[]{:S(2)}) collective-permute-start(bf16[4,4,144,128]{3,2,1,0:T(8,128)(2,1)S(1)} %get-tuple-element.14), channel_id=1, source_target_pairs={{0,1},{1,0},{2,3},{3,2},{4,5},{5,4},{6,7},{7,6},{8,9},{9,8},{10,11... | collective-permute-start | bytes 1769480 | tf_op jit(solution)/shard_map/ppermute | solution.py:46
  68.6 39.9 %all-to-all-start = ((bf16[16,136,128]{2,1,0:T(8,128)(2,1)}), bf16[16,136,128]{2,1,0:T(8,128)(2,1)S(1)}, u32[]{:S(2)}, u32[]{:S(2)}) async-start(bf16[16,136,128]{2,1,0:T(8,128)(2,1)} %pad_maximum_fusion.2), calls=%async_computation | async-start | bytes 1114112 | tf_op jit(solution)/shard_map/all_to_all | solution.py:41
  74.1 8.4 %collective-permute-start.11 = (bf16[512,128]{1,0:T(8,128)(2,1)S(1)}, bf16[512,128]{1,0:T(8,128)(2,1)S(1)}, u32[]{:S(2)}, u32[]{:S(2)}) collective-permute-start(bf16[512,128]{1,0:T(8,128)(2,1)S(1)} %bitcast.151), channel_id=1, source_target_pairs={{0,384},{128,256},{256,128},{384,0},{1,385},{129,257},{257,129},{3... | collective-permute-start | bytes 393224 | tf_op jit(solution)/shard_map/ppermute | solution.py:46
  82.6 7.3 %copy-start = (bf16[128,1024]{1,0:T(8,128)(2,1)S(1)}, bf16[128,1024]{1,0:T(8,128)(2,1)}, u32[]{:S(2)}) copy-start(bf16[128,1024]{1,0:T(8,128)(2,1)} %param.5) | copy-start | bytes 786436
  82.8 6.9 %collective-permute-start.12 = (bf16[512,128]{1,0:T(8,128)(2,1)S(1)}, bf16[512,128]{1,0:T(8,128)(2,1)S(1)}, u32[]{:S(2)}, u32[]{:S(2)}) collective-permute-start(bf16[512,128]{1,0:T(8,128)(2,1)S(1)} %bitcast.150), channel_id=1, source_target_pairs={{0,128},{128,0},{256,384},{384,256},{1,129},{129,1},{257,385},{385... | collective-permute-start | bytes 393224 | tf_op jit(solution)/shard_map/ppermute | solution.py:46
  89.6 29.5 %copy-start.1 = (bf16[128,1024]{1,0:T(8,128)(2,1)S(1)}, bf16[128,1024]{1,0:T(8,128)(2,1)}, u32[]{:S(2)}) copy-start(bf16[128,1024]{1,0:T(8,128)(2,1)} %param.6) | copy-start | bytes 786436
  90.1 3.0 %collective-permute-start.13 = (f32[128]{0:T(128)S(1)}, f32[128]{0:T(128)S(1)}, u32[]{:S(2)}, u32[]{:S(2)}) collective-permute-start(f32[128]{0:T(128)S(1)} %fusion.4), channel_id=1, source_target_pairs={{0,1},{1,0},{2,3},{3,2},{4,5},{5,4},{6,7},{7,6},{8,9},{9,8},{10,11... | collective-permute-start | bytes 1544 | tf_op jit(solution)/shard_map/ppermute | solution.py:46
  93.1 10.1 %collective-permute-start.14 = (f32[128]{0:T(128)S(1)}, f32[128]{0:T(128)S(1)}, u32[]{:S(2)}, u32[]{:S(2)}) collective-permute-start(f32[128]{0:T(128)S(1)} %add.59), channel_id=1, source_target_pairs={{0,2},{2,0},{4,6},{6,4},{1,3},{3,1},{5,7},{7,5},{8,10},{10,8},{12,... | collective-permute-start | bytes 1544 | tf_op jit(solution)/shard_map/ppermute | solution.py:46
  96.4 6.9 %collective-permute-start.15 = (f32[128]{0:T(128)S(1)}, f32[128]{0:T(128)S(1)}, u32[]{:S(2)}, u32[]{:S(2)}) collective-permute-start(f32[128]{0:T(128)S(1)} %add.59), channel_id=1, source_target_pairs={{0,4},{2,6},{4,0},{6,2},{1,5},{3,7},{5,1},{7,3},{8,12},{10,14},{12... | collective-permute-start | bytes 1544 | tf_op jit(solution)/shard_map/ppermute | solution.py:46
  101.2 7.2 %collective-permute-start.16 = (f32[128]{0:T(128)S(1)}, f32[128]{0:T(128)S(1)}, u32[]{:S(2)}, u32[]{:S(2)}) collective-permute-start(f32[128]{0:T(128)S(1)} %add.59), channel_id=1, source_target_pairs={{0,6},{2,4},{4,2},{6,0},{1,7},{3,5},{5,3},{7,1},{8,14},{10,12},{12... | collective-permute-start | bytes 1544 | tf_op jit(solution)/shard_map/ppermute | solution.py:46
  108.6 13.8 %collective-permute-start.17 = (f32[128,128]{1,0:T(8,128)S(1)}, f32[128,128]{1,0:T(8,128)S(1)}, u32[]{:S(2)}, u32[]{:S(2)}) collective-permute-start(f32[128,128]{1,0:T(8,128)S(1)} %convert_reduce_fusion.1), channel_id=1, source_target_pairs={{0,0},{16,1},{32,2},{48,3},{64,4},{80,5},{96,6},{112,7},{8,8},{24,... | collective-permute-start | bytes 196616 | tf_op jit(solution)/shard_map/ppermute | solution.py:131
  114.6 7.7 %all-to-all-start.1 = ((f32[4,2,128]{2,1,0:T(2,128)}), f32[4,2,128]{2,1,0:T(2,128)S(1)}, u32[]{:S(2)}, u32[]{:S(2)}) async-start(f32[4,2,128]{2,1,0:T(2,128)} %broadcast_in_dim.11), calls=%async_computation.1 | async-start | bytes 8192 | tf_op jit(solution)/shard_map/all_to_all | solution.py:41
